TPU v7x, 32 devices: a whole 2x2x4 slice. The times are simulated.
32 devices in a mesh: section: 2 (over core), dp: 4 (over y, x), tensor: 4 (over z).
Axes of the slice: x: 2, y: 2, z: 4, core: 2. Of those that a mesh axis runs over, the one named last changes fastest.
Arguments:
- tokens: bfloat16 [8, 2048, 1024], P('dp', 'tensor'), may hold values from -6 to 6
- segment_ids: int32 [8, 2048], P('dp'), may hold values from 0 to 3, as said below
- cotangent: bfloat16 [8, 2048, 1024], P('dp', 'tensor'), may hold values from -6 to 6
- query_weight: bfloat16 [2, 1024, 1024], P('section', None, 'tensor'), may hold values from -0.1875 to 0.1875
- key_weight: bfloat16 [2, 1024, 1024], P('section', None, 'tensor'), may hold values from -0.1875 to 0.1875
- value_weight: bfloat16 [2, 1024, 1024], P('section', None, 'tensor'), may hold values from -0.1875 to 0.1875
- output_weight: bfloat16 [2, 1024, 1024], P('section', 'tensor'), may hold values from -0.75 to 0.75
- gate_weight: bfloat16 [2, 1024, 2816], P('section', None, 'tensor'), may hold values from -0.1875 to 0.1875
- up_weight: bfloat16 [2, 1024, 2816], P('section', None, 'tensor'), may hold values from -0.1875 to 0.1875
- down_weight: bfloat16 [2, 2816, 1024], P('section', 'tensor'), may hold values from -0.109375 to 0.109375
- attn_gain: float32 [2, 1024], P('section'), may hold values from 0.5 to 1.5
- mlp_gain: float32 [2, 1024], P('section'), may hold values from 0.5 to 1.5
Outputs:
- activations: bfloat16 [8, 2048, 1024], P('dp', 'tensor')
- input_grad: float32 [8, 2048, 1024], P('dp', 'tensor', 'section')
- grad_query: float32 [2, 1024, 1024], P('section', 'dp', 'tensor')
- grad_key: float32 [2, 1024, 1024], P('section', 'dp', 'tensor')
- grad_value: float32 [2, 1024, 1024], P('section', 'dp', 'tensor')
- grad_output: float32 [2, 1024, 1024], P('section', 'tensor', 'dp')
- grad_gate: float32 [2, 1024, 2816], P('section', 'dp', 'tensor')
- grad_up: float32 [2, 1024, 2816], P('section', 'dp', 'tensor')
- grad_down: float32 [2, 2816, 1024], P('section', 'tensor', 'dp')
- grad_attn_gain: float32 [2, 1024], P('section', ('dp', 'tensor'))
- grad_mlp_gain: float32 [2, 1024], P('section', ('dp', 'tensor'))
- grad_norm: float32 [2], P('section')
Inputs may be any that keep to these rules, and one draw needn't show every extreme that they name: `segment_ids`: segment numbers never fall along a row; they are 0 at the first position and 3 at the last. In each group of 2 rows that one index of dp holds, one row drawn from the seed has a document that starts within the first sixteenth of 2048 positions and ends within the last sixteenth.
All inputs are finite; a program needn't handle non-finite values.
Results may differ from a plain program's by a relative error of at most 0.025.
Values may be sent and summed in bfloat16 or wider, within the bound.
No kernel may reach another device: no remote copies, remote signals or barrier semaphores. Data moves between devices by JAX's collectives and lax.ppermute only.
A program may use at most 320 MiB of HBM per device.

v0:
```python
import jax
import jax.numpy as jnp
from jax import lax
from jax.sharding import PartitionSpec as P

HEAD_DIM = 64


epsilon = 1e-05
rope_base = 10000.0
masked_score = -1e30


def shifted(block, axis, distance):
    devices = range(lax.axis_size(axis))
    route = [((i - distance) % len(devices), i) for i in devices]
    return lax.ppermute(block, axis, route)


def matmul(left, right):
    return jnp.dot(left, right, preferred_element_type=jnp.float32)


def matmul_lead(left, right):
    return lax.dot_general(
        left, right, (((0,), (0,)), ((), ())), preferred_element_type=jnp.float32
    )


def matmul_tail(left, right):
    return lax.dot_general(
        left, right, (((1,), (1,)), ((), ())), preferred_element_type=jnp.float32
    )


def norm_forward(inputs, gain):
    inverse = lax.rsqrt(jnp.mean(inputs * inputs, axis=-1, keepdims=True) + epsilon)
    return (inputs * inverse * gain, inverse)


def norm_backward(inputs, inverse, gain, grad_rows):
    normed = inputs * inverse
    scaled_grad = grad_rows * gain
    gain_grad = jnp.sum(grad_rows * normed, axis=0)
    input_grad = inverse * (
        scaled_grad - normed * jnp.mean(scaled_grad * normed, axis=-1, keepdims=True)
    )
    return (input_grad, gain_grad)


def rope_tables(length, width):
    half_width = width // 2
    frequency = rope_base ** (-jnp.arange(half_width, dtype=jnp.float32) / half_width)
    angles = jnp.arange(length, dtype=jnp.float32)[:, None] * frequency[None, :]
    return (jnp.cos(angles), jnp.sin(angles))


def rotate(tensor, cosine_table, sine_table, direction):
    half_width = tensor.shape[-1] // 2
    first_half = tensor[..., :half_width]
    second_half = tensor[..., half_width:]
    cosine = cosine_table[:, None, :]
    sine_part = sine_table[:, None, :] * direction
    return jnp.concatenate(
        [
            first_half * cosine - second_half * sine_part,
            second_half * cosine + first_half * sine_part,
        ],
        axis=-1,
    )


def block_mask(segments, row_start, block_rows):
    length = segments.shape[0]
    query_segments = lax.dynamic_slice_in_dim(segments, row_start, block_rows, 0)
    query_places = row_start + jnp.arange(block_rows, dtype=jnp.int32)
    key_places = jnp.arange(length, dtype=jnp.int32)
    return (query_segments[:, None] == segments[None, :]) & (
        key_places[None, :] <= query_places[:, None]
    )


def attend_forward(query_rows, key_rows, value_rows, segments):
    length, heads, head_width = query_rows.shape
    block_rows = min(512, length)
    score_scale = head_width ** (-0.5)

    def one_block(block_index):
        row_start = block_index * block_rows
        query_block = lax.dynamic_slice_in_dim(query_rows, row_start, block_rows, 0)
        scores = (
            jnp.einsum("qhd,khd->hqk", query_block, key_rows, preferred_element_type=jnp.float32)
            * score_scale
        )
        scores = jnp.where(block_mask(segments, row_start, block_rows)[None], scores, masked_score)
        row_max = jnp.max(scores, axis=-1, keepdims=True)
        exponent = jnp.exp(scores - row_max)
        row_total = jnp.sum(exponent, axis=-1, keepdims=True)
        weights_low = (exponent / row_total).astype(jnp.bfloat16)
        attended = jnp.einsum(
            "hqk,khd->qhd", weights_low, value_rows, preferred_element_type=jnp.float32
        )
        return (attended, (row_max + jnp.log(row_total))[..., 0])

    attended, log_totals = lax.map(one_block, jnp.arange(length // block_rows, dtype=jnp.int32))
    attended = attended.reshape(length, heads, head_width)
    log_totals = jnp.transpose(log_totals, (1, 0, 2)).reshape(heads, length)
    return (attended, log_totals)


def attend_backward(query_rows, key_rows, value_rows, segments, log_totals, grad_rows):
    length, heads, head_width = query_rows.shape
    block_rows = min(512, length)
    score_scale = head_width ** (-0.5)

    def one_block(carry, block_index):
        key_grad, value_grad = carry
        row_start = block_index * block_rows
        query_block = lax.dynamic_slice_in_dim(query_rows, row_start, block_rows, 0)
        grad_block = lax.dynamic_slice_in_dim(grad_rows, row_start, block_rows, 0)
        block_totals = lax.dynamic_slice_in_dim(log_totals, row_start, block_rows, 1)
        scores = (
            jnp.einsum("qhd,khd->hqk", query_block, key_rows, preferred_element_type=jnp.float32)
            * score_scale
        )
        allowed = block_mask(segments, row_start, block_rows)[None]
        probabilities = jnp.where(allowed, jnp.exp(scores - block_totals[..., None]), 0.0)
        prob_grad = jnp.einsum(
            "qhd,khd->hqk", grad_block, value_rows, preferred_element_type=jnp.float32
        )
        score_grad = probabilities * (
            prob_grad - jnp.sum(probabilities * prob_grad, axis=-1, keepdims=True)
        )
        score_low = score_grad.astype(jnp.bfloat16)
        query_grad = (
            jnp.einsum("hqk,khd->qhd", score_low, key_rows, preferred_element_type=jnp.float32)
            * score_scale
        )
        key_grad = (
            key_grad
            + jnp.einsum("hqk,qhd->khd", score_low, query_block, preferred_element_type=jnp.float32)
            * score_scale
        )
        value_grad = value_grad + jnp.einsum(
            "hqk,qhd->khd",
            probabilities.astype(jnp.bfloat16),
            grad_block,
            preferred_element_type=jnp.float32,
        )
        return ((key_grad, value_grad), query_grad)

    zeros_heads = jnp.zeros(query_rows.shape, jnp.float32)
    (key_grad, value_grad), query_grad = lax.scan(
        one_block, (zeros_heads, zeros_heads), jnp.arange(length // block_rows, dtype=jnp.int32)
    )
    return (query_grad.reshape(query_rows.shape), key_grad, value_grad)


def mlp_backward(mlp_rows, gate_pre, up_pre, rows_grad, w_gate, w_up, w_down):
    sigmoid_gate = jax.nn.sigmoid(gate_pre)
    activated = gate_pre * sigmoid_gate
    product = (activated * up_pre).astype(jnp.bfloat16)
    down_grad = matmul_lead(product, rows_grad)
    product_grad = matmul_tail(rows_grad, w_down)
    gate_low = (
        product_grad * up_pre * sigmoid_gate * (1.0 + gate_pre * (1.0 - sigmoid_gate))
    ).astype(jnp.bfloat16)
    up_low = (product_grad * activated).astype(jnp.bfloat16)
    gate_grad = matmul_lead(mlp_rows, gate_low)
    up_grad = matmul_lead(mlp_rows, up_low)
    partial_rows = matmul_tail(gate_low, w_gate) + matmul_tail(up_low, w_up)
    return (gate_grad, up_grad, down_grad, partial_rows)


def layer_forward(inputs, segments, first_values, weights, is_later, tables):
    w_query, w_key, w_value, w_output, w_gate, w_up, w_down, gain_attn, gain_mlp = weights
    cosine_table, sine_table = tables
    normed, attn_inverse = norm_forward(inputs, gain_attn)
    gathered = lax.all_gather(normed.astype(jnp.bfloat16), "tensor", axis=0, tiled=True)
    length = gathered.shape[0]
    heads = w_query.shape[1] // HEAD_DIM
    shape_heads = (length, heads, HEAD_DIM)
    query_rows = rotate(
        matmul(gathered, w_query).reshape(shape_heads), cosine_table, sine_table, 1.0
    ).astype(jnp.bfloat16)
    key_rows = rotate(
        matmul(gathered, w_key).reshape(shape_heads), cosine_table, sine_table, 1.0
    ).astype(jnp.bfloat16)
    raw_values = matmul(gathered, w_value)
    mixed_values = jnp.where(
        is_later, 0.5 * raw_values + 0.5 * first_values.astype(jnp.float32), raw_values
    ).astype(jnp.bfloat16)
    attended, log_totals = attend_forward(
        query_rows, key_rows, mixed_values.reshape(shape_heads), segments
    )
    attended = attended.reshape(length, heads * HEAD_DIM).astype(jnp.bfloat16)
    hidden_state = inputs + lax.psum_scatter(
        matmul(attended, w_output), "tensor", scatter_dimension=0, tiled=True
    )
    normed_mlp, mlp_inverse = norm_forward(hidden_state, gain_mlp)
    mlp_rows = lax.all_gather(normed_mlp.astype(jnp.bfloat16), "tensor", axis=0, tiled=True)
    gate_pre = matmul(mlp_rows, w_gate)
    up_pre = matmul(mlp_rows, w_up)
    product = (jax.nn.silu(gate_pre) * up_pre).astype(jnp.bfloat16)
    layer_out = hidden_state + lax.psum_scatter(
        matmul(product, w_down).astype(jnp.bfloat16), "tensor", scatter_dimension=0, tiled=True
    ).astype(jnp.float32)
    kept = (
        inputs,
        attn_inverse,
        gathered,
        query_rows,
        key_rows,
        mixed_values,
        attended,
        log_totals,
        hidden_state,
        mlp_inverse,
        mlp_rows,
        gate_pre,
        up_pre,
    )
    return (layer_out, mixed_values, kept)


def layer_backward(kept, segments, grad_out, grad_first, weights, is_later, tables):
    w_query, w_key, w_value, w_output, w_gate, w_up, w_down, gain_attn, gain_mlp = weights
    cosine_table, sine_table = tables
    (
        inputs,
        attn_inverse,
        gathered,
        query_rows,
        key_rows,
        mixed_values,
        attended,
        log_totals,
        hidden_state,
        mlp_inverse,
        mlp_rows,
        gate_pre,
        up_pre,
    ) = kept
    length = gathered.shape[0]
    heads = w_query.shape[1] // HEAD_DIM
    shape_heads = (length, heads, HEAD_DIM)
    grad_low = grad_out.astype(jnp.bfloat16)
    rows_grad = lax.all_gather(grad_low, "tensor", axis=0, tiled=True)
    gate_grad, up_grad, down_grad, partial_rows = mlp_backward(
        mlp_rows, gate_pre, up_pre, rows_grad, w_gate, w_up, w_down
    )
    mlp_input_rows = lax.psum_scatter(
        partial_rows.astype(jnp.bfloat16), "tensor", scatter_dimension=0, tiled=True
    ).astype(jnp.float32)
    mlp_norm_grad, mlp_gain_grad = norm_backward(
        hidden_state, mlp_inverse, gain_mlp, mlp_input_rows
    )
    hidden_grad = grad_out + mlp_norm_grad
    branch_grad = lax.all_gather(hidden_grad.astype(jnp.bfloat16), "tensor", axis=0, tiled=True)
    output_grad = matmul_lead(attended, branch_grad)
    attended_grad = matmul_tail(branch_grad, w_output).astype(jnp.bfloat16)
    query_grad, key_grad, value_grad = attend_backward(
        query_rows,
        key_rows,
        mixed_values.reshape(shape_heads),
        segments,
        log_totals,
        attended_grad.reshape(shape_heads),
    )
    query_low = (
        rotate(query_grad, cosine_table, sine_table, -1.0)
        .reshape(length, heads * HEAD_DIM)
        .astype(jnp.bfloat16)
    )
    key_low = (
        rotate(key_grad, cosine_table, sine_table, -1.0)
        .reshape(length, heads * HEAD_DIM)
        .astype(jnp.bfloat16)
    )
    value_grad = value_grad.reshape(length, heads * HEAD_DIM)
    value_low = jnp.where(is_later, 0.5 * value_grad, value_grad + grad_first).astype(jnp.bfloat16)
    query_weight_grad = matmul_lead(gathered, query_low)
    key_weight_grad = matmul_lead(gathered, key_low)
    value_weight_grad = matmul_lead(gathered, value_low)
    partial_rows_attn = (
        matmul_tail(query_low, w_query)
        + matmul_tail(key_low, w_key)
        + matmul_tail(value_low, w_value)
    )
    attn_input_rows = lax.psum_scatter(
        partial_rows_attn.astype(jnp.bfloat16), "tensor", scatter_dimension=0, tiled=True
    ).astype(jnp.float32)
    attn_norm_grad, attn_gain_grad = norm_backward(inputs, attn_inverse, gain_attn, attn_input_rows)
    grads = (
        query_weight_grad,
        key_weight_grad,
        value_weight_grad,
        output_grad,
        gate_grad,
        up_grad,
        down_grad,
    )
    return (hidden_grad + attn_norm_grad, 0.5 * value_grad, grads, attn_gain_grad, mlp_gain_grad)


def per_device(
    tokens,
    segment_ids,
    cotangent,
    query_weight,
    key_weight,
    value_weight,
    output_weight,
    gate_weight,
    up_weight,
    down_weight,
    attn_gain,
    mlp_gain,
):
    section_index = lax.axis_index("section")
    is_later = section_index == 1
    micro_count = tokens.shape[0]
    local_rows = tokens.shape[1]
    width = tokens.shape[2]
    seq_length = segment_ids.shape[1]
    gate_used, up_used, down_used = (gate_weight[0], up_weight[0], down_weight[0])
    weights = (
        query_weight[0],
        key_weight[0],
        value_weight[0],
        output_weight[0],
        gate_used,
        up_used,
        down_used,
        attn_gain[0],
        mlp_gain[0],
    )
    tables = rope_tables(seq_length, HEAD_DIM)
    value_cols = query_weight.shape[2]
    received_rows = jnp.zeros((local_rows, width), jnp.bfloat16)
    received_values = jnp.zeros((seq_length, value_cols), jnp.bfloat16)
    stash = []
    outputs_list = []
    for step_index in range(micro_count + 1):
        own_rows = tokens[min(step_index, micro_count - 1)].astype(jnp.float32)
        layer_in = jnp.where(is_later, received_rows.astype(jnp.float32), own_rows)
        micro_index = jnp.clip(step_index - section_index, 0, micro_count - 1)
        segments = lax.dynamic_index_in_dim(segment_ids, micro_index, 0, keepdims=False)
        layer_out, mixed_values, kept = layer_forward(
            layer_in, segments, received_values, weights, is_later, tables
        )
        out_low = layer_out.astype(jnp.bfloat16)
        received_rows, received_values = shifted((out_low, mixed_values), "section", 1)
        stash.append((kept, segments))
        if step_index >= 1:
            outputs_list.append(jnp.where(is_later, out_low, received_rows))
    grad_sums = tuple((jnp.zeros(weight.shape, jnp.float32) for weight in weights[:7]))
    attn_gain_sum = jnp.zeros((width,), jnp.float32)
    mlp_gain_sum = jnp.zeros((width,), jnp.float32)
    received_grad = jnp.zeros((local_rows, width), jnp.float32)
    received_value_grad = jnp.zeros((seq_length, value_cols), jnp.float32)
    half_width = width // 2
    column_start = section_index * half_width
    input_list = [None] * micro_count
    for step_index in range(micro_count + 1):
        kept, segments = stash[micro_count - step_index]
        micro_index = micro_count - step_index - section_index
        valid = ((micro_index >= 0) & (micro_index < micro_count)).astype(jnp.float32)
        later_grad = cotangent[min(max(micro_count - 1 - step_index, 0), micro_count - 1)].astype(
            jnp.float32
        )
        grad_out = jnp.where(is_later, later_grad, received_grad)
        input_grad, value_send, grads, attn_gain_grad, mlp_gain_grad = layer_backward(
            kept, segments, grad_out, received_value_grad, weights, is_later, tables
        )
        grad_sums = tuple((total + valid * term for total, term in zip(grad_sums, grads)))
        attn_gain_sum = attn_gain_sum + valid * attn_gain_grad
        mlp_gain_sum = mlp_gain_sum + valid * mlp_gain_grad
        received_grad, received_value_grad = (
            shifted(input_grad.astype(jnp.bfloat16), "section", 1).astype(input_grad.dtype),
            shifted(value_send.astype(jnp.bfloat16), "section", 1).astype(value_send.dtype),
        )
        if step_index >= 1:
            whole_grad = jnp.where(is_later, received_grad, input_grad)
            input_list[micro_count - step_index] = lax.dynamic_slice_in_dim(
                whole_grad, column_start, half_width, 1
            )
    activations = jnp.stack(outputs_list)
    input_grads = jnp.stack(input_list)
    gate_sum, up_sum, down_sum = (grad_sums[4], grad_sums[5], grad_sums[6])
    reduced = (
        lax.psum_scatter(
            grad_sums[0].astype(jnp.bfloat16), "dp", scatter_dimension=0, tiled=True
        ).astype(jnp.float32),
        lax.psum_scatter(
            grad_sums[1].astype(jnp.bfloat16), "dp", scatter_dimension=0, tiled=True
        ).astype(jnp.float32),
        lax.psum_scatter(
            grad_sums[2].astype(jnp.bfloat16), "dp", scatter_dimension=0, tiled=True
        ).astype(jnp.float32),
        lax.psum_scatter(
            grad_sums[3].astype(jnp.bfloat16), "dp", scatter_dimension=1, tiled=True
        ).astype(jnp.float32),
        lax.psum_scatter(
            gate_sum.astype(jnp.bfloat16), "dp", scatter_dimension=0, tiled=True
        ).astype(jnp.float32),
        lax.psum_scatter(up_sum.astype(jnp.bfloat16), "dp", scatter_dimension=0, tiled=True).astype(
            jnp.float32
        ),
        lax.psum_scatter(
            down_sum.astype(jnp.bfloat16), "dp", scatter_dimension=1, tiled=True
        ).astype(jnp.float32),
    )
    weight_square = jnp.sum(jnp.stack([jnp.sum(piece * piece) for piece in reduced]))
    gain_rows = jnp.stack([attn_gain_sum, mlp_gain_sum])
    gain_total, weight_total = lax.psum((gain_rows, weight_square), ("dp", "tensor"))
    grad_norm = jnp.sqrt(weight_total + jnp.sum(gain_total * gain_total)).reshape(1)
    shard_width = width // (lax.axis_size("dp") * lax.axis_size("tensor"))
    offset = (
        lax.axis_index("dp") * lax.axis_size("tensor") + lax.axis_index("tensor")
    ) * shard_width
    attn_gain_out = lax.dynamic_slice_in_dim(gain_total[0], offset, shard_width, 0)[None]
    mlp_gain_out = lax.dynamic_slice_in_dim(gain_total[1], offset, shard_width, 0)[None]
    return (
        activations,
        input_grads,
        reduced[0][None],
        reduced[1][None],
        reduced[2][None],
        reduced[3][None],
        reduced[4][None],
        reduced[5][None],
        reduced[6][None],
        attn_gain_out,
        mlp_gain_out,
        grad_norm,
    )


def solution(mesh):
    return jax.shard_map(
        per_device,
        mesh=mesh,
        in_specs=(
            P("dp", "tensor", None),
            P("dp", None),
            P("dp", "tensor", None),
            P("section", None, "tensor"),
            P("section", None, "tensor"),
            P("section", None, "tensor"),
            P("section", "tensor", None),
            P("section", None, "tensor"),
            P("section", None, "tensor"),
            P("section", "tensor", None),
            P("section", None),
            P("section", None),
        ),
        out_specs=(
            P("dp", "tensor", None),
            P("dp", "tensor", "section"),
            P("section", "dp", "tensor"),
            P("section", "dp", "tensor"),
            P("section", "dp", "tensor"),
            P("section", "tensor", "dp"),
            P("section", "dp", "tensor"),
            P("section", "dp", "tensor"),
            P("section", "tensor", "dp"),
            P("section", ("dp", "tensor")),
            P("section", ("dp", "tensor")),
            P("section"),
        ),
        check_vma=False,
    )
```

profile of v0, /device:TPU:0, one launch (start us, length us, event | category | flops | bytes accessed | tf_op | source)
XLA Modules:
  0.0 3632.1 jit_solution(11096114126577810040)
XLA Ops:
  14.7 80.5 %all-gather.13.cloned.1.call-done = bf16[2048,1024]{1,0:T(8,128)(2,1)} async-done(((bf16[512,1024]{1,0:T(8,128)(2,1)}), bf16[2048,1024]{1,0:T(8,128)(2,1)}) %all-gather.13.cloned.1.call-update) | async-done | bytes 4194320 | tf_op jit(solution)/shard_map/all_gather | solution.py:179
  105.1 68.5 %while.81 = (s32[]{:T(128)}, bf16[4,512,4,64]{1,3,2,0:T(8,128)(2,1)}, f32[4,4,512]{2,1,0:T(4,128)}, s32[4]{0:T(128)S(1)}, s32[2048]{0:T(1024)S(1)}, /*index=5*/b...) while((s32[]{:T(128)}, ...), condition=%wide.region_4.5_spmd, body=%wide.region_1.4_spmd.sunk | while | flops 1127217664 | bytes 65882372 | solution.py:105
  182.5 143.1 %reduce-scatter.20.cloned.1.call-done = f32[512,1024]{1,0:T(8,128)} async-done(((f32[2048,1024]{1,0:T(8,128)}), f32[512,1024]{1,0:T(8,128)}) %reduce-scatter.20.cloned.1.call-update) | async-done | bytes 2097168 | tf_op jit(solution)/shard_map/reduce_scatter | solution.py:197
  330.2 81.6 %all-gather.15.cloned.1.call-done = bf16[2048,1024]{1,0:T(8,128)(2,1)} async-done(((bf16[512,1024]{1,0:T(8,128)(2,1)}), bf16[2048,1024]{1,0:T(8,128)(2,1)}) %all-gather.15.cloned.1.call-update) | async-done | bytes 4194320 | tf_op jit(solution)/shard_map/all_gather | solution.py:201
  429.7 75.4 %reduce-scatter.22.cloned.1.call-done = bf16[512,1024]{1,0:T(8,128)(2,1)} async-done(((bf16[2048,1024]{1,0:T(8,128)(2,1)}), bf16[512,1024]{1,0:T(8,128)(2,1)}) %reduce-scatter.22.cloned.1.call-update) | async-done | bytes 1048592 | tf_op jit(solution)/shard_map/reduce_scatter | solution.py:205
  513.3 81.2 %all-gather.17.cloned.1.call-done = bf16[2048,1024]{1,0:T(8,128)(2,1)} async-done(((bf16[512,1024]{1,0:T(8,128)(2,1)}), bf16[2048,1024]{1,0:T(8,128)(2,1)}) %all-gather.17.cloned.1.call-update) | async-done | bytes 4194320 | tf_op jit(solution)/shard_map/all_gather | solution.py:179
  605.8 68.5 %while.82 = (s32[]{:T(128)}, bf16[4,512,4,64]{1,3,2,0:T(8,128)(2,1)}, f32[4,4,512]{2,1,0:T(4,128)}, s32[4]{0:T(128)S(1)}, s32[2048]{0:T(1024)S(1)}, /*index=5*/b...) while((s32[]{:T(128)}, ...), condition=%wide.region_12.13_spmd, body=%wide.region_9.12_spmd.sunk | while | flops 1127217664 | bytes 65882372 | solution.py:105
  683.2 143.1 %reduce-scatter.24.cloned.1.call-done = f32[512,1024]{1,0:T(8,128)} async-done(((f32[2048,1024]{1,0:T(8,128)}), f32[512,1024]{1,0:T(8,128)}) %reduce-scatter.24.cloned.1.call-update) | async-done | bytes 2097168 | tf_op jit(solution)/shard_map/reduce_scatter | solution.py:197
  831.3 81.6 %all-gather.19.cloned.1.call-done = bf16[2048,1024]{1,0:T(8,128)(2,1)} async-done(((bf16[512,1024]{1,0:T(8,128)(2,1)}), bf16[2048,1024]{1,0:T(8,128)(2,1)}) %all-gather.19.cloned.1.call-update) | async-done | bytes 4194320 | tf_op jit(solution)/shard_map/all_gather | solution.py:201
  931.1 75.4 %reduce-scatter.26.cloned.1.call-done = bf16[512,1024]{1,0:T(8,128)(2,1)} async-done(((bf16[2048,1024]{1,0:T(8,128)(2,1)}), bf16[512,1024]{1,0:T(8,128)(2,1)}) %reduce-scatter.26.cloned.1.call-update) | async-done | bytes 1048592 | tf_op jit(solution)/shard_map/reduce_scatter | solution.py:205
  1014.7 81.1 %all-gather.21.cloned.1.call-done = bf16[2048,1024]{1,0:T(8,128)(2,1)} async-done(((bf16[512,1024]{1,0:T(8,128)(2,1)}), bf16[2048,1024]{1,0:T(8,128)(2,1)}) %all-gather.21.cloned.1.call-update) | async-done | bytes 4194320 | tf_op jit(solution)/shard_map/all_gather | solution.py:179
  1107.7 71.1 %while.83 = (s32[]{:T(128)}, bf16[4,512,4,64]{1,3,2,0:T(8,128)(2,1)}, f32[4,4,512]{2,1,0:T(4,128)}, s32[4]{0:T(128)}, s32[2048]{0:T(1024)S(1)}, /*index=5*/bf16[...) while((s32[]{:T(128)}, ...), condition=%wide.region_20.21_spmd, body=%wide.region_17.20_spmd.sunk | while | flops 1127217664 | bytes 65882372 | solution.py:105
  1189.9 140.5 %reduce-scatter.28.cloned.1.call-done = f32[512,1024]{1,0:T(8,128)} async-done(((f32[2048,1024]{1,0:T(8,128)}), f32[512,1024]{1,0:T(8,128)}) %reduce-scatter.28.cloned.1.call-update) | async-done | bytes 2097168 | tf_op jit(solution)/shard_map/reduce_scatter | solution.py:197
  1335.3 78.7 %all-gather.25.cloned.1.call-done = bf16[2048,1024]{1,0:T(8,128)(2,1)} async-done(((bf16[512,1024]{1,0:T(8,128)(2,1)}), bf16[2048,1024]{1,0:T(8,128)(2,1)}) %all-gather.25.cloned.1.call-update) | async-done | bytes 4194320 | tf_op jit(solution)/shard_map/all_gather | solution.py:248
  1421.7 73.7 %all-gather.23.cloned.1.call-done = bf16[2048,1024]{1,0:T(8,128)(2,1)} async-done(((bf16[512,1024]{1,0:T(8,128)(2,1)}), bf16[2048,1024]{1,0:T(8,128)(2,1)}) %all-gather.23.cloned.1.call-update) | async-done | bytes 4194320 | tf_op jit(solution)/shard_map/all_gather | solution.py:201
  1517.2 75.4 %reduce-scatter.32.cloned.1.call-done = bf16[512,1024]{1,0:T(8,128)(2,1)} async-done(((bf16[2048,1024]{1,0:T(8,128)(2,1)}), bf16[512,1024]{1,0:T(8,128)(2,1)}) %reduce-scatter.32.cloned.1.call-update) | async-done | bytes 1048592 | tf_op jit(solution)/shard_map/reduce_scatter | solution.py:252
  1599.0 81.4 %all-gather.27.cloned.1.call-done = bf16[2048,1024]{1,0:T(8,128)(2,1)} async-done(((bf16[512,1024]{1,0:T(8,128)(2,1)}), bf16[2048,1024]{1,0:T(8,128)(2,1)}) %all-gather.27.cloned.1.call-update) | async-done | bytes 4194320 | tf_op jit(solution)/shard_map/all_gather | solution.py:259
  1687.0 285.8 %while.84 = (s32[]{:T(128)}, f32[2048,4,64]{0,2,1:T(8,128)}, f32[2048,4,64]{0,2,1:T(8,128)}, f32[4,512,4,64]{1,0,3,2:T(4,128)}, s32[4]{0:T(128)}, /*index=5*/bf1...) while((s32[]{:T(128)}, f32[2048,4,64]{0,2,1:T(8,128)}, ...), condition=%wide.region_28.29_spmd.clone, body=%wide.region_26.28_spmd.clone.sunk | while | flops 2753165824 | bytes 191441296 | solution.py:153
  1700.3 12.7 multiply_reduce_fusion.12
  1713.0 14.8 multiply_convert_fusion.22
  1747.0 11.1 dynamic_update_slice.53
  1771.2 12.7 multiply_reduce_fusion.12
  1783.9 14.8 multiply_convert_fusion.22
  1818.5 11.1 dynamic_update_slice.53
  1842.7 12.7 multiply_reduce_fusion.12
  1855.4 14.8 multiply_convert_fusion.22
  1890.0 11.1 dynamic_update_slice.53
  1914.2 12.7 multiply_reduce_fusion.12
  1926.9 14.8 multiply_convert_fusion.22
  1961.5 11.1 dynamic_update_slice.53
  1993.7 68.3 %reduce-scatter.34.cloned.1.call-done = bf16[512,1024]{1,0:T(8,128)(2,1)} async-done(((bf16[2048,1024]{1,0:T(8,128)(2,1)}), bf16[512,1024]{1,0:T(8,128)(2,1)}) %reduce-scatter.34.cloned.1.call-update) | async-done | bytes 1048592 | tf_op jit(solution)/shard_map/reduce_scatter | solution.py:290
  2065.6 75.8 %reduce-scatter.30.cloned.1.call-done = bf16[512,1024]{1,0:T(8,128)(2,1)} async-done(((bf16[2048,1024]{1,0:T(8,128)(2,1)}), bf16[512,1024]{1,0:T(8,128)(2,1)}) %reduce-scatter.30.cloned.1.call-update) | async-done | bytes 1048592 | tf_op jit(solution)/shard_map/reduce_scatter | solution.py:205
  2151.4 81.4 %all-gather.29.cloned.1.call-done = bf16[2048,1024]{1,0:T(8,128)(2,1)} async-done(((bf16[512,1024]{1,0:T(8,128)(2,1)}), bf16[2048,1024]{1,0:T(8,128)(2,1)}) %all-gather.29.cloned.1.call-update) | async-done | bytes 4194320 | tf_op jit(solution)/shard_map/all_gather | solution.py:248
  2250.7 75.4 %reduce-scatter.36.cloned.1.call-done = bf16[512,1024]{1,0:T(8,128)(2,1)} async-done(((bf16[2048,1024]{1,0:T(8,128)(2,1)}), bf16[512,1024]{1,0:T(8,128)(2,1)}) %reduce-scatter.36.cloned.1.call-update) | async-done | bytes 1048592 | tf_op jit(solution)/shard_map/reduce_scatter | solution.py:252
  2335.8 78.0 %all-gather.31.cloned.1.call-done = bf16[2048,1024]{1,0:T(8,128)(2,1)} async-done(((bf16[512,1024]{1,0:T(8,128)(2,1)}), bf16[2048,1024]{1,0:T(8,128)(2,1)}) %all-gather.31.cloned.1.call-update) | async-done | bytes 4194320 | tf_op jit(solution)/shard_map/all_gather | solution.py:259
  2420.4 285.6 %while.85 = (s32[]{:T(128)}, f32[2048,4,64]{0,2,1:T(8,128)}, f32[2048,4,64]{0,2,1:T(8,128)}, f32[4,512,4,64]{1,0,3,2:T(4,128)}, s32[4]{0:T(128)}, /*index=5*/bf1...) while((s32[]{:T(128)}, f32[2048,4,64]{0,2,1:T(8,128)}, ...), condition=%wide.region_35.36_spmd.clone, body=%wide.region_33.35_spmd.clone.sunk | while | flops 2753165824 | bytes 191441296 | solution.py:153
  2433.7 12.7 multiply_reduce_fusion.13
  2446.4 14.8 multiply_convert_fusion.23
  2504.6 12.7 multiply_reduce_fusion.13
  2517.3 14.8 multiply_convert_fusion.23
  2576.0 12.7 multiply_reduce_fusion.13
  2588.7 14.8 multiply_convert_fusion.23
  2647.5 12.7 multiply_reduce_fusion.13
  2660.2 14.8 multiply_convert_fusion.23
  2723.7 75.4 %reduce-scatter.38.cloned.1.call-done = bf16[512,1024]{1,0:T(8,128)(2,1)} async-done(((bf16[2048,1024]{1,0:T(8,128)(2,1)}), bf16[512,1024]{1,0:T(8,128)(2,1)}) %reduce-scatter.38.cloned.1.call-update) | async-done | bytes 1048592 | tf_op jit(solution)/shard_map/reduce_scatter | solution.py:290
  2812.1 81.4 %all-gather.33.cloned.1.call-done = bf16[2048,1024]{1,0:T(8,128)(2,1)} async-done(((bf16[512,1024]{1,0:T(8,128)(2,1)}), bf16[2048,1024]{1,0:T(8,128)(2,1)}) %all-gather.33.cloned.1.call-update) | async-done | bytes 4194320 | tf_op jit(solution)/shard_map/all_gather | solution.py:248
  2911.6 75.4 %reduce-scatter.40.cloned.1.call-done = bf16[512,1024]{1,0:T(8,128)(2,1)} async-done(((bf16[2048,1024]{1,0:T(8,128)(2,1)}), bf16[512,1024]{1,0:T(8,128)(2,1)}) %reduce-scatter.40.cloned.1.call-update) | async-done | bytes 1048592 | tf_op jit(solution)/shard_map/reduce_scatter | solution.py:252
  3048.2 26.5 all-gather.35.cloned.1.call-done
  3081.3 286.5 %while.86 = (s32[]{:T(128)}, f32[2048,4,64]{0,2,1:T(8,128)}, f32[2048,4,64]{0,2,1:T(8,128)}, f32[4,512,4,64]{1,0,3,2:T(4,128)}, s32[4]{0:T(128)}, /*index=5*/bf1...) while((s32[]{:T(128)}, f32[2048,4,64]{0,2,1:T(8,128)}, ...), condition=%wide.region_42.43_spmd.clone, body=%wide.region_40.42_spmd.clone.sunk | while | flops 2753165824 | bytes 191441296 | solution.py:153
  3095.0 12.7 multiply_reduce_fusion.14
  3107.7 14.9 multiply_convert_fusion.24
  3142.1 11.1 dynamic_update_slice.55
  3166.3 12.7 multiply_reduce_fusion.14
  3179.0 14.8 multiply_convert_fusion.24
  3213.6 11.1 dynamic_update_slice.55
  3237.8 12.7 multiply_reduce_fusion.14
  3250.5 14.8 multiply_convert_fusion.24
  3309.3 12.7 multiply_reduce_fusion.14
  3322.0 14.8 multiply_convert_fusion.24
  3356.6 11.1 dynamic_update_slice.55
  3439.7 20.6 reduce-scatter.48.cloned.1.call-done
  3462.5 25.3 reduce-scatter.50.cloned.1.call-done
  3496.8 70.1 %reduce-scatter.42.cloned.1.call-done = bf16[512,1024]{1,0:T(8,128)(2,1)} async-done(((bf16[2048,1024]{1,0:T(8,128)(2,1)}), bf16[512,1024]{1,0:T(8,128)(2,1)}) %reduce-scatter.42.cloned.1.call-update) | async-done | bytes 1048592 | tf_op jit(solution)/shard_map/reduce_scatter | solution.py:290
  3574.3 43.5 %all-reduce = (f32[2,1024]{1,0:T(2,128)S(1)}, f32[]{:T(128)}) all-reduce(f32[2,1024]{1,0:T(2,128)S(1)} %pad_maximum_fusion.8, f32[]{:T(128)S(6)} %reduce_sum.340), channel_id=1, replica_groups=mesh['section'=2,'dp'=4,'tensor'=4] {'dp','tensor'}, use_global_device_ids=true, to_apply=%region_58.59 | all-reduce | flops 2049 | bytes 16392 | tf_op jit(solution)/shard_map/psum | solution.py:416
  (1050 shorter events, 1091.3 us)
Async XLA Ops:
  7.2 417.4 %copy-start = (bf16[1,704,1024]{2,1,0:T(8,128)(2,1)S(1)}, bf16[1,704,1024]{2,1,0:T(8,128)(2,1)}, u32[]{:S(2)}) copy-start(bf16[1,704,1024]{2,1,0:T(8,128)(2,1)} %param.33) | copy-start | bytes 4325380
  7.2 88.0 %all-gather.13.cloned.1.call-start = ((), (), s32[]{:S(2)}) async-start(), calls=%async_computation.19 | async-start | bytes 5242880 | tf_op jit(solution)/shard_map/all_gather | solution.py:179
  11.6 314.0 %reduce-scatter.20.cloned.1.call-start = ((), (), s32[]{:S(2)}) async-start(), calls=%async_computation.20 | async-start | bytes 10485760 | tf_op jit(solution)/shard_map/reduce_scatter | solution.py:197
  11.9 87.0 %copy-start.122 = (bf16[1,1024,256]{1,2,0:T(8,128)(2,1)}, bf16[1,1024,256]{1,2,0:T(8,128)(2,1)S(1)}, u32[]{:S(2)}) copy-start(bf16[1,1024,256]{1,2,0:T(8,128)(2,1)S(1)} %copy.34) | copy-start | bytes 1572868
  12.1 86.8 %copy-start.123 = (bf16[1,1024,256]{1,2,0:T(8,128)(2,1)}, bf16[1,1024,256]{1,2,0:T(8,128)(2,1)S(1)}, u32[]{:S(2)}) copy-start(bf16[1,1024,256]{1,2,0:T(8,128)(2,1)S(1)} %copy.33) | copy-start | bytes 1572868
  14.7 85.5 %copy-start.40 = (f32[2048,32]{0,1:T(8,128)}, f32[2048,32]{0,1:T(8,128)S(1)}, u32[]{:S(2)}) copy-start(f32[2048,32]{0,1:T(8,128)S(1)} %get-tuple-element.647) | copy-start | bytes 786436
  14.7 85.5 %copy-start.99 = (f32[2048,32]{0,1:T(8,128)}, f32[2048,32]{0,1:T(8,128)S(1)}, u32[]{:S(2)}) copy-start(f32[2048,32]{0,1:T(8,128)S(1)} %get-tuple-element.646) | copy-start | bytes 786436
  182.4 143.2 %copy-start.5 = (bf16[2,512,1024]{2,1,0:T(8,128)(2,1)S(1)}, bf16[2,512,1024]{2,1,0:T(8,128)(2,1)}, u32[]{:S(2)}) copy-start(bf16[2,512,1024]{2,1,0:T(8,128)(2,1)} %param.24) | copy-start | bytes 6291460
  182.4 146.4 %copy-start.115 = (f32[1,1024]{1,0:T(1,128)S(1)}, f32[1,1024]{1,0:T(1,128)}, u32[]{:S(2)}) copy-start(f32[1,1024]{1,0:T(1,128)} %param.35) | copy-start | bytes 12292
  182.4 229.3 %all-gather.15.cloned.1.call-start = ((), (), s32[]{:S(2)}) async-start(), calls=%async_computation.21 | async-start | bytes 5242880 | tf_op jit(solution)/shard_map/all_gather | solution.py:201
  330.1 175.0 %reduce-scatter.22.cloned.1.call-start = ((), (), s32[]{:S(2)}) async-start(), calls=%async_computation.22 | async-start | bytes 5242880 | tf_op jit(solution)/shard_map/reduce_scatter | solution.py:205
  429.7 164.8 %all-gather.17.cloned.1.call-start = ((), (), s32[]{:S(2)}) async-start(), calls=%async_computation.23 | async-start | bytes 5242880 | tf_op jit(solution)/shard_map/all_gather | solution.py:179
  507.3 2.7 collective-permute-start
  513.0 313.3 %reduce-scatter.24.cloned.1.call-start = ((), (), s32[]{:S(2)}) async-start(), calls=%async_computation.24 | async-start | bytes 10485760 | tf_op jit(solution)/shard_map/reduce_scatter | solution.py:197
  513.1 85.1 %copy-start.124 = (bf16[1,1024,256]{1,2,0:T(8,128)(2,1)S(1)}, bf16[1,1024,256]{1,2,0:T(8,128)(2,1)}, u32[]{:S(2)}) copy-start(bf16[1,1024,256]{1,2,0:T(8,128)(2,1)} %copy-done.123) | copy-start | bytes 1572868
  513.1 88.3 %collective-permute-start.1 = (bf16[2048,256]{0,1:T(8,128)(2,1)}, bf16[2048,256]{0,1:T(8,128)(2,1)}, u32[]{:S(2)}, u32[]{:S(2)}) collective-permute-start(bf16[2048,256]{0,1:T(8,128)(2,1)} %bitcast.538), channel_id=1, source_target_pairs={{16,0},{0,16},{17,1},{1,17},{18,2},{2,18},{19,3},{3,19},{20,4},{4,... | collective-permute-start | bytes 3145736 | tf_op jit(solution)/shard_map/ppermute | solution.py:17
  683.1 143.2 %copy-start.6 = (bf16[2,512,1024]{2,1,0:T(8,128)(2,1)S(1)}, bf16[2,512,1024]{2,1,0:T(8,128)(2,1)}, u32[]{:S(2)}) copy-start(bf16[2,512,1024]{2,1,0:T(8,128)(2,1)} %param.24) | copy-start | bytes 6291460
  683.1 146.9 %copy-start.116 = (f32[1,1024]{1,0:T(1,128)S(1)}, f32[1,1024]{1,0:T(1,128)}, u32[]{:S(2)}) copy-start(f32[1,1024]{1,0:T(1,128)} %param.35) | copy-start | bytes 12292
  683.1 229.7 %all-gather.19.cloned.1.call-start = ((), (), s32[]{:S(2)}) async-start(), calls=%async_computation.25 | async-start | bytes 5242880 | tf_op jit(solution)/shard_map/all_gather | solution.py:201
  831.2 175.3 %reduce-scatter.26.cloned.1.call-start = ((), (), s32[]{:S(2)}) async-start(), calls=%async_computation.26 | async-start | bytes 5242880 | tf_op jit(solution)/shard_map/reduce_scatter | solution.py:205
  931.1 164.8 %all-gather.21.cloned.1.call-start = ((), (), s32[]{:S(2)}) async-start(), calls=%async_computation.27 | async-start | bytes 5242880 | tf_op jit(solution)/shard_map/all_gather | solution.py:179
  1008.8 2.7 collective-permute-start.2
  1014.5 315.9 %reduce-scatter.28.cloned.1.call-start = ((), (), s32[]{:S(2)}) async-start(), calls=%async_computation.28 | async-start | bytes 10485760 | tf_op jit(solution)/shard_map/reduce_scatter | solution.py:197
  1014.5 85.1 %copy-start.125 = (bf16[1,1024,256]{1,2,0:T(8,128)(2,1)S(1)}, bf16[1,1024,256]{1,2,0:T(8,128)(2,1)}, u32[]{:S(2)}) copy-start(bf16[1,1024,256]{1,2,0:T(8,128)(2,1)} %copy-done.123) | copy-start | bytes 1572868
  1014.5 88.3 %collective-permute-start.3 = (bf16[2048,256]{0,1:T(8,128)(2,1)}, bf16[2048,256]{0,1:T(8,128)(2,1)}, u32[]{:S(2)}, u32[]{:S(2)}) collective-permute-start(bf16[2048,256]{0,1:T(8,128)(2,1)} %bitcast.540), channel_id=1, source_target_pairs={{16,0},{0,16},{17,1},{1,17},{18,2},{2,18},{19,3},{3,19},{20,4},{4,... | collective-permute-start | bytes 3145736 | tf_op jit(solution)/shard_map/ppermute | solution.py:17
  1187.2 143.1 %copy-start.27 = (bf16[512,1024]{1,0:T(8,128)(2,1)S(1)}, bf16[512,1024]{1,0:T(8,128)(2,1)}, u32[]{:S(2)}) copy-start(bf16[512,1024]{1,0:T(8,128)(2,1)} %copy-done.26) | copy-start | bytes 3145732
  1187.2 226.8 %all-gather.25.cloned.1.call-start = ((), (), s32[]{:S(2)}) async-start(), calls=%async_computation.31 | async-start | bytes 5242880 | tf_op jit(solution)/shard_map/all_gather | solution.py:248
  1189.8 144.3 %copy-start.117 = (f32[1,1024]{1,0:T(1,128)S(1)}, f32[1,1024]{1,0:T(1,128)}, u32[]{:S(2)}) copy-start(f32[1,1024]{1,0:T(1,128)} %param.35) | copy-start | bytes 12292
  1189.8 305.6 %all-gather.23.cloned.1.call-start = ((), (), s32[]{:S(2)}) async-start(), calls=%async_computation.29 | async-start | bytes 5242880 | tf_op jit(solution)/shard_map/all_gather | solution.py:201
  1332.7 263.2 %copy-start.137 = (f32[512]{0:T(512)}, f32[512]{0:T(512)S(1)}, u32[]{:S(2)}) copy-start(f32[512]{0:T(512)S(1)} %add_rsqrt_fusion) | copy-start | bytes 6148
  1335.3 257.3 %reduce-scatter.32.cloned.1.call-start = ((), (), s32[]{:S(2)}) async-start(), calls=%async_computation.32 | async-start | bytes 5242880 | tf_op jit(solution)/shard_map/reduce_scatter | solution.py:252
  1517.1 163.3 %all-gather.27.cloned.1.call-start = ((), (), s32[]{:S(2)}) async-start(), calls=%async_computation.33 | async-start | bytes 5242880 | tf_op jit(solution)/shard_map/all_gather | solution.py:259
  1599.0 463.1 %reduce-scatter.34.cloned.1.call-start = ((), (), s32[]{:S(2)}) async-start(), calls=%async_computation.34 | async-start | bytes 5242880 | tf_op jit(solution)/shard_map/reduce_scatter | solution.py:290
  1986.6 154.9 %reduce-scatter.30.cloned.1.call-start = ((), (), s32[]{:S(2)}) async-start(), calls=%async_computation.30 | async-start | bytes 5242880 | tf_op jit(solution)/shard_map/reduce_scatter | solution.py:205
  1993.6 147.8 %copy-start.118 = (f32[1,1024]{1,0:T(1,128)S(1)}, f32[1,1024]{1,0:T(1,128)}, u32[]{:S(2)}) copy-start(f32[1,1024]{1,0:T(1,128)} %param.35) | copy-start | bytes 12292
  1993.6 147.8 %copy-start.138 = (f32[512]{0:T(512)S(1)}, f32[512]{0:T(512)}, u32[]{:S(2)}) copy-start(f32[512]{0:T(512)} %copy-done.137) | copy-start | bytes 6148
  1993.7 239.2 %all-gather.29.cloned.1.call-start = ((), (), s32[]{:S(2)}) async-start(), calls=%async_computation.35 | async-start | bytes 5242880 | tf_op jit(solution)/shard_map/all_gather | solution.py:248
  2146.3 2.7 collective-permute-start.5
  2151.4 174.7 %reduce-scatter.36.cloned.1.call-start = ((), (), s32[]{:S(2)}) async-start(), calls=%async_computation.36 | async-start | bytes 5242880 | tf_op jit(solution)/shard_map/reduce_scatter | solution.py:252
  2250.7 163.1 %all-gather.31.cloned.1.call-start = ((), (), s32[]{:S(2)}) async-start(), calls=%async_computation.37 | async-start | bytes 5242880 | tf_op jit(solution)/shard_map/all_gather | solution.py:259
  2332.4 466.7 %reduce-scatter.38.cloned.1.call-start = ((), (), s32[]{:S(2)}) async-start(), calls=%async_computation.38 | async-start | bytes 5242880 | tf_op jit(solution)/shard_map/reduce_scatter | solution.py:290
  2335.8 84.6 %copy-start.4 = (bf16[2048,4,64]{0,2,1:T(8,128)(2,1)S(1)}, bf16[2048,4,64]{0,2,1:T(8,128)(2,1)}, u32[]{:S(2)}) copy-start(bf16[2048,4,64]{0,2,1:T(8,128)(2,1)} %copy-done.3) | copy-start | bytes 3145732
  2335.8 84.6 %copy-start.112 = (s32[1,2048]{1,0:T(1,128)S(1)}, s32[1,2048]{1,0:T(1,128)}, u32[]{:S(2)}) copy-start(s32[1,2048]{1,0:T(1,128)} %get-tuple-element.642) | copy-start | bytes 24580
  2335.8 380.2 %collective-permute-start.6 = (bf16[2048,256]{0,1:T(8,128)(2,1)}, bf16[2048,256]{0,1:T(8,128)(2,1)}, u32[]{:S(2)}, u32[]{:S(2)}) collective-permute-start(bf16[2048,256]{0,1:T(8,128)(2,1)} %get-tuple-element.623), channel_id=1, source_target_pairs={{16,0},{0,16},{17,1},{1,17},{18,2},{2,18},{19,3},{3,19},{20,4},{4,... | collective-permute-start | bytes 3145736 | tf_op jit(solution)/shard_map/ppermute | solution.py:17
  2723.6 169.8 %all-gather.33.cloned.1.call-start = ((), (), s32[]{:S(2)}) async-start(), calls=%async_computation.39 | async-start | bytes 5242880 | tf_op jit(solution)/shard_map/all_gather | solution.py:248
  2806.9 2.7 collective-permute-start.7
  2812.0 175.0 %reduce-scatter.40.cloned.1.call-start = ((), (), s32[]{:S(2)}) async-start(), calls=%async_computation.40 | async-start | bytes 5242880 | tf_op jit(solution)/shard_map/reduce_scatter | solution.py:252
  2911.6 163.1 %all-gather.35.cloned.1.call-start = ((), (), s32[]{:S(2)}) async-start(), calls=%async_computation.41 | async-start | bytes 5242880 | tf_op jit(solution)/shard_map/all_gather | solution.py:259
  2993.3 429.5 %reduce-scatter.52.cloned.1.call-start = ((), (), s32[]{:S(2)}) async-start(), calls=%async_computation.47 | async-start | bytes 1802240 | tf_op jit(solution)/shard_map/reduce_scatter | solution.py:404
  3007.7 416.9 %reduce-scatter.54.cloned.1.call-start = ((), (), s32[]{:S(2)}) async-start(), calls=%async_computation.48 | async-start | bytes 1802240 | tf_op jit(solution)/shard_map/reduce_scatter | solution.py:407
  3026.2 400.3 %reduce-scatter.56.cloned.1.call-start = ((), (), s32[]{:S(2)}) async-start(), calls=%async_computation.49 | async-start | bytes 1802240 | tf_op jit(solution)/shard_map/reduce_scatter | solution.py:410
  3032.5 355.2 %collective-permute-start.8 = (bf16[2048,256]{0,1:T(8,128)(2,1)}, bf16[2048,256]{0,1:T(8,128)(2,1)}, u32[]{:S(2)}, u32[]{:S(2)}) collective-permute-start(bf16[2048,256]{0,1:T(8,128)(2,1)} %get-tuple-element.624), channel_id=1, source_target_pairs={{16,0},{0,16},{17,1},{1,17},{18,2},{2,18},{19,3},{3,19},{20,4},{4,... | collective-permute-start | bytes 3145736 | tf_op jit(solution)/shard_map/ppermute | solution.py:17
  3048.2 387.1 %reduce-scatter.44.cloned.1.call-start = ((), (), s32[]{:S(2)}) async-start(), calls=%async_computation.43 | async-start | bytes 655360 | tf_op jit(solution)/shard_map/reduce_scatter | solution.py:392
  3380.2 56.7 %reduce-scatter.46.cloned.1.call-start = ((), (), s32[]{:S(2)}) async-start(), calls=%async_computation.44 | async-start | bytes 655360 | tf_op jit(solution)/shard_map/reduce_scatter | solution.py:395
  3387.6 72.7 %reduce-scatter.48.cloned.1.call-start = ((), (), s32[]{:S(2)}) async-start(), calls=%async_computation.45 | async-start | bytes 655360 | tf_op jit(solution)/shard_map/reduce_scatter | solution.py:398
  3396.1 91.7 %reduce-scatter.50.cloned.1.call-start = ((), (), s32[]{:S(2)}) async-start(), calls=%async_computation.46 | async-start | bytes 655360 | tf_op jit(solution)/shard_map/reduce_scatter | solution.py:401
  3407.1 159.8 %reduce-scatter.42.cloned.1.call-start = ((), (), s32[]{:S(2)}) async-start(), calls=%async_computation.42 | async-start | bytes 5242880 | tf_op jit(solution)/shard_map/reduce_scatter | solution.py:290
  3414.4 3.1 collective-permute-start.4
  3424.6 142.4 %copy-start.9 = (bf16[2,512,1024]{2,1,0:T(8,128)(2,1)S(1)}, bf16[2,512,1024]{2,1,0:T(8,128)(2,1)}, u32[]{:S(2)}) copy-start(bf16[2,512,1024]{2,1,0:T(8,128)(2,1)} %param.24) | copy-start | bytes 6291460
  3424.6 142.4 %copy-start.130 = (f32[1,1024]{1,0:T(1,128)S(1)}, f32[1,1024]{1,0:T(1,128)}, u32[]{:S(2)}) copy-start(f32[1,1024]{1,0:T(1,128)} %param.34) | copy-start | bytes 12292
  3424.6 142.4 %copy-start.143 = (f32[512]{0:T(512)S(1)}, f32[512]{0:T(512)}, u32[]{:S(2)}) copy-start(f32[512]{0:T(512)} %copy-done.142) | copy-start | bytes 6148
  3430.2 139.0 %copy-start.120 = (f32[1,1024]{1,0:T(1,128)S(1)}, f32[1,1024]{1,0:T(1,128)}, u32[]{:S(2)}) copy-start(f32[1,1024]{1,0:T(1,128)} %param.35) | copy-start | bytes 12292
  3430.2 139.0 %copy-start.136 = (f32[512]{0:T(512)S(1)}, f32[512]{0:T(512)}, u32[]{:S(2)}) copy-start(f32[512]{0:T(512)} %copy-done.134) | copy-start | bytes 6148
  3573.6 47.4 %collective-permute-start.9 = (bf16[512,1024]{1,0:T(8,128)(2,1)}, bf16[512,1024]{1,0:T(8,128)(2,1)S(1)}, u32[]{:S(2)}, u32[]{:S(2)}) collective-permute-start(bf16[512,1024]{1,0:T(8,128)(2,1)} %get-tuple-element.569), channel_id=1, source_target_pairs={{16,0},{0,16},{17,1},{1,17},{18,2},{2,18},{19,3},{3,19},{20,4},{4,... | collective-permute-start | bytes 3145736 | tf_op jit(solution)/shard_map/ppermute | solution.py:17
  (248 other events, 2470.0 us)
Sparse Core Ops, SparseCore 0:
  11.7 83.4 all-gather.12
  182.5 142.9 reduce-scatter.19
  330.2 81.4 all-gather.14
  429.8 75.2 reduce-scatter.21
  513.2 81.2 all-gather.16
  683.2 142.9 reduce-scatter.23
  831.3 81.4 all-gather.18
  931.2 75.2 reduce-scatter.25
  1014.6 81.2 all-gather.20
  1187.3 142.9 reduce-scatter.27
  1332.5 81.4 all-gather.24
  1416.0 79.2 all-gather.22
  1517.3 75.2 reduce-scatter.31
  1599.1 81.2 all-gather.26
  1986.7 75.2 reduce-scatter.33
  2064.2 77.2 reduce-scatter.29
  2151.5 81.2 all-gather.28
  2250.8 75.2 reduce-scatter.35
  2332.5 81.2 all-gather.30
  2723.7 75.2 reduce-scatter.37
  2812.1 81.2 all-gather.32
  2911.7 75.2 reduce-scatter.39
  2993.4 81.2 all-gather.34
  3077.5 28.6 reduce-scatter.51
  3109.4 30.1 reduce-scatter.53
  3142.3 30.0 reduce-scatter.55
  3380.3 24.3 reduce-scatter.43
  3407.6 24.7 reduce-scatter.45
  3435.5 24.7 reduce-scatter.47
  3462.9 24.7 reduce-scatter.49
  3490.2 76.7 reduce-scatter.41
where the time goes:
time: 3650 us; the launch traced here: 3630 us
  waiting for transfers between devices  2060 us (56%)
  matrix products  832 us (23%)
  other arithmetic  392 us (11%)
  local copies, waits for them, and re-layouts  261 us (7%)
  blocking collectives  43.5 us (1%)
    reduce_scatter x3, waiting for transfers between devices, layer_forward(): lax.psum_scatter(matmul(attended, w_output), 'tensor', scatter_dimension=...  427 us
    all_gather x3, waiting for transfers between devices, layer_forward(): lax.all_gather(normed.astype(jnp.bfloat16), 'tensor', axis=0, tiled=True)  243 us
    all_gather x3, waiting for transfers between devices, layer_backward(): rows_grad = lax.all_gather(grad_low, 'tensor', axis=0, tiled=True)  241 us
    all_gather x3, waiting for transfers between devices, layer_forward(): lax.all_gather(normed_mlp.astype(jnp.bfloat16), 'tensor', axis=0, tiled=T...  237 us
    reduce_scatter x3, waiting for transfers between devices, layer_forward(): lax.psum_scatter(matmul(product, w_down).astype(jnp.bfloat16), 'tensor',...  227 us
    reduce_scatter x3, waiting for transfers between devices, layer_backward(): lax.psum_scatter(partial_rows.astype(jnp.bfloat16), 'tensor', scatter_dim...  226 us
    reduce_scatter x3, waiting for transfers between devices, layer_backward(): lax.psum_scatter(partial_rows_attn.astype(jnp.bfloat16), 'tensor', scatte...  214 us
    all_gather x3, waiting for transfers between devices, layer_backward(): lax.all_gather(hidden_grad.astype(jnp.bfloat16), 'tensor', axis=0, tiled=...  186 us
  transfers between devices with their start and end apart: 41, of which 31 were waited for; matrix products, arithmetic and copies ran while one was open for 20% of the time, Pallas kernels for 0%

commit v1 on v0

v1 whole, which is shorter than its diff:
```python
import functools
import math

import jax
import jax.numpy as jnp
from jax import lax
from jax.experimental import pallas as pl
from jax.experimental.pallas import tpu as pltpu
from jax.sharding import PartitionSpec as P

HEAD = 64
EPS = 1e-05
ROPE_BASE = 10000.0
BIG = 1e30
LOG2E = math.log2(math.e)
BF = jnp.bfloat16
F32 = jnp.float32
ALL = ("section", "dp", "tensor")
VMEM_LIMIT = 60 * 1024 * 1024

COL_OF_REL, ABS_OF_REL, REL_OF_ABS, REL_OF_RING, REL_OF_COL, REL_OF_DP = 0, 8, 16, 24, 32, 40


def nn(a, b):
    return jnp.dot(a, b, preferred_element_type=F32)


def nt(a, b):
    return lax.dot_general(a, b, (((1,), (1,)), ((), ())), preferred_element_type=F32)


def tn(a, b):
    return lax.dot_general(a, b, (((0,), (0,)), ((), ())), preferred_element_type=F32)


def vmem_spec():
    return pl.BlockSpec(memory_space=pltpu.VMEM)


def any_spec():
    return pl.BlockSpec(memory_space=pl.ANY)


def smem_spec():
    return pl.BlockSpec(memory_space=pltpu.SMEM)


def sds(shape, dtype):
    return jax.ShapeDtypeStruct(shape, dtype)


def cost(flops, moved):
    return pl.CostEstimate(flops=int(flops), bytes_accessed=int(moved), transcendentals=0)


def params(**more):
    return pltpu.CompilerParams(vmem_limit_bytes=VMEM_LIMIT, **more)


def piece_plan(sources, rows_from, rows):
    plan = []
    if len(sources) == 1:
        return [(0, rows_from, 0, rows, None)]
    half = sources[3].shape[0]
    for side in range(2):
        for place in range(3):
            plan.append((side * 5 + place, rows_from, 0, rows, side * 4 + place))
        top = max(0, min(half, rows_from + rows) - rows_from)
        if top > 0:
            plan.append((side * 5 + 3, rows_from, 0, top, side * 4 + 3))
        if rows - top > 0:
            start = max(rows_from, half)
            plan.append((side * 5 + 4, start - half, start - rows_from, rows - top, side * 4 + 3))
    return plan


def weight_copies(meta, plan, refs, buffer, sems, first_sem):
    copies = []
    for number, (operand, src_row, dst_row, count, rel) in enumerate(plan):
        src = refs[operand].at[pl.ds(src_row, count), :]
        if rel is None:
            dst = buffer.at[pl.ds(dst_row, count), :]
        else:
            offset = pl.multiple_of(meta[COL_OF_REL + rel] * 128, 128)
            dst = buffer.at[pl.ds(dst_row, count), pl.ds(offset, 128)]
        copies.append(pltpu.make_async_copy(src, dst, sems.at[first_sem + number]))
    return copies


def swap_halves(tile):
    lane = lax.broadcasted_iota(jnp.int32, tile.shape, 1)
    return jnp.where(lane % HEAD < HEAD // 2, pltpu.roll(tile, 128 - HEAD // 2, 1), pltpu.roll(tile, HEAD // 2, 1))


def qkv_kernel(blocks, later, meta, *refs):
    a_refs = refs[:blocks]
    w_ref, cos_ref, sin_ref, extq_ref, extk_ref = refs[blocks : blocks + 5]
    rest = refs[blocks + 5 :]
    if later:
        first_ref, rest = rest[0], rest[1:]
    q_ref, k_ref, v_ref = rest
    length = a_refs[0].shape[0]
    cols = w_ref.shape[1] // 3
    lane = lax.broadcasted_iota(jnp.int32, (length, 128), 1)
    low = lane < HEAD
    ones_even = ((lane >= HEAD + 4) & (lane < HEAD + 7)).astype(F32)
    ones_odd = ((lane >= 4) & (lane < 7)).astype(F32)
    for i in range(blocks):
        start = pl.multiple_of(meta[ABS_OF_REL + i] * length, length)
        rows = pl.ds(start, length)
        a = a_refs[i][...]
        cosine, sine = cos_ref[rows, :], sin_ref[rows, :]
        for part, out in ((0, q_ref), (1, k_ref), (2, v_ref)):
            whole = nn(a, w_ref[:, part * cols : (part + 1) * cols])
            for pair in range(cols // 128):
                tile = whole[:, pair * 128 : (pair + 1) * 128]
                if part < 2:
                    tile = tile * cosine + swap_halves(tile) * sine
                    ext = extq_ref if part == 0 else extk_ref
                    if part == 0:
                        tile = tile * (LOG2E * HEAD**-0.5)
                    even_ext = ext[rows, :128].astype(F32)
                    odd_ext = ext[rows, 128:].astype(F32)
                else:
                    if later:
                        first = jnp.where(
                            low,
                            first_ref[2 * pair, rows, :].astype(F32),
                            first_ref[2 * pair + 1, rows, :].astype(F32),
                        )
                        tile = 0.5 * tile + 0.5 * first
                    even_ext, odd_ext = ones_even, ones_odd
                out[2 * pair, rows, :] = jnp.where(low, tile, even_ext).astype(BF)
                out[2 * pair + 1, rows, :] = jnp.where(low, odd_ext, tile).astype(BF)


def project(meta, a_blocks, w, tables, exts, first):
    blocks, (length, width) = len(a_blocks), a_blocks[0].shape
    cols = w.shape[1] // 3
    heads = cols // HEAD
    seq = blocks * length
    out = sds((heads, seq, 128), BF)
    later = first is not None
    operands = [meta, *a_blocks, w, *tables, *exts] + ([first] if later else [])
    return pl.pallas_call(
        functools.partial(qkv_kernel, blocks, later),
        out_shape=(out, out, out),
        in_specs=[smem_spec()] + [vmem_spec()] * (len(operands) - 1),
        out_specs=(vmem_spec(),) * 3,
        compiler_params=params(),
        cost_estimate=cost(2 * seq * width * cols * 3, seq * width * 2 + 8e6),
        name="project",
    )(*operands)


def project_back_kernel(blocks, dp_blocks, meta, *refs):
    a_refs = refs[:blocks]
    dq_ref, dk_ref, dv_ref, w_ref = refs[blocks : blocks + 4]
    da_refs = refs[blocks + 4 : 2 * blocks + 4]
    dw_ref, acc_ref = refs[2 * blocks + 4 :]
    length, width = a_refs[0].shape
    cols = dq_ref.shape[1]
    for i in range(blocks):
        start = pl.multiple_of(meta[ABS_OF_REL + i] * length, length)
        rows = pl.ds(start, length)
        grads = jnp.concatenate([dq_ref[rows, :], dk_ref[rows, :], dv_ref[rows, :]], axis=1)
        da_refs[i][...] = nt(grads, w_ref[...]).astype(BF)
        term = tn(a_refs[i][...], grads)
        if i == 0:
            acc_ref[...] = term
        else:
            acc_ref[...] += term
    size = width // dp_blocks
    for j in range(dp_blocks):
        dw_ref[meta[REL_OF_DP + j]] = acc_ref[j * size : (j + 1) * size, :].astype(BF)


def project_back(meta, a_blocks, grads, w, dp_blocks):
    blocks, (length, width) = len(a_blocks), a_blocks[0].shape
    cols = w.shape[1]
    seq = blocks * length
    results = pl.pallas_call(
        functools.partial(project_back_kernel, blocks, dp_blocks),
        out_shape=tuple(sds((length, width), BF) for _ in range(blocks))
        + (sds((dp_blocks, width // dp_blocks, cols), BF),),
        in_specs=[smem_spec()] + [vmem_spec()] * (blocks + 4),
        out_specs=(vmem_spec(),) * (blocks + 1),
        scratch_shapes=[pltpu.VMEM((width, cols), F32)],
        compiler_params=params(),
        cost_estimate=cost(4 * seq * width * cols, seq * width * 4 + 8e6),
        name="project_back",
    )(meta, *a_blocks, *grads, w)
    return results[:blocks], results[blocks]


def three_parts(value):
    high = value.astype(BF).astype(F32)
    middle = (value - high).astype(BF).astype(F32)
    return high, middle, value - high - middle


def with_parts(base, value, odd):
    lane = lax.broadcasted_iota(jnp.int32, base.shape, 1)
    offset = 4 if odd else HEAD + 4
    high, middle, rest = three_parts(value)
    out = jnp.where(lane == offset, high, base)
    out = jnp.where(lane == offset + 1, middle, out)
    return jnp.where(lane == offset + 2, rest, out)


def attend_kernel(block, meta, q_ref, k_ref, v_ref, o_ref, ql_ref):
    seq = q_ref.shape[1]
    length = o_ref.shape[1]
    lane = lax.broadcasted_iota(jnp.int32, (block, 128), 1)
    low = lane < HEAD
    row = lax.broadcasted_iota(jnp.int32, (block, block), 0)
    col = lax.broadcasted_iota(jnp.int32, (block, block), 1)
    causal = col <= row
    for i in range(seq // block):
        rows = slice(i * block, (i + 1) * block)
        results = []
        for e in range(2):
            q = q_ref[e, rows, :]
            scores = []
            if i > 0:
                scores.append(nt(q, k_ref[e, : i * block, :]))
            scores.append(jnp.where(causal, nt(q, k_ref[e, rows, :]), -BIG))
            top = scores[-1].max(axis=1, keepdims=True)
            if i > 0:
                top = jnp.maximum(top, scores[0].max(axis=1, keepdims=True))
            total = nn(jnp.exp2(scores[-1] - top).astype(BF), v_ref[e, rows, :])
            if i > 0:
                total += nn(jnp.exp2(scores[0] - top).astype(BF), v_ref[e, : i * block, :])
            place = 4 if e else HEAD + 4
            weight = total[:, place : place + 1]
            results.append(total / weight)
            ql_ref[e, rows, :] = with_parts(q.astype(F32), -(top + jnp.log2(weight)), e == 1).astype(BF)
        offset = (i * block) % length
        o_ref[meta[REL_OF_ABS + (i * block) // length], offset : offset + block, :] = jnp.where(
            low, results[0], results[1]
        ).astype(BF)


def attend(meta, q, k, v, blocks):
    heads, seq, _ = q.shape
    pairs = heads // 2
    length = seq // blocks
    head_spec = pl.BlockSpec((2, seq, 128), lambda p: (p, 0, 0))
    return pl.pallas_call(
        functools.partial(attend_kernel, min(256, length)),
        grid=(pairs,),
        out_shape=(sds((blocks, length, pairs * 128), BF), sds(q.shape, BF)),
        in_specs=[smem_spec(), head_spec, head_spec, head_spec],
        out_specs=(pl.BlockSpec((blocks, length, 128), lambda p: (0, 0, p)), head_spec),
        compiler_params=params(),
        cost_estimate=cost(heads * seq * seq * 8 * HEAD, 8e6),
        name="attend",
    )(meta, q, k, v)


def attend_back_kernel(block, blocks, later, meta, q_ref, k_ref, v_ref, o_ref, *refs):
    do_refs = refs[:blocks]
    cos_ref, sin_ref = refs[blocks : blocks + 2]
    rest = refs[blocks + 2 :]
    if not later:
        first_ref, rest = rest[0], rest[1:]
    dq_ref, dk_ref, dv_ref = rest[:3]
    rest = rest[3:]
    if later:
        first_out, rest = rest[0], rest[1:]
    do_scr, dq_scr, dk_scr, dv_scr = rest
    seq = q_ref.shape[1]
    length = o_ref.shape[1]
    lane = lax.broadcasted_iota(jnp.int32, (length, 128), 1)
    low = lane < HEAD
    for i in range(blocks):
        start = pl.multiple_of(meta[ABS_OF_REL + i] * length, length)
        rows = pl.ds(start, length)
        do = do_refs[i][...].astype(F32)
        product = do * o_ref[i].astype(F32)
        for e in range(2):
            mine = low if e == 0 else jnp.logical_not(low)
            delta = jnp.sum(jnp.where(mine, product, 0.0), axis=1, keepdims=True)
            do_scr[e, rows, :] = with_parts(jnp.where(mine, do, 0.0), -delta, e == 1).astype(BF)
    dk_scr[...] = jnp.zeros_like(dk_scr)
    dv_scr[...] = jnp.zeros_like(dv_scr)
    key_row = lax.broadcasted_iota(jnp.int32, (block, block), 0)
    query_col = lax.broadcasted_iota(jnp.int32, (block, block), 1)
    causal = key_row <= query_col
    for e in range(2):
        for i in range(seq // block):
            rows = slice(i * block, (i + 1) * block)
            q = q_ref[e, rows, :]
            do = do_scr[e, rows, :]
            spans = [(i * block, (i + 1) * block, True)]
            spans += [(j, min(j + 512, i * block), False) for j in range(0, i * block, 512)]
            dq = None
            for lo, hi, diagonal in spans:
                keys = k_ref[e, lo:hi, :]
                scores = nt(keys, q)
                if diagonal:
                    scores = jnp.where(causal, scores, -BIG)
                prob = jnp.exp2(scores)
                ds = (prob * nt(v_ref[e, lo:hi, :], do)).astype(BF)
                dv_scr[e, lo:hi, :] += nn(prob.astype(BF), do)
                dk_scr[e, lo:hi, :] += nn(ds, q)
                term = tn(ds, keys)
                dq = term if dq is None else dq + term
            dq_scr[e, rows, :] = dq
    for i in range(blocks):
        rows = slice(i * length, (i + 1) * length)
        cosine, sine = cos_ref[rows, :], sin_ref[rows, :]
        dq = jnp.where(low, dq_scr[0, rows, :], dq_scr[1, rows, :]) * (HEAD**-0.5)
        dk = jnp.where(low, dk_scr[0, rows, :], dk_scr[1, rows, :]) * (1.0 / LOG2E)
        dv = jnp.where(low, dv_scr[0, rows, :], dv_scr[1, rows, :])
        dq_ref[rows, :] = (dq * cosine - swap_halves(dq) * sine).astype(BF)
        dk_ref[rows, :] = (dk * cosine - swap_halves(dk) * sine).astype(BF)
        if later:
            dv_ref[rows, :] = (0.5 * dv).astype(BF)
            first_out[rows, :] = 0.5 * dv
        else:
            dv_ref[rows, :] = (dv + first_ref[rows, :]).astype(BF)


def attend_back(meta, q, k, v, o, do_blocks, tables, first):
    heads, seq, _ = q.shape
    pairs = heads // 2
    blocks, length, cols = o.shape
    later = first is None
    head_spec = pl.BlockSpec((2, seq, 128), lambda p: (p, 0, 0))
    col_spec = pl.BlockSpec((seq, 128), lambda p: (0, p))
    table_spec = pl.BlockSpec((seq, 128), lambda p: (0, 0))
    out = sds((seq, cols), BF)
    return pl.pallas_call(
        functools.partial(attend_back_kernel, min(256, length), blocks, later),
        grid=(pairs,),
        out_shape=(out, out, out) + ((sds((seq, cols), F32),) if later else ()),
        in_specs=[smem_spec(), head_spec, head_spec, head_spec]
        + [pl.BlockSpec((blocks, length, 128), lambda p: (0, 0, p))]
        + [pl.BlockSpec((length, 128), lambda p: (0, p))] * blocks
        + [table_spec] * 2
        + ([] if later else [col_spec]),
        out_specs=(col_spec,) * (4 if later else 3),
        scratch_shapes=[
            pltpu.VMEM((2, seq, 128), BF),
            pltpu.VMEM((2, seq, 128), F32),
            pltpu.VMEM((2, seq, 128), F32),
            pltpu.VMEM((2, seq, 128), F32),
        ],
        compiler_params=params(),
        cost_estimate=cost(heads * seq * seq * 20 * HEAD, 12e6),
        name="attend_back",
    )(meta, q, k, v, o, *do_blocks, *tables, *([] if later else [first]))


def mlp_kernel(blocks, counts, plans, meta, x_ref, gain_ref, *refs):
    o_refs, refs = refs[:blocks], refs[blocks:]
    sources = []
    for count in counts:
        sources.append(refs[:count])
        refs = refs[count:]
    y_ref, h_ref, b_ref, g_ref, u_ref, w_ref, o_scr, sems = refs
    copies, number = [], 0
    for k in range(blocks):
        group = weight_copies(meta, plans[k], sources[k], w_ref.at[k], sems, number)
        number += len(group)
        for copy in group:
            copy.start()
        copies.append(group)
    rows_o = o_refs[0].shape[1]
    hidden = g_ref.shape[2]
    for i in range(blocks):
        o_scr[i] = o_refs[i][...]
    h_ref[...] = x_ref[...].astype(F32)
    for k in range(blocks):
        for copy in copies[k]:
            copy.wait()
        h_ref[...] += nn(o_scr[meta[REL_OF_RING + k]], w_ref[k, :rows_o, :])
    h = h_ref[...]
    inverse = lax.rsqrt(jnp.mean(h * h, axis=1, keepdims=True) + EPS)
    b_ref[...] = (h * inverse * gain_ref[...]).astype(BF)
    total = None
    for k in range(blocks):
        b = b_ref[...]
        g = nt(b, w_ref[k, rows_o : rows_o + hidden, :])
        u = nt(b, w_ref[k, rows_o + hidden : rows_o + 2 * hidden, :])
        g_ref[k] = g.astype(BF)
        u_ref[k] = u.astype(BF)
        m = (g * jax.nn.sigmoid(g) * u).astype(BF)
        term = nn(m, w_ref[k, rows_o + 2 * hidden :, :])
        total = term if total is None else total + term
    y_ref[...] = (h_ref[...] + total).astype(BF)


def flatten(groups):
    return [item for group in groups for item in group]


def mlp_forward(meta, x, gain, o_blocks, weights, hidden):
    blocks, (length, cols) = len(o_blocks), o_blocks[0].shape
    width = x.shape[1]
    rows = cols + 3 * hidden
    plans = [piece_plan(source, 0, rows) for source in weights]
    saved = sds((blocks, length, hidden), BF)
    return pl.pallas_call(
        functools.partial(mlp_kernel, blocks, [len(w) for w in weights], plans),
        out_shape=(sds((length, width), BF), sds((length, width), F32), sds((length, width), BF), saved, saved),
        in_specs=[smem_spec()]
        + [vmem_spec()] * (2 + blocks)
        + [any_spec()] * sum(len(w) for w in weights),
        out_specs=(vmem_spec(),) * 5,
        scratch_shapes=[
            pltpu.VMEM((blocks, rows, width), BF),
            pltpu.VMEM((blocks, length, cols), BF),
            pltpu.SemaphoreType.DMA((sum(len(p) for p in plans),)),
        ],
        compiler_params=params(),
        cost_estimate=cost(2 * length * width * rows * blocks, rows * width * 2 * blocks + 12e6),
        name="mlp",
    )(meta, x, gain, *o_blocks, *flatten(weights))


def mlp_back_kernel(quarters, counts, plans, first, meta, dy_ref, b_ref, g_ref, u_ref, *refs):
    if not first:
        db_in, refs = refs[0], refs[1:]
    sources = []
    for count in counts:
        sources.append(refs[:count])
        refs = refs[count:]
    number = len(quarters)
    outs, refs = refs[: 2 * number], refs[2 * number :]
    db_ref, w_ref, grad_scr, sems, out_sems = refs
    copies, placed = [], 0
    for n in range(number):
        group = weight_copies(meta, plans[n], sources[n], w_ref.at[n], sems, placed)
        placed += len(group)
        for copy in group:
            copy.start()
        copies.append(group)
    hidden = g_ref.shape[2]
    if first:
        db_ref[...] = jnp.zeros_like(db_ref)
    else:
        db_ref[...] = db_in[...]
    sends = []
    for n, k in enumerate(quarters):
        for copy in copies[n]:
            copy.wait()
        dy = dy_ref[...]
        b = b_ref[...]
        dm = nt(dy, w_ref[n, 2 * hidden :, :])
        g = g_ref[k].astype(F32)
        u = u_ref[k].astype(F32)
        gate = jax.nn.sigmoid(g)
        active = g * gate
        m = (active * u).astype(BF)
        dg = (dm * u * gate * (1.0 + g * (1.0 - gate))).astype(BF)
        du = (dm * active).astype(BF)
        db_ref[...] += nn(dg, w_ref[n, :hidden, :]) + nn(du, w_ref[n, hidden : 2 * hidden, :])
        for part, (left, right) in enumerate(((dg, b), (du, b), (m, dy))):
            grad = tn(left, right).astype(BF)
            for j in range(grad.shape[1] // 128):
                grad_scr[n, meta[REL_OF_COL + j], part * hidden : (part + 1) * hidden, :] = grad[
                    :, j * 128 : (j + 1) * 128
                ]
        for side in range(2):
            copy = pltpu.make_async_copy(
                grad_scr.at[n, pl.ds(4 * side, 4)], outs[2 * n + side], out_sems.at[2 * n + side]
            )
            copy.start()
            sends.append(copy)
    for copy in sends:
        copy.wait()


def mlp_backward(meta, dy, b, g, u, db, weights, quarters, rows_from):
    blocks, length, hidden = g.shape
    width = b.shape[1]
    rows = 3 * hidden
    chosen = [weights[k] for k in quarters]
    plans = [piece_plan(source, rows_from, rows) for source in chosen]
    number = len(quarters)
    first = db is None
    results = pl.pallas_call(
        functools.partial(mlp_back_kernel, quarters, [len(w) for w in chosen], plans, first),
        out_shape=tuple(sds((4, rows, 128), BF) for _ in range(2 * number)) + (sds((length, width), F32),),
        in_specs=[smem_spec()]
        + [vmem_spec()] * (4 if first else 5)
        + [any_spec()] * sum(len(w) for w in chosen),
        out_specs=(any_spec(),) * (2 * number) + (vmem_spec(),),
        scratch_shapes=[
            pltpu.VMEM((number, rows, width), BF),
            pltpu.VMEM((number, 8, rows, 128), BF),
            pltpu.SemaphoreType.DMA((sum(len(p) for p in plans),)),
            pltpu.SemaphoreType.DMA((2 * number,)),
        ],
        compiler_params=params(),
        cost_estimate=cost(4 * length * width * rows * number, rows * width * 4 * number + 8e6),
        name="mlp_back",
    )(meta, dy, b, g, u, *([] if first else [db]), *flatten(chosen))
    return results[: 2 * number], results[2 * number]


def norm_back(values, gain, grads):
    inverse = lax.rsqrt(jnp.mean(values * values, axis=1, keepdims=True) + EPS)
    normed = values * inverse
    scaled = grads * gain
    gain_grad = jnp.sum(grads * normed, axis=0, keepdims=True)
    return inverse * (scaled - normed * jnp.mean(scaled * normed, axis=1, keepdims=True)), gain_grad


def middle_kernel(blocks, counts, plans, meta, dy_ref, db_ref, h_ref, gain_ref, *refs):
    o_refs, refs = refs[:blocks], refs[blocks:]
    sources = []
    for count in counts:
        sources.append(refs[:count])
        refs = refs[count:]
    dh_ref, gain_out, do_ref, own_ref, sib_ref, w_ref, o_scr, grad_scr, sems, out_sems = refs
    copies, number = [], 0
    for k in range(blocks):
        group = weight_copies(meta, plans[k], sources[k], w_ref.at[k], sems, number)
        number += len(group)
        for copy in group:
            copy.start()
        copies.append(group)
    cols = o_refs[0].shape[1]
    for i in range(blocks):
        o_scr[i] = o_refs[i][...]
    part, gain_grad = norm_back(h_ref[...], gain_ref[...], db_ref[...])
    dh = dy_ref[...].astype(F32) + part
    dh_ref[...] = dh
    gain_out[...] = gain_grad
    low = dh.astype(BF)
    for k in range(blocks):
        for copy in copies[k]:
            copy.wait()
        place = meta[REL_OF_RING + k]
        do_ref[place] = nt(low, w_ref[k]).astype(BF)
        grad = tn(o_scr[place], low).astype(BF)
        for j in range(grad.shape[1] // 128):
            grad_scr[meta[REL_OF_COL + j], k * cols : (k + 1) * cols, :] = grad[:, j * 128 : (j + 1) * 128]
    sends = []
    for side, out in enumerate((own_ref, sib_ref)):
        copy = pltpu.make_async_copy(grad_scr.at[pl.ds(4 * side, 4)], out, out_sems.at[side])
        copy.start()
        sends.append(copy)
    for copy in sends:
        copy.wait()


def middle(meta, dy, db, h, gain, o_blocks, weights):
    blocks, (length, cols) = len(o_blocks), o_blocks[0].shape
    width = h.shape[1]
    plans = [piece_plan(source, 0, cols) for source in weights]
    half = sds((4, blocks * cols, 128), BF)
    return pl.pallas_call(
        functools.partial(middle_kernel, blocks, [len(w) for w in weights], plans),
        out_shape=(sds((length, width), F32), sds((1, width), F32), sds((blocks, length, cols), BF), half, half),
        in_specs=[smem_spec()]
        + [vmem_spec()] * (4 + blocks)
        + [any_spec()] * sum(len(w) for w in weights),
        out_specs=(vmem_spec(),) * 3 + (any_spec(),) * 2,
        scratch_shapes=[
            pltpu.VMEM((blocks, cols, width), BF),
            pltpu.VMEM((blocks, length, cols), BF),
            pltpu.VMEM((8, blocks * cols, 128), BF),
            pltpu.SemaphoreType.DMA((sum(len(p) for p in plans),)),
            pltpu.SemaphoreType.DMA((2,)),
        ],
        compiler_params=params(),
        cost_estimate=cost(4 * length * width * cols * blocks, 16e6),
        name="middle",
    )(meta, dy, db, h, gain, *o_blocks, *flatten(weights))


def add_low(*terms):
    total = terms[0].astype(F32)
    for term in terms[1:]:
        total = total + term.astype(F32)
    return total.astype(BF)


class Links:
    def __init__(self):
        self.T = lax.axis_size("tensor")
        self.DP = lax.axis_size("dp")
        self.G = self.T // 2
        self.s = lax.axis_index("section")
        self.d = lax.axis_index("dp")
        self.z = lax.axis_index("tensor")
        self.r = self.z // self.G
        self.c = self.z % self.G
        self.home = self.s == self.r
        self.planar = self.DP == 4
        self.order = [0] + list(range(1, self.T, 2)) + list(range(self.T - 2, 0, -2))

    def sibling(self, x):
        return lax.ppermute(x, "section", [(0, 1), (1, 0)])

    def ring(self, x):
        order = self.order
        return lax.ppermute(x, "tensor", [(order[i], order[(i + 1) % self.T]) for i in range(self.T)])

    def along(self, x, bit):
        return lax.ppermute(x, "dp", [(i, i ^ bit) for i in range(self.DP)])

    def along_away(self, x, bit):
        pairs = []
        for d in range(self.DP):
            for z in range(self.T):
                s = 1 - z // self.G
                pairs.append(tuple((s * self.DP + e) * self.T + z for e in (d, d ^ bit)))
        return lax.ppermute(x, ALL, pairs)

    def partner(self, x, from_home):
        pairs = []
        for s in range(2):
            for z in range(self.T):
                if (z // self.G == s) == from_home:
                    pairs.append((s * self.T + z, s * self.T + (z + self.G) % self.T))
        return lax.ppermute(x, ("section", "tensor"), pairs)

    def shift(self, x, k):
        pairs = [(z, z // self.G * self.G + (z + k) % self.G) for z in range(self.T)]
        return lax.ppermute(x, "tensor", pairs)

    def spread(self, x):
        mine = [x] + [self.shift(x, -k) for k in range(1, self.G)]
        return mine + [self.sibling(item) for item in mine]

    def exchange(self, pieces):
        G = self.G
        near, far = [None] * G, [None] * G
        near[0], far[0] = pieces[0], pieces[G]
        for k in range(1, G):
            both = self.shift(jnp.stack([pieces[k], pieces[k + G]]), k)
            near[-k % G], far[-k % G] = both[0], both[1]
        return near + [self.sibling(item) for item in far]

    def combine(self, parts):
        G = self.G
        got = [self.sibling(parts[k + G]) for k in range(G)]
        total = parts[0].astype(F32) + got[0].astype(F32)
        for k in range(1, G):
            total = total + self.shift(add_low(parts[k], got[k]), k).astype(F32)
        return total

    def to_group(self, x):
        got = self.partner(lax.dynamic_index_in_dim(x, 1 - self.s, 0, keepdims=False), True)
        return jnp.where(self.home, lax.dynamic_index_in_dim(x, self.s, 0, keepdims=False), got)

    def from_group(self, x):
        got = self.partner(x, False)
        return jnp.stack([jnp.where(self.r == 0, x, got), jnp.where(self.r == 0, got, x)])

    def table(self):
        T, G, s, c, d = self.T, self.G, self.s, self.c, self.d
        out = [jnp.int32(0)] * 48
        position = jnp.array([self.order.index(z) for z in range(T)], jnp.int32)[self.z]
        order = jnp.array(self.order, jnp.int32)
        for rel in range(8):
            if self.planar:
                out[COL_OF_REL + rel] = ((d ^ (rel % 4)) * 2 + (s ^ (rel // 4))).astype(jnp.int32)
                out[REL_OF_COL + rel] = ((d ^ (rel // 2)) + 4 * (s ^ (rel % 2))).astype(jnp.int32)
            else:
                out[COL_OF_REL + rel] = jnp.int32(rel)
                out[REL_OF_COL + rel] = jnp.int32(rel)
        for i in range(T):
            out[ABS_OF_REL + i] = (c + i % G) % G + G * (s ^ (i // G))
            out[REL_OF_ABS + i] = (i % G - c) % G + G * ((i // G) ^ s)
            quarter = order[(position - i) % T]
            out[REL_OF_RING + i] = (quarter % G - c) % G + G * ((quarter // G) ^ s)
        for i in range(self.DP):
            out[REL_OF_DP + i] = (d ^ i) if self.planar else jnp.int32(i)
        return jnp.stack([jnp.asarray(item, jnp.int32) for item in out])


def gather_weights(links, stacked):
    rows = stacked.shape[0]
    s, d = links.s, links.d
    other = links.sibling(stacked)
    whole = [jnp.where(s == 0, stacked, other), jnp.where(s == 0, other, stacked)]
    weights = [[[item]] for item in whole]
    if not links.planar:
        for layer in range(2):
            current = whole[layer]
            for _ in range(1, links.T):
                current = links.ring(current)
                weights[layer].append([current])
        return weights
    mine = lax.dynamic_slice_in_dim(stacked, (2 * d + s) * 128, 128, 1)
    give = lax.dynamic_slice_in_dim(stacked, (2 * d + 1 - s) * 128, 128, 1)
    got = links.sibling(give)
    start = [jnp.where(s == 0, mine, got), jnp.where(s == 0, got, mine)]
    half = rows // 2
    for layer in range(2):
        current = start[layer]
        for _ in range(1, links.T):
            current = links.ring(current)
            by_x, by_y = links.along(current, 1), links.along(current, 2)
            top = links.along(by_y[:half], 1)
            bottom = links.along(by_x[half:], 2)
            mine = [current, by_x, by_y, top, bottom]
            weights[layer].append(mine + [links.sibling(item) for item in mine])
    return weights


def gather_projection(links, own):
    s, d = links.s, links.d
    other = links.sibling(own)
    whole = [jnp.where(s == 0, own, other), jnp.where(s == 0, other, own)]
    result = []
    for item in whole:
        if not links.planar:
            result.append(jnp.where(links.home, item, links.partner(item, True)))
            continue
        size = item.shape[0] // 4
        piece = links.partner(lax.dynamic_slice_in_dim(item, d * size, size, 0), True)
        by_x, by_y = links.along_away(piece, 1), links.along_away(piece, 2)
        across = jnp.concatenate(
            [links.along_away(by_y[: size // 2], 1), links.along_away(by_x[size // 2 :], 2)]
        )
        buffer = jnp.zeros_like(item)
        for place, part in enumerate((piece, by_x, by_y, across)):
            buffer = lax.dynamic_update_slice_in_dim(buffer, part, (d ^ place) * size, 0)
        result.append(jnp.where(links.home, item, buffer))
    return result


def plane_reduce(links, parts, along):
    half = parts.shape[1] // 2
    from_x = along(parts[3, :half], 1)
    from_y = along(parts[3, half:], 2)
    for_x = jnp.concatenate([parts[1, :half], add_low(parts[1, half:], from_y)])
    for_y = jnp.concatenate([add_low(parts[2, :half], from_x), parts[2, half:]])
    return add_low(parts[0], along(for_x, 1), along(for_y, 2))


def reduce_start(links, own, sib):
    if not links.planar:
        return jnp.concatenate([own, sib])
    return plane_reduce(links, add_low(own, links.sibling(sib)), links.along)


def reduce_end(links, total):
    if links.planar:
        return total
    total = add_low(total, links.sibling(total))
    return lax.psum_scatter(total, "dp", scatter_dimension=0, tiled=True)[0]


def ring_add(links, running, term):
    return term if running is None else add_low(links.ring(running), term)


def home_layers(links, per_layer):
    mine = jnp.where(links.s == 0, per_layer[0], per_layer[1])
    if not links.planar:
        return mine
    got = links.sibling(jnp.where(links.s == 0, per_layer[1], per_layer[0]))
    return jnp.where(
        links.s == 0, jnp.concatenate([mine, got], axis=1), jnp.concatenate([got, mine], axis=1)
    )


def sum_everywhere(links, x):
    x = x + links.sibling(x)
    if links.planar:
        x = x + links.along(x, 1)
        x = x + links.along(x, 2)
    else:
        x = lax.psum(x, "dp")
    step = 1
    while step < links.T:
        x = x + lax.ppermute(x, "tensor", [(z, z ^ step) for z in range(links.T)])
        step *= 2
    return x


def norm_low(x, gain):
    inverse = lax.rsqrt(jnp.mean(x * x, axis=-1, keepdims=True) + EPS)
    return (x * inverse * gain).astype(BF)


def per_device(
    tokens,
    segment_ids,
    cotangent,
    query_weight,
    key_weight,
    value_weight,
    output_weight,
    gate_weight,
    up_weight,
    down_weight,
    attn_gain,
    mlp_gain,
):
    links = Links()
    T, DP, s = links.T, links.DP, links.s
    seq = segment_ids.shape[1]
    width = tokens.shape[2]
    cols = query_weight.shape[2]
    hidden = gate_weight.shape[2]
    meta = links.table()

    half = HEAD // 2
    frequency = ROPE_BASE ** (-jnp.arange(half, dtype=F32) / half)
    angles = jnp.arange(seq, dtype=F32)[:, None] * frequency[None, :]
    cosine, sine = jnp.cos(angles), jnp.sin(angles)
    tables = (
        jnp.concatenate([cosine] * 4, axis=1),
        jnp.concatenate([-sine, sine, -sine, sine], axis=1),
    )
    segments = lax.dynamic_index_in_dim(segment_ids, links.r, 0, keepdims=False)
    lane = jnp.arange(256, dtype=jnp.int32)[None, :]
    place = jnp.where(lane < 128, lane - HEAD, lane - 128)
    same = segments[:, None] == place
    in_seg = (place >= 0) & (place < 4)
    ext_q = jnp.where(in_seg & ~same, -BIG, 0.0).astype(BF)
    ext_k = jnp.where((in_seg & same) | ((place >= 4) & (place < 7)), 1.0, 0.0).astype(BF)

    projection = jnp.concatenate([query_weight[0], key_weight[0], value_weight[0]], axis=1)
    stacked = jnp.concatenate([output_weight[0], gate_weight[0].T, up_weight[0].T, down_weight[0]], axis=0)
    own_gains = jnp.concatenate([attn_gain, mlp_gain])
    other_gains = links.sibling(own_gains)
    gains = [
        jnp.where(s == layer, own_gains, other_gains) for layer in range(2)
    ]
    w_proj = gather_projection(links, projection)
    weights = gather_weights(links, stacked)

    x = links.to_group(tokens)
    kept = []
    first_values = None
    for layer in range(2):
        gain_attn, gain_mlp = gains[layer][0:1], gains[layer][1:2]
        a = norm_low(x.astype(F32), gain_attn)
        a_blocks = links.spread(a)
        q, k, v = project(meta, a_blocks, w_proj[layer], tables, (ext_q, ext_k), first_values)
        if layer == 0:
            first_values = v
        o_rel, q = attend(meta, q, k, v, T)
        o_blocks = links.exchange([o_rel[i] for i in range(T)])
        y, h, b, g, u = mlp_forward(meta, x, gain_mlp, o_blocks, weights[layer], hidden)
        kept.append((x, a_blocks, q, k, v, o_rel, o_blocks, h, b, g, u))
        x = y
    grouped = links.from_group(x)
    activations = jnp.where(links.home, grouped, links.sibling(grouped))

    dy = links.to_group(cotangent)
    first_grad = None
    mlp_sums, out_sums, proj_sums, gain_sums = [None] * 2, [None] * 2, [None] * 2, [None] * 2
    for layer in (1, 0):
        gain_attn, gain_mlp = gains[layer][0:1], gains[layer][1:2]
        x, a_blocks, q, k, v, o_rel, o_blocks, h, b, g, u = kept[layer]
        dy_low = dy.astype(BF)
        running, db = None, None
        for quarter in list(range(1, T)) + [0]:
            (own, sib), db = mlp_backward(meta, dy_low, b, g, u, db, weights[layer], [quarter], cols)
            running = ring_add(links, running, reduce_start(links, own, sib))
        mlp_sums[layer] = running
        dh, mlp_gain_grad, do_rel, own, sib = middle(meta, dy, db, h, gain_mlp, o_blocks, weights[layer])
        do_blocks = links.exchange([do_rel[i] for i in range(T)])
        out_part = reduce_start(links, own, sib)
        running = None
        for quarter in list(range(1, T)) + [0]:
            term = out_part[..., quarter * cols : (quarter + 1) * cols, :]
            running = ring_add(links, running, term)
        out_sums[layer] = running
        back = attend_back(meta, q, k, v, o_rel, do_blocks, tables, first_grad)
        if layer == 1:
            first_grad = back[3]
        da_parts, dw = project_back(meta, a_blocks, back[:3], w_proj[layer], DP)
        if links.planar:
            proj_sums[layer] = plane_reduce(links, dw, links.along)
        else:
            proj_sums[layer] = lax.psum_scatter(dw, "dp", scatter_dimension=0, tiled=True)[0]
        da = links.combine(list(da_parts))
        part, attn_gain_grad = norm_back(x.astype(F32), gain_attn, da)
        gain_sums[layer] = jnp.concatenate([attn_gain_grad, mlp_gain_grad])
        dy = dh + part
    grouped = links.from_group(dy.astype(BF))
    half_width = width // 2
    keep = lax.dynamic_slice_in_dim(grouped, s * half_width, half_width, 2)
    send = lax.dynamic_slice_in_dim(grouped, (1 - s) * half_width, half_width, 2)
    input_grad = jnp.where(links.home, keep, links.sibling(send)).astype(F32)

    own_mlp = home_layers(links, [reduce_end(links, item) for item in mlp_sums]).astype(F32)
    own_out = home_layers(links, [reduce_end(links, item) for item in out_sums]).astype(F32)
    joined = [item.astype(F32) + links.partner(item, False).astype(F32) for item in proj_sums]
    mine = jnp.where(s == 0, joined[0], joined[1])
    got = links.sibling(jnp.where(s == 0, joined[1], joined[0]))
    own_proj = jnp.where(links.home, mine, got)
    squares = jnp.sum(own_mlp * own_mlp) + jnp.sum(own_out * own_out) + jnp.sum(own_proj * own_proj)
    line = jnp.where(jnp.arange(width)[None, :] == s, squares, 0.0)
    summed = sum_everywhere(links, jnp.concatenate([gain_sums[0], gain_sums[1], line]))
    gain_total = jnp.where(s == 0, summed[0:2], summed[2:4])
    weight_total = jnp.where(s == 0, summed[4, 0], summed[4, 1])
    grad_norm = jnp.sqrt(weight_total + jnp.sum(gain_total * gain_total)).reshape(1)
    shard = width // (DP * T)
    gain_out = lax.dynamic_slice_in_dim(gain_total, (links.d * T + links.z) * shard, shard, 1)
    return (
        activations,
        input_grad,
        own_proj[None, :, :cols],
        own_proj[None, :, cols : 2 * cols],
        own_proj[None, :, 2 * cols :],
        own_out[None],
        own_mlp[:hidden].T[None],
        own_mlp[hidden : 2 * hidden].T[None],
        own_mlp[2 * hidden :][None],
        gain_out[0:1],
        gain_out[1:2],
        grad_norm,
    )


def solution(mesh):
    return jax.shard_map(
        per_device,
        mesh=mesh,
        in_specs=(
            P("dp", "tensor", None),
            P("dp", None),
            P("dp", "tensor", None),
            P("section", None, "tensor"),
            P("section", None, "tensor"),
            P("section", None, "tensor"),
            P("section", "tensor", None),
            P("section", None, "tensor"),
            P("section", None, "tensor"),
            P("section", "tensor", None),
            P("section", None),
            P("section", None),
        ),
        out_specs=(
            P("dp", "tensor", None),
            P("dp", "tensor", "section"),
            P("section", "dp", "tensor"),
            P("section", "dp", "tensor"),
            P("section", "dp", "tensor"),
            P("section", "tensor", "dp"),
            P("section", "dp", "tensor"),
            P("section", "dp", "tensor"),
            P("section", "tensor", "dp"),
            P("section", ("dp", "tensor")),
            P("section", ("dp", "tensor")),
            P("section"),
        ),
        check_vma=False,
    )
```

time: 3650 us -> 1040 us (0.28)
  waiting for transfers between devices: 2060 us -> 309 us
  matrix products: 832 us -> 0 us
  Pallas kernels: 0 us -> 348 us
  other arithmetic: 392 us -> 89.5 us
  starting transfers between devices: 2.2 us -> 215 us
  local copies, waits for them, and re-layouts: 261 us -> 52.9 us
  blocking collectives: 43.5 us -> 0 us
    reduce_scatter x19 -> x0, waiting for transfers between devices: 1140 us -> none  [the longest x3 427 us: layer_forward(): lax.psum_scatter(matmul(attended, w_output), 'tensor', scatter_dimension=...]
    all_gather x12 -> x0, waiting for transfers between devices: 907 us -> none  [the longest x3 243 us: layer_forward(): lax.all_gather(normed.astype(jnp.bfloat16), 'tensor', axis=0, tiled=True)]
    dot_general x147 -> x0, matrix products: 832 us -> none  [the longest x24 164 us: one_block(): jnp.einsum('qhd,khd->hqk', query_block, key_rows, preferred_element_type=...]
    pallas_call x0 -> x20, Pallas kernels: none -> 348 us  [the longest x8 123 us: mlp_backward(): pl.pallas_call(functools.partial(mlp_back_kernel, quarters, [len(w) for w...]
    ppermute x10 -> x184, waiting for transfers between devices: 12.1 us -> 309 us  [the longest x74 133 us: along(): return lax.ppermute(x, 'dp', [(i, i ^ bit) for i in range(self.DP)])]
    ppermute x10 -> x184, starting transfers between devices: 0.7 us -> 215 us  [the longest x74 82.5 us: along(): return lax.ppermute(x, 'dp', [(i, i ^ bit) for i in range(self.DP)])]
    convert_element_type x40 -> x46, other arithmetic: 229 us -> 30.7 us  [the longest x38 18.9 us: add_low(): return total.astype(BF)]
    dynamic_update_slice x24 -> x6, local copies, waits for them, and re-layouts: 140 us -> 2.33 us  [gather_projection(): lax.dynamic_update_slice_in_dim(buffer, part, (d ^ place) * size, 0)]
  transfers between devices with their start and end apart: 41 -> 184, of which waited for: 31 -> 68; matrix products, arithmetic and copies ran while one was open for 20% -> 11% of each run, Pallas kernels for 0% -> 25%
where the time goes in v1:
time: 1040 us
  Pallas kernels  348 us (33%)
  waiting for transfers between devices  309 us (30%)
  starting transfers between devices  215 us (21%)
  other arithmetic  89.5 us (9%)
  local copies, waits for them, and re-layouts  52.9 us (5%)
  between operations  22.3 us (2%)
    ppermute x74, waiting for transfers between devices, along(): return lax.ppermute(x, 'dp', [(i, i ^ bit) for i in range(self.DP)])  133 us
    pallas_call x8, Pallas kernels, mlp_backward(): pl.pallas_call(functools.partial(mlp_back_kernel, quarters, [len(w) for w...  123 us
    ppermute x74, starting transfers between devices, along(): return lax.ppermute(x, 'dp', [(i, i ^ bit) for i in range(self.DP)])  82.5 us
    pallas_call x2, Pallas kernels, attend_back(): pl.pallas_call(functools.partial(attend_back_kernel, min(256, length), bl...  75.6 us
    ppermute x18, waiting for transfers between devices, ring(): lax.ppermute(x, 'tensor', [(order[i], order[(i + 1) % self.T]) for i in r...  72.6 us
    ppermute x8, waiting for transfers between devices, partner(): return lax.ppermute(x, ('section', 'tensor'), pairs)  65.9 us
    ppermute x18, starting transfers between devices, ring(): lax.ppermute(x, 'tensor', [(order[i], order[(i + 1) % self.T]) for i in r...  43.9 us
    pallas_call x2, Pallas kernels, attend(): pl.pallas_call(functools.partial(attend_kernel, min(256, length)), grid=(...  42.3 us
  transfers between devices with their start and end apart: 184, of which 68 were waited for; matrix products, arithmetic and copies ran while one was open for 11% of the time, Pallas kernels for 25%

profile of v1, /device:TPU:0, one launch (start us, length us, event | category | flops | bytes accessed | tf_op | source)
XLA Modules:
  0.0 1036.0 jit_solution(11325516740015646872)
XLA Ops:
  0.7 4.2 pad_maximum_fusion
  8.6 7.0 collective-permute-start
  20.7 12.9 %collective-permute-done = bf16[512,1024]{1,0:T(8,128)(2,1)} collective-permute-done((bf16[512,1024]{1,0:T(8,128)(2,1)}, bf16[512,1024]{1,0:T(8,128)(2,1)}, u32[]{:S(2)}, u32[]{:S(2)}) %collective-permute-start) | collective-permute-done | bytes 1048608 | tf_op jit(solution)/shard_map/ppermute | solution.py:621
  34.0 12.4 %collective-permute-done.16.refs_5_.refs_0_ = bf16[2368,128]{1,0:T(8,128)(2,1)} collective-permute-done((bf16[2368,128]{1,0:T(8,128)(2,1)S(1)}, bf16[2368,128]{1,0:T(8,128)(2,1)}, u32[]{:S(2)}, u32[]{:S(2)}) %collective-permute-start.16) | collective-permute-done | bytes 606240 | tf_op jit(solution)/shard_map/ppermute | solution.py:602
  46.5 17.4 %collective-permute-start.26 = (bf16[2368,128]{1,0:T(8,128)(2,1)}, bf16[2368,128]{1,0:T(8,128)(2,1)}, u32[]{:S(2)}, u32[]{:S(2)}) collective-permute-start(bf16[2368,128]{1,0:T(8,128)(2,1)} %collective-permute-done.16.refs_5_.refs_0_), channel_id=1, source_target_pairs={{0,1},{1,3},{3,2},{2,0},{4,5},{5,7},{7,6},{6,4},{8,9},{9,11},{11,1... | collective-permute-start | bytes 1818632 | tf_op jit(solution)/shard_map/ppermute | solution.py:602
  69.2 3.6 collective-permute-start.2
  72.9 7.3 collective-permute-start.6
  82.7 16.8 %collective-permute-done.6 = bf16[256,768]{1,0:T(8,128)(2,1)} collective-permute-done((bf16[256,768]{1,0:T(8,128)(2,1)S(1)}, bf16[256,768]{1,0:T(8,128)(2,1)}, u32[]{:S(2)}, u32[]{:S(2)}) %collective-permute-start.6) | collective-permute-done | bytes 393248 | tf_op jit(solution)/shard_map/ppermute | solution.py:621
  101.0 4.8 fusion.73
  112.2 4.8 collective-permute-done.19.refs_8_.refs_3_
  127.4 4.1 collective-permute-done.27.refs_16_.refs_2_
  164.8 10.2 project.2
  177.8 21.3 %attend.2 = (bf16[4,512,256]{2,1,0:T(8,128)(2,1)}, bf16[4,2048,128]{2,1,0:T(8,128)(2,1)}) custom-call(s32[48]{0:T(128)} %stack.161.meta, bf16[4,2048,128]{2,1,0:T(8,128)(2,1)} %get-tuple-element.83.q_ref, bf16[4,2048,128]{2,1,0:T(8,128)(2,1)} %get-tuple-element.84.k_ref, bf16[4,2048,128]{2,1,0:T(8,128)(2,1)} %get-tuple-element.85.v_ref.refs_9_), custom_call_target="tpu_custom_call" | custom-call | flops 8589934592 | bytes 8000000 | tf_op jit(solution)/shard_map/attend/pallas_call | solution.py:249
  208.2 7.6 collective-permute-done.11
  219.1 15.2 %broadcast_select_fusion = (bf16[2368,1024]{1,0:T(8,128)(2,1)}, bf16[2368,1024]{1,0:T(8,128)(2,1)}) fusion(bf16[2368,1024]{1,0:T(8,128)(2,1)} %collective-permute-done.14, pred[]{:T(512)S(6)} %eq.84, bf16[704,1024]{1,0:T(8,128)(2,1)S(1)} %bitcast.390, bf16[704,1024]{1,0:T(8,128)(2,1)S(1)} %bitcast.392, bf16[704,1024]{1,0:T(8,128)(2,1)S(1)} %bitcast.394, ...), kind=kLoop, calls=%fused_computation.1 | loop fusion | flops 24248320 | bytes 19398656 | tf_op jit(solution)/shard_map/jit(_where)/select_n | solution.py:682
  234.3 7.1 collective-permute-start.89
  243.8 20.3 %mlp.2 = (bf16[512,1024]{1,0:T(8,128)(2,1)}, f32[512,1024]{1,0:T(8,128)}, bf16[512,1024]{1,0:T(8,128)(2,1)}, bf16[4,512,704]{2,1,0:T(8,128)(2,1)}, bf16[4,512,704]{2,1,0:T(8,128)(2,1)}) custom-call(s32[48]{0:T(128)} %stack.161.meta, bf16[512,1024]{1,0:T(8,128)(2,1)} %copy-done.2, f32[1,1024]{1,0:T(1,128)} %get-tuple-element.292.gain_ref, ...), custom_call_target="tpu_custom_call" | custom-call | flops 9932111872 | bytes 31398656 | tf_op jit(solution)/shard_map/mlp/pallas_call | solution.py:405
  274.2 24.2 %collective-permute-done.67.refs_15_.refs_1_ = bf16[2368,128]{1,0:T(8,128)(2,1)S(1)} collective-permute-done((bf16[2368,128]{1,0:T(8,128)(2,1)}, bf16[2368,128]{1,0:T(8,128)(2,1)S(1)}, u32[]{:S(2)}, u32[]{:S(2)}) %collective-permute-start.67) | collective-permute-done | bytes 606240 | tf_op jit(solution)/shard_map/ppermute | solution.py:602
  310.6 4.8 collective-permute-done.69.refs_17_.refs_3_
  320.2 8.4 collective-permute-start.72
  332.1 6.5 collective-permute-done.61.refs_9_.refs_4_
  338.6 4.4 collective-permute-start.64
  347.4 10.9 %project.3 = (bf16[4,2048,128]{2,1,0:T(8,128)(2,1)}, bf16[4,2048,128]{2,1,0:T(8,128)(2,1)}, bf16[4,2048,128]{2,1,0:T(8,128)(2,1)}) custom-call(s32[48]{0:T(128)} %stack.161.meta, bf16[512,1024]{1,0:T(8,128)(2,1)} %copy-done.16, bf16[512,1024]{1,0:T(8,128)(2,1)} %copy-done.54, bf16[512,1024]{1,0:T(8,128)(2,1)} %copy-done.55, bf16[512,1024]{1,0:T(8,128)(2,1)} %copy-done.56, ...), custom_call_target="tpu_custom_call" | custom-call | flops 3221225472 | bytes 12194304 | tf_op jit(solution)/shard_map/project/pallas_call | solution.py:145
  361.9 21.0 %attend.3 = (bf16[4,512,256]{2,1,0:T(8,128)(2,1)}, bf16[4,2048,128]{2,1,0:T(8,128)(2,1)}) custom-call(s32[48]{0:T(128)} %stack.161.meta, bf16[4,2048,128]{2,1,0:T(8,128)(2,1)} %get-tuple-element.88.q_ref, bf16[4,2048,128]{2,1,0:T(8,128)(2,1)} %get-tuple-element.89.k_ref, bf16[4,2048,128]{2,1,0:T(8,128)(2,1)} %get-tuple-element.90.v_ref), custom_call_target="tpu_custom_call" | custom-call | flops 8589934592 | bytes 8000000 | tf_op jit(solution)/shard_map/attend/pallas_call | solution.py:249
  385.8 6.5 collective-permute-start.54
  394.5 7.6 collective-permute-done.80.refs_28_.refs_4_
  410.8 20.3 %mlp.3 = (bf16[512,1024]{1,0:T(8,128)(2,1)}, f32[512,1024]{1,0:T(8,128)}, bf16[512,1024]{1,0:T(8,128)(2,1)}, bf16[4,512,704]{2,1,0:T(8,128)(2,1)}, bf16[4,512,704]{2,1,0:T(8,128)(2,1)}) custom-call(s32[48]{0:T(128)} %stack.161.meta, bf16[512,1024]{1,0:T(8,128)(2,1)} %get-tuple-element.87.x_ref, f32[1,1024]{1,0:T(1,128)} %get-tuple-element.290.gain_ref, ...), custom_call_target="tpu_custom_call" | custom-call | flops 9932111872 | bytes 31398656 | tf_op jit(solution)/shard_map/mlp/pallas_call | solution.py:405
  431.1 15.1 %mlp_back.8 = (bf16[4,2112,128]{2,1,0:T(8,128)(2,1)}, bf16[4,2112,128]{2,1,0:T(8,128)(2,1)}, f32[512,1024]{1,0:T(8,128)}) custom-call(s32[48]{0:T(128)} %stack.161.meta, bf16[512,1024]{1,0:T(8,128)(2,1)} %bitcast_select_fusion.dy_ref, bf16[512,1024]{1,0:T(8,128)(2,1)} %get-tuple-element.93.b_ref, bf16[4,512,704]{2,1,0:T(8,128)(2,1)} %get-tuple-element.94.g_ref, ...), custom_call_target="tpu_custom_call" | custom-call | flops 4429185024 | bytes 16650752 | tf_op jit(solution)/shard_map/mlp_back/pallas_call | solution.py:484
  446.2 15.4 %mlp_back.9 = (bf16[4,2112,128]{2,1,0:T(8,128)(2,1)}, bf16[4,2112,128]{2,1,0:T(8,128)(2,1)}, f32[512,1024]{1,0:T(8,128)}) custom-call(s32[48]{0:T(128)} %stack.161.meta, bf16[512,1024]{1,0:T(8,128)(2,1)} %bitcast_select_fusion.dy_ref, bf16[512,1024]{1,0:T(8,128)(2,1)} %get-tuple-element.93.b_ref, bf16[4,512,704]{2,1,0:T(8,128)(2,1)} %get-tuple-element.94.g_ref, ...), custom_call_target="tpu_custom_call" | custom-call | flops 4429185024 | bytes 16650752 | tf_op jit(solution)/shard_map/mlp_back/pallas_call | solution.py:484
  461.6 15.9 %mlp_back.10 = (bf16[4,2112,128]{2,1,0:T(8,128)(2,1)}, bf16[4,2112,128]{2,1,0:T(8,128)(2,1)}, f32[512,1024]{1,0:T(8,128)}) custom-call(s32[48]{0:T(128)} %stack.161.meta, bf16[512,1024]{1,0:T(8,128)(2,1)} %bitcast_select_fusion.dy_ref, bf16[512,1024]{1,0:T(8,128)(2,1)} %get-tuple-element.93.b_ref, bf16[4,512,704]{2,1,0:T(8,128)(2,1)} %get-tuple-element.94.g_ref, ...), custom_call_target="tpu_custom_call" | custom-call | flops 4429185024 | bytes 16650752 | tf_op jit(solution)/shard_map/mlp_back/pallas_call | solution.py:484
  477.5 15.5 %mlp_back.11 = (bf16[4,2112,128]{2,1,0:T(8,128)(2,1)}, bf16[4,2112,128]{2,1,0:T(8,128)(2,1)}, f32[512,1024]{1,0:T(8,128)}) custom-call(s32[48]{0:T(128)} %stack.161.meta, bf16[512,1024]{1,0:T(8,128)(2,1)} %bitcast_select_fusion.dy_ref, bf16[512,1024]{1,0:T(8,128)(2,1)} %get-tuple-element.93.b_ref, bf16[4,512,704]{2,1,0:T(8,128)(2,1)} %get-tuple-element.94.g_ref, ...), custom_call_target="tpu_custom_call" | custom-call | flops 4429185024 | bytes 16650752 | tf_op jit(solution)/shard_map/mlp_back/pallas_call | solution.py:484
  493.0 10.3 middle.2
  508.6 10.9 %collective-permute-done.90 = bf16[2,512,256]{2,1,0:T(8,128)(2,1)S(1)} collective-permute-done((bf16[2,512,256]{2,1,0:T(8,128)(2,1)S(1)}, bf16[2,512,256]{2,1,0:T(8,128)(2,1)S(1)}, u32[]{:S(2)}, u32[]{:S(2)}) %collective-permute-start.90) | collective-permute-done | bytes 524320 | tf_op jit(solution)/shard_map/ppermute | solution.py:625
  523.0 37.8 %attend_back.2 = (bf16[2048,256]{1,0:T(8,128)(2,1)}, bf16[2048,256]{1,0:T(8,128)(2,1)}, bf16[2048,256]{1,0:T(8,128)(2,1)}, f32[2048,256]{1,0:T(8,128)}) custom-call(s32[48]{0:T(128)} %stack.161.meta, bf16[4,2048,128]{2,1,0:T(8,128)(2,1)} %get-tuple-element.102.q_ref, bf16[4,2048,128]{2,1,0:T(8,128)(2,1)} %get-tuple-element.89.k_ref, ...), custom_call_target="tpu_custom_call" | custom-call | flops 21474836480 | bytes 12000000 | tf_op jit(solution)/shard_map/attend_back/pallas_call | solution.py:334
  560.8 11.9 %project_back.2 = (bf16[512,1024]{1,0:T(8,128)(2,1)}, bf16[512,1024]{1,0:T(8,128)(2,1)}, bf16[512,1024]{1,0:T(8,128)(2,1)}, bf16[512,1024]{1,0:T(8,128)(2,1)}, bf16[4,256,768]{2,1,0:T(8,128)(2,1)}) custom-call(s32[48]{0:T(128)} %stack.161.meta, bf16[512,1024]{1,0:T(8,128)(2,1)} %copy-done.16, bf16[512,1024]{1,0:T(8,128)(2,1)} %copy-done.54, ...), custom_call_target="tpu_custom_call" | custom-call | flops 6442450944 | bytes 16388608 | tf_op jit(solution)/shard_map/project_back/pallas_call | solution.py:182
  576.9 6.6 collective-permute-start.155
  588.0 4.2 collective-permute-done.126
  594.4 12.8 %collective-permute-done.87 = bf16[512,1024]{1,0:T(8,128)(2,1)S(1)} collective-permute-done((bf16[512,1024]{1,0:T(8,128)(2,1)S(1)}, bf16[512,1024]{1,0:T(8,128)(2,1)S(1)}, u32[]{:S(2)}, u32[]{:S(2)}) %collective-permute-start.87) | collective-permute-done | bytes 1048608 | tf_op jit(solution)/shard_map/ppermute | solution.py:621
  609.5 6.9 collective-permute-done.125
  618.1 3.6 collective-permute-done.128
  623.6 4.0 collective-permute-done.129
  666.4 15.1 %mlp_back.12 = (bf16[4,2112,128]{2,1,0:T(8,128)(2,1)}, bf16[4,2112,128]{2,1,0:T(8,128)(2,1)}, f32[512,1024]{1,0:T(8,128)}) custom-call(s32[48]{0:T(128)} %stack.161.meta, bf16[512,1024]{1,0:T(8,128)(2,1)} %get-tuple-element.165.dy_ref, bf16[512,1024]{1,0:T(8,128)(2,1)} %get-tuple-element.111.b_ref, bf16[4,512,704]{2,1,0:T(8,128)(2,1)} %get-tuple-element.112.g_ref, ...), custom_call_target="tpu_custom_call" | custom-call | flops 4429185024 | bytes 16650752 | tf_op jit(solution)/shard_map/mlp_back/pallas_call | solution.py:484
  681.5 15.4 %mlp_back.13 = (bf16[4,2112,128]{2,1,0:T(8,128)(2,1)}, bf16[4,2112,128]{2,1,0:T(8,128)(2,1)}, f32[512,1024]{1,0:T(8,128)}) custom-call(s32[48]{0:T(128)} %stack.161.meta, bf16[512,1024]{1,0:T(8,128)(2,1)} %get-tuple-element.165.dy_ref, bf16[512,1024]{1,0:T(8,128)(2,1)} %get-tuple-element.111.b_ref, bf16[4,512,704]{2,1,0:T(8,128)(2,1)} %get-tuple-element.112.g_ref, ...), custom_call_target="tpu_custom_call" | custom-call | flops 4429185024 | bytes 16650752 | tf_op jit(solution)/shard_map/mlp_back/pallas_call | solution.py:484
  696.9 15.4 %mlp_back.14 = (bf16[4,2112,128]{2,1,0:T(8,128)(2,1)}, bf16[4,2112,128]{2,1,0:T(8,128)(2,1)}, f32[512,1024]{1,0:T(8,128)}) custom-call(s32[48]{0:T(128)} %stack.161.meta, bf16[512,1024]{1,0:T(8,128)(2,1)} %get-tuple-element.165.dy_ref, bf16[512,1024]{1,0:T(8,128)(2,1)} %get-tuple-element.111.b_ref, bf16[4,512,704]{2,1,0:T(8,128)(2,1)} %get-tuple-element.112.g_ref, ...), custom_call_target="tpu_custom_call" | custom-call | flops 4429185024 | bytes 16650752 | tf_op jit(solution)/shard_map/mlp_back/pallas_call | solution.py:484
  712.3 15.8 %mlp_back.15 = (bf16[4,2112,128]{2,1,0:T(8,128)(2,1)}, bf16[4,2112,128]{2,1,0:T(8,128)(2,1)}, f32[512,1024]{1,0:T(8,128)}) custom-call(s32[48]{0:T(128)} %stack.161.meta, bf16[512,1024]{1,0:T(8,128)(2,1)} %get-tuple-element.165.dy_ref, bf16[512,1024]{1,0:T(8,128)(2,1)} %get-tuple-element.111.b_ref, bf16[4,512,704]{2,1,0:T(8,128)(2,1)} %get-tuple-element.112.g_ref, ...), custom_call_target="tpu_custom_call" | custom-call | flops 4429185024 | bytes 16650752 | tf_op jit(solution)/shard_map/mlp_back/pallas_call | solution.py:484
  728.1 10.5 %middle.3 = (f32[512,1024]{1,0:T(8,128)}, f32[1,1024]{1,0:T(1,128)}, bf16[4,512,256]{2,1,0:T(8,128)(2,1)}, bf16[4,1024,128]{2,1,0:T(8,128)(2,1)}, bf16[4,1024,128]{2,1,0:T(8,128)(2,1)}) custom-call(s32[48]{0:T(128)} %stack.161.meta, f32[512,1024]{1,0:T(8,128)} %get-tuple-element.166.dy_ref, f32[512,1024]{1,0:T(8,128)} %get-tuple-element.117.db_ref, ...), custom_call_target="tpu_custom_call" | custom-call | flops 2147483648 | bytes 16000000 | tf_op jit(solution)/shard_map/middle/pallas_call | solution.py:556
  744.4 5.7 collective-permute-done.96
  756.3 37.8 %attend_back.3 = (bf16[2048,256]{1,0:T(8,128)(2,1)}, bf16[2048,256]{1,0:T(8,128)(2,1)}, bf16[2048,256]{1,0:T(8,128)(2,1)}) custom-call(s32[48]{0:T(128)} %stack.161.meta, bf16[4,2048,128]{2,1,0:T(8,128)(2,1)} %get-tuple-element.120.q_ref, bf16[4,2048,128]{2,1,0:T(8,128)(2,1)} %get-tuple-element.84.k_ref, ...), custom_call_target="tpu_custom_call" | custom-call | flops 21474836480 | bytes 12000000 | tf_op jit(solution)/shard_map/attend_back/pallas_call | solution.py:334
  794.2 12.0 %project_back.3 = (bf16[512,1024]{1,0:T(8,128)(2,1)}, bf16[512,1024]{1,0:T(8,128)(2,1)}, bf16[512,1024]{1,0:T(8,128)(2,1)}, bf16[512,1024]{1,0:T(8,128)(2,1)}, bf16[4,256,768]{2,1,0:T(8,128)(2,1)}) custom-call(s32[48]{0:T(128)} %stack.161.meta, bf16[512,1024]{1,0:T(8,128)(2,1)} %fusion.8.refs_0_, bf16[512,1024]{1,0:T(8,128)(2,1)} %collective-permute-done.2.refs_1_, ...), custom_call_target="tpu_custom_call" | custom-call | flops 6442450944 | bytes 16388608 | tf_op jit(solution)/shard_map/project_back/pallas_call | solution.py:182
  823.7 9.3 collective-permute-done.104
  833.0 3.8 collective-permute-done.119
  837.9 13.9 %collective-permute-done.120 = bf16[256,128]{1,0:T(8,128)(2,1)S(1)} collective-permute-done((bf16[256,128]{1,0:T(8,128)(2,1)S(1)}, bf16[256,128]{1,0:T(8,128)(2,1)S(1)}, u32[]{:S(2)}, u32[]{:S(2)}) %collective-permute-start.120) | collective-permute-done | bytes 65568 | tf_op jit(solution)/shard_map/ppermute | solution.py:602
  853.6 3.4 collective-permute-done.121
  859.7 4.1 collective-permute-done.107
  879.7 4.0 collective-permute-done.135
  888.0 3.6 collective-permute-done.141
  906.1 5.1 collective-permute-done.145
  912.7 7.3 collective-permute-done.136
  925.5 9.7 collective-permute-done.142
  940.5 3.5 collective-permute-done.148
  954.2 14.3 %collective-permute-start.172 = (bf16[2112,128]{1,0:T(8,128)(2,1)S(1)}, bf16[2112,128]{1,0:T(8,128)(2,1)S(1)}, u32[]{:S(2)}, u32[]{:S(2)}) collective-permute-start(bf16[2112,128]{1,0:T(8,128)(2,1)S(1)} %add_convert_fusion.13), channel_id=1, source_target_pairs={{0,1},{1,3},{3,2},{2,0},{4,5},{5,7},{7,6},{6,4},{8,9},{9,11},{11,1... | collective-permute-start | bytes 1622024 | tf_op jit(solution)/shard_map/ppermute | solution.py:602
  969.6 20.8 %collective-permute-done.108 = bf16[256,768]{1,0:T(8,128)(2,1)S(1)} collective-permute-done((bf16[256,768]{1,0:T(8,128)(2,1)S(1)}, bf16[256,768]{1,0:T(8,128)(2,1)S(1)}, u32[]{:S(2)}, u32[]{:S(2)}) %collective-permute-start.108) | collective-permute-done | bytes 393248 | tf_op jit(solution)/shard_map/ppermute | solution.py:621
  1022.6 3.5 collective-permute-done.182
  1027.5 3.4 collective-permute-done.183
  (770 shorter events, 314.0 us)
Async XLA Ops:
  8.6 25.0 %collective-permute-start = (bf16[512,1024]{1,0:T(8,128)(2,1)}, bf16[512,1024]{1,0:T(8,128)(2,1)}, u32[]{:S(2)}, u32[]{:S(2)}) collective-permute-start(bf16[512,1024]{1,0:T(8,128)(2,1)} %dynamic-slice_bitcast_fusion.1), channel_id=1, source_target_pairs={{0,2},{1,3},{18,16},{19,17},{4,6},{5,7},{22,20},{23,21},{8,10},{9,... | collective-permute-start | bytes 3145736 | tf_op jit(solution)/shard_map/ppermute | solution.py:621
  16.8 48.8 %collective-permute-start.5 = (bf16[1024,768]{1,0:T(8,128)(2,1)}, bf16[1024,768]{1,0:T(8,128)(2,1)}, u32[]{:S(2)}, u32[]{:S(2)}) collective-permute-start(bf16[1024,768]{1,0:T(8,128)(2,1)} %pad_maximum_fusion.2), channel_id=1, source_target_pairs={{0,16},{16,0},{1,17},{17,1},{2,18},{18,2},{3,19},{19,3},{4,20},{20... | collective-permute-start | bytes 4718600 | tf_op jit(solution)/shard_map/ppermute | solution.py:598
  18.3 28.1 %collective-permute-start.16 = (bf16[2368,128]{1,0:T(8,128)(2,1)S(1)}, bf16[2368,128]{1,0:T(8,128)(2,1)}, u32[]{:S(2)}, u32[]{:S(2)}) collective-permute-start(bf16[2368,128]{1,0:T(8,128)(2,1)S(1)} %get-tuple-element.172), channel_id=1, source_target_pairs={{0,1},{1,3},{3,2},{2,0},{4,5},{5,7},{7,6},{6,4},{8,9},{9,11},{11,1... | collective-permute-start | bytes 1818632 | tf_op jit(solution)/shard_map/ppermute | solution.py:602
  20.6 48.6 %collective-permute-start.57 = (bf16[2368,128]{1,0:T(8,128)(2,1)S(1)}, bf16[2368,128]{1,0:T(8,128)(2,1)}, u32[]{:S(2)}, u32[]{:S(2)}) collective-permute-start(bf16[2368,128]{1,0:T(8,128)(2,1)S(1)} %get-tuple-element.171), channel_id=1, source_target_pairs={{0,1},{1,3},{3,2},{2,0},{4,5},{5,7},{7,6},{6,4},{8,9},{9,11},{11,1... | collective-permute-start | bytes 1818632 | tf_op jit(solution)/shard_map/ppermute | solution.py:602
  46.5 26.5 %collective-permute-start.26 = (bf16[2368,128]{1,0:T(8,128)(2,1)}, bf16[2368,128]{1,0:T(8,128)(2,1)}, u32[]{:S(2)}, u32[]{:S(2)}) collective-permute-start(bf16[2368,128]{1,0:T(8,128)(2,1)} %collective-permute-done.16.refs_5_.refs_0_), channel_id=1, source_target_pairs={{0,1},{1,3},{3,2},{2,0},{4,5},{5,7},{7,6},{6,4},{8,9},{9,11},{11,1... | collective-permute-start | bytes 1818632 | tf_op jit(solution)/shard_map/ppermute | solution.py:602
  65.1 43.8 %collective-permute-start.3 = (bf16[512,1024]{1,0:T(8,128)(2,1)}, bf16[512,1024]{1,0:T(8,128)(2,1)}, u32[]{:S(2)}, u32[]{:S(2)}) collective-permute-start(bf16[512,1024]{1,0:T(8,128)(2,1)} %fusion.8.refs_0_), channel_id=1, source_target_pairs={{0,16},{16,0},{1,17},{17,1},{2,18},{18,2},{3,19},{19,3},{4,20},{20... | collective-permute-start | bytes 3145736 | tf_op jit(solution)/shard_map/ppermute | solution.py:598
  69.2 41.4 %collective-permute-start.2 = (bf16[512,1024]{1,0:T(8,128)(2,1)}, bf16[512,1024]{1,0:T(8,128)(2,1)}, u32[]{:S(2)}, u32[]{:S(2)}) collective-permute-start(bf16[512,1024]{1,0:T(8,128)(2,1)} %fusion.8.refs_0_), channel_id=1, source_target_pairs={{0,1},{1,0},{2,3},{3,2},{4,5},{5,4},{6,7},{7,6},{8,9},{9,8},{10,11... | collective-permute-start | bytes 3145736 | tf_op jit(solution)/shard_map/ppermute | solution.py:625
  72.9 26.6 %collective-permute-start.6 = (bf16[256,768]{1,0:T(8,128)(2,1)S(1)}, bf16[256,768]{1,0:T(8,128)(2,1)}, u32[]{:S(2)}, u32[]{:S(2)}) collective-permute-start(bf16[256,768]{1,0:T(8,128)(2,1)S(1)} %constant_dynamic-slice_fusion.4), channel_id=1, source_target_pairs={{0,2},{1,3},{18,16},{19,17},{4,6},{5,7},{22,20},{23,21},{8,10},{9,... | collective-permute-start | bytes 1179656 | tf_op jit(solution)/shard_map/ppermute | solution.py:621
  80.3 25.5 %collective-permute-start.17 = (bf16[2368,128]{1,0:T(8,128)(2,1)}, bf16[2368,128]{1,0:T(8,128)(2,1)}, u32[]{:S(2)}, u32[]{:S(2)}) collective-permute-start(bf16[2368,128]{1,0:T(8,128)(2,1)} %collective-permute-done.16.refs_5_.refs_0_), channel_id=1, source_target_pairs={{0,4},{4,0},{8,12},{12,8},{1,5},{5,1},{9,13},{13,9},{2,6},{6,2},{1... | collective-permute-start | bytes 1818632 | tf_op jit(solution)/shard_map/ppermute | solution.py:605
  82.7 136.0 %collective-permute-start.14 = (bf16[2368,1024]{1,0:T(8,128)(2,1)}, bf16[2368,1024]{1,0:T(8,128)(2,1)}, u32[]{:S(2)}, u32[]{:S(2)}) collective-permute-start(bf16[2368,1024]{1,0:T(8,128)(2,1)} %pad_maximum_fusion), channel_id=1, source_target_pairs={{0,16},{16,0},{1,17},{17,1},{2,18},{18,2},{3,19},{19,3},{4,20},{20... | collective-permute-start | bytes 14549000 | tf_op jit(solution)/shard_map/ppermute | solution.py:598
  121.5 40.2 %collective-permute-start.4 = (bf16[512,1024]{1,0:T(8,128)(2,1)}, bf16[512,1024]{1,0:T(8,128)(2,1)}, u32[]{:S(2)}, u32[]{:S(2)}) collective-permute-start(bf16[512,1024]{1,0:T(8,128)(2,1)} %collective-permute-done.2.refs_1_), channel_id=1, source_target_pairs={{0,16},{16,0},{1,17},{17,1},{2,18},{18,2},{3,19},{19,3},{4,20},{20... | collective-permute-start | bytes 3145736 | tf_op jit(solution)/shard_map/ppermute | solution.py:598
  127.4 33.6 %collective-permute-start.36 = (bf16[2368,128]{1,0:T(8,128)(2,1)}, bf16[2368,128]{1,0:T(8,128)(2,1)}, u32[]{:S(2)}, u32[]{:S(2)}) collective-permute-start(bf16[2368,128]{1,0:T(8,128)(2,1)} %collective-permute-done.26.refs_15_.refs_1_), channel_id=1, source_target_pairs={{0,1},{1,3},{3,2},{2,0},{4,5},{5,7},{7,6},{6,4},{8,9},{9,11},{11,1... | collective-permute-start | bytes 1818632 | tf_op jit(solution)/shard_map/ppermute | solution.py:602
  131.5 29.6 %collective-permute-start.31 = (bf16[2368,128]{1,0:T(8,128)(2,1)}, bf16[2368,128]{1,0:T(8,128)(2,1)}, u32[]{:S(2)}, u32[]{:S(2)}) collective-permute-start(bf16[2368,128]{1,0:T(8,128)(2,1)} %collective-permute-done.26.refs_15_.refs_1_), channel_id=1, source_target_pairs={{0,16},{16,0},{1,17},{17,1},{2,18},{18,2},{3,19},{19,3},{4,20},{20... | collective-permute-start | bytes 1818632 | tf_op jit(solution)/shard_map/ppermute | solution.py:598
  132.2 22.1 %collective-permute-start.10 = (bf16[128,768]{1,0:T(8,128)(2,1)}, bf16[128,768]{1,0:T(8,128)(2,1)}, u32[]{:S(2)}, u32[]{:S(2)}) collective-permute-start(bf16[128,768]{1,0:T(8,128)(2,1)} %slice.599), channel_id=1, source_target_pairs={{16,24},{17,25},{2,10},{3,11},{20,28},{21,29},{6,14},{7,15},{24,16... | collective-permute-start | bytes 589832 | tf_op jit(solution)/shard_map/ppermute | solution.py:613
  175.0 26.3 %collective-permute-start.30 = (bf16[1184,128]{1,0:T(8,128)(2,1)}, bf16[1184,128]{1,0:T(8,128)(2,1)}, u32[]{:S(2)}, u32[]{:S(2)}) collective-permute-start(bf16[1184,128]{1,0:T(8,128)(2,1)} %slice.605), channel_id=1, source_target_pairs={{0,8},{4,12},{8,0},{12,4},{1,9},{5,13},{9,1},{13,5},{2,10},{6,14},... | collective-permute-start | bytes 909320 | tf_op jit(solution)/shard_map/ppermute | solution.py:605
  176.5 24.9 %collective-permute-start.41 = (bf16[2368,128]{1,0:T(8,128)(2,1)}, bf16[2368,128]{1,0:T(8,128)(2,1)}, u32[]{:S(2)}, u32[]{:S(2)}) collective-permute-start(bf16[2368,128]{1,0:T(8,128)(2,1)} %collective-permute-done.36.refs_25_.refs_1_), channel_id=1, source_target_pairs={{0,16},{16,0},{1,17},{17,1},{2,18},{18,2},{3,19},{19,3},{4,20},{20... | collective-permute-start | bytes 1818632 | tf_op jit(solution)/shard_map/ppermute | solution.py:598
  176.6 25.9 %collective-permute-start.38 = (bf16[2368,128]{1,0:T(8,128)(2,1)}, bf16[2368,128]{1,0:T(8,128)(2,1)S(1)}, u32[]{:S(2)}, u32[]{:S(2)}) collective-permute-start(bf16[2368,128]{1,0:T(8,128)(2,1)} %collective-permute-done.36.refs_25_.refs_1_), channel_id=1, source_target_pairs={{0,8},{4,12},{8,0},{12,4},{1,9},{5,13},{9,1},{13,5},{2,10},{6,14},... | collective-permute-start | bytes 1818632 | tf_op jit(solution)/shard_map/ppermute | solution.py:605
  177.3 25.4 %collective-permute-start.37 = (bf16[2368,128]{1,0:T(8,128)(2,1)}, bf16[2368,128]{1,0:T(8,128)(2,1)S(1)}, u32[]{:S(2)}, u32[]{:S(2)}) collective-permute-start(bf16[2368,128]{1,0:T(8,128)(2,1)} %collective-permute-done.36.refs_25_.refs_1_), channel_id=1, source_target_pairs={{0,4},{4,0},{8,12},{12,8},{1,5},{5,1},{9,13},{13,9},{2,6},{6,2},{1... | collective-permute-start | bytes 1818632 | tf_op jit(solution)/shard_map/ppermute | solution.py:605
  217.2 24.2 %collective-permute-start.43 = (bf16[2368,128]{1,0:T(8,128)(2,1)S(1)}, bf16[2368,128]{1,0:T(8,128)(2,1)S(1)}, u32[]{:S(2)}, u32[]{:S(2)}) collective-permute-start(bf16[2368,128]{1,0:T(8,128)(2,1)S(1)} %collective-permute-done.38.refs_27_.refs_3_), channel_id=1, source_target_pairs={{0,16},{16,0},{1,17},{17,1},{2,18},{18,2},{3,19},{19,3},{4,20},{20... | collective-permute-start | bytes 1818632 | tf_op jit(solution)/shard_map/ppermute | solution.py:598
  217.8 24.4 %collective-permute-start.42 = (bf16[2368,128]{1,0:T(8,128)(2,1)S(1)}, bf16[2368,128]{1,0:T(8,128)(2,1)S(1)}, u32[]{:S(2)}, u32[]{:S(2)}) collective-permute-start(bf16[2368,128]{1,0:T(8,128)(2,1)S(1)} %collective-permute-done.37.refs_26_.refs_2_), channel_id=1, source_target_pairs={{0,16},{16,0},{1,17},{17,1},{2,18},{18,2},{3,19},{19,3},{4,20},{20... | collective-permute-start | bytes 1818632 | tf_op jit(solution)/shard_map/ppermute | solution.py:598
  218.5 23.6 %collective-permute-start.45 = (bf16[1184,128]{1,0:T(8,128)(2,1)S(1)}, bf16[1184,128]{1,0:T(8,128)(2,1)S(1)}, u32[]{:S(2)}, u32[]{:S(2)}) collective-permute-start(bf16[1184,128]{1,0:T(8,128)(2,1)S(1)} %collective-permute-done.40.refs_29_.refs_5_), channel_id=1, source_target_pairs={{0,16},{16,0},{1,17},{17,1},{2,18},{18,2},{3,19},{19,3},{4,20},{20... | collective-permute-start | bytes 909320 | tf_op jit(solution)/shard_map/ppermute | solution.py:598
  218.6 23.6 %collective-permute-start.13 = (bf16[512,256]{1,0:T(8,128)(2,1)S(1)}, bf16[512,256]{1,0:T(8,128)(2,1)S(1)}, u32[]{:S(2)}, u32[]{:S(2)}) collective-permute-start(bf16[512,256]{1,0:T(8,128)(2,1)S(1)} %get-tuple-element.281), channel_id=1, source_target_pairs={{0,16},{16,0},{1,17},{17,1},{2,18},{18,2},{3,19},{19,3},{4,20},{20... | collective-permute-start | bytes 786440 | tf_op jit(solution)/shard_map/ppermute | solution.py:598
  234.3 38.3 %collective-permute-start.89 = (bf16[512,1024]{1,0:T(8,128)(2,1)}, bf16[512,1024]{1,0:T(8,128)(2,1)}, u32[]{:S(2)}, u32[]{:S(2)}) collective-permute-start(bf16[512,1024]{1,0:T(8,128)(2,1)} %dynamic-slice_bitcast_fusion), channel_id=1, source_target_pairs={{0,2},{1,3},{18,16},{19,17},{4,6},{5,7},{22,20},{23,21},{8,10},{9,... | collective-permute-start | bytes 3145736 | tf_op jit(solution)/shard_map/ppermute | solution.py:621
  241.4 31.3 %collective-permute-start.59 = (bf16[2368,128]{1,0:T(8,128)(2,1)}, bf16[2368,128]{1,0:T(8,128)(2,1)S(1)}, u32[]{:S(2)}, u32[]{:S(2)}) collective-permute-start(bf16[2368,128]{1,0:T(8,128)(2,1)} %collective-permute-done.57.refs_5_.refs_0_), channel_id=1, source_target_pairs={{0,8},{4,12},{8,0},{12,4},{1,9},{5,13},{9,1},{13,5},{2,10},{6,14},... | collective-permute-start | bytes 1818632 | tf_op jit(solution)/shard_map/ppermute | solution.py:605
  267.2 42.2 %collective-permute-start.46 = (bf16[512,1024]{1,0:T(8,128)(2,1)S(1)}, bf16[512,1024]{1,0:T(8,128)(2,1)S(1)}, u32[]{:S(2)}, u32[]{:S(2)}) collective-permute-start(bf16[512,1024]{1,0:T(8,128)(2,1)S(1)} %fusion.16.refs_0_), channel_id=1, source_target_pairs={{0,1},{1,0},{2,3},{3,2},{4,5},{5,4},{6,7},{7,6},{8,9},{9,8},{10,11... | collective-permute-start | bytes 3145736 | tf_op jit(solution)/shard_map/ppermute | solution.py:625
  267.8 30.6 %collective-permute-start.67 = (bf16[2368,128]{1,0:T(8,128)(2,1)}, bf16[2368,128]{1,0:T(8,128)(2,1)S(1)}, u32[]{:S(2)}, u32[]{:S(2)}) collective-permute-start(bf16[2368,128]{1,0:T(8,128)(2,1)} %collective-permute-done.57.refs_5_.refs_0_), channel_id=1, source_target_pairs={{0,1},{1,3},{3,2},{2,0},{4,5},{5,7},{7,6},{6,4},{8,9},{9,11},{11,1... | collective-permute-start | bytes 1818632 | tf_op jit(solution)/shard_map/ppermute | solution.py:602
  269.3 33.2 %collective-permute-start.49 = (bf16[256,768]{1,0:T(8,128)(2,1)S(1)}, bf16[256,768]{1,0:T(8,128)(2,1)S(1)}, u32[]{:S(2)}, u32[]{:S(2)}) collective-permute-start(bf16[256,768]{1,0:T(8,128)(2,1)S(1)} %constant_dynamic-slice_fusion.1), channel_id=1, source_target_pairs={{0,2},{1,3},{18,16},{19,17},{4,6},{5,7},{22,20},{23,21},{8,10},{9,... | collective-permute-start | bytes 1179656 | tf_op jit(solution)/shard_map/ppermute | solution.py:621
  272.7 30.5 %collective-permute-start.62 = (bf16[2368,128]{1,0:T(8,128)(2,1)}, bf16[2368,128]{1,0:T(8,128)(2,1)S(1)}, u32[]{:S(2)}, u32[]{:S(2)}) collective-permute-start(bf16[2368,128]{1,0:T(8,128)(2,1)} %collective-permute-done.57.refs_5_.refs_0_), channel_id=1, source_target_pairs={{0,16},{16,0},{1,17},{17,1},{2,18},{18,2},{3,19},{19,3},{4,20},{20... | collective-permute-start | bytes 1818632 | tf_op jit(solution)/shard_map/ppermute | solution.py:598
  272.8 31.5 %collective-permute-start.58 = (bf16[2368,128]{1,0:T(8,128)(2,1)}, bf16[2368,128]{1,0:T(8,128)(2,1)S(1)}, u32[]{:S(2)}, u32[]{:S(2)}) collective-permute-start(bf16[2368,128]{1,0:T(8,128)(2,1)} %collective-permute-done.57.refs_5_.refs_0_), channel_id=1, source_target_pairs={{0,4},{4,0},{8,12},{12,8},{1,5},{5,1},{9,13},{13,9},{2,6},{6,2},{1... | collective-permute-start | bytes 1818632 | tf_op jit(solution)/shard_map/ppermute | solution.py:605
  309.3 34.2 %collective-permute-start.47 = (bf16[512,1024]{1,0:T(8,128)(2,1)S(1)}, bf16[512,1024]{1,0:T(8,128)(2,1)S(1)}, u32[]{:S(2)}, u32[]{:S(2)}) collective-permute-start(bf16[512,1024]{1,0:T(8,128)(2,1)S(1)} %fusion.16.refs_0_), channel_id=1, source_target_pairs={{0,16},{16,0},{1,17},{17,1},{2,18},{18,2},{3,19},{19,3},{4,20},{20... | collective-permute-start | bytes 3145736 | tf_op jit(solution)/shard_map/ppermute | solution.py:598
  309.4 34.2 %collective-permute-start.48 = (bf16[512,1024]{1,0:T(8,128)(2,1)S(1)}, bf16[512,1024]{1,0:T(8,128)(2,1)S(1)}, u32[]{:S(2)}, u32[]{:S(2)}) collective-permute-start(bf16[512,1024]{1,0:T(8,128)(2,1)S(1)} %collective-permute-done.46.refs_1_), channel_id=1, source_target_pairs={{0,16},{16,0},{1,17},{17,1},{2,18},{18,2},{3,19},{19,3},{4,20},{20... | collective-permute-start | bytes 3145736 | tf_op jit(solution)/shard_map/ppermute | solution.py:598
  315.4 27.6 %collective-permute-start.77 = (bf16[2368,128]{1,0:T(8,128)(2,1)S(1)}, bf16[2368,128]{1,0:T(8,128)(2,1)}, u32[]{:S(2)}, u32[]{:S(2)}) collective-permute-start(bf16[2368,128]{1,0:T(8,128)(2,1)S(1)} %collective-permute-done.67.refs_15_.refs_1_), channel_id=1, source_target_pairs={{0,1},{1,3},{3,2},{2,0},{4,5},{5,7},{7,6},{6,4},{8,9},{9,11},{11,1... | collective-permute-start | bytes 1818632 | tf_op jit(solution)/shard_map/ppermute | solution.py:602
  320.2 22.9 %collective-permute-start.72 = (bf16[2368,128]{1,0:T(8,128)(2,1)S(1)}, bf16[2368,128]{1,0:T(8,128)(2,1)S(1)}, u32[]{:S(2)}, u32[]{:S(2)}) collective-permute-start(bf16[2368,128]{1,0:T(8,128)(2,1)S(1)} %collective-permute-done.67.refs_15_.refs_1_), channel_id=1, source_target_pairs={{0,16},{16,0},{1,17},{17,1},{2,18},{18,2},{3,19},{19,3},{4,20},{20... | collective-permute-start | bytes 1818632 | tf_op jit(solution)/shard_map/ppermute | solution.py:598
  358.3 24.6 %collective-permute-start.71 = (bf16[1184,128]{1,0:T(8,128)(2,1)S(1)}, bf16[1184,128]{1,0:T(8,128)(2,1)S(1)}, u32[]{:S(2)}, u32[]{:S(2)}) collective-permute-start(bf16[1184,128]{1,0:T(8,128)(2,1)S(1)} %slice.617), channel_id=1, source_target_pairs={{0,8},{4,12},{8,0},{12,4},{1,9},{5,13},{9,1},{13,5},{2,10},{6,14},... | collective-permute-start | bytes 909320 | tf_op jit(solution)/shard_map/ppermute | solution.py:605
  359.5 32.9 %collective-permute-start.82 = (bf16[2368,128]{1,0:T(8,128)(2,1)}, bf16[2368,128]{1,0:T(8,128)(2,1)}, u32[]{:S(2)}, u32[]{:S(2)}) collective-permute-start(bf16[2368,128]{1,0:T(8,128)(2,1)} %collective-permute-done.77.refs_25_.refs_1_), channel_id=1, source_target_pairs={{0,16},{16,0},{1,17},{17,1},{2,18},{18,2},{3,19},{19,3},{4,20},{20... | collective-permute-start | bytes 1818632 | tf_op jit(solution)/shard_map/ppermute | solution.py:598
  359.5 26.3 %collective-permute-start.79 = (bf16[2368,128]{1,0:T(8,128)(2,1)}, bf16[2368,128]{1,0:T(8,128)(2,1)S(1)}, u32[]{:S(2)}, u32[]{:S(2)}) collective-permute-start(bf16[2368,128]{1,0:T(8,128)(2,1)} %collective-permute-done.77.refs_25_.refs_1_), channel_id=1, source_target_pairs={{0,8},{4,12},{8,0},{12,4},{1,9},{5,13},{9,1},{13,5},{2,10},{6,14},... | collective-permute-start | bytes 1818632 | tf_op jit(solution)/shard_map/ppermute | solution.py:605
  360.4 32.2 %collective-permute-start.78 = (bf16[2368,128]{1,0:T(8,128)(2,1)}, bf16[2368,128]{1,0:T(8,128)(2,1)S(1)}, u32[]{:S(2)}, u32[]{:S(2)}) collective-permute-start(bf16[2368,128]{1,0:T(8,128)(2,1)} %collective-permute-done.77.refs_25_.refs_1_), channel_id=1, source_target_pairs={{0,4},{4,0},{8,12},{12,8},{1,5},{5,1},{9,13},{13,9},{2,6},{6,2},{1... | collective-permute-start | bytes 1818632 | tf_op jit(solution)/shard_map/ppermute | solution.py:605
  361.9 31.4 %collective-permute-start.74 = (bf16[2368,128]{1,0:T(8,128)(2,1)S(1)}, bf16[2368,128]{1,0:T(8,128)(2,1)S(1)}, u32[]{:S(2)}, u32[]{:S(2)}) collective-permute-start(bf16[2368,128]{1,0:T(8,128)(2,1)S(1)} %collective-permute-done.69.refs_17_.refs_3_), channel_id=1, source_target_pairs={{0,16},{16,0},{1,17},{17,1},{2,18},{18,2},{3,19},{19,3},{4,20},{20... | collective-permute-start | bytes 1818632 | tf_op jit(solution)/shard_map/ppermute | solution.py:598
  520.8 64.0 %collective-permute-start.123 = (bf16[4,1024,128]{2,1,0:T(8,128)(2,1)}, bf16[4,1024,128]{2,1,0:T(8,128)(2,1)}, u32[]{:S(2)}, u32[]{:S(2)}) collective-permute-start(bf16[4,1024,128]{2,1,0:T(8,128)(2,1)} %get-tuple-element.135), channel_id=1, source_target_pairs={{0,16},{16,0},{1,17},{17,1},{2,18},{18,2},{3,19},{19,3},{4,20},{20... | collective-permute-start | bytes 3145736 | tf_op jit(solution)/shard_map/ppermute | solution.py:598
  575.6 31.6 %collective-permute-start.87 = (bf16[512,1024]{1,0:T(8,128)(2,1)S(1)}, bf16[512,1024]{1,0:T(8,128)(2,1)S(1)}, u32[]{:S(2)}, u32[]{:S(2)}) collective-permute-start(bf16[512,1024]{1,0:T(8,128)(2,1)S(1)} %copy-done.57), channel_id=1, source_target_pairs={{2,0},{3,1},{16,18},{17,19},{6,4},{7,5},{20,22},{21,23},{10,8},{11... | collective-permute-start | bytes 3145736 | tf_op jit(solution)/shard_map/ppermute | solution.py:621
  576.9 51.7 %collective-permute-start.155 = (bf16[4,2112,128]{2,1,0:T(8,128)(2,1)}, bf16[4,2112,128]{2,1,0:T(8,128)(2,1)S(1)}, u32[]{:S(2)}, u32[]{:S(2)}) collective-permute-start(bf16[4,2112,128]{2,1,0:T(8,128)(2,1)} %get-tuple-element.145), channel_id=1, source_target_pairs={{0,16},{16,0},{1,17},{17,1},{2,18},{18,2},{3,19},{19,3},{4,20},{20... | collective-permute-start | bytes 6488072 | tf_op jit(solution)/shard_map/ppermute | solution.py:598
  583.5 44.0 %collective-permute-start.94 = (bf16[512,1024]{1,0:T(8,128)(2,1)}, bf16[512,1024]{1,0:T(8,128)(2,1)S(1)}, u32[]{:S(2)}, u32[]{:S(2)}) collective-permute-start(bf16[512,1024]{1,0:T(8,128)(2,1)} %get-tuple-element.110), channel_id=1, source_target_pairs={{0,16},{16,0},{1,17},{17,1},{2,18},{18,2},{3,19},{19,3},{4,20},{20... | collective-permute-start | bytes 3145736 | tf_op jit(solution)/shard_map/ppermute | solution.py:598
  592.2 29.6 %collective-permute-start.112 = (bf16[256,768]{1,0:T(8,128)(2,1)S(1)}, bf16[256,768]{1,0:T(8,128)(2,1)S(1)}, u32[]{:S(2)}, u32[]{:S(2)}) collective-permute-start(bf16[256,768]{1,0:T(8,128)(2,1)S(1)} %pad_maximum_fusion.28), channel_id=1, source_target_pairs={{0,8},{4,12},{8,0},{12,4},{1,9},{5,13},{9,1},{13,5},{2,10},{6,14},... | collective-permute-start | bytes 1179656 | tf_op jit(solution)/shard_map/ppermute | solution.py:605
  627.6 33.5 %collective-permute-start.93 = (bf16[512,1024]{1,0:T(8,128)(2,1)S(1)}, bf16[512,1024]{1,0:T(8,128)(2,1)S(1)}, u32[]{:S(2)}, u32[]{:S(2)}) collective-permute-start(bf16[512,1024]{1,0:T(8,128)(2,1)S(1)} %copy-done.126), channel_id=1, source_target_pairs={{0,16},{16,0},{1,17},{17,1},{2,18},{18,2},{3,19},{19,3},{4,20},{20... | collective-permute-start | bytes 3145736 | tf_op jit(solution)/shard_map/ppermute | solution.py:598
  628.6 33.7 %collective-permute-start.95 = (bf16[512,1024]{1,0:T(8,128)(2,1)S(1)}, bf16[512,1024]{1,0:T(8,128)(2,1)S(1)}, u32[]{:S(2)}, u32[]{:S(2)}) collective-permute-start(bf16[512,1024]{1,0:T(8,128)(2,1)S(1)} %add_convert_fusion.11), channel_id=1, source_target_pairs={{0,1},{1,0},{2,3},{3,2},{4,5},{5,4},{6,7},{7,6},{8,9},{9,8},{10,11... | collective-permute-start | bytes 3145736 | tf_op jit(solution)/shard_map/ppermute | solution.py:625
  653.6 97.2 %collective-permute-start.159 = (bf16[2112,128]{1,0:T(8,128)(2,1)}, bf16[2112,128]{1,0:T(8,128)(2,1)}, u32[]{:S(2)}, u32[]{:S(2)}) collective-permute-start(bf16[2112,128]{1,0:T(8,128)(2,1)} %pad_maximum_fusion.14), channel_id=1, source_target_pairs={{0,8},{4,12},{8,0},{12,4},{1,9},{5,13},{9,1},{13,5},{2,10},{6,14},... | collective-permute-start | bytes 1622024 | tf_op jit(solution)/shard_map/ppermute | solution.py:605
  656.5 94.9 %collective-permute-start.157 = (bf16[2112,128]{1,0:T(8,128)(2,1)}, bf16[2112,128]{1,0:T(8,128)(2,1)}, u32[]{:S(2)}, u32[]{:S(2)}) collective-permute-start(bf16[2112,128]{1,0:T(8,128)(2,1)} %pad_maximum_fusion.13), channel_id=1, source_target_pairs={{0,4},{4,0},{8,12},{12,8},{1,5},{5,1},{9,13},{13,9},{2,6},{6,2},{1... | collective-permute-start | bytes 1622024 | tf_op jit(solution)/shard_map/ppermute | solution.py:605
  659.9 156.0 %collective-permute-start.165 = (bf16[2112,128]{1,0:T(8,128)(2,1)}, bf16[2112,128]{1,0:T(8,128)(2,1)}, u32[]{:S(2)}, u32[]{:S(2)}) collective-permute-start(bf16[2112,128]{1,0:T(8,128)(2,1)} %pad_maximum_fusion.16), channel_id=1, source_target_pairs={{0,8},{4,12},{8,0},{12,4},{1,9},{5,13},{9,1},{13,5},{2,10},{6,14},... | collective-permute-start | bytes 1622024 | tf_op jit(solution)/shard_map/ppermute | solution.py:605
  661.1 155.9 %collective-permute-start.163 = (bf16[2112,128]{1,0:T(8,128)(2,1)}, bf16[2112,128]{1,0:T(8,128)(2,1)}, u32[]{:S(2)}, u32[]{:S(2)}) collective-permute-start(bf16[2112,128]{1,0:T(8,128)(2,1)} %pad_maximum_fusion.15), channel_id=1, source_target_pairs={{0,4},{4,0},{8,12},{12,8},{1,5},{5,1},{9,13},{13,9},{2,6},{6,2},{1... | collective-permute-start | bytes 1622024 | tf_op jit(solution)/shard_map/ppermute | solution.py:605
  750.9 55.3 %collective-permute-start.115 = (bf16[4,1024,128]{2,1,0:T(8,128)(2,1)}, bf16[4,1024,128]{2,1,0:T(8,128)(2,1)}, u32[]{:S(2)}, u32[]{:S(2)}) collective-permute-start(bf16[4,1024,128]{2,1,0:T(8,128)(2,1)} %get-tuple-element.133), channel_id=1, source_target_pairs={{0,16},{16,0},{1,17},{17,1},{2,18},{18,2},{3,19},{19,3},{4,20},{20... | collective-permute-start | bytes 3145736 | tf_op jit(solution)/shard_map/ppermute | solution.py:598
  753.8 64.2 %collective-permute-start.160 = (bf16[2112,128]{1,0:T(8,128)(2,1)}, bf16[2112,128]{1,0:T(8,128)(2,1)}, u32[]{:S(2)}, u32[]{:S(2)}) collective-permute-start(bf16[2112,128]{1,0:T(8,128)(2,1)} %fusion.33), channel_id=1, source_target_pairs={{0,1},{1,3},{3,2},{2,0},{4,5},{5,7},{7,6},{6,4},{8,9},{9,11},{11,1... | collective-permute-start | bytes 1622024 | tf_op jit(solution)/shard_map/ppermute | solution.py:602
  813.5 38.5 %collective-permute-start.171 = (bf16[2112,128]{1,0:T(8,128)(2,1)S(1)}, bf16[2112,128]{1,0:T(8,128)(2,1)S(1)}, u32[]{:S(2)}, u32[]{:S(2)}) collective-permute-start(bf16[2112,128]{1,0:T(8,128)(2,1)S(1)} %copy-done.82), channel_id=1, source_target_pairs={{0,8},{4,12},{8,0},{12,4},{1,9},{5,13},{9,1},{13,5},{2,10},{6,14},... | collective-permute-start | bytes 1622024 | tf_op jit(solution)/shard_map/ppermute | solution.py:605
  821.9 30.1 %collective-permute-start.169 = (bf16[2112,128]{1,0:T(8,128)(2,1)S(1)}, bf16[2112,128]{1,0:T(8,128)(2,1)S(1)}, u32[]{:S(2)}, u32[]{:S(2)}) collective-permute-start(bf16[2112,128]{1,0:T(8,128)(2,1)S(1)} %copy-done.81), channel_id=1, source_target_pairs={{0,4},{4,0},{8,12},{12,8},{1,5},{5,1},{9,13},{13,9},{2,6},{6,2},{1... | collective-permute-start | bytes 1622024 | tf_op jit(solution)/shard_map/ppermute | solution.py:605
  832.9 38.8 %collective-permute-start.132 = (bf16[4,2112,128]{2,1,0:T(8,128)(2,1)S(1)}, bf16[4,2112,128]{2,1,0:T(8,128)(2,1)S(1)}, u32[]{:S(2)}, u32[]{:S(2)}) collective-permute-start(bf16[4,2112,128]{2,1,0:T(8,128)(2,1)S(1)} %copy-done.121), channel_id=1, source_target_pairs={{0,16},{16,0},{1,17},{17,1},{2,18},{18,2},{3,19},{19,3},{4,20},{20... | collective-permute-start | bytes 6488072 | tf_op jit(solution)/shard_map/ppermute | solution.py:598
  868.9 83.5 %collective-permute-start.113 = (bf16[256,768]{1,0:T(8,128)(2,1)S(1)}, bf16[256,768]{1,0:T(8,128)(2,1)S(1)}, u32[]{:S(2)}, u32[]{:S(2)}) collective-permute-start(bf16[256,768]{1,0:T(8,128)(2,1)S(1)} %fusion.49), channel_id=1, source_target_pairs={{2,0},{3,1},{16,18},{17,19},{6,4},{7,5},{20,22},{21,23},{10,8},{11... | collective-permute-start | bytes 1179656 | tf_op jit(solution)/shard_map/ppermute | solution.py:621
  871.8 51.2 %collective-permute-start.99 = (bf16[512,1024]{1,0:T(8,128)(2,1)S(1)}, bf16[512,1024]{1,0:T(8,128)(2,1)S(1)}, u32[]{:S(2)}, u32[]{:S(2)}) collective-permute-start(bf16[512,1024]{1,0:T(8,128)(2,1)S(1)} %copy-done.125), channel_id=1, source_target_pairs={{0,16},{16,0},{1,17},{17,1},{2,18},{18,2},{3,19},{19,3},{4,20},{20... | collective-permute-start | bytes 3145736 | tf_op jit(solution)/shard_map/ppermute | solution.py:598
  872.8 51.2 %collective-permute-start.101 = (bf16[512,1024]{1,0:T(8,128)(2,1)S(1)}, bf16[512,1024]{1,0:T(8,128)(2,1)S(1)}, u32[]{:S(2)}, u32[]{:S(2)}) collective-permute-start(bf16[512,1024]{1,0:T(8,128)(2,1)S(1)} %add_convert_fusion.10), channel_id=1, source_target_pairs={{0,1},{1,0},{2,3},{3,2},{4,5},{5,4},{6,7},{7,6},{8,9},{9,8},{10,11... | collective-permute-start | bytes 3145736 | tf_op jit(solution)/shard_map/ppermute | solution.py:625
  923.0 21.0 %collective-permute-start.148 = (bf16[2112,128]{1,0:T(8,128)(2,1)S(1)}, bf16[2112,128]{1,0:T(8,128)(2,1)S(1)}, u32[]{:S(2)}, u32[]{:S(2)}) collective-permute-start(bf16[2112,128]{1,0:T(8,128)(2,1)S(1)} %pad_maximum_fusion.10), channel_id=1, source_target_pairs={{0,8},{4,12},{8,0},{12,4},{1,9},{5,13},{9,1},{13,5},{2,10},{6,14},... | collective-permute-start | bytes 1622024 | tf_op jit(solution)/shard_map/ppermute | solution.py:605
  939.0 51.9 %collective-permute-start.102 = (bf16[512,1024]{1,0:T(8,128)(2,1)S(1)}, bf16[512,1024]{1,0:T(8,128)(2,1)S(1)}, u32[]{:S(2)}, u32[]{:S(2)}) collective-permute-start(bf16[512,1024]{1,0:T(8,128)(2,1)S(1)} %fusion.13), channel_id=1, source_target_pairs={{2,0},{3,1},{16,18},{17,19},{6,4},{7,5},{20,22},{21,23},{10,8},{11... | collective-permute-start | bytes 3145736 | tf_op jit(solution)/shard_map/ppermute | solution.py:621
  947.2 21.3 %collective-permute-start.175 = (bf16[2112,128]{1,0:T(8,128)(2,1)S(1)}, bf16[2112,128]{1,0:T(8,128)(2,1)S(1)}, u32[]{:S(2)}, u32[]{:S(2)}) collective-permute-start(bf16[2112,128]{1,0:T(8,128)(2,1)S(1)} %copy-done.79), channel_id=1, source_target_pairs={{0,4},{4,0},{8,12},{12,8},{1,5},{5,1},{9,13},{13,9},{2,6},{6,2},{1... | collective-permute-start | bytes 1622024 | tf_op jit(solution)/shard_map/ppermute | solution.py:605
  950.9 39.6 %collective-permute-start.108 = (bf16[256,768]{1,0:T(8,128)(2,1)S(1)}, bf16[256,768]{1,0:T(8,128)(2,1)S(1)}, u32[]{:S(2)}, u32[]{:S(2)}) collective-permute-start(bf16[256,768]{1,0:T(8,128)(2,1)S(1)} %fusion.51), channel_id=1, source_target_pairs={{2,0},{3,1},{16,18},{17,19},{6,4},{7,5},{20,22},{21,23},{10,8},{11... | collective-permute-start | bytes 1179656 | tf_op jit(solution)/shard_map/ppermute | solution.py:621
  952.5 51.4 %collective-permute-start.88 = (bf16[2,512,1024]{2,1,0:T(8,128)(2,1)S(1)}, bf16[2,512,1024]{2,1,0:T(8,128)(2,1)S(1)}, u32[]{:S(2)}, u32[]{:S(2)}) collective-permute-start(bf16[2,512,1024]{2,1,0:T(8,128)(2,1)S(1)} %copy-done.35), channel_id=1, source_target_pairs={{0,16},{16,0},{1,17},{17,1},{2,18},{18,2},{3,19},{19,3},{4,20},{20... | collective-permute-start | bytes 6291464 | tf_op jit(solution)/shard_map/ppermute | solution.py:598
  954.2 42.0 %collective-permute-start.172 = (bf16[2112,128]{1,0:T(8,128)(2,1)S(1)}, bf16[2112,128]{1,0:T(8,128)(2,1)S(1)}, u32[]{:S(2)}, u32[]{:S(2)}) collective-permute-start(bf16[2112,128]{1,0:T(8,128)(2,1)S(1)} %add_convert_fusion.13), channel_id=1, source_target_pairs={{0,1},{1,3},{3,2},{2,0},{4,5},{5,7},{7,6},{6,4},{8,9},{9,11},{11,1... | collective-permute-start | bytes 1622024 | tf_op jit(solution)/shard_map/ppermute | solution.py:602
  968.5 27.7 %collective-permute-start.154 = (bf16[2112,128]{1,0:T(8,128)(2,1)S(1)}, bf16[2112,128]{1,0:T(8,128)(2,1)S(1)}, u32[]{:S(2)}, u32[]{:S(2)}) collective-permute-start(bf16[2112,128]{1,0:T(8,128)(2,1)S(1)} %pad_maximum_fusion.12), channel_id=1, source_target_pairs={{0,8},{4,12},{8,0},{12,4},{1,9},{5,13},{9,1},{13,5},{2,10},{6,14},... | collective-permute-start | bytes 1622024 | tf_op jit(solution)/shard_map/ppermute | solution.py:605
  (252 other events, 3058.1 us)

commit v2 on v1

v2 whole, which is shorter than its diff:
```python
import functools
import math

import jax
import jax.numpy as jnp
import numpy as np
from jax import lax
from jax.experimental import pallas as pl
from jax.experimental.pallas import tpu as pltpu
from jax.sharding import PartitionSpec as P

HEAD = 64
EPS = 1e-05
ROPE_BASE = 10000.0
BIG = 1e30
LOG2E = math.log2(math.e)
BF = jnp.bfloat16
F32 = jnp.float32
ALL = ("section", "dp", "tensor")
VMEM_LIMIT = 60 * 1024 * 1024
STEP = 256
CHUNK = 32
STRIP = 256

COL_OF_REL, ABS_OF_REL, OUT_OF_ABS, ABS_OF_OUT, CHIP_OF_RING, SIDE_OF_RING, REL_OF_DP, SECTION = 0, 8, 16, 24, 32, 40, 48, 56
PLACES = 64


def nn(a, b):
    return jnp.dot(a, b, preferred_element_type=F32)


def nt(a, b):
    return lax.dot_general(a, b, (((1,), (1,)), ((), ())), preferred_element_type=F32)


def tn(a, b):
    return lax.dot_general(a, b, (((0,), (0,)), ((), ())), preferred_element_type=F32)


def vmem_spec():
    return pl.BlockSpec(memory_space=pltpu.VMEM)


def any_spec():
    return pl.BlockSpec(memory_space=pl.ANY)


def smem_spec():
    return pl.BlockSpec(memory_space=pltpu.SMEM)


def sds(shape, dtype):
    return jax.ShapeDtypeStruct(shape, dtype)


def cost(micros):
    return pl.CostEstimate(flops=int(micros * 1.15e9), bytes_accessed=0, transcendentals=0)


def params(**more):
    return pltpu.CompilerParams(vmem_limit_bytes=VMEM_LIMIT, **more)


def call(kernel, deps, operands, *, in_specs, **rest):
    count, extra = len(operands), len(deps)

    def body(*refs):
        kernel(*refs[:count], *refs[count + extra :])

    return pl.pallas_call(body, in_specs=in_specs + [any_spec()] * extra, **rest)(*operands, *deps)


class Weights:
    def __init__(self, arrays, offset=0):
        self.arrays, self.offset = arrays, offset

    def copies(self, meta, refs, parts, sems, first):
        found = []
        for n, ref in enumerate(refs):
            for row, rows, target in parts:
                dst = target
                if len(refs) > 1:
                    width = ref.shape[1]
                    dst = target.at[:, pl.ds(pl.multiple_of(meta[COL_OF_REL + n] * width, width), width)]
                src = ref.at[pl.ds(self.offset + row, rows), :]
                found.append(pltpu.make_async_copy(src, dst, sems.at[first + len(found)]))
        return found


class Blocks:
    def __init__(self, arrays, places, by_section=()):
        self.arrays, self.places, self.by_section = arrays, places, by_section

    def copies(self, meta, refs, target, sems, first):
        found = []
        for i, (n, place) in enumerate(self.places):
            place = meta[SECTION] ^ place if i in self.by_section else place
            found.append(pltpu.make_async_copy(refs[n].at[place], target(i), sems.at[first + i]))
        return found


def unique(weights):
    operands, places = [], []
    for item in weights:
        mine = []
        for array in item.arrays:
            for n, other in enumerate(operands):
                if other is array:
                    mine.append(n)
                    break
            else:
                mine.append(len(operands))
                operands.append(array)
        places.append(mine)
    return operands, places


def start_all(copies):
    for copy in copies:
        copy.start()
    return copies


def wait_all(copies):
    for copy in copies:
        copy.wait()


def swap_halves(tile):
    lane = lax.broadcasted_iota(jnp.int32, tile.shape, 1)
    return jnp.where(lane % HEAD < HEAD // 2, pltpu.roll(tile, 128 - HEAD // 2, 1), pltpu.roll(tile, HEAD // 2, 1))


def column_of(part, pair, cols):
    side = cols // 2
    if side % 128:
        return part * cols + pair * 128
    per_side = side // 128
    return (pair // per_side * 3 + part) * side + pair % per_side * 128


def qkv_kernel(a_blocks, later, meta, *refs):
    blocks, held = len(a_blocks.places), len(a_blocks.arrays)
    a_refs = refs[:held]
    w_ref, cos_ref, sin_ref, extq_ref, extk_ref = refs[held : held + 5]
    rest = refs[held + 5 :]
    if later:
        first_ref, rest = rest[0], rest[1:]
    outs, (a_scr, w_scr, q_scr, k_scr, v_scr, cos_scr, sin_scr, extq_scr, extk_scr), rest = rest[:3], rest[3:12], rest[12:]
    if later:
        first_scr, rest = rest[0], rest[1:]
    sems, out_sems = rest
    length = a_scr.shape[1]
    cols = w_ref.shape[1] // 3
    loads = [
        pltpu.make_async_copy(w_ref, w_scr, sems.at[0]),
        pltpu.make_async_copy(cos_ref, cos_scr, sems.at[2]),
        pltpu.make_async_copy(sin_ref, sin_scr, sems.at[3]),
        pltpu.make_async_copy(extq_ref, extq_scr, sems.at[4]),
        pltpu.make_async_copy(extk_ref, extk_scr, sems.at[5]),
    ]
    if later:
        loads.append(pltpu.make_async_copy(first_ref, first_scr, sems.at[6]))
    more = a_blocks.copies(meta, a_refs, lambda i: a_scr.at[i], sems, 7)
    start_all(loads)
    start_all(more)
    lane = lax.broadcasted_iota(jnp.int32, (length, 128), 1)
    low = lane < HEAD
    ones_even = ((lane >= HEAD + 4) & (lane < HEAD + 7)).astype(F32)
    ones_odd = ((lane >= 4) & (lane < 7)).astype(F32)
    stores = []
    for i in range(blocks):
        start = pl.multiple_of(meta[ABS_OF_REL + i] * length, length)
        rows = pl.ds(start, length)
        if i == 0:
            wait_all(loads)
        more[i].wait()
        a = a_scr[i]
        cosine, sine = cos_scr[rows, :], sin_scr[rows, :]
        whole = nn(a, w_scr[...])
        for part, out in ((0, q_scr), (1, k_scr), (2, v_scr)):
            for pair in range(cols // 128):
                column = column_of(part, pair, cols)
                tile = whole[:, column : column + 128]
                if part < 2:
                    tile = tile * cosine + swap_halves(tile) * sine
                    ext = extq_scr if part == 0 else extk_scr
                    if part == 0:
                        tile = tile * (LOG2E * HEAD**-0.5)
                    even_ext = ext[rows, :128].astype(F32)
                    odd_ext = ext[rows, 128:].astype(F32)
                else:
                    if later:
                        first = jnp.where(
                            low,
                            first_scr[2 * pair, rows, :].astype(F32),
                            first_scr[2 * pair + 1, rows, :].astype(F32),
                        )
                        tile = 0.5 * tile + 0.5 * first
                    even_ext, odd_ext = ones_even, ones_odd
                out[i, 2 * pair] = jnp.where(low, tile, even_ext).astype(BF)
                out[i, 2 * pair + 1] = jnp.where(low, odd_ext, tile).astype(BF)
        for n, (scr, out) in enumerate(zip((q_scr, k_scr, v_scr), outs)):
            stores += start_all([pltpu.make_async_copy(scr.at[i], out.at[:, rows, :], out_sems.at[3 * i + n])])
    wait_all(stores)


def project(meta, a_blocks, w, tables, exts, first, deps):
    blocks, (_, length, width) = len(a_blocks.places), a_blocks.arrays[0].shape
    cols = w.shape[1] // 3
    heads = cols // HEAD
    seq = blocks * length
    out = sds((heads, seq, 128), BF)
    later = first is not None
    operands = [meta, *a_blocks.arrays, w, *tables, *exts] + ([first] if later else [])
    block = pltpu.VMEM((blocks, heads, length, 128), BF)
    return call(
        functools.partial(qkv_kernel, a_blocks, later),
        deps,
        operands,
        out_shape=(out, out, out),
        in_specs=[smem_spec()] + [any_spec()] * (len(operands) - 1),
        out_specs=(any_spec(),) * 3,
        scratch_shapes=[
            pltpu.VMEM((blocks, length, width), BF),
            pltpu.VMEM(w.shape, BF),
            block,
            block,
            block,
            pltpu.VMEM((seq, 128), F32),
            pltpu.VMEM((seq, 128), F32),
            pltpu.VMEM((seq, 256), BF),
            pltpu.VMEM((seq, 256), BF),
        ]
        + ([pltpu.VMEM(out.shape, BF)] if later else [])
        + [pltpu.SemaphoreType.DMA((blocks + 7,)), pltpu.SemaphoreType.DMA((3 * blocks,))],
        compiler_params=params(),
        cost_estimate=cost(10),
        name="project",
    )


def project_back_kernel(a_blocks, dp_blocks, meta, *refs):
    blocks, held = len(a_blocks.places), len(a_blocks.arrays)
    a_refs = refs[:held]
    dq_ref, dk_ref, dv_ref, w_ref, near_ref, far_ref, dw_ref = refs[held : held + 7]
    a_scr, d_scr, w_scr, da_scr, dw_scr, sems, out_sems = refs[held + 7 :]
    _, length, width = da_scr.shape
    cols = dq_ref.shape[1]
    loads = [pltpu.make_async_copy(w_ref, w_scr, sems.at[0])]
    for part, ref in enumerate((dq_ref, dk_ref, dv_ref)):
        for pair in range(cols // 128):
            target = d_scr.at[:, pl.ds(column_of(part, pair, cols), 128)]
            source = ref.at[:, pl.ds(pair * 128, 128)]
            loads.append(pltpu.make_async_copy(source, target, sems.at[len(loads)]))

    def place(i):
        start = pl.multiple_of(meta[ABS_OF_REL + i] * length, length)
        return a_scr.at[pl.ds(start, length)]

    more = a_blocks.copies(meta, a_refs, place, sems, len(loads))
    start_all(loads)
    start_all(more)
    wait_all(loads)
    order = list(range(1, blocks, 2)) + list(range(2, blocks, 2)) + [0]
    stores = []
    for i in order:
        start = pl.multiple_of(meta[ABS_OF_REL + i] * length, length)
        da_scr[i] = nt(d_scr[pl.ds(start, length), :], w_scr[...]).astype(BF)
        out = far_ref if i % 2 else near_ref
        stores += start_all([pltpu.make_async_copy(da_scr.at[i], out.at[i // 2], out_sems.at[i])])
    wait_all(more)
    size = width // dp_blocks
    for j in range(dp_blocks):
        dw_scr[meta[REL_OF_DP + j]] = tn(a_scr[:, j * size : (j + 1) * size], d_scr[...]).astype(BF)
    stores += start_all([pltpu.make_async_copy(dw_scr, dw_ref, out_sems.at[blocks])])
    wait_all(stores)


def project_back(meta, a_blocks, grads, w, dp_blocks, deps):
    blocks, (_, length, width) = len(a_blocks.places), a_blocks.arrays[0].shape
    cols = w.shape[1]
    seq = blocks * length
    half = sds((blocks // 2, length, width), BF)
    dw = (dp_blocks, width // dp_blocks, cols)
    return call(
        functools.partial(project_back_kernel, a_blocks, dp_blocks),
        deps,
        [meta, *a_blocks.arrays, *grads, w],
        out_shape=(half, half, sds(dw, BF)),
        in_specs=[smem_spec()] + [any_spec()] * (len(a_blocks.arrays) + 4),
        out_specs=(any_spec(),) * 3,
        scratch_shapes=[
            pltpu.VMEM((seq, width), BF),
            pltpu.VMEM((seq, cols), BF),
            pltpu.VMEM(w.shape, BF),
            pltpu.VMEM((blocks, length, width), BF),
            pltpu.VMEM(dw, BF),
            pltpu.SemaphoreType.DMA((blocks + 1 + cols // 128,)),
            pltpu.SemaphoreType.DMA((blocks + 1,)),
        ],
        compiler_params=params(),
        cost_estimate=cost(12),
        name="project_back",
    )


def three_parts(value):
    high = value.astype(BF).astype(F32)
    middle = (value - high).astype(BF).astype(F32)
    return high, middle, value - high - middle


def with_parts(base, value, odd):
    lane = lax.broadcasted_iota(jnp.int32, base.shape, 1)
    offset = 4 if odd else HEAD + 4
    high, middle, rest = three_parts(value)
    out = jnp.where(lane == offset, high, base)
    out = jnp.where(lane == offset + 1, middle, out)
    return jnp.where(lane == offset + 2, rest, out)


def attend_kernel(block, meta, q_ref, k_ref, v_ref, o_ref, ql_ref, vt_scr, tot_scr, top_scr, s_scr, p_scr):
    seq = q_ref.shape[1]
    length = o_ref.shape[1]
    key_row = lax.broadcasted_iota(jnp.int32, (STEP, block), 0)
    query_col = lax.broadcasted_iota(jnp.int32, (STEP, block), 1)
    for e in range(2):
        vt_scr[e] = v_ref[e].T

    def score(i, e):
        q = q_ref[e, i * block : (i + 1) * block, :]
        best = None
        for lo in range(0, (i + 1) * block, STEP):
            tile = nt(k_ref[e, lo : lo + STEP, :], q)
            if lo >= i * block:
                tile = jnp.where(key_row + (lo - i * block) <= query_col, tile, -BIG)
            s_scr[e, i % 2, lo : lo + STEP, :] = tile
            best = tile if best is None else jnp.maximum(best, tile)
        top_scr[e, :, i * block : (i + 1) * block] = best.max(axis=0, keepdims=True)

    def weigh(i, e):
        cols = slice(i * block, (i + 1) * block)
        top = top_scr[e, :, cols]
        for lo in range(0, (i + 1) * block, STEP):
            p_scr[e, lo : lo + STEP, :] = jnp.exp2(s_scr[e, i % 2, lo : lo + STEP, :] - top).astype(BF)
        tot_scr[e, :, cols] = nn(vt_scr[e, :, : (i + 1) * block], p_scr[e, : (i + 1) * block, :])

    count = seq // block
    for i in range(count + 1):
        for e in range(2):
            if i < count:
                score(i, e)
            if i > 0:
                weigh(i - 1, e)
    low = lax.broadcasted_iota(jnp.int32, (length, 128), 1) < HEAD
    lane = lax.broadcasted_iota(jnp.int32, (length, 128), 1)
    row = lax.broadcasted_iota(jnp.int32, (128, length), 0)
    for i in range(seq // length):
        rows = slice(i * length, (i + 1) * length)
        results = []
        for e in range(2):
            place = 4 if e else HEAD + 4
            total = tot_scr[e, :, rows]
            weight = total[place : place + 1, :]
            total = total * (1.0 / weight)
            for n, value in enumerate(three_parts(-(top_scr[e, :, rows] + jnp.log2(weight)))):
                total = jnp.where(row == place + n, value, total)
            turned = total.T
            results.append(turned)
            parts = (lane >= place) & (lane < place + 3)
            ql_ref[e, rows, :] = jnp.where(parts, turned, q_ref[e, rows, :].astype(F32)).astype(BF)
        o_ref[meta[OUT_OF_ABS + i]] = jnp.where(low, results[0], results[1]).astype(BF)


def attend(meta, q, k, v, blocks, deps):
    heads, seq, _ = q.shape
    pairs = heads // 2
    length = seq // blocks
    head_spec = pl.BlockSpec((2, seq, 128), lambda p: (p, 0, 0))
    return call(
        functools.partial(attend_kernel, min(256, length)),
        deps,
        [meta, q, k, v],
        grid=(pairs,),
        out_shape=(sds((blocks, length, pairs * 128), BF), sds(q.shape, BF)),
        in_specs=[smem_spec(), head_spec, head_spec, head_spec],
        out_specs=(pl.BlockSpec((blocks, length, 128), lambda p: (0, 0, p)), head_spec),
        scratch_shapes=[
            pltpu.VMEM((2, 128, seq), BF),
            pltpu.VMEM((2, 128, seq), F32),
            pltpu.VMEM((2, 1, seq), F32),
            pltpu.VMEM((2, 2, seq, min(256, length)), F32),
            pltpu.VMEM((2, seq, min(256, length)), BF),
        ],
        compiler_params=params(),
        cost_estimate=cost(14.5),
        name="attend",
    )


def attend_back_kernel(block, blocks, later, meta, q_ref, k_ref, v_ref, o_ref, *refs):
    do_refs = refs[:blocks]
    cos_ref, sin_ref = refs[blocks : blocks + 2]
    rest = refs[blocks + 2 :]
    if not later:
        first_ref, rest = rest[0], rest[1:]
    dq_ref, dk_ref, dv_ref = rest[:3]
    rest = rest[3:]
    if later:
        first_out, rest = rest[0], rest[1:]
    do_scr, dq_scr, dk_scr, dv_scr, kt_scr, p_scr, ds_scr = rest
    seq = q_ref.shape[1]
    length = o_ref.shape[1]
    lane = lax.broadcasted_iota(jnp.int32, (length, 128), 1)
    low = lane < HEAD
    for i in range(blocks):
        start = pl.multiple_of(meta[ABS_OF_OUT + i] * length, length)
        rows = pl.ds(start, length)
        do = do_refs[i][...].astype(F32)
        product = do * o_ref[i].astype(F32)
        for e in range(2):
            mine = low if e == 0 else jnp.logical_not(low)
            delta = jnp.sum(jnp.where(mine, product, 0.0), axis=1, keepdims=True)
            do_scr[e, rows, :] = with_parts(jnp.where(mine, do, 0.0), -delta, e == 1).astype(BF)
    key_row = lax.broadcasted_iota(jnp.int32, (STEP, block), 0)
    query_col = lax.broadcasted_iota(jnp.int32, (STEP, block), 1)
    for e in range(2):
        kt_scr[e] = k_ref[e].T
    count = seq // block

    def weigh(i, e):
        cols = slice(i * block, (i + 1) * block)
        q = q_ref[e, cols, :]
        do = do_scr[e, cols, :]
        for lo in range(0, (i + 1) * block, STEP):
            rows = slice(lo, lo + STEP)
            scores = nt(k_ref[e, rows, :], q)
            if lo >= i * block:
                scores = jnp.where(key_row + (lo - i * block) <= query_col, scores, -BIG)
            prob = jnp.exp2(scores)
            p_scr[e, rows, cols] = prob.astype(BF)
            ds_scr[e, rows, cols] = (prob * nt(v_ref[e, rows, :], do)).astype(BF)

    def query_grad(i, e):
        cols = slice(i * block, (i + 1) * block)
        dq_scr[e, :, cols] = nn(kt_scr[e, :, : (i + 1) * block], ds_scr[e, : (i + 1) * block, cols])

    def key_grads(i, e):
        rows, cols = slice(i * block, (i + 1) * block), slice(i * block, seq)
        dv_scr[e, rows, :] = nn(p_scr[e, rows, cols], do_scr[e, cols, :])
        dk_scr[e, rows, :] = nn(ds_scr[e, rows, cols], q_ref[e, cols, :])

    for i in range(count + 1):
        for e in range(2):
            if i < count:
                weigh(i, e)
            if i > 0:
                query_grad(i - 1, e)
    for i in range(count):
        for e in range(2):
            key_grads(i, e)
    for i in range(blocks):
        rows = slice(i * length, (i + 1) * length)
        cosine, sine = cos_ref[rows, :], sin_ref[rows, :]
        dq = jnp.where(low, dq_scr[0, :, rows].T, dq_scr[1, :, rows].T) * (HEAD**-0.5)
        dk = jnp.where(low, dk_scr[0, rows, :], dk_scr[1, rows, :]) * (1.0 / LOG2E)
        dv = jnp.where(low, dv_scr[0, rows, :], dv_scr[1, rows, :])
        dq_ref[rows, :] = (dq * cosine - swap_halves(dq) * sine).astype(BF)
        dk_ref[rows, :] = (dk * cosine - swap_halves(dk) * sine).astype(BF)
        if later:
            dv_ref[rows, :] = (0.5 * dv).astype(BF)
            first_out[rows, :] = 0.5 * dv
        else:
            dv_ref[rows, :] = (dv + first_ref[rows, :]).astype(BF)


def attend_back(meta, q, k, v, o, do_blocks, tables, first, deps):
    heads, seq, _ = q.shape
    pairs = heads // 2
    blocks, length, cols = o.shape
    later = first is None
    head_spec = pl.BlockSpec((2, seq, 128), lambda p: (p, 0, 0))
    col_spec = pl.BlockSpec((seq, 128), lambda p: (0, p))
    table_spec = pl.BlockSpec((seq, 128), lambda p: (0, 0))
    out = sds((seq, cols), BF)
    return call(
        functools.partial(attend_back_kernel, min(256, length), blocks, later),
        deps,
        [meta, q, k, v, o, *[do_blocks.arrays[n] for n, _ in do_blocks.places], *tables, *([] if later else [first])],
        grid=(pairs,),
        out_shape=(out, out, out) + ((sds((seq, cols), F32),) if later else ()),
        in_specs=[smem_spec(), head_spec, head_spec, head_spec]
        + [pl.BlockSpec((blocks, length, 128), lambda p: (0, 0, p))]
        + [pl.BlockSpec((None, length, 128), functools.partial(lambda n, p: (n, 0, p), n)) for _, n in do_blocks.places]
        + [table_spec] * 2
        + ([] if later else [col_spec]),
        out_specs=(col_spec,) * (4 if later else 3),
        scratch_shapes=[
            pltpu.VMEM((2, seq, 128), BF),
            pltpu.VMEM((2, 128, seq), F32),
            pltpu.VMEM((2, seq, 128), F32),
            pltpu.VMEM((2, seq, 128), F32),
            pltpu.VMEM((2, 128, seq), BF),
            pltpu.VMEM((2, seq, seq), BF),
            pltpu.VMEM((2, seq, seq), BF),
        ],
        compiler_params=params(),
        cost_estimate=cost(29.5),
        name="attend_back",
    )


def place_output(weights, places, meta, refs, target, sems, first):
    found = []
    rows = target.shape[1] // 2
    for k, item in enumerate(weights):
        side = pl.multiple_of(meta[SIDE_OF_RING + k] * rows, rows)
        part = (0, rows, target.at[meta[CHIP_OF_RING + k], pl.ds(side, rows)])
        found += item.copies(meta, [refs[n] for n in places[k]], [part], sems, first + 4 * k)
    return found


def output_kernel(o_blocks, weights, places, meta, *refs):
    o_refs, refs = refs[: len(o_blocks.arrays)], refs[len(o_blocks.arrays) :]
    number = len({n for place in places for n in place})
    w_refs, (p_ref, o_scr, w_scr, sems) = refs[:number], refs[number:]
    count = len(o_blocks.places)
    length = o_scr.shape[1] // 2
    loads = o_blocks.copies(meta, o_refs, lambda i: o_scr.at[i // 2, pl.ds(i % 2 * length, length)], sems, 0)
    loads += place_output(weights, places, meta, w_refs, w_scr, sems, count)
    wait_all(start_all(loads))
    for f in range(2):
        rows = slice(f * length, (f + 1) * length)
        total = nn(o_scr[0, rows, :], w_scr[0])
        for n in range(1, count // 2):
            total += nn(o_scr[n, rows, :], w_scr[n])
        p_ref[rows, :] = total.astype(BF)


def output_forward(meta, o_blocks, weights, width, deps):
    count = len(o_blocks.places)
    _, length, cols = o_blocks.arrays[0].shape
    operands, places = unique(weights)
    return call(
        functools.partial(output_kernel, o_blocks, weights, places),
        deps,
        [meta, *o_blocks.arrays, *operands],
        out_shape=sds((2 * length, width), BF),
        in_specs=[smem_spec()] + [any_spec()] * (len(o_blocks.arrays) + len(operands)),
        out_specs=vmem_spec(),
        scratch_shapes=[
            pltpu.VMEM((count // 2, 2 * length, cols), BF),
            pltpu.VMEM((count // 2, cols, width), BF),
            pltpu.SemaphoreType.DMA((5 * count,)),
        ],
        compiler_params=params(),
        cost_estimate=cost(5),
        name="output",
    )


def place_hidden(batch, weights, places, meta, refs, target, sems, first, row):
    hidden = target.shape[1] // len(batch)
    found = []
    for n, k in enumerate(batch):
        parts = [(row + m * hidden, hidden, target.at[m, pl.ds(n * hidden, hidden)]) for m in range(3)]
        found += weights[k].copies(meta, [refs[i] for i in places[k]], parts, sems, first + 12 * n)
    return found


def mlp_kernel(batches, weights, places, row, meta, x_ref, p_ref, other_ref, gain_ref, *refs):
    number = len({n for place in places for n in place})
    w_refs, refs = refs[:number], refs[number:]
    count = len(batches)
    y_ref, h_ref, b_ref = refs[:3]
    g_refs, u_refs, refs = refs[3 : 3 + count], refs[3 + count : 3 + 2 * count], refs[3 + 2 * count :]
    w_scr, sems = refs
    first = [12 * sum(len(other) for other in batches[:n]) for n in range(count)]

    def loads(n):
        return place_hidden(batches[n], weights, places, meta, w_refs, w_scr.at[n], sems, first[n], row)

    @pl.when(pl.program_id(0) == 0)
    def _():
        for n in range(count):
            start_all(loads(n))

    gain = gain_ref[...]
    for start in range(0, x_ref.shape[0], CHUNK):
        rows = slice(start, start + CHUNK)
        h = x_ref[rows, :].astype(F32) + (p_ref[rows, :].astype(F32) + other_ref[rows, :].astype(F32))
        h_ref[rows, :] = h
        inverse = lax.rsqrt(jnp.mean(h * h, axis=1, keepdims=True) + EPS)
        b_ref[rows, :] = (h * inverse * gain).astype(BF)

    @pl.when(pl.program_id(0) == 0)
    def _():
        for n in range(count):
            wait_all(loads(n))

    for start in range(0, x_ref.shape[0], STRIP):
        rows = slice(start, start + STRIP)
        b = b_ref[rows, :]
        total = None
        for n in range(count):
            g = nt(b, w_scr[n, 0])
            u = nt(b, w_scr[n, 1])
            g_refs[n][rows, :] = g.astype(BF)
            u_refs[n][rows, :] = u.astype(BF)
            m = (g * jax.nn.sigmoid(g) * u).astype(BF)
            term = nn(m, w_scr[n, 2])
            total = term if total is None else total + term
        y_ref[rows, :] = total.astype(BF)


def mlp_forward(meta, x, p, other, gain, weights, batches, hidden, row, deps):
    rows, width = x.shape
    operands, places = unique(weights)
    size = [len(batch) * hidden for batch in batches]
    quarters = sum(len(batch) for batch in batches)
    low = sds((rows, width), BF)
    saved = tuple(sds((rows, n), BF) for n in size)
    block = min(256, rows)

    def by_rows(n):
        return pl.BlockSpec((block, n), lambda i: (i, 0))

    return call(
        functools.partial(mlp_kernel, batches, weights, places, row),
        deps,
        [meta, x, p, other, gain, *operands],
        grid=(rows // block,),
        out_shape=(low, sds((rows, width), F32), low) + saved + saved,
        in_specs=[smem_spec()]
        + [by_rows(width)] * 3
        + [pl.BlockSpec((1, width), lambda i: (0, 0))]
        + [any_spec()] * len(operands),
        out_specs=(by_rows(width),) * 3 + tuple(by_rows(n) for n in size) * 2,
        scratch_shapes=[
            pltpu.VMEM((len(batches), 3, size[0], width), BF),
            pltpu.SemaphoreType.DMA((12 * quarters,)),
        ],
        compiler_params=params(),
        cost_estimate=cost(19),
        name="mlp",
    )


def mlp_back_kernel(batches, weights, places, row, meta, dy_ref, b_ref, *refs):
    count = len(batches)
    g_refs, u_refs, refs = refs[:count], refs[count : 2 * count], refs[2 * count :]
    number = len({n for place in places for n in place})
    w_refs, refs = refs[:number], refs[number:]
    out_refs, refs = refs[:count], refs[count:]
    db_ref, dy_scr, b_scr, g_scr, u_scr, w_scr, low_scr, grad_scr, sems, out_sems = refs
    dy_load = pltpu.make_async_copy(dy_ref, dy_scr, sems.at[0])
    b_load = pltpu.make_async_copy(b_ref, b_scr, sems.at[1])
    dy_load.start()
    loads, used = [], 2
    for n, batch in enumerate(batches):
        group = place_hidden(batch, weights, places, meta, w_refs, w_scr.at[n], sems, used, row)
        used += 12 * len(batch)
        for source, target in ((g_refs[n], g_scr.at[n]), (u_refs[n], u_scr.at[n])):
            group.append(pltpu.make_async_copy(source, target, sems.at[used]))
            used += 1
        loads.append(start_all(group))
    b_load.start()
    total_rows, width = dy_scr.shape
    hidden = w_scr.shape[2] // len(batches[0])
    columns, _, size = out_refs[0].shape
    stores = []
    dy_load.wait()
    for n, batch in enumerate(batches):
        wait_all(loads[n])
        for start in range(0, total_rows, STRIP):
            rows = slice(start, start + STRIP)
            dm = nt(dy_scr[rows, :], w_scr[n, 2])
            g = g_scr[n, rows, :].astype(F32)
            u = u_scr[n, rows, :].astype(F32)
            gate = jax.nn.sigmoid(g)
            active = g * gate
            low_scr[n, 0, rows, :] = (dm * u * (gate + active * (1.0 - gate))).astype(BF)
            low_scr[n, 1, rows, :] = (dm * active).astype(BF)
            low_scr[n, 2, rows, :] = (active * u).astype(BF)
    b_load.wait()
    for n, batch in enumerate(batches):
        for m in range(3):
            grad_scr[n, m] = tn(low_scr[n, m], dy_scr[...] if m == 2 else b_scr[...]).astype(BF)
            for q in range(len(batch)):
                for j in range(columns):
                    copy = pltpu.make_async_copy(
                        grad_scr.at[n, m, pl.ds(q * hidden, hidden), pl.ds(j * size, size)],
                        out_refs[n].at[meta[REL_OF_DP + j], pl.ds((q * 3 + m) * hidden, hidden), :],
                        out_sems.at[((n * 3 + m) * len(batch) + q) * columns + j],
                    )
                    copy.start()
                    stores.append(copy)
    for start in range(0, total_rows, 256):
        rows = slice(start, start + 256)
        db = None
        for n in range(count):
            term = nn(low_scr[n, 0, rows, :], w_scr[n, 0]) + nn(low_scr[n, 1, rows, :], w_scr[n, 1])
            db = term if db is None else db + term
        db_ref[rows, :] = db.astype(BF)
    wait_all(stores)


def mlp_backward(meta, dy, b, saved, weights, batches, row, dp_blocks, deps):
    rows, width = b.shape
    count = len(batches)
    size = saved[0].shape[1]
    operands, places = unique(weights)
    copies = sum(12 * len(batch) + 2 for batch in batches)
    return call(
        functools.partial(mlp_back_kernel, batches, weights, places, row),
        deps,
        [meta, dy, b, *saved, *operands],
        out_shape=(sds((dp_blocks, 3 * size, width // dp_blocks), BF),) * count + (sds((rows, width), BF),),
        in_specs=[smem_spec()] + [any_spec()] * (2 + 2 * count + len(operands)),
        out_specs=(any_spec(),) * count + (vmem_spec(),),
        scratch_shapes=[
            pltpu.VMEM((rows, width), BF),
            pltpu.VMEM((rows, width), BF),
            pltpu.VMEM((count, rows, size), BF),
            pltpu.VMEM((count, rows, size), BF),
            pltpu.VMEM((count, 3, size, width), BF),
            pltpu.VMEM((count, 3, rows, size), BF),
            pltpu.VMEM((count, 3, size, width), BF),
            pltpu.SemaphoreType.DMA((2 + copies,)),
            pltpu.SemaphoreType.DMA((3 * dp_blocks * sum(len(batch) for batch in batches),)),
        ],
        compiler_params=params(),
        cost_estimate=cost(28),
        name="mlp_back",
    )


def norm_back(values, gain, grads):
    inverse = lax.rsqrt(jnp.mean(values * values, axis=1, keepdims=True) + EPS)
    normed = values * inverse
    scaled = grads * gain
    gain_grad = jnp.sum(grads * normed, axis=0, keepdims=True)
    return inverse * (scaled - normed * jnp.mean(scaled * normed, axis=1, keepdims=True)), gain_grad


def middle_kernel(o_blocks, weights, places, meta, dy_ref, db_ref, other_ref, h_ref, gain_ref, *refs):
    o_refs, refs = refs[: len(o_blocks.arrays)], refs[len(o_blocks.arrays) :]
    number = len({n for place in places for n in place})
    w_refs, refs = refs[:number], refs[number:]
    dh_ref, gain_out, do_ref, grad_ref, w_scr, o_scr, low_scr, grad_scr, sems, out_sems = refs
    count = len(o_blocks.places)
    length = o_scr.shape[1] // 2
    step, steps = pl.program_id(0), pl.num_programs(0)

    def loads():
        found = o_blocks.copies(meta, o_refs, lambda i: o_scr.at[i // 2, pl.ds(i % 2 * length, length)], sems, 0)
        return found + place_output(weights, places, meta, w_refs, w_scr, sems, count)

    @pl.when(step == 0)
    def _():
        start_all(loads())
        gain_out[...] = jnp.zeros_like(gain_out)

    gain = gain_ref[...]
    block = dy_ref.shape[0]
    first = pl.multiple_of(step * block, block)
    total = None
    for start in range(0, block, CHUNK):
        rows = slice(start, start + CHUNK)
        db = db_ref[rows, :].astype(F32) + other_ref[rows, :].astype(F32)
        part, gain_grad = norm_back(h_ref[rows, :], gain, db)
        dh = dy_ref[rows, :].astype(F32) + part
        dh_ref[rows, :] = dh
        low_scr[pl.ds(first + start, CHUNK), :] = dh.astype(BF)
        total = gain_grad if total is None else total + gain_grad
    gain_out[...] += total

    @pl.when(step == 0)
    def _():
        wait_all(loads())

    low = low_scr[pl.ds(first, block), :]
    for n in range(count // 2):
        do_ref[n] = nt(low, w_scr[n]).astype(BF)

    @pl.when(step == steps - 1)
    def _():
        for n in range(count // 2):
            grad_scr[n] = tn(o_scr[n], low_scr[...]).astype(BF)
        stores = []
        columns = grad_ref.shape[0]
        size = grad_ref.shape[2]
        rows = o_scr.shape[2] // 2
        for k in range(count):
            side = pl.multiple_of(meta[SIDE_OF_RING + k] * rows, rows)
            for j in range(columns):
                stores.append(
                    pltpu.make_async_copy(
                        grad_scr.at[meta[CHIP_OF_RING + k], pl.ds(side, rows), pl.ds(j * size, size)],
                        grad_ref.at[meta[REL_OF_DP + j], pl.ds(k * rows, rows), :],
                        out_sems.at[k * columns + j],
                    )
                )
        wait_all(start_all(stores))


def middle(meta, dy, db, other, h, gain, o_blocks, weights, dp_blocks, deps):
    count = len(o_blocks.places)
    _, length, cols = o_blocks.arrays[0].shape
    width = h.shape[1]
    operands, places = unique(weights)
    block = 256
    by_rows = pl.BlockSpec((block, width), lambda i: (i, 0))
    fixed = pl.BlockSpec((1, width), lambda i: (0, 0))
    return call(
        functools.partial(middle_kernel, o_blocks, weights, places),
        deps,
        [meta, dy, db, other, h, gain, *o_blocks.arrays, *operands],
        grid=(2 * length // block,),
        out_shape=(
            sds((2 * length, width), F32),
            sds((1, width), F32),
            sds((count // 2, 2 * length, cols), BF),
            sds((dp_blocks, count * cols // 2, width // dp_blocks), BF),
        ),
        in_specs=[smem_spec()]
        + [by_rows] * 4
        + [fixed]
        + [any_spec()] * (len(o_blocks.arrays) + len(operands)),
        out_specs=(by_rows, fixed, pl.BlockSpec((count // 2, block, cols), lambda i: (0, i, 0)), any_spec()),
        scratch_shapes=[
            pltpu.VMEM((count // 2, cols, width), BF),
            pltpu.VMEM((count // 2, 2 * length, cols), BF),
            pltpu.VMEM((2 * length, width), BF),
            pltpu.VMEM((count // 2, cols, width), BF),
            pltpu.SemaphoreType.DMA((5 * count,)),
            pltpu.SemaphoreType.DMA((count * dp_blocks,)),
        ],
        compiler_params=params(),
        cost_estimate=cost(13),
        name="middle",
    )


def add_low(*terms):
    total = terms[0].astype(F32)
    for term in terms[1:]:
        total = total + term.astype(F32)
    return total.astype(BF)


def hold(x, *after):
    return lax.optimization_barrier((x, *after))[0] if after else x


class Links:
    def __init__(self):
        self.T = lax.axis_size("tensor")
        self.DP = lax.axis_size("dp")
        self.G = self.T // 2
        self.s = lax.axis_index("section")
        self.d = lax.axis_index("dp")
        self.z = lax.axis_index("tensor")
        self.r = self.z // self.G
        self.home = self.s == self.r
        self.planar = self.DP == 4 and self.T == 4
        self.order = [0] + list(range(1, self.T, 2)) + list(range(self.T - 2, 0, -2))

    def sibling(self, x):
        return lax.ppermute(x, "section", [(0, 1), (1, 0)])

    def ring(self, x):
        order = self.order
        return lax.ppermute(x, "tensor", [(order[i], order[(i + 1) % self.T]) for i in range(self.T)])

    def along(self, x, bit):
        return lax.ppermute(x, "dp", [(i, i ^ bit) for i in range(self.DP)])

    def across(self, x):
        return lax.ppermute(x, "tensor", [(z, (z + self.G) % self.T) for z in range(self.T)])

    def shift(self, x, k):
        pairs = [(z, z // self.G * self.G + (z + k) % self.G) for z in range(self.T)]
        return lax.ppermute(x, "tensor", pairs)

    def swap_blocks(self, x):
        pairs = []
        for s in range(2):
            z0 = s * self.G
            for z in range(z0, z0 + self.G):
                pairs.append((s * self.T + z, s * self.T + (z + self.G) % self.T))
        give = lax.dynamic_index_in_dim(x, 1 - self.r, 0, keepdims=False)
        got = lax.ppermute(give, ("section", "tensor"), pairs)
        got = jnp.where(self.home, self.sibling(got), got)
        mine = (jnp.arange(2) == self.r)[:, None, None]
        return jnp.where(mine, x, got[None])

    def spread(self, x):
        give = lax.dynamic_index_in_dim(x, self.s, 0)
        arrays, places = [x], [(0, 0), (0, 1)]
        for k in range(1, self.G):
            got = self.shift(give, -k)
            arrays += [got, self.sibling(got)]
            places += [(len(arrays) - 2, 0), (len(arrays) - 1, 0)]
        return Blocks(arrays, places, (0, 1))

    def exchange(self, x, length):
        cols = x.shape[-1]
        arrays, places = [x.reshape(self.T, length, cols)], [(0, 0), (0, 1)] + [None] * (self.T - 2)
        for k in range(1, self.G):
            got = self.shift(x.reshape(self.G, 2 * length, cols)[k], k)
            chip = -k % self.G
            places[2 * chip], places[2 * chip + 1] = (len(arrays), 0), (len(arrays), 1)
            arrays.append(got.reshape(2, length, cols))
        return Blocks(arrays, places)

    def combine(self, near, far):
        got = self.sibling(far)
        terms = [near[0], got[0]]
        for k in range(1, self.G):
            terms.append(self.shift(add_low(near[k], got[k]), k))
        mine = add_low(*terms)
        both = (jnp.arange(2) == self.s)[:, None, None]
        return jnp.where(both, mine[None], self.sibling(mine)[None])

    def table(self):
        T, G, DP, order = self.T, self.G, self.DP, self.order
        table = np.zeros((2, DP, T, PLACES), np.int32)
        for s in range(2):
            for d in range(DP):
                for z in range(T):
                    out, c, r, position = table[s, d, z], z % G, z // G, order.index(z)
                    for rel in range(4):
                        out[COL_OF_REL + rel] = d ^ rel if self.planar else rel
                    for i in range(T):
                        quarter = order[(position - i) % T]
                        out[ABS_OF_REL + i] = (c + i // 2) % G + G * (s ^ (i % 2))
                        out[OUT_OF_ABS + i] = 2 * ((i % G - c) % G) + i // G
                        out[ABS_OF_OUT + i] = (c + i // 2) % G + G * (i % 2)
                        out[CHIP_OF_RING + i] = (quarter % G - c) % G
                        out[SIDE_OF_RING + i] = (quarter // G) ^ r
                    for i in range(DP):
                        out[REL_OF_DP + i] = (d ^ i) if self.planar else i
                    out[SECTION] = s
        index = (self.s * DP + self.d) * T + self.z
        return lax.dynamic_index_in_dim(jnp.asarray(table.reshape(-1, PLACES)), index, 0, keepdims=False)


def gather_weights(links, output_weight, gate_weight, up_weight, down_weight, after):
    s, d = links.s, links.d
    width = output_weight.shape[1]

    def half(which):
        def cut(x, dim):
            size = x.shape[dim] // 2
            return lax.dynamic_slice_in_dim(x, which * size, size, dim)

        return jnp.concatenate(
            [cut(output_weight, 0), cut(gate_weight, 1).T, cut(up_weight, 1).T, cut(down_weight, 0)]
        )

    mine = half(s)
    got = links.sibling(half(1 - s))
    weights, rings = [[], []], [[], []]
    for layer in range(2):
        own = jnp.where(s == layer, mine, got)
        weights[layer].append(Weights([own]))
        if not links.planar:
            for _ in range(1, links.T):
                own = links.ring(own)
                weights[layer].append(Weights([own]))
            continue
        size = width // 4
        current = lax.dynamic_slice_in_dim(own, d * size, size, 1)
        current = hold(current, *after)
        steps = []
        for _ in range(1, links.T):
            current = links.ring(current)
            steps.append(current)
        rings[layer] = steps
        rows = current.shape[0]
        for batch in ([0], [1], [2]) if layer == 0 else ([0], [1, 2]):
            part = steps[batch[0]] if len(batch) == 1 else jnp.concatenate([steps[n] for n in batch])
            pieces = [part] + [links.along(part, bit) for bit in (1, 2, 3)]
            for n in range(len(batch)):
                weights[layer].append(Weights(pieces, n * rows))
    return weights, rings


def gather_projection(links, query_weight, key_weight, value_weight):
    s, d = links.s, links.d
    depth, cols = query_weight.shape

    def half(which):
        return jnp.concatenate(
            [lax.dynamic_slice_in_dim(w, which * (cols // 2), cols // 2, 1) for w in (query_weight, key_weight, value_weight)],
            axis=1,
        )

    mine = half(s)
    got = links.sibling(half(1 - s))
    result, early = [], []
    for layer in range(2):
        own = jnp.where(s == layer, mine, got)
        if links.planar:
            other = links.across(lax.dynamic_slice_in_dim(own, d * (depth // 4), depth // 4, 0))
            early.append(other)
            for bit in (1, 2):
                far = links.along(other, bit)
                other = jnp.where(
                    d & bit == 0, jnp.concatenate([other, far]), jnp.concatenate([far, other])
                )
        else:
            other = links.across(own)
        if cols // 2 % 128:
            both = jnp.stack([own.reshape(depth, 3, cols // 2), other.reshape(depth, 3, cols // 2)], axis=2)
            result.append(both.reshape(depth, 3 * cols))
        else:
            result.append(jnp.concatenate([own, other], axis=1))
    return result, early


class PlaneSum:
    def __init__(self, links, part):
        self.links, self.part, self.half = links, part, part.shape[1] // 2

    def begin(self, *after):
        part = hold(self.part, *after)
        self.x = self.links.along(part[1::2, : self.half], 1)
        self.y = self.links.along(part[2:4, self.half :], 2)
        return [self.x, self.y]

    def finish(self, *after):
        part = hold(self.part, *after)
        self.x_end = self.links.along(add_low(part[1, self.half :], self.y[1]), 1)
        self.y_end = self.links.along(add_low(part[2, : self.half], self.x[1]), 2)
        return [self.x_end, self.y_end]

    def total(self, first, rows, more, after):
        part = hold(self.part, *after)
        here = slice(first, first + rows)
        if first + rows <= self.half:
            terms = [part[0, here], self.x[0, here], self.y_end[here]]
        else:
            there = slice(first - self.half, first - self.half + rows)
            terms = [part[0, here], self.y[0, there], self.x_end[there]]
        return add_low(*terms, *more)


class RingSum:
    def __init__(self, links, part_of):
        self.links, self.part_of, self.count, self.passed = links, part_of, 0, []

    def step(self, *after):
        self.total = self.part_of(self.count, self.passed, after)
        self.count += 1
        if self.count < self.links.T:
            self.passed = [self.links.ring(self.total)]
        return [self.passed[0] if self.count < self.links.T else self.total]


class LayerSums:
    def __init__(self, links, parts, out_part, rows, out_rows, order):
        first, second = PlaneSum(links, parts[0]), PlaneSum(links, parts[1])
        out = PlaneSum(links, out_part)
        self.links, self.first, self.second, self.out = links, first, second, out
        self.mlp_ring = RingSum(
            links, lambda n, more, after: (first, second)[n // 2].total(n % 2 * rows, rows, more, after)
        )
        self.out_ring = RingSum(
            links, lambda n, more, after: out.total(order[n] * out_rows, out_rows, more, after)
        )

    def stage(self, number, *after):
        if number == 0:
            return self.second.finish(*after) + self.out.begin(*after) + self.mlp_ring.step(*after)
        if number == 1:
            return self.out.finish(*after) + self.proj.begin(*after) + self.mlp_ring.step(*after)
        if number == 2:
            return self.mlp_ring.step(*after) + self.proj.finish(*after) + self.out_ring.step(*after)
        if number == 3:
            size = self.proj.part.shape[1] // 2
            self.proj_total = jnp.concatenate([self.proj.total(n * size, size, [], after) for n in range(2)])
            return self.mlp_ring.step(*after) + self.out_ring.step(*after) + [self.proj_total]
        return self.out_ring.step(*after)


def both_halves(links, per_layer):
    mine = jnp.where(links.s == 0, per_layer[0], per_layer[1])
    got = links.sibling(jnp.where(links.s == 0, per_layer[1], per_layer[0]))
    return jnp.where(links.s == 0, mine, got), jnp.where(links.s == 0, got, mine)


def sum_everywhere(links, x):
    if links.planar:
        x = x + links.along(x, 1)
        x = x + links.along(x, 2)
    else:
        x = lax.psum(x, "dp")
    step = 1
    while step < links.T:
        x = x + lax.ppermute(x, "tensor", [(z, z ^ step) for z in range(links.T)])
        step *= 2
    return x


def norm_low(x, gain):
    inverse = lax.rsqrt(jnp.mean(x * x, axis=-1, keepdims=True) + EPS)
    return (x * inverse * gain).astype(BF)


def per_device(
    tokens,
    segment_ids,
    cotangent,
    query_weight,
    key_weight,
    value_weight,
    output_weight,
    gate_weight,
    up_weight,
    down_weight,
    attn_gain,
    mlp_gain,
):
    links = Links()
    T, DP, s = links.T, links.DP, links.s
    seq = segment_ids.shape[1]
    length, width = tokens.shape[1:]
    cols = query_weight.shape[2]
    hidden = gate_weight.shape[2] // 2
    meta = links.table()

    half = HEAD // 2
    frequency = np.float32(ROPE_BASE) ** (-np.arange(half, dtype=np.float32) / np.float32(half))
    angles = np.arange(seq, dtype=np.float32)[:, None] * frequency[None, :].astype(np.float32)
    cosine, sine = np.cos(angles), np.sin(angles)
    tables = (
        jnp.asarray(np.concatenate([cosine] * 4, axis=1), F32),
        jnp.asarray(np.concatenate([-sine, sine, -sine, sine], axis=1), F32),
    )
    segments = lax.dynamic_index_in_dim(segment_ids, links.r, 0, keepdims=False)
    lane = jnp.arange(256, dtype=jnp.int32)[None, :]
    place = jnp.where(lane < 128, lane - HEAD, lane - 128)
    same = segments[:, None] == place
    in_seg = (place >= 0) & (place < 4)
    ext_q = jnp.where(in_seg & ~same, -BIG, 0.0).astype(BF)
    ext_k = jnp.where((in_seg & same) | ((place >= 4) & (place < 7)), 1.0, 0.0).astype(BF)

    own_gains = jnp.concatenate([attn_gain, mlp_gain])
    other_gains = links.sibling(own_gains)
    gains = [
        jnp.where(s == layer, own_gains, other_gains) for layer in range(2)
    ]
    w_proj, early = gather_projection(links, query_weight[0], key_weight[0], value_weight[0])
    def flat(item):
        return item.reshape(2 * length, width)

    def blocked(item):
        return item.reshape(2, length, width)

    x = flat(links.swap_blocks(tokens))
    weights, rings = gather_weights(links, output_weight[0], gate_weight[0], up_weight[0], down_weight[0], [x] + early[:1])
    planar = links.planar
    order = list(range(1, T)) + [0]
    batches = [order[: T // 2], order[T // 2 :]]
    out_rows = cols // 2
    rows = 3 * hidden

    a = norm_low(x.astype(F32), gains[0][0:1])
    kept = []
    first_values = None
    for layer in range(2):
        gain_mlp = gains[layer][1:2]
        a_blocks = links.spread(blocked(a))
        deps = [[], [], [], []]
        if planar and layer == 0:
            deps = [[], rings[0][:2] + w_proj[1:], rings[0][2:] + weights[0][1].arrays[1:], rings[1][:1]]
        elif planar:
            deps = [rings[1][1:] + weights[1][1].arrays[1:], [], [], []]
        q, k, v = project(meta, a_blocks, w_proj[layer], tables, (ext_q, ext_k), first_values, deps[0])
        o_rel, q = attend(meta, q, k, v, T, deps[1])
        o_blocks = links.exchange(o_rel, length)
        p = output_forward(meta, o_blocks, weights[layer], width, deps[2])
        if layer:
            dy = flat(links.swap_blocks(cotangent))
            deps[3] = [dy]
        y, h, b, *saved = mlp_forward(
            meta, x, p, links.sibling(p), gain_mlp, weights[layer], batches, hidden, out_rows, deps[3]
        )
        kept.append((x, a_blocks, q, k, v, o_rel, o_blocks, h, b, saved))
        x = (h + (y.astype(F32) + links.sibling(y).astype(F32))).astype(BF)
        if layer == 0:
            a, first_values = norm_low(x.astype(F32), gains[1][0:1]), v
    activations = links.swap_blocks(blocked(x))

    first_grad = None
    mlp_sums, out_sums, proj_sums, gain_sums, sums = [None] * 2, [None] * 2, [None] * 2, [None] * 2, [None] * 2
    for layer in (1, 0):
        gain_attn, gain_mlp = gains[layer][0:1], gains[layer][1:2]
        x, a_blocks, q, k, v, o_rel, o_blocks, h, b, saved = kept[layer]
        dy_low = dy.astype(BF)
        due = {name: [] for name in ("middle", "attend", "project")}
        before = sums[1] if planar and layer == 0 else None
        *parts, db = mlp_backward(meta, dy_low, b, saved, weights[layer], batches, out_rows, DP, [])
        if before:
            due["middle"] = passing
            due["attend"] = before.stage(2, parts[0])
        dh, mlp_gain_grad, do_rel, out_part = middle(
            meta, dy, db, links.sibling(db), h, gain_mlp, o_blocks, weights[layer], DP, due["middle"]
        )
        do_blocks = links.exchange(do_rel, length)
        if planar:
            mine = sums[layer] = LayerSums(links, parts, out_part, rows, out_rows, order)
            begun = mine.first.begin() + mine.second.begin()
            due["attend"] = due["attend"] + begun[:2]
            due["project"] = mine.first.finish(do_rel)
            if before:
                due["project"] = due["project"] + before.stage(3, do_rel)
            else:
                due["attend"] = due["attend"] + [activations]
        back = attend_back(meta, q, k, v, o_rel, do_blocks, tables, first_grad, due["attend"])
        if planar:
            passing = mine.stage(0, back[0])
            if before:
                before.stage(4, back[0])
        if layer == 1:
            first_grad = back[3]
        near, far, dw = project_back(meta, a_blocks, back[:3], w_proj[layer], DP, due["project"])
        if planar:
            mine.proj = PlaneSum(links, dw)
            passing = passing + mine.stage(1, near)
            if before:
                before.stage(4)
                for number in (2, 3, 4, 4):
                    mine.stage(number)
        else:
            running = None
            for part in parts:
                for n in range(T // 2):
                    term = part[:, n * rows : (n + 1) * rows]
                    running = term if running is None else add_low(term, links.ring(running))
            mlp_sums[layer] = lax.psum_scatter(running, "dp", scatter_dimension=0, tiled=True)[0]
            running = None
            for n in order:
                term = out_part[:, n * out_rows : (n + 1) * out_rows]
                running = term if running is None else add_low(term, links.ring(running))
            out_sums[layer] = lax.psum_scatter(running, "dp", scatter_dimension=0, tiled=True)[0]
            proj_sums[layer] = lax.psum_scatter(dw, "dp", scatter_dimension=0, tiled=True)[0]
        da = flat(links.combine(near, far)).astype(F32)
        part, attn_gain_grad = norm_back(x.astype(F32), gain_attn, da)
        gain_sums[layer] = jnp.concatenate([attn_gain_grad, mlp_gain_grad])
        dy = dh + part
    if planar:
        mlp_sums = [item.mlp_ring.total for item in sums]
        out_sums = [item.out_ring.total for item in sums]
        proj_sums = [item.proj_total for item in sums]
    half_width = width // 2
    mine = blocked(dy)
    mine = lax.dynamic_slice_in_dim(mine, s * half_width, half_width, 2)
    give = lax.dynamic_index_in_dim(mine, 1 - links.r, 0, keepdims=False).astype(BF)
    input_grad = jnp.where((jnp.arange(2) == links.r)[:, None, None], mine, links.across(give).astype(F32)[None])

    halves = both_halves(links, [jnp.concatenate([mlp_sums[n], out_sums[n]]) for n in range(2)])
    joined = []
    for item in proj_sums:
        if out_rows % 128:
            item = item.reshape(-1, 3, 2, out_rows)
            sides = [item[:, :, e].reshape(-1, 3 * out_rows) for e in range(2)]
        else:
            sides = [item[:, : 3 * out_rows], item[:, 3 * out_rows :]]
        joined.append(add_low(sides[0], links.across(sides[1])))
    proj = [item.astype(F32) for item in both_halves(links, joined)]
    halves = [item.astype(F32) for item in halves]
    squares = sum(jnp.sum(item * item) for item in halves + proj)
    gain_mine = jnp.where(s == 0, gain_sums[0], gain_sums[1])
    line = jnp.where(jnp.arange(width)[None, :] == 0, squares, 0.0)
    summed = sum_everywhere(links, jnp.concatenate([gain_mine, line]))
    gain_total = summed[0:2]
    grad_norm = jnp.sqrt(summed[2, 0] + jnp.sum(gain_total * gain_total)).reshape(1)
    shard = width // (DP * T)
    gain_out = lax.dynamic_slice_in_dim(gain_total, (links.d * T + links.z) * shard, shard, 1)
    grads = [
        jnp.concatenate([item[m * hidden : (m + 1) * hidden] for item in halves]) for m in range(3)
    ]
    own_out = jnp.concatenate([item[rows:] for item in halves])
    own_proj = [
        jnp.concatenate([item[:, m * out_rows : (m + 1) * out_rows] for item in proj], axis=1) for m in range(3)
    ]
    return (
        activations,
        input_grad,
        own_proj[0][None],
        own_proj[1][None],
        own_proj[2][None],
        own_out[None],
        grads[0].T[None],
        grads[1].T[None],
        grads[2][None],
        gain_out[0:1],
        gain_out[1:2],
        grad_norm,
    )


def solution(mesh):
    return jax.shard_map(
        per_device,
        mesh=mesh,
        in_specs=(
            P("dp", "tensor", None),
            P("dp", None),
            P("dp", "tensor", None),
            P("section", None, "tensor"),
            P("section", None, "tensor"),
            P("section", None, "tensor"),
            P("section", "tensor", None),
            P("section", None, "tensor"),
            P("section", None, "tensor"),
            P("section", "tensor", None),
            P("section", None),
            P("section", None),
        ),
        out_specs=(
            P("dp", "tensor", None),
            P("dp", "tensor", "section"),
            P("section", "dp", "tensor"),
            P("section", "dp", "tensor"),
            P("section", "dp", "tensor"),
            P("section", "tensor", "dp"),
            P("section", "dp", "tensor"),
            P("section", "dp", "tensor"),
            P("section", "tensor", "dp"),
            P("section", ("dp", "tensor")),
            P("section", ("dp", "tensor")),
            P("section"),
        ),
        check_vma=False,
    )
```

time: 1040 us -> 897 us (0.86)
  Pallas kernels: 348 us -> 258 us
  starting transfers between devices: 215 us -> 140 us
  waiting for transfers between devices: 309 us -> 342 us
  between operations: 22.3 us -> 7.51 us
    pallas_call x20 -> x16, Pallas kernels: 348 us -> 258 us  [call(): pl.pallas_call(body, in_specs=in_specs + [any_spec()] * extra, **rest)]
    ppermute x8, waiting for transfers between devices: 26.1 us -> 99.6 us  [shift(): return lax.ppermute(x, 'tensor', pairs)]
    ppermute x74 -> x53, starting transfers between devices: 82.5 us -> 54.7 us  [along(): return lax.ppermute(x, 'dp', [(i, i ^ bit) for i in range(self.DP)])]
    ppermute x16 -> x8, waiting for transfers between devices: 65.9 us -> 38.1 us  [the longest x5 28.1 us: across(): lax.ppermute(x, 'tensor', [(z, (z + self.G) % self.T) for z in range(self...]
    ppermute x18, starting transfers between devices: 43.9 us -> 23.4 us  [ring(): lax.ppermute(x, 'tensor', [(order[i], order[(i + 1) % self.T]) for i in r...]
    convert_element_type x38 -> x30, other arithmetic: 18.9 us -> 38.5 us  [add_low(): return total.astype(BF)]
    ppermute x74 -> x53, waiting for transfers between devices: 133 us -> 117 us  [along(): return lax.ppermute(x, 'dp', [(i, i ^ bit) for i in range(self.DP)])]
    ppermute x16 -> x8, starting transfers between devices: 37.8 us -> 24.1 us  [the longest x3 16.7 us: swap_blocks(): got = lax.ppermute(give, ('section', 'tensor'), pairs)]
  transfers between devices with their start and end apart: 184 -> 109, of which waited for: 68 -> 43; matrix products, arithmetic and copies ran while one was open for 11% -> 13% of each run, Pallas kernels for 25% -> 23%
where the time goes in v2:
time: 897 us; the launch traced here: 889 us
  waiting for transfers between devices  342 us (38%)
  Pallas kernels  258 us (29%)
  starting transfers between devices  140 us (16%)
  other arithmetic  97 us (11%)
  local copies, waits for them, and re-layouts  43.7 us (5%)
    pallas_call x16, Pallas kernels, call(): pl.pallas_call(body, in_specs=in_specs + [any_spec()] * extra, **rest)  258 us
    ppermute x53, waiting for transfers between devices, along(): return lax.ppermute(x, 'dp', [(i, i ^ bit) for i in range(self.DP)])  117 us
    ppermute x8, waiting for transfers between devices, shift(): return lax.ppermute(x, 'tensor', pairs)  99.6 us
    ppermute x18, waiting for transfers between devices, ring(): lax.ppermute(x, 'tensor', [(order[i], order[(i + 1) % self.T]) for i in r...  64.1 us
    ppermute x53, starting transfers between devices, along(): return lax.ppermute(x, 'dp', [(i, i ^ bit) for i in range(self.DP)])  54.7 us
    convert_element_type x30, other arithmetic, add_low(): return total.astype(BF)  38.5 us
    ppermute x5, waiting for transfers between devices, across(): lax.ppermute(x, 'tensor', [(z, (z + self.G) % self.T) for z in range(self...  28.1 us
    ppermute x20, starting transfers between devices, sibling(): return lax.ppermute(x, 'section', [(0, 1), (1, 0)])  24.7 us
  transfers between devices with their start and end apart: 109, of which 43 were waited for; matrix products, arithmetic and copies ran while one was open for 13% of the time, Pallas kernels for 23%

profile of v2, /device:TPU:0, one launch (start us, length us, event | category | flops | bytes accessed | tf_op | source)
XLA Modules:
  0.0 889.3 jit_solution(12541616056539299005)
XLA Ops:
  3.1 7.0 collective-permute-start
  21.7 10.0 %collective-permute-start.1 = (bf16[512,1024]{1,0:T(8,128)(2,1)}, bf16[512,1024]{1,0:T(8,128)(2,1)S(1)}, u32[]{:S(2)}, u32[]{:S(2)}) collective-permute-start(bf16[512,1024]{1,0:T(8,128)(2,1)} %collective-permute-done), channel_id=1, source_target_pairs={{0,16},{16,0},{1,17},{17,1},{2,18},{18,2},{3,19},{19,3},{4,20},{20... | collective-permute-start | bytes 3145736 | tf_op jit(solution)/shard_map/ppermute | solution.py:872
  34.1 3.0 collective-permute-start.12
  37.1 13.3 %collective-permute-done.6 = bf16[256,384]{1,0:T(8,128)(2,1)S(1)} collective-permute-done((bf16[256,384]{1,0:T(8,128)(2,1)S(1)}, bf16[256,384]{1,0:T(8,128)(2,1)S(1)}, u32[]{:S(2)}, u32[]{:S(2)}) %collective-permute-start.6) | collective-permute-done | bytes 196640 | tf_op jit(solution)/shard_map/ppermute | solution.py:882
  63.5 3.5 broadcast_select_fusion
  69.1 29.1 %collective-permute-done.3.refs_2_ = bf16[1,512,1024]{2,1,0:T(8,128)(2,1)} collective-permute-done((bf16[1,512,1024]{2,1,0:T(8,128)(2,1)S(1)}, bf16[1,512,1024]{2,1,0:T(8,128)(2,1)}, u32[]{:S(2)}, u32[]{:S(2)}) %collective-permute-start.3) | collective-permute-done | bytes 1048608 | tf_op jit(solution)/shard_map/ppermute | solution.py:886
  109.0 8.3 collective-permute-done.11.refs_5_.refs_8_.refs_10_.refs_12_.refs_13_
  118.4 10.2 %project.2 = (bf16[4,2048,128]{2,1,0:T(8,128)(2,1)}, bf16[4,2048,128]{2,1,0:T(8,128)(2,1)}, bf16[4,2048,128]{2,1,0:T(8,128)(2,1)}) custom-call(s32[64]{0:T(128)} %fusion.75.refs_0_, bf16[2,512,1024]{2,1,0:T(8,128)(2,1)} %copy-done.10, bf16[1,512,1024]{2,1,0:T(8,128)(2,1)} %collective-permute-done.3.refs_2_, ...), custom_call_target="tpu_custom_call" | custom-call | flops 11500000256 | tf_op jit(solution)/shard_map/project/pallas_call | solution.py:71
  129.2 6.7 collective-permute-done.17.refs_6_.refs_18_.refs_8_.refs_10_.refs_11_
  139.4 8.8 collective-permute-done.19.refs_9_.refs_11_.refs_13_.refs_14_
  149.1 14.2 %attend.2 = (bf16[4,512,256]{2,1,0:T(8,128)(2,1)}, bf16[4,2048,128]{2,1,0:T(8,128)(2,1)}) custom-call(s32[64]{0:T(128)} %fusion.75.refs_0_, bf16[4,2048,128]{2,1,0:T(8,128)(2,1)} %get-tuple-element.86.refs_1_, bf16[4,2048,128]{2,1,0:T(8,128)(2,1)} %get-tuple-element.87.refs_2_, bf16[4,2048,128]{2,1,0:T(8,128)(2,1)} %get-tuple-element.88.refs_3_.refs_9_, ...), custom_call_target="tpu_custom_call" | custom-call | flops 16675000320 | tf_op jit(solution)/shard_map/attend/pallas_call | solution.py:71
  167.2 10.6 %collective-permute-done.15 = bf16[1024,256]{1,0:T(8,128)(2,1)S(1)} collective-permute-done((bf16[1024,256]{1,0:T(8,128)(2,1)S(1)}, bf16[1024,256]{1,0:T(8,128)(2,1)S(1)}, u32[]{:S(2)}, u32[]{:S(2)}) %collective-permute-start.15) | collective-permute-done | bytes 524320 | tf_op jit(solution)/shard_map/ppermute | solution.py:886
  177.8 9.7 %collective-permute-done.24.refs_14_.refs_16_.refs_18_.refs_19_ = bf16[1184,256]{1,0:T(8,128)(2,1)} collective-permute-done((bf16[1184,256]{1,0:T(8,128)(2,1)S(1)}, bf16[1184,256]{1,0:T(8,128)(2,1)}, u32[]{:S(2)}, u32[]{:S(2)}) %collective-permute-start.24) | collective-permute-done | bytes 606240 | tf_op jit(solution)/shard_map/ppermute | solution.py:879
  187.5 4.9 output.2.refs_2_
  196.4 14.6 %collective-permute-done.27.refs_18_.refs_4_.refs_6_.refs_8_.refs_9_ = bf16[1184,256]{1,0:T(8,128)(2,1)S(1)} collective-permute-done((bf16[1184,256]{1,0:T(8,128)(2,1)S(1)}, bf16[1184,256]{1,0:T(8,128)(2,1)S(1)}, u32[]{:S(2)}, u32[]{:S(2)}) %collective-permute-start.27) | collective-permute-done | bytes 606240 | tf_op jit(solution)/shard_map/ppermute | solution.py:876
  212.5 18.3 %mlp.2 = (bf16[1024,1024]{1,0:T(8,128)(2,1)}, f32[1024,1024]{1,0:T(8,128)}, bf16[1024,1024]{1,0:T(8,128)(2,1)}, bf16[1024,704]{1,0:T(8,128)(2,1)}, bf16[1024,704...) custom-call(s32[64]{0:T(128)} %fusion.75.refs_0_, bf16[1024,1024]{1,0:T(8,128)(2,1)} %bitcast.267, ...), custom_call_target="tpu_custom_call" | custom-call | flops 21849999360 | tf_op jit(solution)/shard_map/mlp/pallas_call | solution.py:71
  231.5 3.8 collective-permute-done.28
  235.2 3.9 fusion.13
  243.4 35.4 %collective-permute-done.29.refs_2_ = bf16[1,512,1024]{2,1,0:T(8,128)(2,1)S(1)} collective-permute-done((bf16[1,512,1024]{2,1,0:T(8,128)(2,1)S(1)}, bf16[1,512,1024]{2,1,0:T(8,128)(2,1)S(1)}, u32[]{:S(2)}, u32[]{:S(2)}) %collective-permute-start.29) | collective-permute-done | bytes 1048608 | tf_op jit(solution)/shard_map/ppermute | solution.py:886
  284.6 11.1 %collective-permute-done.32.refs_11_ = bf16[1184,256]{1,0:T(8,128)(2,1)S(1)} collective-permute-done((bf16[1184,256]{1,0:T(8,128)(2,1)S(1)}, bf16[1184,256]{1,0:T(8,128)(2,1)S(1)}, u32[]{:S(2)}, u32[]{:S(2)}) %collective-permute-start.32) | collective-permute-done | bytes 606240 | tf_op jit(solution)/shard_map/ppermute | solution.py:876
  298.6 9.9 %collective-permute-done.34.refs_13_.refs_6_.refs_8_.refs_10_.refs_11_ = bf16[1184,256]{1,0:T(8,128)(2,1)S(1)} collective-permute-done((bf16[1184,256]{1,0:T(8,128)(2,1)S(1)}, bf16[1184,256]{1,0:T(8,128)(2,1)S(1)}, u32[]{:S(2)}, u32[]{:S(2)}) %collective-permute-start.34) | collective-permute-done | bytes 606240 | tf_op jit(solution)/shard_map/ppermute | solution.py:879
  311.7 10.9 %project.3 = (bf16[4,2048,128]{2,1,0:T(8,128)(2,1)}, bf16[4,2048,128]{2,1,0:T(8,128)(2,1)}, bf16[4,2048,128]{2,1,0:T(8,128)(2,1)}) custom-call(s32[64]{0:T(128)} %fusion.75.refs_0_, bf16[2,512,1024]{2,1,0:T(8,128)(2,1)} %bitcast.273, bf16[1,512,1024]{2,1,0:T(8,128)(2,1)} %copy-done.82, bf16[1,512,1024]{2,1,0:T(8,128)(2,1)} %copy-done.83, ...), custom_call_target="tpu_custom_call" | custom-call | flops 11500000256 | tf_op jit(solution)/shard_map/project/pallas_call | solution.py:71
  322.6 14.5 %attend.3 = (bf16[4,512,256]{2,1,0:T(8,128)(2,1)}, bf16[4,2048,128]{2,1,0:T(8,128)(2,1)}) custom-call(s32[64]{0:T(128)} %fusion.75.refs_0_, bf16[4,2048,128]{2,1,0:T(8,128)(2,1)} %get-tuple-element.94.refs_1_, bf16[4,2048,128]{2,1,0:T(8,128)(2,1)} %get-tuple-element.95.refs_2_, bf16[4,2048,128]{2,1,0:T(8,128)(2,1)} %get-tuple-element.96.refs_3_), custom_call_target="tpu_custom_call" | custom-call | flops 16675000320 | tf_op jit(solution)/shard_map/attend/pallas_call | solution.py:71
  339.9 4.2 collective-permute-start.41
  344.0 16.8 %collective-permute-done.38.refs_10_.refs_12_.refs_14_.refs_15_ = bf16[2368,256]{1,0:T(8,128)(2,1)} collective-permute-done((bf16[2368,256]{1,0:T(8,128)(2,1)}, bf16[2368,256]{1,0:T(8,128)(2,1)}, u32[]{:S(2)}, u32[]{:S(2)}) %collective-permute-start.38) | collective-permute-done | bytes 1212448 | tf_op jit(solution)/shard_map/ppermute | solution.py:879
  361.7 4.9 output.3.refs_2_
  367.1 5.0 collective-permute-done.42
  373.9 18.2 %mlp.3 = (bf16[1024,1024]{1,0:T(8,128)(2,1)}, f32[1024,1024]{1,0:T(8,128)}, bf16[1024,1024]{1,0:T(8,128)(2,1)}, bf16[1024,704]{1,0:T(8,128)(2,1)}, bf16[1024,704...) custom-call(s32[64]{0:T(128)} %fusion.75.refs_0_, bf16[1024,1024]{1,0:T(8,128)(2,1)} %copy-done.4, ...), custom_call_target="tpu_custom_call" | custom-call | flops 21849999360 | tf_op jit(solution)/shard_map/mlp/pallas_call | solution.py:71
  393.8 27.9 %mlp_back.2 = (bf16[4,2112,256]{2,1,0:T(8,128)(2,1)}, bf16[4,2112,256]{2,1,0:T(8,128)(2,1)}, bf16[1024,1024]{1,0:T(8,128)(2,1)}) custom-call(s32[64]{0:T(128)} %fusion.75.refs_0_, bf16[1024,1024]{1,0:T(8,128)(2,1)} %bitcast.276, bf16[1024,1024]{1,0:T(8,128)(2,1)} %get-tuple-element.100.refs_2_, bf16[1024,704]{1,0:T(8,128)(2,1)} %get-tuple-element.101.refs_3_, ...), custom_call_target="tpu_custom_call" | custom-call | flops 32199999488 | tf_op jit(solution)/shard_map/mlp_back/pallas_call | solution.py:71
  423.0 4.7 add_convert_fusion
  427.9 5.6 collective-permute-start.44
  436.7 8.1 collective-permute-done.44
  444.8 11.3 %collective-permute-start.45 = (bf16[512,1024]{1,0:T(8,128)(2,1)}, bf16[512,1024]{1,0:T(8,128)(2,1)}, u32[]{:S(2)}, u32[]{:S(2)}) collective-permute-start(bf16[512,1024]{1,0:T(8,128)(2,1)} %collective-permute-done.44), channel_id=1, source_target_pairs={{0,16},{16,0},{1,17},{17,1},{2,18},{18,2},{3,19},{19,3},{4,20},{20... | collective-permute-start | bytes 3145736 | tf_op jit(solution)/shard_map/ppermute | solution.py:872
  456.1 12.3 %middle.2 = (f32[1024,1024]{1,0:T(8,128)}, f32[1,1024]{1,0:T(1,128)}, bf16[2,1024,256]{2,1,0:T(8,128)(2,1)}, bf16[4,512,256]{2,1,0:T(8,128)(2,1)}) custom-call(s32[64]{0:T(128)} %fusion.75.refs_0_, bf16[1024,1024]{1,0:T(8,128)(2,1)} %bitcast.277, bf16[1024,1024]{1,0:T(8,128)(2,1)} %get-tuple-element.105.refs_2_, ...), custom_call_target="tpu_custom_call" | custom-call | flops 14949999616 | tf_op jit(solution)/shard_map/middle/pallas_call | solution.py:71
  478.1 5.3 collective-permute-done.47
  484.2 29.8 %attend_back.2 = (bf16[2048,256]{1,0:T(8,128)(2,1)}, bf16[2048,256]{1,0:T(8,128)(2,1)}, bf16[2048,256]{1,0:T(8,128)(2,1)}, f32[2048,256]{1,0:T(8,128)}) custom-call(s32[64]{0:T(128)} %fusion.75.refs_0_, bf16[4,2048,128]{2,1,0:T(8,128)(2,1)} %get-tuple-element.107.refs_1_, bf16[4,2048,128]{2,1,0:T(8,128)(2,1)} %get-tuple-element.95.refs_2_, ...), custom_call_target="tpu_custom_call" | custom-call | flops 33924999168 | tf_op jit(solution)/shard_map/attend_back/pallas_call | solution.py:71
  514.0 11.2 %project_back.2 = (bf16[2,512,1024]{2,1,0:T(8,128)(2,1)}, bf16[2,512,1024]{2,1,0:T(8,128)(2,1)}, bf16[4,256,768]{2,1,0:T(8,128)(2,1)}) custom-call(s32[64]{0:T(128)} %fusion.75.refs_0_, bf16[2,512,1024]{2,1,0:T(8,128)(2,1)} %bitcast.274, bf16[1,512,1024]{2,1,0:T(8,128)(2,1)} %copy-done.82, bf16[1,512,1024]{2,1,0:T(8,128)(2,1)} %copy-done.83, ...), custom_call_target="tpu_custom_call" | custom-call | flops 13799999488 | tf_op jit(solution)/shard_map/project_back/pallas_call | solution.py:71
  525.3 3.2 fusion.82
  534.1 20.9 %collective-permute-done.58 = bf16[2,1056,256]{2,1,0:T(8,128)(2,1)} collective-permute-done((bf16[2,1056,256]{2,1,0:T(8,128)(2,1)}, bf16[2,1056,256]{2,1,0:T(8,128)(2,1)}, u32[]{:S(2)}, u32[]{:S(2)}) %collective-permute-start.58) | collective-permute-done | bytes 1081376 | tf_op jit(solution)/shard_map/ppermute | solution.py:879
  555.5 3.0 fusion.39
  567.6 10.4 %collective-permute-done.60.refs_23_ = bf16[2,256,256]{2,1,0:T(8,128)(2,1)S(1)} collective-permute-done((bf16[2,256,256]{2,1,0:T(8,128)(2,1)S(1)}, bf16[2,256,256]{2,1,0:T(8,128)(2,1)S(1)}, u32[]{:S(2)}, u32[]{:S(2)}) %collective-permute-start.60) | collective-permute-done | bytes 262176 | tf_op jit(solution)/shard_map/ppermute | solution.py:879
  587.1 3.8 fusion.78
  590.8 27.7 %mlp_back.3 = (bf16[4,2112,256]{2,1,0:T(8,128)(2,1)}, bf16[4,2112,256]{2,1,0:T(8,128)(2,1)}, bf16[1024,1024]{1,0:T(8,128)(2,1)}) custom-call(s32[64]{0:T(128)} %fusion.75.refs_0_, bf16[1024,1024]{1,0:T(8,128)(2,1)} %get-tuple-element.175.refs_1_, bf16[1024,1024]{1,0:T(8,128)(2,1)} %get-tuple-element.116.refs_2_, ...), custom_call_target="tpu_custom_call" | custom-call | flops 32199999488 | tf_op jit(solution)/shard_map/mlp_back/pallas_call | solution.py:71
  618.6 3.2 fusion.81
  629.0 6.4 collective-permute-done.66.refs_29_
  635.4 3.5 collective-permute-start.69
  645.3 12.9 %middle.3 = (f32[1024,1024]{1,0:T(8,128)}, f32[1,1024]{1,0:T(1,128)}, bf16[2,1024,256]{2,1,0:T(8,128)(2,1)}, bf16[4,512,256]{2,1,0:T(8,128)(2,1)}) custom-call(s32[64]{0:T(128)} %fusion.75.refs_0_, f32[1024,1024]{1,0:T(8,128)} %get-tuple-element.176.refs_1_, bf16[1024,1024]{1,0:T(8,128)(2,1)} %get-tuple-element.121.refs_2_, ...), custom_call_target="tpu_custom_call" | custom-call | flops 14949999616 | tf_op jit(solution)/shard_map/middle/pallas_call | solution.py:71
  662.6 6.4 collective-permute-done.73.refs_16_
  670.1 3.5 collective-permute-done.74.refs_17_
  686.6 29.8 %attend_back.3 = (bf16[2048,256]{1,0:T(8,128)(2,1)}, bf16[2048,256]{1,0:T(8,128)(2,1)}, bf16[2048,256]{1,0:T(8,128)(2,1)}) custom-call(s32[64]{0:T(128)} %fusion.75.refs_0_, bf16[4,2048,128]{2,1,0:T(8,128)(2,1)} %get-tuple-element.132.refs_1_, bf16[4,2048,128]{2,1,0:T(8,128)(2,1)} %get-tuple-element.87.refs_2_, ...), custom_call_target="tpu_custom_call" | custom-call | flops 33924999168 | tf_op jit(solution)/shard_map/attend_back/pallas_call | solution.py:71
  724.5 11.2 %project_back.3 = (bf16[2,512,1024]{2,1,0:T(8,128)(2,1)}, bf16[2,512,1024]{2,1,0:T(8,128)(2,1)}, bf16[4,256,768]{2,1,0:T(8,128)(2,1)}) custom-call(s32[64]{0:T(128)} %fusion.75.refs_0_, bf16[2,512,1024]{2,1,0:T(8,128)(2,1)} %copy-done.10, bf16[1,512,1024]{2,1,0:T(8,128)(2,1)} %collective-permute-done.3.refs_2_, ...), custom_call_target="tpu_custom_call" | custom-call | flops 13799999488 | tf_op jit(solution)/shard_map/project_back/pallas_call | solution.py:71
  741.6 5.4 collective-permute-done.97
  759.2 6.0 collective-permute-done.101
  767.3 3.5 collective-permute-done.85
  776.0 7.5 collective-permute-done.86
  787.2 11.5 %collective-permute-done.94 = bf16[1056,256]{1,0:T(8,128)(2,1)S(1)} collective-permute-done((bf16[1056,256]{1,0:T(8,128)(2,1)S(1)}, bf16[1056,256]{1,0:T(8,128)(2,1)S(1)}, u32[]{:S(2)}, u32[]{:S(2)}) %collective-permute-start.94) | collective-permute-done | bytes 540704 | tf_op jit(solution)/shard_map/ppermute | solution.py:876
  803.5 11.3 %collective-permute-done.95 = bf16[1056,256]{1,0:T(8,128)(2,1)S(1)} collective-permute-done((bf16[1056,256]{1,0:T(8,128)(2,1)S(1)}, bf16[1056,256]{1,0:T(8,128)(2,1)S(1)}, u32[]{:S(2)}, u32[]{:S(2)}) %collective-permute-start.95) | collective-permute-done | bytes 540704 | tf_op jit(solution)/shard_map/ppermute | solution.py:876
  818.6 18.6 %collective-permute-done.79 = bf16[512,1024]{1,0:T(8,128)(2,1)S(1)} collective-permute-done((bf16[512,1024]{1,0:T(8,128)(2,1)S(1)}, bf16[512,1024]{1,0:T(8,128)(2,1)S(1)}, u32[]{:S(2)}, u32[]{:S(2)}) %collective-permute-start.79) | collective-permute-done | bytes 1048608 | tf_op jit(solution)/shard_map/ppermute | solution.py:886
  843.9 3.0 fusion.15
  851.6 3.0 collective-permute-done.106
  854.7 2.9 multiply_add_fusion
  862.4 12.2 %collective-permute-done.108 = f32[3,1024]{1,0:T(4,128)S(1)} collective-permute-done((f32[3,1024]{1,0:T(4,128)S(1)}, f32[3,1024]{1,0:T(4,128)S(1)}, u32[]{:S(2)}, u32[]{:S(2)}) %collective-permute-start.108) | collective-permute-done | bytes 12320 | tf_op jit(solution)/shard_map/ppermute | solution.py:1104
  877.7 6.8 collective-permute-done.81
  884.6 3.3 dynamic-slice_select_fusion
  (503 shorter events, 214.4 us)
Async XLA Ops:
  10.7 22.7 %collective-permute-start.2 = (f32[2,1024]{1,0:T(2,128)}, f32[2,1024]{1,0:T(2,128)}, u32[]{:S(2)}, u32[]{:S(2)}) collective-permute-start(f32[2,1024]{1,0:T(2,128)} %pad_maximum_fusion.11), channel_id=1, source_target_pairs={{0,16},{16,0},{1,17},{17,1},{2,18},{18,2},{3,19},{19,3},{4,20},{20... | collective-permute-start | bytes 24584 | tf_op jit(solution)/shard_map/ppermute | solution.py:872
  19.7 42.1 %collective-permute-start.9 = (bf16[1184,1024]{1,0:T(8,128)(2,1)}, bf16[1184,1024]{1,0:T(8,128)(2,1)}, u32[]{:S(2)}, u32[]{:S(2)}) collective-permute-start(bf16[1184,1024]{1,0:T(8,128)(2,1)} %pad_maximum_fusion.1), channel_id=1, source_target_pairs={{0,16},{16,0},{1,17},{17,1},{2,18},{18,2},{3,19},{19,3},{4,20},{20... | collective-permute-start | bytes 7274504 | tf_op jit(solution)/shard_map/ppermute | solution.py:872
  21.7 37.4 %collective-permute-start.1 = (bf16[512,1024]{1,0:T(8,128)(2,1)}, bf16[512,1024]{1,0:T(8,128)(2,1)S(1)}, u32[]{:S(2)}, u32[]{:S(2)}) collective-permute-start(bf16[512,1024]{1,0:T(8,128)(2,1)} %collective-permute-done), channel_id=1, source_target_pairs={{0,16},{16,0},{1,17},{17,1},{2,18},{18,2},{3,19},{19,3},{4,20},{20... | collective-permute-start | bytes 3145736 | tf_op jit(solution)/shard_map/ppermute | solution.py:872
  34.1 19.5 %collective-permute-start.12 = (bf16[256,384]{1,0:T(8,128)(2,1)S(1)}, bf16[256,384]{1,0:T(8,128)(2,1)S(1)}, u32[]{:S(2)}, u32[]{:S(2)}) collective-permute-start(bf16[256,384]{1,0:T(8,128)(2,1)S(1)} %constant_dynamic-slice_fusion.3), channel_id=1, source_target_pairs={{0,2},{1,3},{2,0},{3,1},{4,6},{5,7},{6,4},{7,5},{8,10},{9,11},{10,... | collective-permute-start | bytes 589832 | tf_op jit(solution)/shard_map/ppermute | solution.py:882
  56.7 44.6 %collective-permute-start.8 = (bf16[512,384]{1,0:T(8,128)(2,1)S(1)}, bf16[512,384]{1,0:T(8,128)(2,1)}, u32[]{:S(2)}, u32[]{:S(2)}) collective-permute-start(bf16[512,384]{1,0:T(8,128)(2,1)S(1)} %maximum_select_fusion.2), channel_id=1, source_target_pairs={{0,8},{4,12},{8,0},{12,4},{1,9},{5,13},{9,1},{13,5},{2,10},{6,14},... | collective-permute-start | bytes 1179656 | tf_op jit(solution)/shard_map/ppermute | solution.py:879
  61.7 36.5 %collective-permute-start.3 = (bf16[1,512,1024]{2,1,0:T(8,128)(2,1)S(1)}, bf16[1,512,1024]{2,1,0:T(8,128)(2,1)}, u32[]{:S(2)}, u32[]{:S(2)}) collective-permute-start(bf16[1,512,1024]{2,1,0:T(8,128)(2,1)S(1)} %constant_dynamic-slice_fusion.7), channel_id=1, source_target_pairs={{0,1},{1,0},{2,3},{3,2},{4,5},{5,4},{6,7},{7,6},{8,9},{9,8},{10,11... | collective-permute-start | bytes 3145736 | tf_op jit(solution)/shard_map/ppermute | solution.py:886
  68.5 31.6 %collective-permute-start.10 = (bf16[1184,256]{1,0:T(8,128)(2,1)S(1)}, bf16[1184,256]{1,0:T(8,128)(2,1)}, u32[]{:S(2)}, u32[]{:S(2)}) collective-permute-start(bf16[1184,256]{1,0:T(8,128)(2,1)S(1)} %constant_dynamic-slice_fusion.4), channel_id=1, source_target_pairs={{0,1},{1,3},{3,2},{2,0},{4,5},{5,7},{7,6},{6,4},{8,9},{9,11},{11,1... | collective-permute-start | bytes 1818632 | tf_op jit(solution)/shard_map/ppermute | solution.py:876
  69.0 33.7 %collective-permute-start.14 = (bf16[512,384]{1,0:T(8,128)(2,1)S(1)}, bf16[512,384]{1,0:T(8,128)(2,1)S(1)}, u32[]{:S(2)}, u32[]{:S(2)}) collective-permute-start(bf16[512,384]{1,0:T(8,128)(2,1)S(1)} %maximum_select_fusion.3), channel_id=1, source_target_pairs={{0,8},{4,12},{8,0},{12,4},{1,9},{5,13},{9,1},{13,5},{2,10},{6,14},... | collective-permute-start | bytes 1179656 | tf_op jit(solution)/shard_map/ppermute | solution.py:879
  98.2 20.0 %collective-permute-start.4 = (bf16[1,512,1024]{2,1,0:T(8,128)(2,1)}, bf16[1,512,1024]{2,1,0:T(8,128)(2,1)}, u32[]{:S(2)}, u32[]{:S(2)}) collective-permute-start(bf16[1,512,1024]{2,1,0:T(8,128)(2,1)} %collective-permute-done.3.refs_2_), channel_id=1, source_target_pairs={{0,16},{16,0},{1,17},{17,1},{2,18},{18,2},{3,19},{19,3},{4,20},{20... | collective-permute-start | bytes 3145736 | tf_op jit(solution)/shard_map/ppermute | solution.py:872
  105.5 23.0 %collective-permute-start.16 = (bf16[1184,256]{1,0:T(8,128)(2,1)}, bf16[1184,256]{1,0:T(8,128)(2,1)S(1)}, u32[]{:S(2)}, u32[]{:S(2)}) collective-permute-start(bf16[1184,256]{1,0:T(8,128)(2,1)} %collective-permute-done.10.refs_4_.refs_6_.refs_8_.refs_9_), channel_id=1, source_target_pairs={{0,4},{4,0},{8,12},{12,8},{1,5},{5,1},{9,13},{13,9},{2,6},{6,2},{1... | collective-permute-start | bytes 1818632 | tf_op jit(solution)/shard_map/ppermute | solution.py:879
  106.4 29.5 %collective-permute-start.17 = (bf16[1184,256]{1,0:T(8,128)(2,1)}, bf16[1184,256]{1,0:T(8,128)(2,1)S(1)}, u32[]{:S(2)}, u32[]{:S(2)}) collective-permute-start(bf16[1184,256]{1,0:T(8,128)(2,1)} %collective-permute-done.10.refs_4_.refs_6_.refs_8_.refs_9_), channel_id=1, source_target_pairs={{0,8},{4,12},{8,0},{12,4},{1,9},{5,13},{9,1},{13,5},{2,10},{6,14},... | collective-permute-start | bytes 1818632 | tf_op jit(solution)/shard_map/ppermute | solution.py:879
  106.9 30.5 %collective-permute-start.18 = (bf16[1184,256]{1,0:T(8,128)(2,1)}, bf16[1184,256]{1,0:T(8,128)(2,1)S(1)}, u32[]{:S(2)}, u32[]{:S(2)}) collective-permute-start(bf16[1184,256]{1,0:T(8,128)(2,1)} %collective-permute-done.10.refs_4_.refs_6_.refs_8_.refs_9_), channel_id=1, source_target_pairs={{0,12},{4,8},{8,4},{12,0},{1,13},{5,9},{9,5},{13,1},{2,14},{6,10},... | collective-permute-start | bytes 1818632 | tf_op jit(solution)/shard_map/ppermute | solution.py:879
  117.3 30.9 %collective-permute-start.19 = (bf16[1184,256]{1,0:T(8,128)(2,1)S(1)}, bf16[1184,256]{1,0:T(8,128)(2,1)S(1)}, u32[]{:S(2)}, u32[]{:S(2)}) collective-permute-start(bf16[1184,256]{1,0:T(8,128)(2,1)S(1)} %collective-permute-done.11.refs_5_.refs_8_.refs_10_.refs_12_.refs_13_), channel_id=1, source_target_pairs={{0,4},{4,0},{8,12},{12,8},{1,5},{5,1},{9,13},{13,9},{2,6},{6,2},{1... | collective-permute-start | bytes 1818632 | tf_op jit(solution)/shard_map/ppermute | solution.py:879
  128.6 35.8 %collective-permute-start.20 = (bf16[1184,256]{1,0:T(8,128)(2,1)S(1)}, bf16[1184,256]{1,0:T(8,128)(2,1)}, u32[]{:S(2)}, u32[]{:S(2)}) collective-permute-start(bf16[1184,256]{1,0:T(8,128)(2,1)S(1)} %collective-permute-done.11.refs_5_.refs_8_.refs_10_.refs_12_.refs_13_), channel_id=1, source_target_pairs={{0,8},{4,12},{8,0},{12,4},{1,9},{5,13},{9,1},{13,5},{2,10},{6,14},... | collective-permute-start | bytes 1818632 | tf_op jit(solution)/shard_map/ppermute | solution.py:879
  135.9 31.2 %collective-permute-start.21 = (bf16[1184,256]{1,0:T(8,128)(2,1)S(1)}, bf16[1184,256]{1,0:T(8,128)(2,1)}, u32[]{:S(2)}, u32[]{:S(2)}) collective-permute-start(bf16[1184,256]{1,0:T(8,128)(2,1)S(1)} %collective-permute-done.11.refs_5_.refs_8_.refs_10_.refs_12_.refs_13_), channel_id=1, source_target_pairs={{0,12},{4,8},{8,4},{12,0},{1,13},{5,9},{9,5},{13,1},{2,14},{6,10},... | collective-permute-start | bytes 1818632 | tf_op jit(solution)/shard_map/ppermute | solution.py:879
  136.4 41.4 %collective-permute-start.23 = (bf16[1184,256]{1,0:T(8,128)(2,1)S(1)}, bf16[1184,256]{1,0:T(8,128)(2,1)}, u32[]{:S(2)}, u32[]{:S(2)}) collective-permute-start(bf16[1184,256]{1,0:T(8,128)(2,1)S(1)} %collective-permute-done.22.refs_12_.refs_16_.refs_14_.refs_17_), channel_id=1, source_target_pairs={{0,4},{4,0},{8,12},{12,8},{1,5},{5,1},{9,13},{13,9},{2,6},{6,2},{1... | collective-permute-start | bytes 1818632 | tf_op jit(solution)/shard_map/ppermute | solution.py:879
  137.4 50.1 %collective-permute-start.24 = (bf16[1184,256]{1,0:T(8,128)(2,1)S(1)}, bf16[1184,256]{1,0:T(8,128)(2,1)}, u32[]{:S(2)}, u32[]{:S(2)}) collective-permute-start(bf16[1184,256]{1,0:T(8,128)(2,1)S(1)} %collective-permute-done.22.refs_12_.refs_16_.refs_14_.refs_17_), channel_id=1, source_target_pairs={{0,8},{4,12},{8,0},{12,4},{1,9},{5,13},{9,1},{13,5},{2,10},{6,14},... | collective-permute-start | bytes 1818632 | tf_op jit(solution)/shard_map/ppermute | solution.py:879
  148.3 39.3 %collective-permute-start.25 = (bf16[1184,256]{1,0:T(8,128)(2,1)S(1)}, bf16[1184,256]{1,0:T(8,128)(2,1)}, u32[]{:S(2)}, u32[]{:S(2)}) collective-permute-start(bf16[1184,256]{1,0:T(8,128)(2,1)S(1)} %collective-permute-done.22.refs_12_.refs_16_.refs_14_.refs_17_), channel_id=1, source_target_pairs={{0,12},{4,8},{8,4},{12,0},{1,13},{5,9},{9,5},{13,1},{2,14},{6,10},... | collective-permute-start | bytes 1818632 | tf_op jit(solution)/shard_map/ppermute | solution.py:879
  192.4 18.6 %collective-permute-start.26 = (bf16[1024,1024]{1,0:T(8,128)(2,1)}, bf16[1024,1024]{1,0:T(8,128)(2,1)S(1)}, u32[]{:S(2)}, u32[]{:S(2)}) collective-permute-start(bf16[1024,1024]{1,0:T(8,128)(2,1)} %output.2.refs_2_), channel_id=1, source_target_pairs={{0,16},{16,0},{1,17},{17,1},{2,18},{18,2},{3,19},{19,3},{4,20},{20... | collective-permute-start | bytes 6291464 | tf_op jit(solution)/shard_map/ppermute | solution.py:872
  240.5 38.3 %collective-permute-start.29 = (bf16[1,512,1024]{2,1,0:T(8,128)(2,1)S(1)}, bf16[1,512,1024]{2,1,0:T(8,128)(2,1)S(1)}, u32[]{:S(2)}, u32[]{:S(2)}) collective-permute-start(bf16[1,512,1024]{2,1,0:T(8,128)(2,1)S(1)} %constant_dynamic-slice_fusion.1), channel_id=1, source_target_pairs={{0,1},{1,0},{2,3},{3,2},{4,5},{5,4},{6,7},{7,6},{8,9},{9,8},{10,11... | collective-permute-start | bytes 3145736 | tf_op jit(solution)/shard_map/ppermute | solution.py:886
  242.0 36.8 %collective-permute-start.31 = (bf16[1184,256]{1,0:T(8,128)(2,1)S(1)}, bf16[1184,256]{1,0:T(8,128)(2,1)S(1)}, u32[]{:S(2)}, u32[]{:S(2)}) collective-permute-start(bf16[1184,256]{1,0:T(8,128)(2,1)S(1)} %copy-done.91), channel_id=1, source_target_pairs={{0,1},{1,3},{3,2},{2,0},{4,5},{5,7},{7,6},{6,4},{8,9},{9,11},{11,1... | collective-permute-start | bytes 1818632 | tf_op jit(solution)/shard_map/ppermute | solution.py:876
  278.8 31.9 %collective-permute-start.30 = (bf16[1,512,1024]{2,1,0:T(8,128)(2,1)S(1)}, bf16[1,512,1024]{2,1,0:T(8,128)(2,1)S(1)}, u32[]{:S(2)}, u32[]{:S(2)}) collective-permute-start(bf16[1,512,1024]{2,1,0:T(8,128)(2,1)S(1)} %collective-permute-done.29.refs_2_), channel_id=1, source_target_pairs={{0,16},{16,0},{1,17},{17,1},{2,18},{18,2},{3,19},{19,3},{4,20},{20... | collective-permute-start | bytes 3145736 | tf_op jit(solution)/shard_map/ppermute | solution.py:872
  280.8 27.7 %collective-permute-start.34 = (bf16[1184,256]{1,0:T(8,128)(2,1)S(1)}, bf16[1184,256]{1,0:T(8,128)(2,1)S(1)}, u32[]{:S(2)}, u32[]{:S(2)}) collective-permute-start(bf16[1184,256]{1,0:T(8,128)(2,1)S(1)} %copy-done.91), channel_id=1, source_target_pairs={{0,8},{4,12},{8,0},{12,4},{1,9},{5,13},{9,1},{13,5},{2,10},{6,14},... | collective-permute-start | bytes 1818632 | tf_op jit(solution)/shard_map/ppermute | solution.py:879
  282.0 27.8 %collective-permute-start.35 = (bf16[1184,256]{1,0:T(8,128)(2,1)S(1)}, bf16[1184,256]{1,0:T(8,128)(2,1)S(1)}, u32[]{:S(2)}, u32[]{:S(2)}) collective-permute-start(bf16[1184,256]{1,0:T(8,128)(2,1)S(1)} %copy-done.91), channel_id=1, source_target_pairs={{0,12},{4,8},{8,4},{12,0},{1,13},{5,9},{9,5},{13,1},{2,14},{6,10},... | collective-permute-start | bytes 1818632 | tf_op jit(solution)/shard_map/ppermute | solution.py:879
  296.8 47.3 %collective-permute-start.37 = (bf16[2368,256]{1,0:T(8,128)(2,1)}, bf16[2368,256]{1,0:T(8,128)(2,1)}, u32[]{:S(2)}, u32[]{:S(2)}) collective-permute-start(bf16[2368,256]{1,0:T(8,128)(2,1)} %constant_dynamic-update-slice_fusion.refs_8_.refs_10_.refs_12_.refs_13_), channel_id=1, source_target_pairs={{0,4},{4,0},{8,12},{12,8},{1,5},{5,1},{9,13},{13,9},{2,6},{6,2},{1... | collective-permute-start | bytes 3637256 | tf_op jit(solution)/shard_map/ppermute | solution.py:879
  297.9 63.0 %collective-permute-start.38 = (bf16[2368,256]{1,0:T(8,128)(2,1)}, bf16[2368,256]{1,0:T(8,128)(2,1)}, u32[]{:S(2)}, u32[]{:S(2)}) collective-permute-start(bf16[2368,256]{1,0:T(8,128)(2,1)} %constant_dynamic-update-slice_fusion.refs_8_.refs_10_.refs_12_.refs_13_), channel_id=1, source_target_pairs={{0,8},{4,12},{8,0},{12,4},{1,9},{5,13},{9,1},{13,5},{2,10},{6,14},... | collective-permute-start | bytes 3637256 | tf_op jit(solution)/shard_map/ppermute | solution.py:879
  308.4 52.4 %collective-permute-start.39 = (bf16[2368,256]{1,0:T(8,128)(2,1)}, bf16[2368,256]{1,0:T(8,128)(2,1)}, u32[]{:S(2)}, u32[]{:S(2)}) collective-permute-start(bf16[2368,256]{1,0:T(8,128)(2,1)} %constant_dynamic-update-slice_fusion.refs_8_.refs_10_.refs_12_.refs_13_), channel_id=1, source_target_pairs={{0,12},{4,8},{8,4},{12,0},{1,13},{5,9},{9,5},{13,1},{2,14},{6,10},... | collective-permute-start | bytes 3637256 | tf_op jit(solution)/shard_map/ppermute | solution.py:879
  338.1 22.8 %collective-permute-start.36 = (bf16[1024,256]{1,0:T(8,128)(2,1)S(1)}, bf16[1024,256]{1,0:T(8,128)(2,1)S(1)}, u32[]{:S(2)}, u32[]{:S(2)}) collective-permute-start(bf16[1024,256]{1,0:T(8,128)(2,1)S(1)} %bitcast.278), channel_id=1, source_target_pairs={{0,1},{1,0},{2,3},{3,2},{4,5},{5,4},{6,7},{7,6},{8,9},{9,8},{10,11... | collective-permute-start | bytes 1572872 | tf_op jit(solution)/shard_map/ppermute | solution.py:886
  339.9 26.8 %collective-permute-start.41 = (bf16[512,1024]{1,0:T(8,128)(2,1)S(1)}, bf16[512,1024]{1,0:T(8,128)(2,1)}, u32[]{:S(2)}, u32[]{:S(2)}) collective-permute-start(bf16[512,1024]{1,0:T(8,128)(2,1)S(1)} %dynamic-slice_bitcast_fusion.1), channel_id=1, source_target_pairs={{0,2},{1,3},{18,16},{19,17},{4,6},{5,7},{22,20},{23,21},{8,10},{9,... | collective-permute-start | bytes 3145736 | tf_op jit(solution)/shard_map/ppermute | solution.py:895
  392.1 29.6 %collective-permute-start.43 = (bf16[1024,1024]{1,0:T(8,128)(2,1)}, bf16[1024,1024]{1,0:T(8,128)(2,1)S(1)}, u32[]{:S(2)}, u32[]{:S(2)}) collective-permute-start(bf16[1024,1024]{1,0:T(8,128)(2,1)} %get-tuple-element.99), channel_id=1, source_target_pairs={{0,16},{16,0},{1,17},{17,1},{2,18},{18,2},{3,19},{19,3},{4,20},{20... | collective-permute-start | bytes 6291464 | tf_op jit(solution)/shard_map/ppermute | solution.py:872
  421.6 34.5 %collective-permute-start.46 = (bf16[1024,1024]{1,0:T(8,128)(2,1)}, bf16[1024,1024]{1,0:T(8,128)(2,1)}, u32[]{:S(2)}, u32[]{:S(2)}) collective-permute-start(bf16[1024,1024]{1,0:T(8,128)(2,1)} %get-tuple-element.105.refs_2_), channel_id=1, source_target_pairs={{0,16},{16,0},{1,17},{17,1},{2,18},{18,2},{3,19},{19,3},{4,20},{20... | collective-permute-start | bytes 6291464 | tf_op jit(solution)/shard_map/ppermute | solution.py:872
  434.9 34.6 %collective-permute-start.48 = (bf16[2,1056,256]{2,1,0:T(8,128)(2,1)}, bf16[2,1056,256]{2,1,0:T(8,128)(2,1)}, u32[]{:S(2)}, u32[]{:S(2)}) collective-permute-start(bf16[2,1056,256]{2,1,0:T(8,128)(2,1)} %get-tuple-element.198), channel_id=1, source_target_pairs={{0,4},{4,0},{8,12},{12,8},{1,5},{5,1},{9,13},{13,9},{2,6},{6,2},{1... | collective-permute-start | bytes 3244040 | tf_op jit(solution)/shard_map/ppermute | solution.py:879
  435.8 33.8 %collective-permute-start.49 = (bf16[2,1056,256]{2,1,0:T(8,128)(2,1)}, bf16[2,1056,256]{2,1,0:T(8,128)(2,1)S(1)}, u32[]{:S(2)}, u32[]{:S(2)}) collective-permute-start(bf16[2,1056,256]{2,1,0:T(8,128)(2,1)} %get-tuple-element.197), channel_id=1, source_target_pairs={{0,8},{4,12},{8,0},{12,4},{1,9},{5,13},{9,1},{13,5},{2,10},{6,14},... | collective-permute-start | bytes 3244040 | tf_op jit(solution)/shard_map/ppermute | solution.py:879
  444.8 30.3 %collective-permute-start.45 = (bf16[512,1024]{1,0:T(8,128)(2,1)}, bf16[512,1024]{1,0:T(8,128)(2,1)}, u32[]{:S(2)}, u32[]{:S(2)}) collective-permute-start(bf16[512,1024]{1,0:T(8,128)(2,1)} %collective-permute-done.44), channel_id=1, source_target_pairs={{0,16},{16,0},{1,17},{17,1},{2,18},{18,2},{3,19},{19,3},{4,20},{20... | collective-permute-start | bytes 3145736 | tf_op jit(solution)/shard_map/ppermute | solution.py:872
  472.4 41.5 %collective-permute-start.50 = (bf16[1056,256]{1,0:T(8,128)(2,1)}, bf16[1056,256]{1,0:T(8,128)(2,1)}, u32[]{:S(2)}, u32[]{:S(2)}) collective-permute-start(bf16[1056,256]{1,0:T(8,128)(2,1)} %get-tuple-element.196), channel_id=1, source_target_pairs={{0,4},{4,0},{8,12},{12,8},{1,5},{5,1},{9,13},{13,9},{2,6},{6,2},{1... | collective-permute-start | bytes 1622024 | tf_op jit(solution)/shard_map/ppermute | solution.py:879
  473.6 40.4 %collective-permute-start.51 = (bf16[1056,256]{1,0:T(8,128)(2,1)S(1)}, bf16[1056,256]{1,0:T(8,128)(2,1)}, u32[]{:S(2)}, u32[]{:S(2)}) collective-permute-start(bf16[1056,256]{1,0:T(8,128)(2,1)S(1)} %get-tuple-element.195), channel_id=1, source_target_pairs={{0,8},{4,12},{8,0},{12,4},{1,9},{5,13},{9,1},{13,5},{2,10},{6,14},... | collective-permute-start | bytes 1622024 | tf_op jit(solution)/shard_map/ppermute | solution.py:879
  528.5 26.6 %collective-permute-start.58 = (bf16[2,1056,256]{2,1,0:T(8,128)(2,1)}, bf16[2,1056,256]{2,1,0:T(8,128)(2,1)}, u32[]{:S(2)}, u32[]{:S(2)}) collective-permute-start(bf16[2,1056,256]{2,1,0:T(8,128)(2,1)} %get-tuple-element.193), channel_id=1, source_target_pairs={{0,4},{4,0},{8,12},{12,8},{1,5},{5,1},{9,13},{13,9},{2,6},{6,2},{1... | collective-permute-start | bytes 3244040 | tf_op jit(solution)/shard_map/ppermute | solution.py:879
  529.3 26.2 %collective-permute-start.56 = (bf16[2,1056,256]{2,1,0:T(8,128)(2,1)}, bf16[2,1056,256]{2,1,0:T(8,128)(2,1)S(1)}, u32[]{:S(2)}, u32[]{:S(2)}) collective-permute-start(bf16[2,1056,256]{2,1,0:T(8,128)(2,1)} %get-tuple-element.194), channel_id=1, source_target_pairs={{0,8},{4,12},{8,0},{12,4},{1,9},{5,13},{9,1},{13,5},{2,10},{6,14},... | collective-permute-start | bytes 3244040 | tf_op jit(solution)/shard_map/ppermute | solution.py:879
  532.6 32.0 %collective-permute-start.53 = (bf16[512,1024]{1,0:T(8,128)(2,1)S(1)}, bf16[512,1024]{1,0:T(8,128)(2,1)S(1)}, u32[]{:S(2)}, u32[]{:S(2)}) collective-permute-start(bf16[512,1024]{1,0:T(8,128)(2,1)S(1)} %fusion.34), channel_id=1, source_target_pairs={{0,1},{1,0},{2,3},{3,2},{4,5},{5,4},{6,7},{7,6},{8,9},{9,8},{10,11... | collective-permute-start | bytes 3145736 | tf_op jit(solution)/shard_map/ppermute | solution.py:886
  558.5 84.3 %collective-permute-start.57 = (bf16[1056,256]{1,0:T(8,128)(2,1)}, bf16[1056,256]{1,0:T(8,128)(2,1)}, u32[]{:S(2)}, u32[]{:S(2)}) collective-permute-start(bf16[1056,256]{1,0:T(8,128)(2,1)} %get-tuple-element.192), channel_id=1, source_target_pairs={{0,4},{4,0},{8,12},{12,8},{1,5},{5,1},{9,13},{13,9},{2,6},{6,2},{1... | collective-permute-start | bytes 1622024 | tf_op jit(solution)/shard_map/ppermute | solution.py:879
  578.0 45.4 %collective-permute-start.59 = (bf16[1056,256]{1,0:T(8,128)(2,1)}, bf16[1056,256]{1,0:T(8,128)(2,1)S(1)}, u32[]{:S(2)}, u32[]{:S(2)}) collective-permute-start(bf16[1056,256]{1,0:T(8,128)(2,1)} %get-tuple-element.191), channel_id=1, source_target_pairs={{0,8},{4,12},{8,0},{12,4},{1,9},{5,13},{9,1},{13,5},{2,10},{6,14},... | collective-permute-start | bytes 1622024 | tf_op jit(solution)/shard_map/ppermute | solution.py:879
  578.9 48.5 %collective-permute-start.65 = (bf16[2,128,768]{2,1,0:T(8,128)(2,1)}, bf16[2,128,768]{2,1,0:T(8,128)(2,1)S(1)}, u32[]{:S(2)}, u32[]{:S(2)}) collective-permute-start(bf16[2,128,768]{2,1,0:T(8,128)(2,1)} %get-tuple-element.212), channel_id=1, source_target_pairs={{0,4},{4,0},{8,12},{12,8},{1,5},{5,1},{9,13},{13,9},{2,6},{6,2},{1... | collective-permute-start | bytes 1179656 | tf_op jit(solution)/shard_map/ppermute | solution.py:879
  583.1 40.8 %collective-permute-start.67 = (bf16[1056,256]{1,0:T(8,128)(2,1)}, bf16[1056,256]{1,0:T(8,128)(2,1)S(1)}, u32[]{:S(2)}, u32[]{:S(2)}) collective-permute-start(bf16[1056,256]{1,0:T(8,128)(2,1)} %fusion.32), channel_id=1, source_target_pairs={{0,1},{1,3},{3,2},{2,0},{4,5},{5,7},{7,6},{6,4},{8,9},{9,11},{11,1... | collective-permute-start | bytes 1622024 | tf_op jit(solution)/shard_map/ppermute | solution.py:876
  618.6 25.2 %collective-permute-start.55 = (bf16[1024,1024]{1,0:T(8,128)(2,1)}, bf16[1024,1024]{1,0:T(8,128)(2,1)}, u32[]{:S(2)}, u32[]{:S(2)}) collective-permute-start(bf16[1024,1024]{1,0:T(8,128)(2,1)} %get-tuple-element.121.refs_2_), channel_id=1, source_target_pairs={{0,16},{16,0},{1,17},{17,1},{2,18},{18,2},{3,19},{19,3},{4,20},{20... | collective-permute-start | bytes 6291464 | tf_op jit(solution)/shard_map/ppermute | solution.py:872
  635.4 45.9 %collective-permute-start.69 = (bf16[1056,256]{1,0:T(8,128)(2,1)}, bf16[1056,256]{1,0:T(8,128)(2,1)S(1)}, u32[]{:S(2)}, u32[]{:S(2)}) collective-permute-start(bf16[1056,256]{1,0:T(8,128)(2,1)} %fusion.30), channel_id=1, source_target_pairs={{0,1},{1,3},{3,2},{2,0},{4,5},{5,7},{7,6},{6,4},{8,9},{9,11},{11,1... | collective-permute-start | bytes 1622024 | tf_op jit(solution)/shard_map/ppermute | solution.py:876
  639.7 19.6 %collective-permute-start.70 = (bf16[128,768]{1,0:T(8,128)(2,1)}, bf16[128,768]{1,0:T(8,128)(2,1)S(1)}, u32[]{:S(2)}, u32[]{:S(2)}) collective-permute-start(bf16[128,768]{1,0:T(8,128)(2,1)} %get-tuple-element.210), channel_id=1, source_target_pairs={{0,4},{4,0},{8,12},{12,8},{1,5},{5,1},{9,13},{13,9},{2,6},{6,2},{1... | collective-permute-start | bytes 589832 | tf_op jit(solution)/shard_map/ppermute | solution.py:879
  642.8 26.2 %collective-permute-start.73 = (bf16[2,1056,256]{2,1,0:T(8,128)(2,1)}, bf16[2,1056,256]{2,1,0:T(8,128)(2,1)}, u32[]{:S(2)}, u32[]{:S(2)}) collective-permute-start(bf16[2,1056,256]{2,1,0:T(8,128)(2,1)} %get-tuple-element.190), channel_id=1, source_target_pairs={{0,4},{4,0},{8,12},{12,8},{1,5},{5,1},{9,13},{13,9},{2,6},{6,2},{1... | collective-permute-start | bytes 3244040 | tf_op jit(solution)/shard_map/ppermute | solution.py:879
  643.8 29.9 %collective-permute-start.74 = (bf16[2,1056,256]{2,1,0:T(8,128)(2,1)}, bf16[2,1056,256]{2,1,0:T(8,128)(2,1)}, u32[]{:S(2)}, u32[]{:S(2)}) collective-permute-start(bf16[2,1056,256]{2,1,0:T(8,128)(2,1)} %get-tuple-element.189), channel_id=1, source_target_pairs={{0,8},{4,12},{8,0},{12,4},{1,9},{5,13},{9,1},{13,5},{2,10},{6,14},... | collective-permute-start | bytes 3244040 | tf_op jit(solution)/shard_map/ppermute | solution.py:879
  659.3 20.2 %collective-permute-start.72 = (bf16[128,256]{1,0:T(8,128)(2,1)}, bf16[128,256]{1,0:T(8,128)(2,1)S(1)}, u32[]{:S(2)}, u32[]{:S(2)}) collective-permute-start(bf16[128,256]{1,0:T(8,128)(2,1)} %fusion.73), channel_id=1, source_target_pairs={{0,1},{1,3},{3,2},{2,0},{4,5},{5,7},{7,6},{6,4},{8,9},{9,11},{11,1... | collective-permute-start | bytes 196616 | tf_op jit(solution)/shard_map/ppermute | solution.py:876
  660.9 59.1 %collective-permute-start.89 = (bf16[2,1056,256]{2,1,0:T(8,128)(2,1)}, bf16[2,1056,256]{2,1,0:T(8,128)(2,1)S(1)}, u32[]{:S(2)}, u32[]{:S(2)}) collective-permute-start(bf16[2,1056,256]{2,1,0:T(8,128)(2,1)} %get-tuple-element.185), channel_id=1, source_target_pairs={{0,8},{4,12},{8,0},{12,4},{1,9},{5,13},{9,1},{13,5},{2,10},{6,14},... | collective-permute-start | bytes 3244040 | tf_op jit(solution)/shard_map/ppermute | solution.py:879
  669.0 51.0 %collective-permute-start.91 = (bf16[2,1056,256]{2,1,0:T(8,128)(2,1)}, bf16[2,1056,256]{2,1,0:T(8,128)(2,1)}, u32[]{:S(2)}, u32[]{:S(2)}) collective-permute-start(bf16[2,1056,256]{2,1,0:T(8,128)(2,1)} %get-tuple-element.186), channel_id=1, source_target_pairs={{0,4},{4,0},{8,12},{12,8},{1,5},{5,1},{9,13},{13,9},{2,6},{6,2},{1... | collective-permute-start | bytes 3244040 | tf_op jit(solution)/shard_map/ppermute | solution.py:879
  679.5 43.9 %collective-permute-start.75 = (bf16[1056,256]{1,0:T(8,128)(2,1)}, bf16[1056,256]{1,0:T(8,128)(2,1)}, u32[]{:S(2)}, u32[]{:S(2)}) collective-permute-start(bf16[1056,256]{1,0:T(8,128)(2,1)} %get-tuple-element.188), channel_id=1, source_target_pairs={{0,4},{4,0},{8,12},{12,8},{1,5},{5,1},{9,13},{13,9},{2,6},{6,2},{1... | collective-permute-start | bytes 1622024 | tf_op jit(solution)/shard_map/ppermute | solution.py:879
  681.3 43.1 %collective-permute-start.76 = (bf16[1056,256]{1,0:T(8,128)(2,1)}, bf16[1056,256]{1,0:T(8,128)(2,1)}, u32[]{:S(2)}, u32[]{:S(2)}) collective-permute-start(bf16[1056,256]{1,0:T(8,128)(2,1)} %get-tuple-element.187), channel_id=1, source_target_pairs={{0,8},{4,12},{8,0},{12,4},{1,9},{5,13},{9,1},{13,5},{2,10},{6,14},... | collective-permute-start | bytes 1622024 | tf_op jit(solution)/shard_map/ppermute | solution.py:879
  684.9 31.5 %collective-permute-start.77 = (bf16[128,256]{1,0:T(8,128)(2,1)S(1)}, bf16[128,256]{1,0:T(8,128)(2,1)S(1)}, u32[]{:S(2)}, u32[]{:S(2)}) collective-permute-start(bf16[128,256]{1,0:T(8,128)(2,1)S(1)} %fusion.72), channel_id=1, source_target_pairs={{0,1},{1,3},{3,2},{2,0},{4,5},{5,7},{7,6},{6,4},{8,9},{9,11},{11,1... | collective-permute-start | bytes 196616 | tf_op jit(solution)/shard_map/ppermute | solution.py:876
  716.4 57.4 %collective-permute-start.87 = (bf16[256,384]{1,0:T(8,128)(2,1)}, bf16[256,384]{1,0:T(8,128)(2,1)}, u32[]{:S(2)}, u32[]{:S(2)}) collective-permute-start(bf16[256,384]{1,0:T(8,128)(2,1)} %fusion.55), channel_id=1, source_target_pairs={{0,2},{1,3},{2,0},{3,1},{4,6},{5,7},{6,4},{7,5},{8,10},{9,11},{10,... | collective-permute-start | bytes 589832 | tf_op jit(solution)/shard_map/ppermute | solution.py:882
  720.0 28.2 %collective-permute-start.103 = (bf16[128,256]{1,0:T(8,128)(2,1)}, bf16[128,256]{1,0:T(8,128)(2,1)}, u32[]{:S(2)}, u32[]{:S(2)}) collective-permute-start(bf16[128,256]{1,0:T(8,128)(2,1)} %fusion.61), channel_id=1, source_target_pairs={{0,1},{1,3},{3,2},{2,0},{4,5},{5,7},{7,6},{6,4},{8,9},{9,11},{11,1... | collective-permute-start | bytes 196616 | tf_op jit(solution)/shard_map/ppermute | solution.py:876
  736.9 18.8 %collective-permute-start.82 = (bf16[2,128,768]{2,1,0:T(8,128)(2,1)S(1)}, bf16[2,128,768]{2,1,0:T(8,128)(2,1)S(1)}, u32[]{:S(2)}, u32[]{:S(2)}) collective-permute-start(bf16[2,128,768]{2,1,0:T(8,128)(2,1)S(1)} %get-tuple-element.205), channel_id=1, source_target_pairs={{0,4},{4,0},{8,12},{12,8},{1,5},{5,1},{9,13},{13,9},{2,6},{6,2},{1... | collective-permute-start | bytes 1179656 | tf_op jit(solution)/shard_map/ppermute | solution.py:879
  737.9 19.6 %collective-permute-start.84 = (bf16[2,128,768]{2,1,0:T(8,128)(2,1)S(1)}, bf16[2,128,768]{2,1,0:T(8,128)(2,1)S(1)}, u32[]{:S(2)}, u32[]{:S(2)}) collective-permute-start(bf16[2,128,768]{2,1,0:T(8,128)(2,1)S(1)} %get-tuple-element.206), channel_id=1, source_target_pairs={{0,8},{4,12},{8,0},{12,4},{1,9},{5,13},{9,1},{13,5},{2,10},{6,14},... | collective-permute-start | bytes 1179656 | tf_op jit(solution)/shard_map/ppermute | solution.py:879
  752.0 35.1 %collective-permute-start.92 = (bf16[1056,256]{1,0:T(8,128)(2,1)S(1)}, bf16[1056,256]{1,0:T(8,128)(2,1)S(1)}, u32[]{:S(2)}, u32[]{:S(2)}) collective-permute-start(bf16[1056,256]{1,0:T(8,128)(2,1)S(1)} %copy-done.34), channel_id=1, source_target_pairs={{0,8},{4,12},{8,0},{12,4},{1,9},{5,13},{9,1},{13,5},{2,10},{6,14},... | collective-permute-start | bytes 1622024 | tf_op jit(solution)/shard_map/ppermute | solution.py:879
  766.1 37.4 %collective-permute-start.90 = (bf16[1056,256]{1,0:T(8,128)(2,1)S(1)}, bf16[1056,256]{1,0:T(8,128)(2,1)S(1)}, u32[]{:S(2)}, u32[]{:S(2)}) collective-permute-start(bf16[1056,256]{1,0:T(8,128)(2,1)S(1)} %get-tuple-element.183), channel_id=1, source_target_pairs={{0,4},{4,0},{8,12},{12,8},{1,5},{5,1},{9,13},{13,9},{2,6},{6,2},{1... | collective-permute-start | bytes 1622024 | tf_op jit(solution)/shard_map/ppermute | solution.py:879
  770.8 29.7 %collective-permute-start.78 = (bf16[2,512,1024]{2,1,0:T(8,128)(2,1)S(1)}, bf16[2,512,1024]{2,1,0:T(8,128)(2,1)S(1)}, u32[]{:S(2)}, u32[]{:S(2)}) collective-permute-start(bf16[2,512,1024]{2,1,0:T(8,128)(2,1)S(1)} %copy-done.80), channel_id=1, source_target_pairs={{0,16},{16,0},{1,17},{17,1},{2,18},{18,2},{3,19},{19,3},{4,20},{20... | collective-permute-start | bytes 6291464 | tf_op jit(solution)/shard_map/ppermute | solution.py:872
  800.9 36.2 %collective-permute-start.79 = (bf16[512,1024]{1,0:T(8,128)(2,1)S(1)}, bf16[512,1024]{1,0:T(8,128)(2,1)S(1)}, u32[]{:S(2)}, u32[]{:S(2)}) collective-permute-start(bf16[512,1024]{1,0:T(8,128)(2,1)S(1)} %fusion.35), channel_id=1, source_target_pairs={{0,1},{1,0},{2,3},{3,2},{4,5},{5,4},{6,7},{7,6},{8,9},{9,8},{10,11... | collective-permute-start | bytes 3145736 | tf_op jit(solution)/shard_map/ppermute | solution.py:886
  816.3 21.6 %collective-permute-start.104 = (bf16[1184,256]{1,0:T(8,128)(2,1)S(1)}, bf16[1184,256]{1,0:T(8,128)(2,1)S(1)}, u32[]{:S(2)}, u32[]{:S(2)}) collective-permute-start(bf16[1184,256]{1,0:T(8,128)(2,1)S(1)} %broadcast_select_fusion.10), channel_id=1, source_target_pairs={{0,16},{16,0},{1,17},{17,1},{2,18},{18,2},{3,19},{19,3},{4,20},{20... | collective-permute-start | bytes 1818632 | tf_op jit(solution)/shard_map/ppermute | solution.py:872
  860.5 24.0 %collective-permute-start.81 = (bf16[512,512]{1,0:T(8,128)(2,1)S(1)}, bf16[512,512]{1,0:T(8,128)(2,1)S(1)}, u32[]{:S(2)}, u32[]{:S(2)}) collective-permute-start(bf16[512,512]{1,0:T(8,128)(2,1)S(1)} %fusion.44), channel_id=1, source_target_pairs={{0,2},{1,3},{2,0},{3,1},{4,6},{5,7},{6,4},{7,5},{8,10},{9,11},{10,... | collective-permute-start | bytes 1572872 | tf_op jit(solution)/shard_map/ppermute | solution.py:882
  (144 other events, 1686.6 us)

commit v3 on v2

--- a/solution.py
+++ b/solution.py
@@ -875,6 +875,10 @@
         order = self.order
         return lax.ppermute(x, "tensor", [(order[i], order[(i + 1) % self.T]) for i in range(self.T)])
 
+    def back(self, x, k):
+        order = self.order
+        return lax.ppermute(x, "tensor", [(order[i], order[(i - k) % self.T]) for i in range(self.T)])
+
     def along(self, x, bit):
         return lax.ppermute(x, "dp", [(i, i ^ bit) for i in range(self.DP)])
 
@@ -885,14 +889,16 @@
         pairs = [(z, z // self.G * self.G + (z + k) % self.G) for z in range(self.T)]
         return lax.ppermute(x, "tensor", pairs)
 
-    def swap_blocks(self, x):
+    def swap_blocks(self, x, *after):
         pairs = []
         for s in range(2):
             z0 = s * self.G
             for z in range(z0, z0 + self.G):
                 pairs.append((s * self.T + z, s * self.T + (z + self.G) % self.T))
-        give = lax.dynamic_index_in_dim(x, 1 - self.r, 0, keepdims=False)
-        got = lax.ppermute(give, ("section", "tensor"), pairs)
+        give = hold(lax.dynamic_index_in_dim(x, 1 - self.r, 0, keepdims=False), *after)
+        return lax.ppermute(give, ("section", "tensor"), pairs)
+
+    def swap_end(self, x, got):
         got = jnp.where(self.home, self.sibling(got), got)
         mine = (jnp.arange(2) == self.r)[:, None, None]
         return jnp.where(mine, x, got[None])
@@ -918,12 +924,13 @@
 
     def combine(self, near, far):
         got = self.sibling(far)
-        terms = [near[0], got[0]]
+        terms, sent = [near[0], got[0]], []
         for k in range(1, self.G):
-            terms.append(self.shift(add_low(near[k], got[k]), k))
+            sent.append(add_low(near[k], got[k]))
+            terms.append(self.shift(sent[-1], k))
         mine = add_low(*terms)
         both = (jnp.arange(2) == self.s)[:, None, None]
-        return jnp.where(both, mine[None], self.sibling(mine)[None])
+        return jnp.where(both, mine[None], self.sibling(mine)[None]), sent[0], mine
 
     def table(self):
         T, G, DP, order = self.T, self.G, self.DP, self.order
@@ -948,78 +955,80 @@
         return lax.dynamic_index_in_dim(jnp.asarray(table.reshape(-1, PLACES)), index, 0, keepdims=False)
 
 
-def gather_weights(links, output_weight, gate_weight, up_weight, down_weight, after):
-    s, d = links.s, links.d
-    width = output_weight.shape[1]
-
-    def half(which):
-        def cut(x, dim):
-            size = x.shape[dim] // 2
-            return lax.dynamic_slice_in_dim(x, which * size, size, dim)
-
-        return jnp.concatenate(
-            [cut(output_weight, 0), cut(gate_weight, 1).T, cut(up_weight, 1).T, cut(down_weight, 0)]
-        )
-
-    mine = half(s)
-    got = links.sibling(half(1 - s))
-    weights, rings = [[], []], [[], []]
-    for layer in range(2):
-        own = jnp.where(s == layer, mine, got)
-        weights[layer].append(Weights([own]))
-        if not links.planar:
-            for _ in range(1, links.T):
-                own = links.ring(own)
-                weights[layer].append(Weights([own]))
-            continue
-        size = width // 4
-        current = lax.dynamic_slice_in_dim(own, d * size, size, 1)
-        current = hold(current, *after)
-        steps = []
-        for _ in range(1, links.T):
-            current = links.ring(current)
-            steps.append(current)
-        rings[layer] = steps
-        rows = current.shape[0]
-        for batch in ([0], [1], [2]) if layer == 0 else ([0], [1, 2]):
-            part = steps[batch[0]] if len(batch) == 1 else jnp.concatenate([steps[n] for n in batch])
-            pieces = [part] + [links.along(part, bit) for bit in (1, 2, 3)]
-            for n in range(len(batch)):
-                weights[layer].append(Weights(pieces, n * rows))
-    return weights, rings
-
-
-def gather_projection(links, query_weight, key_weight, value_weight):
-    s, d = links.s, links.d
-    depth, cols = query_weight.shape
-
-    def half(which):
-        return jnp.concatenate(
-            [lax.dynamic_slice_in_dim(w, which * (cols // 2), cols // 2, 1) for w in (query_weight, key_weight, value_weight)],
-            axis=1,
-        )
-
-    mine = half(s)
-    got = links.sibling(half(1 - s))
-    result, early = [], []
-    for layer in range(2):
-        own = jnp.where(s == layer, mine, got)
+class Gather:
+    def __init__(self, links, output_weight, gate_weight, up_weight, down_weight):
+        s, d = links.s, links.d
+
+        def half(which):
+            def cut(x, dim):
+                size = x.shape[dim] // 2
+                return lax.dynamic_slice_in_dim(x, which * size, size, dim)
+
+            return jnp.concatenate(
+                [cut(output_weight, 0), cut(gate_weight, 1).T, cut(up_weight, 1).T, cut(down_weight, 0)]
+            )
+
+        mine = half(s)
+        got = links.sibling(half(1 - s))
+        self.links = links
+        whole = [jnp.where(s == layer, mine, got) for layer in range(2)]
+        self.weights = [[Weights([item])] for item in whole]
         if links.planar:
-            other = links.across(lax.dynamic_slice_in_dim(own, d * (depth // 4), depth // 4, 0))
-            early.append(other)
+            size = output_weight.shape[1] // 4
+            whole = [lax.dynamic_slice_in_dim(item, d * size, size, 1) for item in whole]
+        self.current = whole
+
+    def step(self, layer, *after):
+        ring = self.links.ring(hold(self.current[layer], *after))
+        self.current[layer] = ring
+        plane = [self.links.along(ring, bit) for bit in (1, 2, 3)] if self.links.planar else []
+        self.weights[layer].append(Weights([ring] + plane))
+        return [ring], plane
+
+    def two_steps(self, layer):
+        once = self.links.ring(self.current[layer])
+        self.current[layer] = self.links.ring(once)
+        joined = jnp.concatenate([once, self.current[layer]])
+        pieces = [joined] + [self.links.along(joined, bit) for bit in (1, 2, 3)]
+        self.weights[layer] += [Weights(pieces), Weights(pieces, once.shape[0])]
+        return [once, self.current[layer]]
+
+
+class Projection:
+    def __init__(self, links, query_weight, key_weight, value_weight):
+        s = links.s
+        self.depth, self.cols = query_weight.shape
+        side = self.cols // 2
+
+        def half(which):
+            return jnp.concatenate(
+                [lax.dynamic_slice_in_dim(w, which * side, side, 1) for w in (query_weight, key_weight, value_weight)],
+                axis=1,
+            )
+
+        mine = half(s)
+        got = links.sibling(half(1 - s))
+        self.links = links
+        self.own = [jnp.where(s == layer, mine, got) for layer in range(2)]
+
+    def layer(self, layer, *after):
+        self.early = []
+        links, own, depth, side = self.links, self.own[layer], self.depth, self.cols // 2
+        if links.planar:
+            size = depth // 4
+            other = links.across(hold(lax.dynamic_slice_in_dim(own, links.d * size, size, 0), *after))
+            self.early.append(other)
             for bit in (1, 2):
                 far = links.along(other, bit)
                 other = jnp.where(
-                    d & bit == 0, jnp.concatenate([other, far]), jnp.concatenate([far, other])
+                    links.d & bit == 0, jnp.concatenate([other, far]), jnp.concatenate([far, other])
                 )
         else:
             other = links.across(own)
-        if cols // 2 % 128:
-            both = jnp.stack([own.reshape(depth, 3, cols // 2), other.reshape(depth, 3, cols // 2)], axis=2)
-            result.append(both.reshape(depth, 3 * cols))
-        else:
-            result.append(jnp.concatenate([own, other], axis=1))
-    return result, early
+        if side % 128:
+            both = jnp.stack([own.reshape(depth, 3, side), other.reshape(depth, 3, side)], axis=2)
+            return both.reshape(depth, 6 * side)
+        return jnp.concatenate([own, other], axis=1)
 
 
 class PlaneSum:
@@ -1049,42 +1058,35 @@
         return add_low(*terms, *more)
 
 
-class RingSum:
-    def __init__(self, links, part_of):
-        self.links, self.part_of, self.count, self.passed = links, part_of, 0, []
+class StarSum:
+    def __init__(self, links, term_of, order):
+        self.links, self.term_of, self.order, self.got = links, term_of, order, []
 
     def step(self, *after):
-        self.total = self.part_of(self.count, self.passed, after)
-        self.count += 1
-        if self.count < self.links.T:
-            self.passed = [self.links.ring(self.total)]
-        return [self.passed[0] if self.count < self.links.T else self.total]
+        n = len(self.got)
+        if n < len(self.order) - 1:
+            self.got.append(self.links.back(self.term_of(n, [], after), self.order[n]))
+            return self.got[-1:]
+        self.total = self.term_of(n, self.got, after)
+        return [self.total]
 
 
 class LayerSums:
     def __init__(self, links, parts, out_part, rows, out_rows, order):
         first, second = PlaneSum(links, parts[0]), PlaneSum(links, parts[1])
         out = PlaneSum(links, out_part)
-        self.links, self.first, self.second, self.out = links, first, second, out
-        self.mlp_ring = RingSum(
-            links, lambda n, more, after: (first, second)[n // 2].total(n % 2 * rows, rows, more, after)
+        self.first, self.second, self.out = first, second, out
+        self.mlp = StarSum(
+            links, lambda n, more, after: (first, second)[n // 2].total(n % 2 * rows, rows, more, after), order
         )
-        self.out_ring = RingSum(
-            links, lambda n, more, after: out.total(order[n] * out_rows, out_rows, more, after)
+        self.star = StarSum(
+            links, lambda n, more, after: out.total(order[n] * out_rows, out_rows, more, after), order
         )
 
-    def stage(self, number, *after):
-        if number == 0:
-            return self.second.finish(*after) + self.out.begin(*after) + self.mlp_ring.step(*after)
-        if number == 1:
-            return self.out.finish(*after) + self.proj.begin(*after) + self.mlp_ring.step(*after)
-        if number == 2:
-            return self.mlp_ring.step(*after) + self.proj.finish(*after) + self.out_ring.step(*after)
-        if number == 3:
-            size = self.proj.part.shape[1] // 2
-            self.proj_total = jnp.concatenate([self.proj.total(n * size, size, [], after) for n in range(2)])
-            return self.mlp_ring.step(*after) + self.out_ring.step(*after) + [self.proj_total]
-        return self.out_ring.step(*after)
+    def proj_total(self, *after):
+        size = self.proj.part.shape[1] // 2
+        self.proj_sum = jnp.concatenate([self.proj.total(n * size, size, [], after) for n in range(2)])
+        return [self.proj_sum]
 
 
 def both_halves(links, per_layer):
@@ -1095,15 +1097,9 @@
 
 def sum_everywhere(links, x):
     if links.planar:
-        x = x + links.along(x, 1)
-        x = x + links.along(x, 2)
-    else:
-        x = lax.psum(x, "dp")
-    step = 1
-    while step < links.T:
-        x = x + lax.ppermute(x, "tensor", [(z, z ^ step) for z in range(links.T)])
-        step *= 2
-    return x
+        x = sum([x] + [links.along(x, bit) for bit in (1, 2, 3)])
+        return sum([x] + [links.back(x, k) for k in (1, 2, 3)])
+    return lax.psum(x, ("dp", "tensor"))
 
 
 def norm_low(x, gain):
@@ -1154,47 +1150,63 @@
     gains = [
         jnp.where(s == layer, own_gains, other_gains) for layer in range(2)
     ]
-    w_proj, early = gather_projection(links, query_weight[0], key_weight[0], value_weight[0])
     def flat(item):
         return item.reshape(2 * length, width)
 
     def blocked(item):
         return item.reshape(2, length, width)
 
-    x = flat(links.swap_blocks(tokens))
-    weights, rings = gather_weights(links, output_weight[0], gate_weight[0], up_weight[0], down_weight[0], [x] + early[:1])
     planar = links.planar
     order = list(range(1, T)) + [0]
     batches = [order[: T // 2], order[T // 2 :]]
     out_rows = cols // 2
     rows = 3 * hidden
 
+    x = flat(links.swap_end(tokens, links.swap_blocks(tokens)))
     a = norm_low(x.astype(F32), gains[0][0:1])
+    gather = Gather(links, output_weight[0], gate_weight[0], up_weight[0], down_weight[0])
+    weights = gather.weights
+    projection = Projection(links, query_weight[0], key_weight[0], value_weight[0])
+    w_proj = [projection.layer(0), None]
+    if planar:
+        early = projection.early
+        w_proj[1] = projection.layer(1)
+        first = gather.step(0, x, *early)
+        rings = first[0] + gather.step(0)[0] + gather.step(0)[0]
+        begun = gather.step(1, x, *early)
+        later_rings = gather.two_steps(1)
     kept = []
     first_values = None
     for layer in range(2):
         gain_mlp = gains[layer][1:2]
         a_blocks = links.spread(blocked(a))
         deps = [[], [], [], []]
-        if planar and layer == 0:
-            deps = [[], rings[0][:2] + w_proj[1:], rings[0][2:] + weights[0][1].arrays[1:], rings[1][:1]]
-        elif planar:
-            deps = [rings[1][1:] + weights[1][1].arrays[1:], [], [], []]
+        if not planar:
+            for _ in range(1, T):
+                gather.step(layer)
+            w_proj[1] = projection.layer(1)
+        elif layer == 0:
+            deps[1] = rings[:2] + w_proj[1:]
+            deps[2] = rings[2:] + first[1]
+        else:
+            deps[0] = later_rings + begun[1]
         q, k, v = project(meta, a_blocks, w_proj[layer], tables, (ext_q, ext_k), first_values, deps[0])
         o_rel, q = attend(meta, q, k, v, T, deps[1])
         o_blocks = links.exchange(o_rel, length)
         p = output_forward(meta, o_blocks, weights[layer], width, deps[2])
         if layer:
-            dy = flat(links.swap_blocks(cotangent))
+            dy = flat(links.swap_end(cotangent, links.swap_blocks(cotangent)))
             deps[3] = [dy]
         y, h, b, *saved = mlp_forward(
             meta, x, p, links.sibling(p), gain_mlp, weights[layer], batches, hidden, out_rows, deps[3]
         )
         kept.append((x, a_blocks, q, k, v, o_rel, o_blocks, h, b, saved))
+        if planar and layer == 0:
+            y = hold(y, *begun[0])
         x = (h + (y.astype(F32) + links.sibling(y).astype(F32))).astype(BF)
         if layer == 0:
             a, first_values = norm_low(x.astype(F32), gains[1][0:1]), v
-    activations = links.swap_blocks(blocked(x))
+    last = x
 
     first_grad = None
     mlp_sums, out_sums, proj_sums, gain_sums, sums = [None] * 2, [None] * 2, [None] * 2, [None] * 2, [None] * 2
@@ -1207,36 +1219,57 @@
         *parts, db = mlp_backward(meta, dy_low, b, saved, weights[layer], batches, out_rows, DP, [])
         if before:
             due["middle"] = passing
-            due["attend"] = before.stage(2, parts[0])
+            due["attend"] = before.mlp.step(parts[0]) + before.star.step() + before.star.step() + before.star.step()
+            due["attend"].append(activations)
         dh, mlp_gain_grad, do_rel, out_part = middle(
             meta, dy, db, links.sibling(db), h, gain_mlp, o_blocks, weights[layer], DP, due["middle"]
         )
-        do_blocks = links.exchange(do_rel, length)
         if planar:
             mine = sums[layer] = LayerSums(links, parts, out_part, rows, out_rows, order)
             begun = mine.first.begin() + mine.second.begin()
+            if before:
+                do_rel = hold(do_rel, *begun[:2])
+        do_blocks = links.exchange(do_rel, length)
+        if planar:
             due["attend"] = due["attend"] + begun[:2]
-            due["project"] = mine.first.finish(do_rel)
+            due["project"] = begun[2:] + mine.first.finish(do_rel)
             if before:
-                due["project"] = due["project"] + before.stage(3, do_rel)
-            else:
-                due["attend"] = due["attend"] + [activations]
+                begun = begun + mine.out.begin()
+                due["project"] = due["project"] + before.mlp.step(do_rel) + before.star.step(do_rel)
+                due["project"] = due["project"] + before.proj_total(do_rel)
+        if layer:
+            sent = links.swap_blocks(blocked(last), parts[0])
+            due["attend"] = due["attend"] + [sent]
         back = attend_back(meta, q, k, v, o_rel, do_blocks, tables, first_grad, due["attend"])
-        if planar:
-            passing = mine.stage(0, back[0])
-            if before:
-                before.stage(4, back[0])
+        if before:
+            mine.second.finish(back[0])
+            mine.out.finish(back[0])
+            mine.mlp.step(back[0])
+            mine.mlp.step(back[0])
         if layer == 1:
             first_grad = back[3]
         near, far, dw = project_back(meta, a_blocks, back[:3], w_proj[layer], DP, due["project"])
+        da, sending, summed = links.combine(near, far)
+        da = flat(da).astype(F32)
+        part, attn_gain_grad = norm_back(x.astype(F32), gain_attn, da)
+        gain_sums[layer] = jnp.concatenate([attn_gain_grad, mlp_gain_grad])
+        dy = dh + part
         if planar:
             mine.proj = PlaneSum(links, dw)
-            passing = passing + mine.stage(1, near)
             if before:
-                before.stage(4)
-                for number in (2, 3, 4, 4):
-                    mine.stage(number)
+                for _ in range(3):
+                    mine.star.step(sending)
+                mine.proj.begin(sending)
+                mine.mlp.step(summed)
+                mine.proj.finish(summed)
+            else:
+                activations = links.swap_end(blocked(last), hold(sent, near))
+                passing = mine.second.finish(sending) + mine.out.begin(sending) + mine.proj.begin(sending)
+                passing = passing + mine.mlp.step(sending) + mine.mlp.step(sending)
+                passing = passing + mine.out.finish(summed) + mine.proj.finish(summed)
         else:
+            if layer:
+                activations = links.swap_end(blocked(last), sent)
             running = None
             for part in parts:
                 for n in range(T // 2):
@@ -1249,20 +1282,18 @@
                 running = term if running is None else add_low(term, links.ring(running))
             out_sums[layer] = lax.psum_scatter(running, "dp", scatter_dimension=0, tiled=True)[0]
             proj_sums[layer] = lax.psum_scatter(dw, "dp", scatter_dimension=0, tiled=True)[0]
-        da = flat(links.combine(near, far)).astype(F32)
-        part, attn_gain_grad = norm_back(x.astype(F32), gain_attn, da)
-        gain_sums[layer] = jnp.concatenate([attn_gain_grad, mlp_gain_grad])
-        dy = dh + part
+    half_width = width // 2
+    mine = lax.dynamic_slice_in_dim(blocked(dy), s * half_width, half_width, 2)
+    give = lax.dynamic_index_in_dim(mine, 1 - links.r, 0, keepdims=False).astype(BF)
+    got = links.across(give)
+    input_grad = jnp.where((jnp.arange(2) == links.r)[:, None, None], mine, got.astype(F32)[None])
     if planar:
-        mlp_sums = [item.mlp_ring.total for item in sums]
-        out_sums = [item.out_ring.total for item in sums]
-        proj_sums = [item.proj_total for item in sums]
-    half_width = width // 2
-    mine = blocked(dy)
-    mine = lax.dynamic_slice_in_dim(mine, s * half_width, half_width, 2)
-    give = lax.dynamic_index_in_dim(mine, 1 - links.r, 0, keepdims=False).astype(BF)
-    input_grad = jnp.where((jnp.arange(2) == links.r)[:, None, None], mine, links.across(give).astype(F32)[None])
-
+        sums[0].star.step(got)
+        sums[0].mlp.step(got)
+        sums[0].proj_total(got)
+        mlp_sums = [item.mlp.total for item in sums]
+        out_sums = [item.star.total for item in sums]
+        proj_sums = [item.proj_sum for item in sums]
     halves = both_halves(links, [jnp.concatenate([mlp_sums[n], out_sums[n]]) for n in range(2)])
     joined = []
     for item in proj_sums:

time: 897 us -> 882 us (0.983)
  other arithmetic: 97 us -> 85.5 us
    ppermute x18 -> x6, waiting for transfers between devices: 64.1 us -> 19 us  [ring(): lax.ppermute(x, 'tensor', [(order[i], order[(i + 1) % self.T]) for i in r...]
    ppermute x53 -> x54, waiting for transfers between devices: 117 us -> 73.9 us  [along(): return lax.ppermute(x, 'dp', [(i, i ^ bit) for i in range(self.DP)])]
    ppermute x5 -> x18, waiting for transfers between devices: 23 us -> 60.5 us  [the longest x15 56.1 us: back(): lax.ppermute(x, 'tensor', [(order[i], order[(i - k) % self.T]) for i in r...]
    ppermute x8, waiting for transfers between devices: 99.6 us -> 131 us  [shift(): return lax.ppermute(x, 'tensor', pairs)]
    ppermute x18 -> x6, starting transfers between devices: 23.4 us -> 6.3 us  [ring(): lax.ppermute(x, 'tensor', [(order[i], order[(i + 1) % self.T]) for i in r...]
    ppermute x5 -> x18, starting transfers between devices: 18.5 us -> 34.4 us  [the longest x15 18.3 us: back(): lax.ppermute(x, 'tensor', [(order[i], order[(i - k) % self.T]) for i in r...]
    ppermute x5, waiting for transfers between devices: 28.1 us -> 42.1 us  [across(): lax.ppermute(x, 'tensor', [(z, (z + self.G) % self.T) for z in range(self...]
    ppermute x20, starting transfers between devices: 24.7 us -> 15.2 us  [sibling(): return lax.ppermute(x, 'section', [(0, 1), (1, 0)])]
  transfers between devices with their start and end apart: 109 -> 111, of which waited for: 43 -> 40; matrix products, arithmetic and copies ran while one was open for 13% -> 12% of each run, Pallas kernels for 23% -> 24%
where the time goes in v3:
time: 882 us; the launch traced here: 875 us
  waiting for transfers between devices  342 us (39%)
  Pallas kernels  259 us (29%)
  starting transfers between devices  134 us (15%)
  other arithmetic  85.5 us (10%)
  local copies, waits for them, and re-layouts  46.2 us (5%)
    pallas_call x16, Pallas kernels, call(): pl.pallas_call(body, in_specs=in_specs + [any_spec()] * extra, **rest)  259 us
    ppermute x8, waiting for transfers between devices, shift(): return lax.ppermute(x, 'tensor', pairs)  131 us
    ppermute x54, waiting for transfers between devices, along(): return lax.ppermute(x, 'dp', [(i, i ^ bit) for i in range(self.DP)])  73.9 us
    ppermute x54, starting transfers between devices, along(): return lax.ppermute(x, 'dp', [(i, i ^ bit) for i in range(self.DP)])  60.5 us
    ppermute x15, waiting for transfers between devices, back(): lax.ppermute(x, 'tensor', [(order[i], order[(i - k) % self.T]) for i in r...  56.1 us
    ppermute x5, waiting for transfers between devices, across(): lax.ppermute(x, 'tensor', [(z, (z + self.G) % self.T) for z in range(self...  42.1 us
    convert_element_type x24, other arithmetic, add_low(): return total.astype(BF)  35.3 us
    ppermute x6, waiting for transfers between devices, ring(): lax.ppermute(x, 'tensor', [(order[i], order[(i + 1) % self.T]) for i in r...  19 us
  transfers between devices with their start and end apart: 111, of which 40 were waited for; matrix products, arithmetic and copies ran while one was open for 12% of the time, Pallas kernels for 24%

profile of v3, /device:TPU:0, one launch (start us, length us, event | category | flops | bytes accessed | tf_op | source)
XLA Modules:
  0.0 874.7 jit_solution(549206510609802193)
XLA Ops:
  7.1 6.6 collective-permute-start
  21.0 4.4 collective-permute-done
  25.4 10.7 %collective-permute-start.1 = (bf16[512,1024]{1,0:T(8,128)(2,1)}, bf16[512,1024]{1,0:T(8,128)(2,1)S(1)}, u32[]{:S(2)}, u32[]{:S(2)}) collective-permute-start(bf16[512,1024]{1,0:T(8,128)(2,1)} %collective-permute-done), channel_id=1, source_target_pairs={{0,16},{16,0},{1,17},{17,1},{2,18},{18,2},{3,19},{19,3},{4,20},{20... | collective-permute-start | bytes 3145736 | tf_op jit(solution)/shard_map/ppermute | solution.py:872
  38.5 3.0 collective-permute-start.6
  41.5 13.3 %collective-permute-done.12 = bf16[256,384]{1,0:T(8,128)(2,1)S(1)} collective-permute-done((bf16[256,384]{1,0:T(8,128)(2,1)S(1)}, bf16[256,384]{1,0:T(8,128)(2,1)S(1)}, u32[]{:S(2)}, u32[]{:S(2)}) %collective-permute-start.12) | collective-permute-done | bytes 196640 | tf_op jit(solution)/shard_map/ppermute | solution.py:886
  67.9 3.4 broadcast_select_fusion
  74.6 29.2 %collective-permute-done.3.refs_2_ = bf16[1,512,1024]{2,1,0:T(8,128)(2,1)} collective-permute-done((bf16[1,512,1024]{2,1,0:T(8,128)(2,1)S(1)}, bf16[1,512,1024]{2,1,0:T(8,128)(2,1)}, u32[]{:S(2)}, u32[]{:S(2)}) %collective-permute-start.3) | collective-permute-done | bytes 1048608 | tf_op jit(solution)/shard_map/ppermute | solution.py:890
  114.7 8.1 collective-permute-done.11.refs_5_.refs_8_.refs_10_.refs_12_.refs_13_
  124.0 10.2 %project.2 = (bf16[4,2048,128]{2,1,0:T(8,128)(2,1)}, bf16[4,2048,128]{2,1,0:T(8,128)(2,1)}, bf16[4,2048,128]{2,1,0:T(8,128)(2,1)}) custom-call(s32[64]{0:T(128)} %fusion.75.refs_0_, bf16[2,512,1024]{2,1,0:T(8,128)(2,1)} %copy-done.10, bf16[1,512,1024]{2,1,0:T(8,128)(2,1)} %collective-permute-done.3.refs_2_, ...), custom_call_target="tpu_custom_call" | custom-call | flops 11500000256 | tf_op jit(solution)/shard_map/project/pallas_call | solution.py:71
  134.8 6.8 collective-permute-done.17.refs_6_.refs_18_.refs_8_.refs_10_.refs_11_
  145.1 8.8 %collective-permute-done.19.refs_9_.refs_11_.refs_13_.refs_14_ = bf16[1184,256]{1,0:T(8,128)(2,1)S(1)} collective-permute-done((bf16[1184,256]{1,0:T(8,128)(2,1)S(1)}, bf16[1184,256]{1,0:T(8,128)(2,1)S(1)}, u32[]{:S(2)}, u32[]{:S(2)}) %collective-permute-start.19) | collective-permute-done | bytes 606240 | tf_op jit(solution)/shard_map/ppermute | solution.py:883
  154.8 14.3 %attend.2 = (bf16[4,512,256]{2,1,0:T(8,128)(2,1)}, bf16[4,2048,128]{2,1,0:T(8,128)(2,1)}) custom-call(s32[64]{0:T(128)} %fusion.75.refs_0_, bf16[4,2048,128]{2,1,0:T(8,128)(2,1)} %get-tuple-element.91.refs_1_, bf16[4,2048,128]{2,1,0:T(8,128)(2,1)} %get-tuple-element.92.refs_2_, bf16[4,2048,128]{2,1,0:T(8,128)(2,1)} %get-tuple-element.93.refs_3_.refs_9_, ...), custom_call_target="tpu_custom_call" | custom-call | flops 16675000320 | tf_op jit(solution)/shard_map/attend/pallas_call | solution.py:71
  170.2 2.7 collective-permute-start.15
  172.9 10.6 %collective-permute-done.15 = bf16[1024,256]{1,0:T(8,128)(2,1)S(1)} collective-permute-done((bf16[1024,256]{1,0:T(8,128)(2,1)S(1)}, bf16[1024,256]{1,0:T(8,128)(2,1)S(1)}, u32[]{:S(2)}, u32[]{:S(2)}) %collective-permute-start.15) | collective-permute-done | bytes 524320 | tf_op jit(solution)/shard_map/ppermute | solution.py:890
  183.6 9.7 %collective-permute-done.24.refs_14_.refs_16_.refs_18_.refs_19_ = bf16[1184,256]{1,0:T(8,128)(2,1)} collective-permute-done((bf16[1184,256]{1,0:T(8,128)(2,1)S(1)}, bf16[1184,256]{1,0:T(8,128)(2,1)}, u32[]{:S(2)}, u32[]{:S(2)}) %collective-permute-start.24) | collective-permute-done | bytes 606240 | tf_op jit(solution)/shard_map/ppermute | solution.py:883
  193.2 4.9 output.2.refs_2_
  199.3 2.8 collective-permute-start.27
  203.8 18.4 %mlp.2 = (bf16[1024,1024]{1,0:T(8,128)(2,1)}, f32[1024,1024]{1,0:T(8,128)}, bf16[1024,1024]{1,0:T(8,128)(2,1)}, bf16[1024,704]{1,0:T(8,128)(2,1)}, bf16[1024,704...) custom-call(s32[64]{0:T(128)} %fusion.75.refs_0_, bf16[1024,1024]{1,0:T(8,128)(2,1)} %bitcast.267, ...), custom_call_target="tpu_custom_call" | custom-call | flops 21849999360 | tf_op jit(solution)/shard_map/mlp/pallas_call | solution.py:71
  223.0 3.6 collective-permute-done.28
  226.6 3.9 fusion.13
  234.4 36.4 %collective-permute-done.29.refs_2_ = bf16[1,512,1024]{2,1,0:T(8,128)(2,1)S(1)} collective-permute-done((bf16[1,512,1024]{2,1,0:T(8,128)(2,1)S(1)}, bf16[1,512,1024]{2,1,0:T(8,128)(2,1)S(1)}, u32[]{:S(2)}, u32[]{:S(2)}) %collective-permute-start.29) | collective-permute-done | bytes 1048608 | tf_op jit(solution)/shard_map/ppermute | solution.py:890
  276.9 10.9 %collective-permute-done.32.refs_11_ = bf16[1184,256]{1,0:T(8,128)(2,1)S(1)} collective-permute-done((bf16[1184,256]{1,0:T(8,128)(2,1)S(1)}, bf16[1184,256]{1,0:T(8,128)(2,1)S(1)}, u32[]{:S(2)}, u32[]{:S(2)}) %collective-permute-start.32) | collective-permute-done | bytes 606240 | tf_op jit(solution)/shard_map/ppermute | solution.py:876
  290.5 8.4 collective-permute-done.34.refs_13_.refs_6_.refs_8_.refs_10_.refs_11_
  304.0 10.8 %project.3 = (bf16[4,2048,128]{2,1,0:T(8,128)(2,1)}, bf16[4,2048,128]{2,1,0:T(8,128)(2,1)}, bf16[4,2048,128]{2,1,0:T(8,128)(2,1)}) custom-call(s32[64]{0:T(128)} %fusion.75.refs_0_, bf16[2,512,1024]{2,1,0:T(8,128)(2,1)} %bitcast.273, bf16[1,512,1024]{2,1,0:T(8,128)(2,1)} %copy-done.90, bf16[1,512,1024]{2,1,0:T(8,128)(2,1)} %copy-done.91, ...), custom_call_target="tpu_custom_call" | custom-call | flops 11500000256 | tf_op jit(solution)/shard_map/project/pallas_call | solution.py:71
  314.8 14.4 %attend.3 = (bf16[4,512,256]{2,1,0:T(8,128)(2,1)}, bf16[4,2048,128]{2,1,0:T(8,128)(2,1)}) custom-call(s32[64]{0:T(128)} %fusion.75.refs_0_, bf16[4,2048,128]{2,1,0:T(8,128)(2,1)} %get-tuple-element.100.refs_1_, bf16[4,2048,128]{2,1,0:T(8,128)(2,1)} %get-tuple-element.101.refs_2_, bf16[4,2048,128]{2,1,0:T(8,128)(2,1)} %get-tuple-element.102.refs_3_), custom_call_target="tpu_custom_call" | custom-call | flops 16675000320 | tf_op jit(solution)/shard_map/attend/pallas_call | solution.py:71
  332.3 4.1 collective-permute-start.41
  336.4 16.1 %collective-permute-done.38.refs_10_.refs_12_.refs_14_.refs_15_ = bf16[2368,256]{1,0:T(8,128)(2,1)} collective-permute-done((bf16[2368,256]{1,0:T(8,128)(2,1)}, bf16[2368,256]{1,0:T(8,128)(2,1)}, u32[]{:S(2)}, u32[]{:S(2)}) %collective-permute-start.38) | collective-permute-done | bytes 1212448 | tf_op jit(solution)/shard_map/ppermute | solution.py:883
  353.3 4.9 output.3.refs_2_
  358.8 5.0 collective-permute-done.42
  365.6 18.2 %mlp.3 = (bf16[1024,1024]{1,0:T(8,128)(2,1)}, f32[1024,1024]{1,0:T(8,128)}, bf16[1024,1024]{1,0:T(8,128)(2,1)}, bf16[1024,704]{1,0:T(8,128)(2,1)}, bf16[1024,704...) custom-call(s32[64]{0:T(128)} %fusion.75.refs_0_, bf16[1024,1024]{1,0:T(8,128)(2,1)} %copy-done.4, ...), custom_call_target="tpu_custom_call" | custom-call | flops 21849999360 | tf_op jit(solution)/shard_map/mlp/pallas_call | solution.py:71
  385.5 27.9 %mlp_back.2 = (bf16[4,2112,256]{2,1,0:T(8,128)(2,1)}, bf16[4,2112,256]{2,1,0:T(8,128)(2,1)}, bf16[1024,1024]{1,0:T(8,128)(2,1)}) custom-call(s32[64]{0:T(128)} %fusion.75.refs_0_, bf16[1024,1024]{1,0:T(8,128)(2,1)} %bitcast.276, bf16[1024,1024]{1,0:T(8,128)(2,1)} %get-tuple-element.106.refs_2_, bf16[1024,704]{1,0:T(8,128)(2,1)} %get-tuple-element.107.refs_3_, ...), custom_call_target="tpu_custom_call" | custom-call | flops 32199999488 | tf_op jit(solution)/shard_map/mlp_back/pallas_call | solution.py:71
  413.5 3.2 fusion.82
  422.9 3.5 add_convert_fusion
  427.5 5.4 collective-permute-start.44
  432.9 12.3 %middle.2 = (f32[1024,1024]{1,0:T(8,128)}, f32[1,1024]{1,0:T(1,128)}, bf16[2,1024,256]{2,1,0:T(8,128)(2,1)}, bf16[4,512,256]{2,1,0:T(8,128)(2,1)}) custom-call(s32[64]{0:T(128)} %fusion.75.refs_0_, bf16[1024,1024]{1,0:T(8,128)(2,1)} %bitcast.277, bf16[1024,1024]{1,0:T(8,128)(2,1)} %get-tuple-element.114.refs_2_, ...), custom_call_target="tpu_custom_call" | custom-call | flops 14949999616 | tf_op jit(solution)/shard_map/middle/pallas_call | solution.py:71
  447.2 2.6 fusion.37
  450.5 15.9 %collective-permute-done.46 = bf16[1024,256]{1,0:T(8,128)(2,1)S(1)} collective-permute-done((bf16[1024,256]{1,0:T(8,128)(2,1)S(1)}, bf16[1024,256]{1,0:T(8,128)(2,1)S(1)}, u32[]{:S(2)}, u32[]{:S(2)}) %collective-permute-start.46) | collective-permute-done | bytes 524320 | tf_op jit(solution)/shard_map/ppermute | solution.py:890
  468.5 29.8 %attend_back.2 = (bf16[2048,256]{1,0:T(8,128)(2,1)}, bf16[2048,256]{1,0:T(8,128)(2,1)}, bf16[2048,256]{1,0:T(8,128)(2,1)}, f32[2048,256]{1,0:T(8,128)}) custom-call(s32[64]{0:T(128)} %fusion.75.refs_0_, bf16[4,2048,128]{2,1,0:T(8,128)(2,1)} %get-tuple-element.113.refs_1_, bf16[4,2048,128]{2,1,0:T(8,128)(2,1)} %get-tuple-element.101.refs_2_, ...), custom_call_target="tpu_custom_call" | custom-call | flops 33924999168 | tf_op jit(solution)/shard_map/attend_back/pallas_call | solution.py:71
  499.2 11.2 %project_back.2 = (bf16[2,512,1024]{2,1,0:T(8,128)(2,1)}, bf16[2,512,1024]{2,1,0:T(8,128)(2,1)}, bf16[4,256,768]{2,1,0:T(8,128)(2,1)}) custom-call(s32[64]{0:T(128)} %fusion.75.refs_0_, bf16[2,512,1024]{2,1,0:T(8,128)(2,1)} %bitcast.274, bf16[1,512,1024]{2,1,0:T(8,128)(2,1)} %copy-done.90, bf16[1,512,1024]{2,1,0:T(8,128)(2,1)} %copy-done.91, ...), custom_call_target="tpu_custom_call" | custom-call | flops 13799999488 | tf_op jit(solution)/shard_map/project_back/pallas_call | solution.py:71
  511.6 4.8 collective-permute-done.54
  525.5 18.1 %collective-permute-done.55 = bf16[512,1024]{1,0:T(8,128)(2,1)S(1)} collective-permute-done((bf16[512,1024]{1,0:T(8,128)(2,1)S(1)}, bf16[512,1024]{1,0:T(8,128)(2,1)S(1)}, u32[]{:S(2)}, u32[]{:S(2)}) %collective-permute-start.55) | collective-permute-done | bytes 1048608 | tf_op jit(solution)/shard_map/ppermute | solution.py:890
  545.6 2.8 fusion.32
  548.4 2.9 fusion.39
  551.4 2.5 collective-permute-start.64
  558.8 4.0 fusion.77
  562.8 27.8 %mlp_back.3 = (bf16[4,2112,256]{2,1,0:T(8,128)(2,1)}, bf16[4,2112,256]{2,1,0:T(8,128)(2,1)}, bf16[1024,1024]{1,0:T(8,128)(2,1)}) custom-call(s32[64]{0:T(128)} %fusion.75.refs_0_, bf16[1024,1024]{1,0:T(8,128)(2,1)} %get-tuple-element.185.refs_1_, bf16[1024,1024]{1,0:T(8,128)(2,1)} %get-tuple-element.125.refs_2_, ...), custom_call_target="tpu_custom_call" | custom-call | flops 32199999488 | tf_op jit(solution)/shard_map/mlp_back/pallas_call | solution.py:71
  598.7 3.2 fusion.80
  604.9 4.8 collective-permute-done.59.refs_22_
  618.8 12.8 %middle.3 = (f32[1024,1024]{1,0:T(8,128)}, f32[1,1024]{1,0:T(1,128)}, bf16[2,1024,256]{2,1,0:T(8,128)(2,1)}, bf16[4,512,256]{2,1,0:T(8,128)(2,1)}) custom-call(s32[64]{0:T(128)} %fusion.75.refs_0_, f32[1024,1024]{1,0:T(8,128)} %get-tuple-element.186.refs_1_, bf16[1024,1024]{1,0:T(8,128)(2,1)} %get-tuple-element.130.refs_2_, bf16[1024,1024]{1,0:T(8,128)(2,1)} %copy-done.88, ...), custom_call_target="tpu_custom_call" | custom-call | flops 14949999616 | tf_op jit(solution)/shard_map/middle/pallas_call | solution.py:71
  631.6 7.1 collective-permute-done.70.refs_17_
  644.1 2.7 fusion.41
  653.3 2.8 fusion.30.refs_12_
  656.1 5.3 collective-permute-done.72
  662.2 29.8 %attend_back.3 = (bf16[2048,256]{1,0:T(8,128)(2,1)}, bf16[2048,256]{1,0:T(8,128)(2,1)}, bf16[2048,256]{1,0:T(8,128)(2,1)}) custom-call(s32[64]{0:T(128)} %fusion.75.refs_0_, bf16[4,2048,128]{2,1,0:T(8,128)(2,1)} %get-tuple-element.140.refs_1_, bf16[4,2048,128]{2,1,0:T(8,128)(2,1)} %get-tuple-element.92.refs_2_, ...), custom_call_target="tpu_custom_call" | custom-call | flops 33924999168 | tf_op jit(solution)/shard_map/attend_back/pallas_call | solution.py:71
  693.3 11.3 %project_back.3 = (bf16[2,512,1024]{2,1,0:T(8,128)(2,1)}, bf16[2,512,1024]{2,1,0:T(8,128)(2,1)}, bf16[4,256,768]{2,1,0:T(8,128)(2,1)}) custom-call(s32[64]{0:T(128)} %fusion.75.refs_0_, bf16[2,512,1024]{2,1,0:T(8,128)(2,1)} %copy-done.10, bf16[1,512,1024]{2,1,0:T(8,128)(2,1)} %collective-permute-done.3.refs_2_, ...), custom_call_target="tpu_custom_call" | custom-call | flops 13799999488 | tf_op jit(solution)/shard_map/project_back/pallas_call | solution.py:71
  720.5 15.5 %collective-permute-done.82 = bf16[512,1024]{1,0:T(8,128)(2,1)S(1)} collective-permute-done((bf16[512,1024]{1,0:T(8,128)(2,1)S(1)}, bf16[512,1024]{1,0:T(8,128)(2,1)S(1)}, u32[]{:S(2)}, u32[]{:S(2)}) %collective-permute-start.82) | collective-permute-done | bytes 1048608 | tf_op jit(solution)/shard_map/ppermute | solution.py:890
  741.5 2.4 collective-permute-start.102
  749.6 4.2 collective-permute-done.95
  756.9 21.9 %collective-permute-done.84 = bf16[512,512]{1,0:T(8,128)(2,1)S(1)} collective-permute-done((bf16[512,512]{1,0:T(8,128)(2,1)S(1)}, bf16[512,512]{1,0:T(8,128)(2,1)S(1)}, u32[]{:S(2)}, u32[]{:S(2)}) %collective-permute-start.84) | collective-permute-done | bytes 524320 | tf_op jit(solution)/shard_map/ppermute | solution.py:886
  783.3 34.9 %collective-permute-done.103 = bf16[128,256]{1,0:T(8,128)(2,1)S(1)} collective-permute-done((bf16[128,256]{1,0:T(8,128)(2,1)S(1)}, bf16[128,256]{1,0:T(8,128)(2,1)S(1)}, u32[]{:S(2)}, u32[]{:S(2)}) %collective-permute-start.103) | collective-permute-done | bytes 65568 | tf_op jit(solution)/shard_map/ppermute | solution.py:880
  818.2 7.9 collective-permute-done.99
  826.2 3.0 collective-permute-start.89
  829.2 10.5 %collective-permute-done.96 = bf16[1056,256]{1,0:T(8,128)(2,1)S(1)} collective-permute-done((bf16[1056,256]{1,0:T(8,128)(2,1)S(1)}, bf16[1056,256]{1,0:T(8,128)(2,1)S(1)}, u32[]{:S(2)}, u32[]{:S(2)}) %collective-permute-start.96) | collective-permute-done | bytes 540704 | tf_op jit(solution)/shard_map/ppermute | solution.py:880
  843.8 4.1 collective-permute-done.89
  (513 shorter events, 203.7 us)
Async XLA Ops:
  5.6 30.4 %collective-permute-start.5 = (bf16[1024,384]{1,0:T(8,128)(2,1)}, bf16[1024,384]{1,0:T(8,128)(2,1)}, u32[]{:S(2)}, u32[]{:S(2)}) collective-permute-start(bf16[1024,384]{1,0:T(8,128)(2,1)} %pad_maximum_fusion.5), channel_id=1, source_target_pairs={{0,16},{16,0},{1,17},{17,1},{2,18},{18,2},{3,19},{19,3},{4,20},{20... | collective-permute-start | bytes 2359304 | tf_op jit(solution)/shard_map/ppermute | solution.py:872
  19.8 47.5 %collective-permute-start.9 = (bf16[1184,1024]{1,0:T(8,128)(2,1)}, bf16[1184,1024]{1,0:T(8,128)(2,1)}, u32[]{:S(2)}, u32[]{:S(2)}) collective-permute-start(bf16[1184,1024]{1,0:T(8,128)(2,1)} %pad_maximum_fusion.1), channel_id=1, source_target_pairs={{0,16},{16,0},{1,17},{17,1},{2,18},{18,2},{3,19},{19,3},{4,20},{20... | collective-permute-start | bytes 7274504 | tf_op jit(solution)/shard_map/ppermute | solution.py:872
  25.4 38.1 %collective-permute-start.1 = (bf16[512,1024]{1,0:T(8,128)(2,1)}, bf16[512,1024]{1,0:T(8,128)(2,1)S(1)}, u32[]{:S(2)}, u32[]{:S(2)}) collective-permute-start(bf16[512,1024]{1,0:T(8,128)(2,1)} %collective-permute-done), channel_id=1, source_target_pairs={{0,16},{16,0},{1,17},{17,1},{2,18},{18,2},{3,19},{19,3},{4,20},{20... | collective-permute-start | bytes 3145736 | tf_op jit(solution)/shard_map/ppermute | solution.py:872
  61.1 45.8 %collective-permute-start.14 = (bf16[512,384]{1,0:T(8,128)(2,1)S(1)}, bf16[512,384]{1,0:T(8,128)(2,1)}, u32[]{:S(2)}, u32[]{:S(2)}) collective-permute-start(bf16[512,384]{1,0:T(8,128)(2,1)S(1)} %maximum_select_fusion.3), channel_id=1, source_target_pairs={{0,8},{4,12},{8,0},{12,4},{1,9},{5,13},{9,1},{13,5},{2,10},{6,14},... | collective-permute-start | bytes 1179656 | tf_op jit(solution)/shard_map/ppermute | solution.py:883
  67.3 36.5 %collective-permute-start.3 = (bf16[1,512,1024]{2,1,0:T(8,128)(2,1)S(1)}, bf16[1,512,1024]{2,1,0:T(8,128)(2,1)}, u32[]{:S(2)}, u32[]{:S(2)}) collective-permute-start(bf16[1,512,1024]{2,1,0:T(8,128)(2,1)S(1)} %constant_dynamic-slice_fusion.7), channel_id=1, source_target_pairs={{0,1},{1,0},{2,3},{3,2},{4,5},{5,4},{6,7},{7,6},{8,9},{9,8},{10,11... | collective-permute-start | bytes 3145736 | tf_op jit(solution)/shard_map/ppermute | solution.py:890
  72.8 32.9 %collective-permute-start.10 = (bf16[1184,256]{1,0:T(8,128)(2,1)S(1)}, bf16[1184,256]{1,0:T(8,128)(2,1)}, u32[]{:S(2)}, u32[]{:S(2)}) collective-permute-start(bf16[1184,256]{1,0:T(8,128)(2,1)S(1)} %constant_dynamic-slice_fusion.4), channel_id=1, source_target_pairs={{0,1},{1,3},{3,2},{2,0},{4,5},{5,7},{7,6},{6,4},{8,9},{9,11},{11,1... | collective-permute-start | bytes 1818632 | tf_op jit(solution)/shard_map/ppermute | solution.py:876
  74.5 33.7 %collective-permute-start.8 = (bf16[512,384]{1,0:T(8,128)(2,1)S(1)}, bf16[512,384]{1,0:T(8,128)(2,1)S(1)}, u32[]{:S(2)}, u32[]{:S(2)}) collective-permute-start(bf16[512,384]{1,0:T(8,128)(2,1)S(1)} %maximum_select_fusion.2), channel_id=1, source_target_pairs={{0,8},{4,12},{8,0},{12,4},{1,9},{5,13},{9,1},{13,5},{2,10},{6,14},... | collective-permute-start | bytes 1179656 | tf_op jit(solution)/shard_map/ppermute | solution.py:883
  111.3 23.0 %collective-permute-start.16 = (bf16[1184,256]{1,0:T(8,128)(2,1)}, bf16[1184,256]{1,0:T(8,128)(2,1)S(1)}, u32[]{:S(2)}, u32[]{:S(2)}) collective-permute-start(bf16[1184,256]{1,0:T(8,128)(2,1)} %collective-permute-done.10.refs_4_.refs_6_.refs_8_.refs_9_), channel_id=1, source_target_pairs={{0,4},{4,0},{8,12},{12,8},{1,5},{5,1},{9,13},{13,9},{2,6},{6,2},{1... | collective-permute-start | bytes 1818632 | tf_op jit(solution)/shard_map/ppermute | solution.py:883
  112.1 29.5 %collective-permute-start.17 = (bf16[1184,256]{1,0:T(8,128)(2,1)}, bf16[1184,256]{1,0:T(8,128)(2,1)S(1)}, u32[]{:S(2)}, u32[]{:S(2)}) collective-permute-start(bf16[1184,256]{1,0:T(8,128)(2,1)} %collective-permute-done.10.refs_4_.refs_6_.refs_8_.refs_9_), channel_id=1, source_target_pairs={{0,8},{4,12},{8,0},{12,4},{1,9},{5,13},{9,1},{13,5},{2,10},{6,14},... | collective-permute-start | bytes 1818632 | tf_op jit(solution)/shard_map/ppermute | solution.py:883
  112.6 30.5 %collective-permute-start.18 = (bf16[1184,256]{1,0:T(8,128)(2,1)}, bf16[1184,256]{1,0:T(8,128)(2,1)S(1)}, u32[]{:S(2)}, u32[]{:S(2)}) collective-permute-start(bf16[1184,256]{1,0:T(8,128)(2,1)} %collective-permute-done.10.refs_4_.refs_6_.refs_8_.refs_9_), channel_id=1, source_target_pairs={{0,12},{4,8},{8,4},{12,0},{1,13},{5,9},{9,5},{13,1},{2,14},{6,10},... | collective-permute-start | bytes 1818632 | tf_op jit(solution)/shard_map/ppermute | solution.py:883
  123.1 30.9 %collective-permute-start.19 = (bf16[1184,256]{1,0:T(8,128)(2,1)S(1)}, bf16[1184,256]{1,0:T(8,128)(2,1)S(1)}, u32[]{:S(2)}, u32[]{:S(2)}) collective-permute-start(bf16[1184,256]{1,0:T(8,128)(2,1)S(1)} %collective-permute-done.11.refs_5_.refs_8_.refs_10_.refs_12_.refs_13_), channel_id=1, source_target_pairs={{0,4},{4,0},{8,12},{12,8},{1,5},{5,1},{9,13},{13,9},{2,6},{6,2},{1... | collective-permute-start | bytes 1818632 | tf_op jit(solution)/shard_map/ppermute | solution.py:883
  134.3 35.9 %collective-permute-start.20 = (bf16[1184,256]{1,0:T(8,128)(2,1)S(1)}, bf16[1184,256]{1,0:T(8,128)(2,1)}, u32[]{:S(2)}, u32[]{:S(2)}) collective-permute-start(bf16[1184,256]{1,0:T(8,128)(2,1)S(1)} %collective-permute-done.11.refs_5_.refs_8_.refs_10_.refs_12_.refs_13_), channel_id=1, source_target_pairs={{0,8},{4,12},{8,0},{12,4},{1,9},{5,13},{9,1},{13,5},{2,10},{6,14},... | collective-permute-start | bytes 1818632 | tf_op jit(solution)/shard_map/ppermute | solution.py:883
  141.6 31.3 %collective-permute-start.21 = (bf16[1184,256]{1,0:T(8,128)(2,1)S(1)}, bf16[1184,256]{1,0:T(8,128)(2,1)}, u32[]{:S(2)}, u32[]{:S(2)}) collective-permute-start(bf16[1184,256]{1,0:T(8,128)(2,1)S(1)} %collective-permute-done.11.refs_5_.refs_8_.refs_10_.refs_12_.refs_13_), channel_id=1, source_target_pairs={{0,12},{4,8},{8,4},{12,0},{1,13},{5,9},{9,5},{13,1},{2,14},{6,10},... | collective-permute-start | bytes 1818632 | tf_op jit(solution)/shard_map/ppermute | solution.py:883
  142.1 41.5 %collective-permute-start.23 = (bf16[1184,256]{1,0:T(8,128)(2,1)S(1)}, bf16[1184,256]{1,0:T(8,128)(2,1)}, u32[]{:S(2)}, u32[]{:S(2)}) collective-permute-start(bf16[1184,256]{1,0:T(8,128)(2,1)S(1)} %collective-permute-done.22.refs_12_.refs_16_.refs_14_.refs_17_), channel_id=1, source_target_pairs={{0,4},{4,0},{8,12},{12,8},{1,5},{5,1},{9,13},{13,9},{2,6},{6,2},{1... | collective-permute-start | bytes 1818632 | tf_op jit(solution)/shard_map/ppermute | solution.py:883
  143.1 50.1 %collective-permute-start.24 = (bf16[1184,256]{1,0:T(8,128)(2,1)S(1)}, bf16[1184,256]{1,0:T(8,128)(2,1)}, u32[]{:S(2)}, u32[]{:S(2)}) collective-permute-start(bf16[1184,256]{1,0:T(8,128)(2,1)S(1)} %collective-permute-done.22.refs_12_.refs_16_.refs_14_.refs_17_), channel_id=1, source_target_pairs={{0,8},{4,12},{8,0},{12,4},{1,9},{5,13},{9,1},{13,5},{2,10},{6,14},... | collective-permute-start | bytes 1818632 | tf_op jit(solution)/shard_map/ppermute | solution.py:883
  154.0 39.2 %collective-permute-start.25 = (bf16[1184,256]{1,0:T(8,128)(2,1)S(1)}, bf16[1184,256]{1,0:T(8,128)(2,1)}, u32[]{:S(2)}, u32[]{:S(2)}) collective-permute-start(bf16[1184,256]{1,0:T(8,128)(2,1)S(1)} %collective-permute-done.22.refs_12_.refs_16_.refs_14_.refs_17_), channel_id=1, source_target_pairs={{0,12},{4,8},{8,4},{12,0},{1,13},{5,9},{9,5},{13,1},{2,14},{6,10},... | collective-permute-start | bytes 1818632 | tf_op jit(solution)/shard_map/ppermute | solution.py:883
  199.3 22.9 %collective-permute-start.27 = (bf16[1184,256]{1,0:T(8,128)(2,1)S(1)}, bf16[1184,256]{1,0:T(8,128)(2,1)S(1)}, u32[]{:S(2)}, u32[]{:S(2)}) collective-permute-start(bf16[1184,256]{1,0:T(8,128)(2,1)S(1)} %constant_dynamic-slice_fusion.2), channel_id=1, source_target_pairs={{0,1},{1,3},{3,2},{2,0},{4,5},{5,7},{7,6},{6,4},{8,9},{9,11},{11,1... | collective-permute-start | bytes 1818632 | tf_op jit(solution)/shard_map/ppermute | solution.py:876
  231.9 38.9 %collective-permute-start.29 = (bf16[1,512,1024]{2,1,0:T(8,128)(2,1)S(1)}, bf16[1,512,1024]{2,1,0:T(8,128)(2,1)S(1)}, u32[]{:S(2)}, u32[]{:S(2)}) collective-permute-start(bf16[1,512,1024]{2,1,0:T(8,128)(2,1)S(1)} %constant_dynamic-slice_fusion.1), channel_id=1, source_target_pairs={{0,1},{1,0},{2,3},{3,2},{4,5},{5,4},{6,7},{7,6},{8,9},{9,8},{10,11... | collective-permute-start | bytes 3145736 | tf_op jit(solution)/shard_map/ppermute | solution.py:890
  234.3 36.5 %collective-permute-start.31 = (bf16[1184,256]{1,0:T(8,128)(2,1)S(1)}, bf16[1184,256]{1,0:T(8,128)(2,1)S(1)}, u32[]{:S(2)}, u32[]{:S(2)}) collective-permute-start(bf16[1184,256]{1,0:T(8,128)(2,1)S(1)} %collective-permute-done.27.refs_4_.refs_6_.refs_8_.refs_9_), channel_id=1, source_target_pairs={{0,1},{1,3},{3,2},{2,0},{4,5},{5,7},{7,6},{6,4},{8,9},{9,11},{11,1... | collective-permute-start | bytes 1818632 | tf_op jit(solution)/shard_map/ppermute | solution.py:876
  270.8 32.2 %collective-permute-start.30 = (bf16[1,512,1024]{2,1,0:T(8,128)(2,1)S(1)}, bf16[1,512,1024]{2,1,0:T(8,128)(2,1)S(1)}, u32[]{:S(2)}, u32[]{:S(2)}) collective-permute-start(bf16[1,512,1024]{2,1,0:T(8,128)(2,1)S(1)} %collective-permute-done.29.refs_2_), channel_id=1, source_target_pairs={{0,16},{16,0},{1,17},{17,1},{2,18},{18,2},{3,19},{19,3},{4,20},{20... | collective-permute-start | bytes 3145736 | tf_op jit(solution)/shard_map/ppermute | solution.py:872
  273.1 25.9 %collective-permute-start.34 = (bf16[1184,256]{1,0:T(8,128)(2,1)S(1)}, bf16[1184,256]{1,0:T(8,128)(2,1)S(1)}, u32[]{:S(2)}, u32[]{:S(2)}) collective-permute-start(bf16[1184,256]{1,0:T(8,128)(2,1)S(1)} %collective-permute-done.27.refs_4_.refs_6_.refs_8_.refs_9_), channel_id=1, source_target_pairs={{0,8},{4,12},{8,0},{12,4},{1,9},{5,13},{9,1},{13,5},{2,10},{6,14},... | collective-permute-start | bytes 1818632 | tf_op jit(solution)/shard_map/ppermute | solution.py:883
  274.4 27.8 %collective-permute-start.35 = (bf16[1184,256]{1,0:T(8,128)(2,1)S(1)}, bf16[1184,256]{1,0:T(8,128)(2,1)S(1)}, u32[]{:S(2)}, u32[]{:S(2)}) collective-permute-start(bf16[1184,256]{1,0:T(8,128)(2,1)S(1)} %collective-permute-done.27.refs_4_.refs_6_.refs_8_.refs_9_), channel_id=1, source_target_pairs={{0,12},{4,8},{8,4},{12,0},{1,13},{5,9},{9,5},{13,1},{2,14},{6,10},... | collective-permute-start | bytes 1818632 | tf_op jit(solution)/shard_map/ppermute | solution.py:883
  288.7 47.6 %collective-permute-start.37 = (bf16[2368,256]{1,0:T(8,128)(2,1)}, bf16[2368,256]{1,0:T(8,128)(2,1)}, u32[]{:S(2)}, u32[]{:S(2)}) collective-permute-start(bf16[2368,256]{1,0:T(8,128)(2,1)} %constant_dynamic-update-slice_fusion.refs_8_.refs_10_.refs_12_.refs_13_), channel_id=1, source_target_pairs={{0,4},{4,0},{8,12},{12,8},{1,5},{5,1},{9,13},{13,9},{2,6},{6,2},{1... | collective-permute-start | bytes 3637256 | tf_op jit(solution)/shard_map/ppermute | solution.py:883
  289.3 63.2 %collective-permute-start.38 = (bf16[2368,256]{1,0:T(8,128)(2,1)}, bf16[2368,256]{1,0:T(8,128)(2,1)}, u32[]{:S(2)}, u32[]{:S(2)}) collective-permute-start(bf16[2368,256]{1,0:T(8,128)(2,1)} %constant_dynamic-update-slice_fusion.refs_8_.refs_10_.refs_12_.refs_13_), channel_id=1, source_target_pairs={{0,8},{4,12},{8,0},{12,4},{1,9},{5,13},{9,1},{13,5},{2,10},{6,14},... | collective-permute-start | bytes 3637256 | tf_op jit(solution)/shard_map/ppermute | solution.py:883
  299.0 53.5 %collective-permute-start.39 = (bf16[2368,256]{1,0:T(8,128)(2,1)}, bf16[2368,256]{1,0:T(8,128)(2,1)}, u32[]{:S(2)}, u32[]{:S(2)}) collective-permute-start(bf16[2368,256]{1,0:T(8,128)(2,1)} %constant_dynamic-update-slice_fusion.refs_8_.refs_10_.refs_12_.refs_13_), channel_id=1, source_target_pairs={{0,12},{4,8},{8,4},{12,0},{1,13},{5,9},{9,5},{13,1},{2,14},{6,10},... | collective-permute-start | bytes 3637256 | tf_op jit(solution)/shard_map/ppermute | solution.py:883
  332.3 26.0 %collective-permute-start.41 = (bf16[512,1024]{1,0:T(8,128)(2,1)S(1)}, bf16[512,1024]{1,0:T(8,128)(2,1)}, u32[]{:S(2)}, u32[]{:S(2)}) collective-permute-start(bf16[512,1024]{1,0:T(8,128)(2,1)S(1)} %dynamic-slice_bitcast_fusion.1), channel_id=1, source_target_pairs={{0,2},{1,3},{18,16},{19,17},{4,6},{5,7},{22,20},{23,21},{8,10},{9,... | collective-permute-start | bytes 3145736 | tf_op jit(solution)/shard_map/ppermute | solution.py:899
  383.8 37.7 %collective-permute-start.43 = (bf16[1024,1024]{1,0:T(8,128)(2,1)}, bf16[1024,1024]{1,0:T(8,128)(2,1)S(1)}, u32[]{:S(2)}, u32[]{:S(2)}) collective-permute-start(bf16[1024,1024]{1,0:T(8,128)(2,1)} %get-tuple-element.105), channel_id=1, source_target_pairs={{0,16},{16,0},{1,17},{17,1},{2,18},{18,2},{3,19},{19,3},{4,20},{20... | collective-permute-start | bytes 6291464 | tf_op jit(solution)/shard_map/ppermute | solution.py:872
  416.7 29.6 %collective-permute-start.47 = (bf16[2,1056,256]{2,1,0:T(8,128)(2,1)}, bf16[2,1056,256]{2,1,0:T(8,128)(2,1)S(1)}, u32[]{:S(2)}, u32[]{:S(2)}) collective-permute-start(bf16[2,1056,256]{2,1,0:T(8,128)(2,1)} %get-tuple-element.212), channel_id=1, source_target_pairs={{0,4},{4,0},{8,12},{12,8},{1,5},{5,1},{9,13},{13,9},{2,6},{6,2},{1... | collective-permute-start | bytes 3244040 | tf_op jit(solution)/shard_map/ppermute | solution.py:883
  418.2 29.0 %collective-permute-start.48 = (bf16[2,1056,256]{2,1,0:T(8,128)(2,1)}, bf16[2,1056,256]{2,1,0:T(8,128)(2,1)}, u32[]{:S(2)}, u32[]{:S(2)}) collective-permute-start(bf16[2,1056,256]{2,1,0:T(8,128)(2,1)} %get-tuple-element.211), channel_id=1, source_target_pairs={{0,8},{4,12},{8,0},{12,4},{1,9},{5,13},{9,1},{13,5},{2,10},{6,14},... | collective-permute-start | bytes 3244040 | tf_op jit(solution)/shard_map/ppermute | solution.py:883
  420.2 78.1 %collective-permute-start.49 = (bf16[2,1056,256]{2,1,0:T(8,128)(2,1)}, bf16[2,1056,256]{2,1,0:T(8,128)(2,1)}, u32[]{:S(2)}, u32[]{:S(2)}) collective-permute-start(bf16[2,1056,256]{2,1,0:T(8,128)(2,1)} %get-tuple-element.210), channel_id=1, source_target_pairs={{0,4},{4,0},{8,12},{12,8},{1,5},{5,1},{9,13},{13,9},{2,6},{6,2},{1... | collective-permute-start | bytes 3244040 | tf_op jit(solution)/shard_map/ppermute | solution.py:883
  421.6 76.8 %collective-permute-start.50 = (bf16[2,1056,256]{2,1,0:T(8,128)(2,1)}, bf16[2,1056,256]{2,1,0:T(8,128)(2,1)}, u32[]{:S(2)}, u32[]{:S(2)}) collective-permute-start(bf16[2,1056,256]{2,1,0:T(8,128)(2,1)} %get-tuple-element.209), channel_id=1, source_target_pairs={{0,8},{4,12},{8,0},{12,4},{1,9},{5,13},{9,1},{13,5},{2,10},{6,14},... | collective-permute-start | bytes 3244040 | tf_op jit(solution)/shard_map/ppermute | solution.py:883
  427.5 41.0 %collective-permute-start.44 = (bf16[512,1024]{1,0:T(8,128)(2,1)}, bf16[512,1024]{1,0:T(8,128)(2,1)}, u32[]{:S(2)}, u32[]{:S(2)}) collective-permute-start(bf16[512,1024]{1,0:T(8,128)(2,1)} %dynamic-slice_bitcast_fusion), channel_id=1, source_target_pairs={{0,2},{1,3},{18,16},{19,17},{4,6},{5,7},{22,20},{23,21},{8,10},{9,... | collective-permute-start | bytes 3145736 | tf_op jit(solution)/shard_map/ppermute | solution.py:899
  449.9 48.5 %collective-permute-start.51 = (bf16[1056,256]{1,0:T(8,128)(2,1)}, bf16[1056,256]{1,0:T(8,128)(2,1)S(1)}, u32[]{:S(2)}, u32[]{:S(2)}) collective-permute-start(bf16[1056,256]{1,0:T(8,128)(2,1)} %get-tuple-element.208), channel_id=1, source_target_pairs={{0,4},{4,0},{8,12},{12,8},{1,5},{5,1},{9,13},{13,9},{2,6},{6,2},{1... | collective-permute-start | bytes 1622024 | tf_op jit(solution)/shard_map/ppermute | solution.py:883
  467.2 31.1 %collective-permute-start.52 = (bf16[1056,256]{1,0:T(8,128)(2,1)}, bf16[1056,256]{1,0:T(8,128)(2,1)}, u32[]{:S(2)}, u32[]{:S(2)}) collective-permute-start(bf16[1056,256]{1,0:T(8,128)(2,1)} %get-tuple-element.207), channel_id=1, source_target_pairs={{0,8},{4,12},{8,0},{12,4},{1,9},{5,13},{9,1},{13,5},{2,10},{6,14},... | collective-permute-start | bytes 1622024 | tf_op jit(solution)/shard_map/ppermute | solution.py:883
  518.4 25.3 %collective-permute-start.55 = (bf16[512,1024]{1,0:T(8,128)(2,1)S(1)}, bf16[512,1024]{1,0:T(8,128)(2,1)S(1)}, u32[]{:S(2)}, u32[]{:S(2)}) collective-permute-start(bf16[512,1024]{1,0:T(8,128)(2,1)S(1)} %fusion.34), channel_id=1, source_target_pairs={{0,1},{1,0},{2,3},{3,2},{4,5},{5,4},{6,7},{7,6},{8,9},{9,8},{10,11... | collective-permute-start | bytes 3145736 | tf_op jit(solution)/shard_map/ppermute | solution.py:890
  521.3 69.3 %collective-permute-start.62 = (bf16[2,128,768]{2,1,0:T(8,128)(2,1)}, bf16[2,128,768]{2,1,0:T(8,128)(2,1)S(1)}, u32[]{:S(2)}, u32[]{:S(2)}) collective-permute-start(bf16[2,128,768]{2,1,0:T(8,128)(2,1)} %get-tuple-element.226), channel_id=1, source_target_pairs={{0,4},{4,0},{8,12},{12,8},{1,5},{5,1},{9,13},{13,9},{2,6},{6,2},{1... | collective-permute-start | bytes 1179656 | tf_op jit(solution)/shard_map/ppermute | solution.py:883
  522.3 69.4 %collective-permute-start.63 = (bf16[2,128,768]{2,1,0:T(8,128)(2,1)}, bf16[2,128,768]{2,1,0:T(8,128)(2,1)}, u32[]{:S(2)}, u32[]{:S(2)}) collective-permute-start(bf16[2,128,768]{2,1,0:T(8,128)(2,1)} %get-tuple-element.225), channel_id=1, source_target_pairs={{0,8},{4,12},{8,0},{12,4},{1,9},{5,13},{9,1},{13,5},{2,10},{6,14},... | collective-permute-start | bytes 1179656 | tf_op jit(solution)/shard_map/ppermute | solution.py:883
  522.8 28.5 %collective-permute-start.60 = (bf16[2,256,256]{2,1,0:T(8,128)(2,1)S(1)}, bf16[2,256,256]{2,1,0:T(8,128)(2,1)S(1)}, u32[]{:S(2)}, u32[]{:S(2)}) collective-permute-start(bf16[2,256,256]{2,1,0:T(8,128)(2,1)S(1)} %get-tuple-element.254), channel_id=1, source_target_pairs={{0,4},{4,0},{8,12},{12,8},{1,5},{5,1},{9,13},{13,9},{2,6},{6,2},{1... | collective-permute-start | bytes 786440 | tf_op jit(solution)/shard_map/ppermute | solution.py:883
  524.2 29.6 %collective-permute-start.61 = (bf16[2,256,256]{2,1,0:T(8,128)(2,1)S(1)}, bf16[2,256,256]{2,1,0:T(8,128)(2,1)S(1)}, u32[]{:S(2)}, u32[]{:S(2)}) collective-permute-start(bf16[2,256,256]{2,1,0:T(8,128)(2,1)S(1)} %get-tuple-element.253), channel_id=1, source_target_pairs={{0,8},{4,12},{8,0},{12,4},{1,9},{5,13},{9,1},{13,5},{2,10},{6,14},... | collective-permute-start | bytes 786440 | tf_op jit(solution)/shard_map/ppermute | solution.py:883
  551.4 52.1 %collective-permute-start.64 = (bf16[1056,256]{1,0:T(8,128)(2,1)}, bf16[1056,256]{1,0:T(8,128)(2,1)}, u32[]{:S(2)}, u32[]{:S(2)}) collective-permute-start(bf16[1056,256]{1,0:T(8,128)(2,1)} %get-tuple-element.204), channel_id=1, source_target_pairs={{0,2},{1,0},{3,1},{2,3},{4,6},{5,4},{7,5},{6,7},{8,10},{9,8},{11,9... | collective-permute-start | bytes 1622024 | tf_op jit(solution)/shard_map/ppermute | solution.py:880
  553.8 59.1 %collective-permute-start.65 = (bf16[1056,256]{1,0:T(8,128)(2,1)S(1)}, bf16[1056,256]{1,0:T(8,128)(2,1)}, u32[]{:S(2)}, u32[]{:S(2)}) collective-permute-start(bf16[1056,256]{1,0:T(8,128)(2,1)S(1)} %get-tuple-element.203), channel_id=1, source_target_pairs={{0,3},{1,2},{3,0},{2,1},{4,7},{5,6},{7,4},{6,5},{8,11},{9,10},{11,... | collective-permute-start | bytes 1622024 | tf_op jit(solution)/shard_map/ppermute | solution.py:880
  555.9 36.8 %collective-permute-start.66 = (bf16[256,256]{1,0:T(8,128)(2,1)}, bf16[256,256]{1,0:T(8,128)(2,1)S(1)}, u32[]{:S(2)}, u32[]{:S(2)}) collective-permute-start(bf16[256,256]{1,0:T(8,128)(2,1)} %get-tuple-element.252), channel_id=1, source_target_pairs={{0,4},{4,0},{8,12},{12,8},{1,5},{5,1},{9,13},{13,9},{2,6},{6,2},{1... | collective-permute-start | bytes 393224 | tf_op jit(solution)/shard_map/ppermute | solution.py:883
  591.6 25.8 %collective-permute-start.57 = (bf16[1024,1024]{1,0:T(8,128)(2,1)}, bf16[1024,1024]{1,0:T(8,128)(2,1)S(1)}, u32[]{:S(2)}, u32[]{:S(2)}) collective-permute-start(bf16[1024,1024]{1,0:T(8,128)(2,1)} %get-tuple-element.130.refs_2_), channel_id=1, source_target_pairs={{0,16},{16,0},{1,17},{17,1},{2,18},{18,2},{3,19},{19,3},{4,20},{20... | collective-permute-start | bytes 6291464 | tf_op jit(solution)/shard_map/ppermute | solution.py:872
  612.9 34.7 %collective-permute-start.74 = (bf16[128,256]{1,0:T(8,128)(2,1)}, bf16[128,256]{1,0:T(8,128)(2,1)S(1)}, u32[]{:S(2)}, u32[]{:S(2)}) collective-permute-start(bf16[128,256]{1,0:T(8,128)(2,1)} %get-tuple-element.250), channel_id=1, source_target_pairs={{0,2},{1,0},{3,1},{2,3},{4,6},{5,4},{7,5},{6,7},{8,10},{9,8},{11,9... | collective-permute-start | bytes 196616 | tf_op jit(solution)/shard_map/ppermute | solution.py:880
  613.4 35.1 %collective-permute-start.75 = (bf16[128,256]{1,0:T(8,128)(2,1)}, bf16[128,256]{1,0:T(8,128)(2,1)S(1)}, u32[]{:S(2)}, u32[]{:S(2)}) collective-permute-start(bf16[128,256]{1,0:T(8,128)(2,1)} %get-tuple-element.232), channel_id=1, source_target_pairs={{0,3},{1,2},{3,0},{2,1},{4,7},{5,6},{7,4},{6,5},{8,11},{9,10},{11,... | collective-permute-start | bytes 196616 | tf_op jit(solution)/shard_map/ppermute | solution.py:880
  615.7 34.0 %collective-permute-start.76 = (bf16[128,256]{1,0:T(8,128)(2,1)}, bf16[128,256]{1,0:T(8,128)(2,1)}, u32[]{:S(2)}, u32[]{:S(2)}) collective-permute-start(bf16[128,256]{1,0:T(8,128)(2,1)} %get-tuple-element.231), channel_id=1, source_target_pairs={{0,1},{1,3},{3,2},{2,0},{4,5},{5,7},{7,6},{6,4},{8,9},{9,11},{11,1... | collective-permute-start | bytes 196616 | tf_op jit(solution)/shard_map/ppermute | solution.py:880
  617.4 23.5 %collective-permute-start.71 = (bf16[2,1056,256]{2,1,0:T(8,128)(2,1)}, bf16[2,1056,256]{2,1,0:T(8,128)(2,1)}, u32[]{:S(2)}, u32[]{:S(2)}) collective-permute-start(bf16[2,1056,256]{2,1,0:T(8,128)(2,1)} %get-tuple-element.201), channel_id=1, source_target_pairs={{0,8},{4,12},{8,0},{12,4},{1,9},{5,13},{9,1},{13,5},{2,10},{6,14},... | collective-permute-start | bytes 3244040 | tf_op jit(solution)/shard_map/ppermute | solution.py:883
  641.0 51.0 %collective-permute-start.77 = (bf16[2,1056,256]{2,1,0:T(8,128)(2,1)}, bf16[2,1056,256]{2,1,0:T(8,128)(2,1)}, u32[]{:S(2)}, u32[]{:S(2)}) collective-permute-start(bf16[2,1056,256]{2,1,0:T(8,128)(2,1)} %get-tuple-element.200), channel_id=1, source_target_pairs={{0,4},{4,0},{8,12},{12,8},{1,5},{5,1},{9,13},{13,9},{2,6},{6,2},{1... | collective-permute-start | bytes 3244040 | tf_op jit(solution)/shard_map/ppermute | solution.py:883
  647.6 44.4 %collective-permute-start.78 = (bf16[2,1056,256]{2,1,0:T(8,128)(2,1)}, bf16[2,1056,256]{2,1,0:T(8,128)(2,1)S(1)}, u32[]{:S(2)}, u32[]{:S(2)}) collective-permute-start(bf16[2,1056,256]{2,1,0:T(8,128)(2,1)} %get-tuple-element.199), channel_id=1, source_target_pairs={{0,8},{4,12},{8,0},{12,4},{1,9},{5,13},{9,1},{13,5},{2,10},{6,14},... | collective-permute-start | bytes 3244040 | tf_op jit(solution)/shard_map/ppermute | solution.py:883
  649.1 42.9 %collective-permute-start.79 = (bf16[1056,256]{1,0:T(8,128)(2,1)}, bf16[1056,256]{1,0:T(8,128)(2,1)S(1)}, u32[]{:S(2)}, u32[]{:S(2)}) collective-permute-start(bf16[1056,256]{1,0:T(8,128)(2,1)} %get-tuple-element.198), channel_id=1, source_target_pairs={{0,4},{4,0},{8,12},{12,8},{1,5},{5,1},{9,13},{13,9},{2,6},{6,2},{1... | collective-permute-start | bytes 1622024 | tf_op jit(solution)/shard_map/ppermute | solution.py:883
  649.7 42.3 %collective-permute-start.80 = (bf16[1056,256]{1,0:T(8,128)(2,1)}, bf16[1056,256]{1,0:T(8,128)(2,1)S(1)}, u32[]{:S(2)}, u32[]{:S(2)}) collective-permute-start(bf16[1056,256]{1,0:T(8,128)(2,1)} %get-tuple-element.197), channel_id=1, source_target_pairs={{0,8},{4,12},{8,0},{12,4},{1,9},{5,13},{9,1},{13,5},{2,10},{6,14},... | collective-permute-start | bytes 1622024 | tf_op jit(solution)/shard_map/ppermute | solution.py:883
  710.7 25.3 %collective-permute-start.82 = (bf16[512,1024]{1,0:T(8,128)(2,1)S(1)}, bf16[512,1024]{1,0:T(8,128)(2,1)S(1)}, u32[]{:S(2)}, u32[]{:S(2)}) collective-permute-start(bf16[512,1024]{1,0:T(8,128)(2,1)S(1)} %fusion.35), channel_id=1, source_target_pairs={{0,1},{1,0},{2,3},{3,2},{4,5},{5,4},{6,7},{7,6},{8,9},{9,8},{10,11... | collective-permute-start | bytes 3145736 | tf_op jit(solution)/shard_map/ppermute | solution.py:890
  714.6 24.1 %collective-permute-start.101 = (bf16[256,256]{1,0:T(8,128)(2,1)S(1)}, bf16[256,256]{1,0:T(8,128)(2,1)S(1)}, u32[]{:S(2)}, u32[]{:S(2)}) collective-permute-start(bf16[256,256]{1,0:T(8,128)(2,1)S(1)} %get-tuple-element.247), channel_id=1, source_target_pairs={{0,4},{4,0},{8,12},{12,8},{1,5},{5,1},{9,13},{13,9},{2,6},{6,2},{1... | collective-permute-start | bytes 393224 | tf_op jit(solution)/shard_map/ppermute | solution.py:883
  716.0 23.9 %collective-permute-start.98 = (bf16[256,256]{1,0:T(8,128)(2,1)S(1)}, bf16[256,256]{1,0:T(8,128)(2,1)S(1)}, u32[]{:S(2)}, u32[]{:S(2)}) collective-permute-start(bf16[256,256]{1,0:T(8,128)(2,1)S(1)} %get-tuple-element.246), channel_id=1, source_target_pairs={{0,8},{4,12},{8,0},{12,4},{1,9},{5,13},{9,1},{13,5},{2,10},{6,14},... | collective-permute-start | bytes 393224 | tf_op jit(solution)/shard_map/ppermute | solution.py:883
  719.3 24.7 %collective-permute-start.87 = (bf16[2,128,768]{2,1,0:T(8,128)(2,1)S(1)}, bf16[2,128,768]{2,1,0:T(8,128)(2,1)S(1)}, u32[]{:S(2)}, u32[]{:S(2)}) collective-permute-start(bf16[2,128,768]{2,1,0:T(8,128)(2,1)S(1)} %get-tuple-element.220), channel_id=1, source_target_pairs={{0,8},{4,12},{8,0},{12,4},{1,9},{5,13},{9,1},{13,5},{2,10},{6,14},... | collective-permute-start | bytes 1179656 | tf_op jit(solution)/shard_map/ppermute | solution.py:883
  740.0 86.2 %collective-permute-start.92 = (bf16[1056,256]{1,0:T(8,128)(2,1)S(1)}, bf16[1056,256]{1,0:T(8,128)(2,1)S(1)}, u32[]{:S(2)}, u32[]{:S(2)}) collective-permute-start(bf16[1056,256]{1,0:T(8,128)(2,1)S(1)} %get-tuple-element.193), channel_id=1, source_target_pairs={{0,4},{4,0},{8,12},{12,8},{1,5},{5,1},{9,13},{13,9},{2,6},{6,2},{1... | collective-permute-start | bytes 1622024 | tf_op jit(solution)/shard_map/ppermute | solution.py:883
  741.5 37.3 %collective-permute-start.102 = (bf16[128,256]{1,0:T(8,128)(2,1)S(1)}, bf16[128,256]{1,0:T(8,128)(2,1)S(1)}, u32[]{:S(2)}, u32[]{:S(2)}) collective-permute-start(bf16[128,256]{1,0:T(8,128)(2,1)S(1)} %get-tuple-element.229), channel_id=1, source_target_pairs={{0,3},{1,2},{3,0},{2,1},{4,7},{5,6},{7,4},{6,5},{8,11},{9,10},{11,... | collective-permute-start | bytes 196616 | tf_op jit(solution)/shard_map/ppermute | solution.py:880
  744.0 37.1 %collective-permute-start.86 = (bf16[128,768]{1,0:T(8,128)(2,1)S(1)}, bf16[128,768]{1,0:T(8,128)(2,1)S(1)}, u32[]{:S(2)}, u32[]{:S(2)}) collective-permute-start(bf16[128,768]{1,0:T(8,128)(2,1)S(1)} %get-tuple-element.217), channel_id=1, source_target_pairs={{0,8},{4,12},{8,0},{12,4},{1,9},{5,13},{9,1},{13,5},{2,10},{6,14},... | collective-permute-start | bytes 589832 | tf_op jit(solution)/shard_map/ppermute | solution.py:883
  745.5 36.8 %collective-permute-start.88 = (bf16[128,768]{1,0:T(8,128)(2,1)S(1)}, bf16[128,768]{1,0:T(8,128)(2,1)S(1)}, u32[]{:S(2)}, u32[]{:S(2)}) collective-permute-start(bf16[128,768]{1,0:T(8,128)(2,1)S(1)} %get-tuple-element.218), channel_id=1, source_target_pairs={{0,4},{4,0},{8,12},{12,8},{1,5},{5,1},{9,13},{13,9},{2,6},{6,2},{1... | collective-permute-start | bytes 589832 | tf_op jit(solution)/shard_map/ppermute | solution.py:883
  753.8 25.0 %collective-permute-start.84 = (bf16[512,512]{1,0:T(8,128)(2,1)S(1)}, bf16[512,512]{1,0:T(8,128)(2,1)S(1)}, u32[]{:S(2)}, u32[]{:S(2)}) collective-permute-start(bf16[512,512]{1,0:T(8,128)(2,1)S(1)} %fusion.44), channel_id=1, source_target_pairs={{0,2},{1,3},{2,0},{3,1},{4,6},{5,7},{6,4},{7,5},{8,10},{9,11},{10,... | collective-permute-start | bytes 1572872 | tf_op jit(solution)/shard_map/ppermute | solution.py:886
  778.7 50.4 %collective-permute-start.93 = (bf16[1056,256]{1,0:T(8,128)(2,1)S(1)}, bf16[1056,256]{1,0:T(8,128)(2,1)S(1)}, u32[]{:S(2)}, u32[]{:S(2)}) collective-permute-start(bf16[1056,256]{1,0:T(8,128)(2,1)S(1)} %get-tuple-element.195), channel_id=1, source_target_pairs={{0,2},{1,0},{3,1},{2,3},{4,6},{5,4},{7,5},{6,7},{8,10},{9,8},{11,9... | collective-permute-start | bytes 1622024 | tf_op jit(solution)/shard_map/ppermute | solution.py:880
  778.8 50.4 %collective-permute-start.94 = (bf16[1056,256]{1,0:T(8,128)(2,1)S(1)}, bf16[1056,256]{1,0:T(8,128)(2,1)S(1)}, u32[]{:S(2)}, u32[]{:S(2)}) collective-permute-start(bf16[1056,256]{1,0:T(8,128)(2,1)S(1)} %get-tuple-element.196), channel_id=1, source_target_pairs={{0,3},{1,2},{3,0},{2,1},{4,7},{5,6},{7,4},{6,5},{8,11},{9,10},{11,... | collective-permute-start | bytes 1622024 | tf_op jit(solution)/shard_map/ppermute | solution.py:880
  781.2 37.0 %collective-permute-start.103 = (bf16[128,256]{1,0:T(8,128)(2,1)S(1)}, bf16[128,256]{1,0:T(8,128)(2,1)S(1)}, u32[]{:S(2)}, u32[]{:S(2)}) collective-permute-start(bf16[128,256]{1,0:T(8,128)(2,1)S(1)} %get-tuple-element.230), channel_id=1, source_target_pairs={{0,1},{1,3},{3,2},{2,0},{4,5},{5,7},{7,6},{6,4},{8,9},{9,11},{11,1... | collective-permute-start | bytes 196616 | tf_op jit(solution)/shard_map/ppermute | solution.py:880
  782.3 57.3 %collective-permute-start.96 = (bf16[1056,256]{1,0:T(8,128)(2,1)S(1)}, bf16[1056,256]{1,0:T(8,128)(2,1)S(1)}, u32[]{:S(2)}, u32[]{:S(2)}) collective-permute-start(bf16[1056,256]{1,0:T(8,128)(2,1)S(1)} %fusion.20), channel_id=1, source_target_pairs={{0,1},{1,3},{3,2},{2,0},{4,5},{5,7},{7,6},{6,4},{8,9},{9,11},{11,1... | collective-permute-start | bytes 1622024 | tf_op jit(solution)/shard_map/ppermute | solution.py:880
  (153 other events, 1815.1 us)

commit v4 on v3

--- a/solution.py
+++ b/solution.py
@@ -903,11 +903,11 @@
         mine = (jnp.arange(2) == self.r)[:, None, None]
         return jnp.where(mine, x, got[None])
 
-    def spread(self, x):
+    def spread(self, x, *also):
         give = lax.dynamic_index_in_dim(x, self.s, 0)
         arrays, places = [x], [(0, 0), (0, 1)]
         for k in range(1, self.G):
-            got = self.shift(give, -k)
+            got = hold(self.shift(give, -k), *also)
             arrays += [got, self.sibling(got)]
             places += [(len(arrays) - 2, 0), (len(arrays) - 1, 0)]
         return Blocks(arrays, places, (0, 1))
@@ -1174,12 +1174,11 @@
         first = gather.step(0, x, *early)
         rings = first[0] + gather.step(0)[0] + gather.step(0)[0]
         begun = gather.step(1, x, *early)
-        later_rings = gather.two_steps(1)
     kept = []
     first_values = None
     for layer in range(2):
         gain_mlp = gains[layer][1:2]
-        a_blocks = links.spread(blocked(a))
+        a_blocks = links.spread(blocked(a), *(begun[1] if planar and layer else []))
         deps = [[], [], [], []]
         if not planar:
             for _ in range(1, T):
@@ -1189,7 +1188,8 @@
             deps[1] = rings[:2] + w_proj[1:]
             deps[2] = rings[2:] + first[1]
         else:
-            deps[0] = later_rings + begun[1]
+            deps[1] = gather.step(1, a_blocks.arrays[1])[0]
+            gather.step(1)
         q, k, v = project(meta, a_blocks, w_proj[layer], tables, (ext_q, ext_k), first_values, deps[0])
         o_rel, q = attend(meta, q, k, v, T, deps[1])
         o_blocks = links.exchange(o_rel, length)

time: 882 us -> 872 us (0.989)
  waiting for transfers between devices: 342 us -> 317 us
  starting transfers between devices: 134 us -> 150 us
    ppermute x8, waiting for transfers between devices: 131 us -> 108 us  [shift(): return lax.ppermute(x, 'tensor', pairs)]
    ppermute x15, waiting for transfers between devices: 56.1 us -> 39.2 us  [back(): lax.ppermute(x, 'tensor', [(order[i], order[(i - k) % self.T]) for i in r...]
    ppermute x15, starting transfers between devices: 18.3 us -> 31.5 us  [back(): lax.ppermute(x, 'tensor', [(order[i], order[(i - k) % self.T]) for i in r...]
    ppermute x54 -> x57, starting transfers between devices: 60.5 us -> 64 us  [along(): return lax.ppermute(x, 'dp', [(i, i ^ bit) for i in range(self.DP)])]
    ppermute x54 -> x57, waiting for transfers between devices: 73.9 us -> 74.8 us  [along(): return lax.ppermute(x, 'dp', [(i, i ^ bit) for i in range(self.DP)])]
  transfers between devices with their start and end apart: 111 -> 114, of which waited for: 40 -> 39; matrix products, arithmetic and copies ran while one was open for 12% -> 12% of each run, Pallas kernels for 24% -> 25%
where the time goes in v4:
time: 872 us; the launch traced here: 865 us
  waiting for transfers between devices  317 us (36%)
  Pallas kernels  259 us (30%)
  starting transfers between devices  150 us (17%)
  other arithmetic  85.5 us (10%)
  local copies, waits for them, and re-layouts  45.1 us (5%)
    pallas_call x16, Pallas kernels, call(): pl.pallas_call(body, in_specs=in_specs + [any_spec()] * extra, **rest)  259 us
    ppermute x8, waiting for transfers between devices, shift(): return lax.ppermute(x, 'tensor', pairs)  108 us
    ppermute x57, waiting for transfers between devices, along(): return lax.ppermute(x, 'dp', [(i, i ^ bit) for i in range(self.DP)])  74.8 us
    ppermute x57, starting transfers between devices, along(): return lax.ppermute(x, 'dp', [(i, i ^ bit) for i in range(self.DP)])  64 us
    ppermute x5, waiting for transfers between devices, across(): lax.ppermute(x, 'tensor', [(z, (z + self.G) % self.T) for z in range(self...  50 us
    ppermute x15, waiting for transfers between devices, back(): lax.ppermute(x, 'tensor', [(order[i], order[(i - k) % self.T]) for i in r...  39.2 us
    convert_element_type x24, other arithmetic, add_low(): return total.astype(BF)  35.4 us
    ppermute x15, starting transfers between devices, back(): lax.ppermute(x, 'tensor', [(order[i], order[(i - k) % self.T]) for i in r...  31.5 us
  transfers between devices with their start and end apart: 114, of which 39 were waited for; matrix products, arithmetic and copies ran while one was open for 12% of the time, Pallas kernels for 25%

profile of v4, /device:TPU:0, one launch (start us, length us, event | category | flops | bytes accessed | tf_op | source)
XLA Modules:
  0.0 864.7 jit_solution(3283826010798832997)
XLA Ops:
  7.1 6.6 collective-permute-start
  21.1 4.3 collective-permute-done
  25.4 10.7 %collective-permute-start.1 = (bf16[512,1024]{1,0:T(8,128)(2,1)}, bf16[512,1024]{1,0:T(8,128)(2,1)S(1)}, u32[]{:S(2)}, u32[]{:S(2)}) collective-permute-start(bf16[512,1024]{1,0:T(8,128)(2,1)} %collective-permute-done), channel_id=1, source_target_pairs={{0,16},{16,0},{1,17},{17,1},{2,18},{18,2},{3,19},{19,3},{4,20},{20... | collective-permute-start | bytes 3145736 | tf_op jit(solution)/shard_map/ppermute | solution.py:872
  38.5 3.0 collective-permute-start.6
  41.5 13.3 %collective-permute-done.12 = bf16[256,384]{1,0:T(8,128)(2,1)S(1)} collective-permute-done((bf16[256,384]{1,0:T(8,128)(2,1)S(1)}, bf16[256,384]{1,0:T(8,128)(2,1)S(1)}, u32[]{:S(2)}, u32[]{:S(2)}) %collective-permute-start.12) | collective-permute-done | bytes 196640 | tf_op jit(solution)/shard_map/ppermute | solution.py:886
  67.9 3.5 broadcast_select_fusion
  74.6 29.2 %collective-permute-done.3.refs_2_ = bf16[1,512,1024]{2,1,0:T(8,128)(2,1)} collective-permute-done((bf16[1,512,1024]{2,1,0:T(8,128)(2,1)S(1)}, bf16[1,512,1024]{2,1,0:T(8,128)(2,1)}, u32[]{:S(2)}, u32[]{:S(2)}) %collective-permute-start.3) | collective-permute-done | bytes 1048608 | tf_op jit(solution)/shard_map/ppermute | solution.py:890
  114.6 8.2 collective-permute-done.11.refs_5_.refs_8_.refs_10_.refs_12_.refs_13_
  124.0 10.2 %project.2 = (bf16[4,2048,128]{2,1,0:T(8,128)(2,1)}, bf16[4,2048,128]{2,1,0:T(8,128)(2,1)}, bf16[4,2048,128]{2,1,0:T(8,128)(2,1)}) custom-call(s32[64]{0:T(128)} %fusion.75.refs_0_, bf16[2,512,1024]{2,1,0:T(8,128)(2,1)} %copy-done.10, bf16[1,512,1024]{2,1,0:T(8,128)(2,1)} %collective-permute-done.3.refs_2_, ...), custom_call_target="tpu_custom_call" | custom-call | flops 11500000256 | tf_op jit(solution)/shard_map/project/pallas_call | solution.py:71
  134.8 6.7 collective-permute-done.17.refs_6_.refs_18_.refs_8_.refs_10_.refs_11_
  145.0 8.8 %collective-permute-done.19.refs_9_.refs_11_.refs_13_.refs_14_ = bf16[1184,256]{1,0:T(8,128)(2,1)S(1)} collective-permute-done((bf16[1184,256]{1,0:T(8,128)(2,1)S(1)}, bf16[1184,256]{1,0:T(8,128)(2,1)S(1)}, u32[]{:S(2)}, u32[]{:S(2)}) %collective-permute-start.19) | collective-permute-done | bytes 606240 | tf_op jit(solution)/shard_map/ppermute | solution.py:883
  154.7 14.2 %attend.2 = (bf16[4,512,256]{2,1,0:T(8,128)(2,1)}, bf16[4,2048,128]{2,1,0:T(8,128)(2,1)}) custom-call(s32[64]{0:T(128)} %fusion.75.refs_0_, bf16[4,2048,128]{2,1,0:T(8,128)(2,1)} %get-tuple-element.93.refs_1_, bf16[4,2048,128]{2,1,0:T(8,128)(2,1)} %get-tuple-element.94.refs_2_, bf16[4,2048,128]{2,1,0:T(8,128)(2,1)} %get-tuple-element.95.refs_3_.refs_9_, ...), custom_call_target="tpu_custom_call" | custom-call | flops 16675000320 | tf_op jit(solution)/shard_map/attend/pallas_call | solution.py:71
  170.0 2.7 collective-permute-start.15
  172.8 10.6 %collective-permute-done.15 = bf16[1024,256]{1,0:T(8,128)(2,1)S(1)} collective-permute-done((bf16[1024,256]{1,0:T(8,128)(2,1)S(1)}, bf16[1024,256]{1,0:T(8,128)(2,1)S(1)}, u32[]{:S(2)}, u32[]{:S(2)}) %collective-permute-start.15) | collective-permute-done | bytes 524320 | tf_op jit(solution)/shard_map/ppermute | solution.py:890
  183.4 9.7 %collective-permute-done.24.refs_14_.refs_16_.refs_18_.refs_19_ = bf16[1184,256]{1,0:T(8,128)(2,1)} collective-permute-done((bf16[1184,256]{1,0:T(8,128)(2,1)S(1)}, bf16[1184,256]{1,0:T(8,128)(2,1)}, u32[]{:S(2)}, u32[]{:S(2)}) %collective-permute-start.24) | collective-permute-done | bytes 606240 | tf_op jit(solution)/shard_map/ppermute | solution.py:883
  193.1 4.9 output.2.refs_2_
  199.2 2.8 collective-permute-start.27
  203.7 18.3 %mlp.2 = (bf16[1024,1024]{1,0:T(8,128)(2,1)}, f32[1024,1024]{1,0:T(8,128)}, bf16[1024,1024]{1,0:T(8,128)(2,1)}, bf16[1024,704]{1,0:T(8,128)(2,1)}, bf16[1024,704...) custom-call(s32[64]{0:T(128)} %fusion.75.refs_0_, bf16[1024,1024]{1,0:T(8,128)(2,1)} %bitcast.267, ...), custom_call_target="tpu_custom_call" | custom-call | flops 21849999360 | tf_op jit(solution)/shard_map/mlp/pallas_call | solution.py:71
  222.9 3.6 collective-permute-done.28
  226.5 3.9 fusion.13
  239.0 13.1 %collective-permute-done.30.refs_5_.refs_7_.refs_9_.refs_10_ = bf16[1184,256]{1,0:T(8,128)(2,1)S(1)} collective-permute-done((bf16[1184,256]{1,0:T(8,128)(2,1)S(1)}, bf16[1184,256]{1,0:T(8,128)(2,1)S(1)}, u32[]{:S(2)}, u32[]{:S(2)}) %collective-permute-start.30) | collective-permute-done | bytes 606240 | tf_op jit(solution)/shard_map/ppermute | solution.py:883
  252.1 12.1 %collective-permute-done.31.refs_6_.refs_8_.refs_10_.refs_11_ = bf16[1184,256]{1,0:T(8,128)(2,1)S(1)} collective-permute-done((bf16[1184,256]{1,0:T(8,128)(2,1)S(1)}, bf16[1184,256]{1,0:T(8,128)(2,1)S(1)}, u32[]{:S(2)}, u32[]{:S(2)}) %collective-permute-start.31) | collective-permute-done | bytes 606240 | tf_op jit(solution)/shard_map/ppermute | solution.py:883
  265.5 16.7 %collective-permute-done.34.refs_4_.refs_8_.refs_10_.refs_12_.refs_13_ = bf16[1184,256]{1,0:T(8,128)(2,1)} collective-permute-done((bf16[1184,256]{1,0:T(8,128)(2,1)S(1)}, bf16[1184,256]{1,0:T(8,128)(2,1)}, u32[]{:S(2)}, u32[]{:S(2)}) %collective-permute-start.34) | collective-permute-done | bytes 606240 | tf_op jit(solution)/shard_map/ppermute | solution.py:876
  286.6 10.8 %project.3 = (bf16[4,2048,128]{2,1,0:T(8,128)(2,1)}, bf16[4,2048,128]{2,1,0:T(8,128)(2,1)}, bf16[4,2048,128]{2,1,0:T(8,128)(2,1)}) custom-call(s32[64]{0:T(128)} %fusion.75.refs_0_, bf16[2,512,1024]{2,1,0:T(8,128)(2,1)} %bitcast.273, bf16[1,512,1024]{2,1,0:T(8,128)(2,1)} %copy-done.88, bf16[1,512,1024]{2,1,0:T(8,128)(2,1)} %copy-done.89, ...), custom_call_target="tpu_custom_call" | custom-call | flops 11500000256 | tf_op jit(solution)/shard_map/project/pallas_call | solution.py:71
  302.0 14.4 %attend.3 = (bf16[4,512,256]{2,1,0:T(8,128)(2,1)}, bf16[4,2048,128]{2,1,0:T(8,128)(2,1)}) custom-call(s32[64]{0:T(128)} %fusion.75.refs_0_, bf16[4,2048,128]{2,1,0:T(8,128)(2,1)} %get-tuple-element.103.refs_1_, bf16[4,2048,128]{2,1,0:T(8,128)(2,1)} %get-tuple-element.104.refs_2_, bf16[4,2048,128]{2,1,0:T(8,128)(2,1)} %get-tuple-element.105.refs_3_, ...), custom_call_target="tpu_custom_call" | custom-call | flops 16675000320 | tf_op jit(solution)/shard_map/attend/pallas_call | solution.py:71
  319.6 4.1 collective-permute-start.44
  323.7 13.7 %collective-permute-done.35 = bf16[1024,256]{1,0:T(8,128)(2,1)S(1)} collective-permute-done((bf16[1024,256]{1,0:T(8,128)(2,1)S(1)}, bf16[1024,256]{1,0:T(8,128)(2,1)S(1)}, u32[]{:S(2)}, u32[]{:S(2)}) %collective-permute-start.35) | collective-permute-done | bytes 524320 | tf_op jit(solution)/shard_map/ppermute | solution.py:890
  338.2 4.9 output.3.refs_2_
  344.8 4.2 collective-permute-done.45
  350.9 18.2 %mlp.3 = (bf16[1024,1024]{1,0:T(8,128)(2,1)}, f32[1024,1024]{1,0:T(8,128)}, bf16[1024,1024]{1,0:T(8,128)(2,1)}, bf16[1024,704]{1,0:T(8,128)(2,1)}, bf16[1024,704...) custom-call(s32[64]{0:T(128)} %fusion.75.refs_0_, bf16[1024,1024]{1,0:T(8,128)(2,1)} %copy-done.4, ...), custom_call_target="tpu_custom_call" | custom-call | flops 21849999360 | tf_op jit(solution)/shard_map/mlp/pallas_call | solution.py:71
  370.5 27.8 %mlp_back.2 = (bf16[4,2112,256]{2,1,0:T(8,128)(2,1)}, bf16[4,2112,256]{2,1,0:T(8,128)(2,1)}, bf16[1024,1024]{1,0:T(8,128)(2,1)}) custom-call(s32[64]{0:T(128)} %fusion.75.refs_0_, bf16[1024,1024]{1,0:T(8,128)(2,1)} %bitcast.276, bf16[1024,1024]{1,0:T(8,128)(2,1)} %get-tuple-element.110.refs_2_, bf16[1024,704]{1,0:T(8,128)(2,1)} %get-tuple-element.111.refs_3_, ...), custom_call_target="tpu_custom_call" | custom-call | flops 32199999488 | tf_op jit(solution)/shard_map/mlp_back/pallas_call | solution.py:71
  398.5 3.2 fusion.82
  408.1 3.5 add_convert_fusion
  412.7 4.4 collective-permute-start.47
  417.1 12.4 %middle.2 = (f32[1024,1024]{1,0:T(8,128)}, f32[1,1024]{1,0:T(1,128)}, bf16[2,1024,256]{2,1,0:T(8,128)(2,1)}, bf16[4,512,256]{2,1,0:T(8,128)(2,1)}) custom-call(s32[64]{0:T(128)} %fusion.75.refs_0_, bf16[1024,1024]{1,0:T(8,128)(2,1)} %bitcast.277, bf16[1024,1024]{1,0:T(8,128)(2,1)} %get-tuple-element.118.refs_2_, ...), custom_call_target="tpu_custom_call" | custom-call | flops 14949999616 | tf_op jit(solution)/shard_map/middle/pallas_call | solution.py:71
  430.6 2.8 collective-permute-start.49
  437.3 14.6 %collective-permute-done.49 = bf16[1024,256]{1,0:T(8,128)(2,1)S(1)} collective-permute-done((bf16[1024,256]{1,0:T(8,128)(2,1)S(1)}, bf16[1024,256]{1,0:T(8,128)(2,1)S(1)}, u32[]{:S(2)}, u32[]{:S(2)}) %collective-permute-start.49) | collective-permute-done | bytes 524320 | tf_op jit(solution)/shard_map/ppermute | solution.py:890
  454.0 29.8 %attend_back.2 = (bf16[2048,256]{1,0:T(8,128)(2,1)}, bf16[2048,256]{1,0:T(8,128)(2,1)}, bf16[2048,256]{1,0:T(8,128)(2,1)}, f32[2048,256]{1,0:T(8,128)}) custom-call(s32[64]{0:T(128)} %fusion.75.refs_0_, bf16[4,2048,128]{2,1,0:T(8,128)(2,1)} %get-tuple-element.117.refs_1_, bf16[4,2048,128]{2,1,0:T(8,128)(2,1)} %get-tuple-element.104.refs_2_, ...), custom_call_target="tpu_custom_call" | custom-call | flops 33924999168 | tf_op jit(solution)/shard_map/attend_back/pallas_call | solution.py:71
  484.6 11.2 %project_back.2 = (bf16[2,512,1024]{2,1,0:T(8,128)(2,1)}, bf16[2,512,1024]{2,1,0:T(8,128)(2,1)}, bf16[4,256,768]{2,1,0:T(8,128)(2,1)}) custom-call(s32[64]{0:T(128)} %fusion.75.refs_0_, bf16[2,512,1024]{2,1,0:T(8,128)(2,1)} %bitcast.274, bf16[1,512,1024]{2,1,0:T(8,128)(2,1)} %copy-done.88, bf16[1,512,1024]{2,1,0:T(8,128)(2,1)} %copy-done.89, ...), custom_call_target="tpu_custom_call" | custom-call | flops 13799999488 | tf_op jit(solution)/shard_map/project_back/pallas_call | solution.py:71
  497.0 4.9 collective-permute-done.57
  511.0 18.1 %collective-permute-done.58 = bf16[512,1024]{1,0:T(8,128)(2,1)S(1)} collective-permute-done((bf16[512,1024]{1,0:T(8,128)(2,1)S(1)}, bf16[512,1024]{1,0:T(8,128)(2,1)S(1)}, u32[]{:S(2)}, u32[]{:S(2)}) %collective-permute-start.58) | collective-permute-done | bytes 1048608 | tf_op jit(solution)/shard_map/ppermute | solution.py:890
  531.1 2.8 fusion.32
  533.9 2.9 fusion.39
  543.7 3.7 fusion.77
  547.5 27.9 %mlp_back.3 = (bf16[4,2112,256]{2,1,0:T(8,128)(2,1)}, bf16[4,2112,256]{2,1,0:T(8,128)(2,1)}, bf16[1024,1024]{1,0:T(8,128)(2,1)}) custom-call(s32[64]{0:T(128)} %fusion.75.refs_0_, bf16[1024,1024]{1,0:T(8,128)(2,1)} %get-tuple-element.189.refs_1_, bf16[1024,1024]{1,0:T(8,128)(2,1)} %get-tuple-element.129.refs_2_, ...), custom_call_target="tpu_custom_call" | custom-call | flops 32199999488 | tf_op jit(solution)/shard_map/mlp_back/pallas_call | solution.py:71
  583.8 3.3 fusion.80
  589.5 4.9 collective-permute-done.62.refs_22_
  603.5 13.0 %middle.3 = (f32[1024,1024]{1,0:T(8,128)}, f32[1,1024]{1,0:T(1,128)}, bf16[2,1024,256]{2,1,0:T(8,128)(2,1)}, bf16[4,512,256]{2,1,0:T(8,128)(2,1)}) custom-call(s32[64]{0:T(128)} %fusion.75.refs_0_, f32[1024,1024]{1,0:T(8,128)} %get-tuple-element.190.refs_1_, bf16[1024,1024]{1,0:T(8,128)(2,1)} %get-tuple-element.134.refs_2_, bf16[1024,1024]{1,0:T(8,128)(2,1)} %copy-done.86, ...), custom_call_target="tpu_custom_call" | custom-call | flops 14949999616 | tf_op jit(solution)/shard_map/middle/pallas_call | solution.py:71
  616.4 7.4 collective-permute-done.73.refs_17_
  628.7 2.7 fusion.41
  638.0 2.8 fusion.30.refs_12_
  640.8 6.0 collective-permute-done.75
  647.6 29.7 %attend_back.3 = (bf16[2048,256]{1,0:T(8,128)(2,1)}, bf16[2048,256]{1,0:T(8,128)(2,1)}, bf16[2048,256]{1,0:T(8,128)(2,1)}) custom-call(s32[64]{0:T(128)} %fusion.75.refs_0_, bf16[4,2048,128]{2,1,0:T(8,128)(2,1)} %get-tuple-element.144.refs_1_, bf16[4,2048,128]{2,1,0:T(8,128)(2,1)} %get-tuple-element.94.refs_2_, ...), custom_call_target="tpu_custom_call" | custom-call | flops 33924999168 | tf_op jit(solution)/shard_map/attend_back/pallas_call | solution.py:71
  678.7 11.3 %project_back.3 = (bf16[2,512,1024]{2,1,0:T(8,128)(2,1)}, bf16[2,512,1024]{2,1,0:T(8,128)(2,1)}, bf16[4,256,768]{2,1,0:T(8,128)(2,1)}) custom-call(s32[64]{0:T(128)} %fusion.75.refs_0_, bf16[2,512,1024]{2,1,0:T(8,128)(2,1)} %copy-done.10, bf16[1,512,1024]{2,1,0:T(8,128)(2,1)} %collective-permute-done.3.refs_2_, ...), custom_call_target="tpu_custom_call" | custom-call | flops 13799999488 | tf_op jit(solution)/shard_map/project_back/pallas_call | solution.py:71
  705.6 15.7 %collective-permute-done.85 = bf16[512,1024]{1,0:T(8,128)(2,1)S(1)} collective-permute-done((bf16[512,1024]{1,0:T(8,128)(2,1)S(1)}, bf16[512,1024]{1,0:T(8,128)(2,1)S(1)}, u32[]{:S(2)}, u32[]{:S(2)}) %collective-permute-start.85) | collective-permute-done | bytes 1048608 | tf_op jit(solution)/shard_map/ppermute | solution.py:890
  733.9 5.3 collective-permute-done.98
  742.0 22.2 %collective-permute-done.87 = bf16[512,512]{1,0:T(8,128)(2,1)S(1)} collective-permute-done((bf16[512,512]{1,0:T(8,128)(2,1)S(1)}, bf16[512,512]{1,0:T(8,128)(2,1)S(1)}, u32[]{:S(2)}, u32[]{:S(2)}) %collective-permute-start.87) | collective-permute-done | bytes 524320 | tf_op jit(solution)/shard_map/ppermute | solution.py:886
  768.4 24.1 %collective-permute-done.105 = bf16[128,256]{1,0:T(8,128)(2,1)S(1)} collective-permute-done((bf16[128,256]{1,0:T(8,128)(2,1)S(1)}, bf16[128,256]{1,0:T(8,128)(2,1)S(1)}, u32[]{:S(2)}, u32[]{:S(2)}) %collective-permute-start.105) | collective-permute-done | bytes 65568 | tf_op jit(solution)/shard_map/ppermute | solution.py:880
  792.5 13.0 %collective-permute-start.106 = (bf16[128,256]{1,0:T(8,128)(2,1)S(1)}, bf16[128,256]{1,0:T(8,128)(2,1)S(1)}, u32[]{:S(2)}, u32[]{:S(2)}) collective-permute-start(bf16[128,256]{1,0:T(8,128)(2,1)S(1)} %get-tuple-element.234), channel_id=1, source_target_pairs={{0,1},{1,3},{3,2},{2,0},{4,5},{5,7},{7,6},{6,4},{8,9},{9,11},{11,1... | collective-permute-start | bytes 196616 | tf_op jit(solution)/shard_map/ppermute | solution.py:880
  805.5 12.3 %collective-permute-done.106 = bf16[128,256]{1,0:T(8,128)(2,1)S(1)} collective-permute-done((bf16[128,256]{1,0:T(8,128)(2,1)S(1)}, bf16[128,256]{1,0:T(8,128)(2,1)S(1)}, u32[]{:S(2)}, u32[]{:S(2)}) %collective-permute-start.106) | collective-permute-done | bytes 65568 | tf_op jit(solution)/shard_map/ppermute | solution.py:880
  817.9 3.0 collective-permute-start.92
  822.7 9.9 %collective-permute-done.93 = bf16[256,384]{1,0:T(8,128)(2,1)S(1)} collective-permute-done((bf16[256,384]{1,0:T(8,128)(2,1)S(1)}, bf16[256,384]{1,0:T(8,128)(2,1)S(1)}, u32[]{:S(2)}, u32[]{:S(2)}) %collective-permute-start.93) | collective-permute-done | bytes 196640 | tf_op jit(solution)/shard_map/ppermute | solution.py:886
  832.6 4.1 collective-permute-done.92
  852.9 2.7 collective-permute-start.112
  (515 shorter events, 206.2 us)
Async XLA Ops:
  5.6 30.4 %collective-permute-start.5 = (bf16[1024,384]{1,0:T(8,128)(2,1)}, bf16[1024,384]{1,0:T(8,128)(2,1)}, u32[]{:S(2)}, u32[]{:S(2)}) collective-permute-start(bf16[1024,384]{1,0:T(8,128)(2,1)} %pad_maximum_fusion.5), channel_id=1, source_target_pairs={{0,16},{16,0},{1,17},{17,1},{2,18},{18,2},{3,19},{19,3},{4,20},{20... | collective-permute-start | bytes 2359304 | tf_op jit(solution)/shard_map/ppermute | solution.py:872
  19.9 47.4 %collective-permute-start.9 = (bf16[1184,1024]{1,0:T(8,128)(2,1)}, bf16[1184,1024]{1,0:T(8,128)(2,1)}, u32[]{:S(2)}, u32[]{:S(2)}) collective-permute-start(bf16[1184,1024]{1,0:T(8,128)(2,1)} %pad_maximum_fusion.1), channel_id=1, source_target_pairs={{0,16},{16,0},{1,17},{17,1},{2,18},{18,2},{3,19},{19,3},{4,20},{20... | collective-permute-start | bytes 7274504 | tf_op jit(solution)/shard_map/ppermute | solution.py:872
  25.4 38.1 %collective-permute-start.1 = (bf16[512,1024]{1,0:T(8,128)(2,1)}, bf16[512,1024]{1,0:T(8,128)(2,1)S(1)}, u32[]{:S(2)}, u32[]{:S(2)}) collective-permute-start(bf16[512,1024]{1,0:T(8,128)(2,1)} %collective-permute-done), channel_id=1, source_target_pairs={{0,16},{16,0},{1,17},{17,1},{2,18},{18,2},{3,19},{19,3},{4,20},{20... | collective-permute-start | bytes 3145736 | tf_op jit(solution)/shard_map/ppermute | solution.py:872
  61.1 45.8 %collective-permute-start.14 = (bf16[512,384]{1,0:T(8,128)(2,1)S(1)}, bf16[512,384]{1,0:T(8,128)(2,1)}, u32[]{:S(2)}, u32[]{:S(2)}) collective-permute-start(bf16[512,384]{1,0:T(8,128)(2,1)S(1)} %maximum_select_fusion.3), channel_id=1, source_target_pairs={{0,8},{4,12},{8,0},{12,4},{1,9},{5,13},{9,1},{13,5},{2,10},{6,14},... | collective-permute-start | bytes 1179656 | tf_op jit(solution)/shard_map/ppermute | solution.py:883
  67.3 36.5 %collective-permute-start.3 = (bf16[1,512,1024]{2,1,0:T(8,128)(2,1)S(1)}, bf16[1,512,1024]{2,1,0:T(8,128)(2,1)}, u32[]{:S(2)}, u32[]{:S(2)}) collective-permute-start(bf16[1,512,1024]{2,1,0:T(8,128)(2,1)S(1)} %constant_dynamic-slice_fusion.7), channel_id=1, source_target_pairs={{0,1},{1,0},{2,3},{3,2},{4,5},{5,4},{6,7},{7,6},{8,9},{9,8},{10,11... | collective-permute-start | bytes 3145736 | tf_op jit(solution)/shard_map/ppermute | solution.py:890
  72.8 32.8 %collective-permute-start.10 = (bf16[1184,256]{1,0:T(8,128)(2,1)S(1)}, bf16[1184,256]{1,0:T(8,128)(2,1)}, u32[]{:S(2)}, u32[]{:S(2)}) collective-permute-start(bf16[1184,256]{1,0:T(8,128)(2,1)S(1)} %constant_dynamic-slice_fusion.4), channel_id=1, source_target_pairs={{0,1},{1,3},{3,2},{2,0},{4,5},{5,7},{7,6},{6,4},{8,9},{9,11},{11,1... | collective-permute-start | bytes 1818632 | tf_op jit(solution)/shard_map/ppermute | solution.py:876
  74.5 33.7 %collective-permute-start.8 = (bf16[512,384]{1,0:T(8,128)(2,1)S(1)}, bf16[512,384]{1,0:T(8,128)(2,1)S(1)}, u32[]{:S(2)}, u32[]{:S(2)}) collective-permute-start(bf16[512,384]{1,0:T(8,128)(2,1)S(1)} %maximum_select_fusion.2), channel_id=1, source_target_pairs={{0,8},{4,12},{8,0},{12,4},{1,9},{5,13},{9,1},{13,5},{2,10},{6,14},... | collective-permute-start | bytes 1179656 | tf_op jit(solution)/shard_map/ppermute | solution.py:883
  112.0 29.5 %collective-permute-start.17 = (bf16[1184,256]{1,0:T(8,128)(2,1)}, bf16[1184,256]{1,0:T(8,128)(2,1)S(1)}, u32[]{:S(2)}, u32[]{:S(2)}) collective-permute-start(bf16[1184,256]{1,0:T(8,128)(2,1)} %collective-permute-done.10.refs_4_.refs_6_.refs_8_.refs_9_), channel_id=1, source_target_pairs={{0,8},{4,12},{8,0},{12,4},{1,9},{5,13},{9,1},{13,5},{2,10},{6,14},... | collective-permute-start | bytes 1818632 | tf_op jit(solution)/shard_map/ppermute | solution.py:883
  112.5 30.5 %collective-permute-start.18 = (bf16[1184,256]{1,0:T(8,128)(2,1)}, bf16[1184,256]{1,0:T(8,128)(2,1)S(1)}, u32[]{:S(2)}, u32[]{:S(2)}) collective-permute-start(bf16[1184,256]{1,0:T(8,128)(2,1)} %collective-permute-done.10.refs_4_.refs_6_.refs_8_.refs_9_), channel_id=1, source_target_pairs={{0,12},{4,8},{8,4},{12,0},{1,13},{5,9},{9,5},{13,1},{2,14},{6,10},... | collective-permute-start | bytes 1818632 | tf_op jit(solution)/shard_map/ppermute | solution.py:883
  123.0 30.8 %collective-permute-start.19 = (bf16[1184,256]{1,0:T(8,128)(2,1)S(1)}, bf16[1184,256]{1,0:T(8,128)(2,1)S(1)}, u32[]{:S(2)}, u32[]{:S(2)}) collective-permute-start(bf16[1184,256]{1,0:T(8,128)(2,1)S(1)} %collective-permute-done.11.refs_5_.refs_8_.refs_10_.refs_12_.refs_13_), channel_id=1, source_target_pairs={{0,4},{4,0},{8,12},{12,8},{1,5},{5,1},{9,13},{13,9},{2,6},{6,2},{1... | collective-permute-start | bytes 1818632 | tf_op jit(solution)/shard_map/ppermute | solution.py:883
  134.2 35.8 %collective-permute-start.20 = (bf16[1184,256]{1,0:T(8,128)(2,1)S(1)}, bf16[1184,256]{1,0:T(8,128)(2,1)}, u32[]{:S(2)}, u32[]{:S(2)}) collective-permute-start(bf16[1184,256]{1,0:T(8,128)(2,1)S(1)} %collective-permute-done.11.refs_5_.refs_8_.refs_10_.refs_12_.refs_13_), channel_id=1, source_target_pairs={{0,8},{4,12},{8,0},{12,4},{1,9},{5,13},{9,1},{13,5},{2,10},{6,14},... | collective-permute-start | bytes 1818632 | tf_op jit(solution)/shard_map/ppermute | solution.py:883
  141.5 31.2 %collective-permute-start.21 = (bf16[1184,256]{1,0:T(8,128)(2,1)S(1)}, bf16[1184,256]{1,0:T(8,128)(2,1)}, u32[]{:S(2)}, u32[]{:S(2)}) collective-permute-start(bf16[1184,256]{1,0:T(8,128)(2,1)S(1)} %collective-permute-done.11.refs_5_.refs_8_.refs_10_.refs_12_.refs_13_), channel_id=1, source_target_pairs={{0,12},{4,8},{8,4},{12,0},{1,13},{5,9},{9,5},{13,1},{2,14},{6,10},... | collective-permute-start | bytes 1818632 | tf_op jit(solution)/shard_map/ppermute | solution.py:883
  142.0 41.4 %collective-permute-start.23 = (bf16[1184,256]{1,0:T(8,128)(2,1)S(1)}, bf16[1184,256]{1,0:T(8,128)(2,1)}, u32[]{:S(2)}, u32[]{:S(2)}) collective-permute-start(bf16[1184,256]{1,0:T(8,128)(2,1)S(1)} %collective-permute-done.22.refs_12_.refs_16_.refs_14_.refs_17_), channel_id=1, source_target_pairs={{0,4},{4,0},{8,12},{12,8},{1,5},{5,1},{9,13},{13,9},{2,6},{6,2},{1... | collective-permute-start | bytes 1818632 | tf_op jit(solution)/shard_map/ppermute | solution.py:883
  143.0 50.1 %collective-permute-start.24 = (bf16[1184,256]{1,0:T(8,128)(2,1)S(1)}, bf16[1184,256]{1,0:T(8,128)(2,1)}, u32[]{:S(2)}, u32[]{:S(2)}) collective-permute-start(bf16[1184,256]{1,0:T(8,128)(2,1)S(1)} %collective-permute-done.22.refs_12_.refs_16_.refs_14_.refs_17_), channel_id=1, source_target_pairs={{0,8},{4,12},{8,0},{12,4},{1,9},{5,13},{9,1},{13,5},{2,10},{6,14},... | collective-permute-start | bytes 1818632 | tf_op jit(solution)/shard_map/ppermute | solution.py:883
  153.8 39.2 %collective-permute-start.25 = (bf16[1184,256]{1,0:T(8,128)(2,1)S(1)}, bf16[1184,256]{1,0:T(8,128)(2,1)}, u32[]{:S(2)}, u32[]{:S(2)}) collective-permute-start(bf16[1184,256]{1,0:T(8,128)(2,1)S(1)} %collective-permute-done.22.refs_12_.refs_16_.refs_14_.refs_17_), channel_id=1, source_target_pairs={{0,12},{4,8},{8,4},{12,0},{1,13},{5,9},{9,5},{13,1},{2,14},{6,10},... | collective-permute-start | bytes 1818632 | tf_op jit(solution)/shard_map/ppermute | solution.py:883
  233.1 31.9 %collective-permute-start.29 = (bf16[1,512,1024]{2,1,0:T(8,128)(2,1)S(1)}, bf16[1,512,1024]{2,1,0:T(8,128)(2,1)S(1)}, u32[]{:S(2)}, u32[]{:S(2)}) collective-permute-start(bf16[1,512,1024]{2,1,0:T(8,128)(2,1)S(1)} %constant_dynamic-slice_fusion.1), channel_id=1, source_target_pairs={{0,1},{1,0},{2,3},{3,2},{4,5},{5,4},{6,7},{7,6},{8,9},{9,8},{10,11... | collective-permute-start | bytes 3145736 | tf_op jit(solution)/shard_map/ppermute | solution.py:890
  236.1 28.2 %collective-permute-start.31 = (bf16[1184,256]{1,0:T(8,128)(2,1)S(1)}, bf16[1184,256]{1,0:T(8,128)(2,1)S(1)}, u32[]{:S(2)}, u32[]{:S(2)}) collective-permute-start(bf16[1184,256]{1,0:T(8,128)(2,1)S(1)} %collective-permute-done.27.refs_4_.refs_6_.refs_8_.refs_9_), channel_id=1, source_target_pairs={{0,8},{4,12},{8,0},{12,4},{1,9},{5,13},{9,1},{13,5},{2,10},{6,14},... | collective-permute-start | bytes 1818632 | tf_op jit(solution)/shard_map/ppermute | solution.py:883
  237.4 26.9 %collective-permute-start.32 = (bf16[1184,256]{1,0:T(8,128)(2,1)S(1)}, bf16[1184,256]{1,0:T(8,128)(2,1)S(1)}, u32[]{:S(2)}, u32[]{:S(2)}) collective-permute-start(bf16[1184,256]{1,0:T(8,128)(2,1)S(1)} %collective-permute-done.27.refs_4_.refs_6_.refs_8_.refs_9_), channel_id=1, source_target_pairs={{0,12},{4,8},{8,4},{12,0},{1,13},{5,9},{9,5},{13,1},{2,14},{6,10},... | collective-permute-start | bytes 1818632 | tf_op jit(solution)/shard_map/ppermute | solution.py:883
  283.6 33.8 %collective-permute-start.37 = (bf16[1184,256]{1,0:T(8,128)(2,1)}, bf16[1184,256]{1,0:T(8,128)(2,1)}, u32[]{:S(2)}, u32[]{:S(2)}) collective-permute-start(bf16[1184,256]{1,0:T(8,128)(2,1)} %collective-permute-done.34.refs_4_.refs_8_.refs_10_.refs_12_.refs_13_), channel_id=1, source_target_pairs={{0,8},{4,12},{8,0},{12,4},{1,9},{5,13},{9,1},{13,5},{2,10},{6,14},... | collective-permute-start | bytes 1818632 | tf_op jit(solution)/shard_map/ppermute | solution.py:883
  284.2 35.4 %collective-permute-start.38 = (bf16[1184,256]{1,0:T(8,128)(2,1)}, bf16[1184,256]{1,0:T(8,128)(2,1)}, u32[]{:S(2)}, u32[]{:S(2)}) collective-permute-start(bf16[1184,256]{1,0:T(8,128)(2,1)} %collective-permute-done.34.refs_4_.refs_8_.refs_10_.refs_12_.refs_13_), channel_id=1, source_target_pairs={{0,12},{4,8},{8,4},{12,0},{1,13},{5,9},{9,5},{13,1},{2,14},{6,10},... | collective-permute-start | bytes 1818632 | tf_op jit(solution)/shard_map/ppermute | solution.py:883
  298.5 38.9 %collective-permute-start.40 = (bf16[1184,256]{1,0:T(8,128)(2,1)S(1)}, bf16[1184,256]{1,0:T(8,128)(2,1)}, u32[]{:S(2)}, u32[]{:S(2)}) collective-permute-start(bf16[1184,256]{1,0:T(8,128)(2,1)S(1)} %collective-permute-done.39.refs_12_.refs_14_.refs_16_.refs_17_), channel_id=1, source_target_pairs={{0,4},{4,0},{8,12},{12,8},{1,5},{5,1},{9,13},{13,9},{2,6},{6,2},{1... | collective-permute-start | bytes 1818632 | tf_op jit(solution)/shard_map/ppermute | solution.py:883
  300.0 37.9 %collective-permute-start.41 = (bf16[1184,256]{1,0:T(8,128)(2,1)S(1)}, bf16[1184,256]{1,0:T(8,128)(2,1)}, u32[]{:S(2)}, u32[]{:S(2)}) collective-permute-start(bf16[1184,256]{1,0:T(8,128)(2,1)S(1)} %collective-permute-done.39.refs_12_.refs_14_.refs_16_.refs_17_), channel_id=1, source_target_pairs={{0,8},{4,12},{8,0},{12,4},{1,9},{5,13},{9,1},{13,5},{2,10},{6,14},... | collective-permute-start | bytes 1818632 | tf_op jit(solution)/shard_map/ppermute | solution.py:883
  300.5 37.4 %collective-permute-start.42 = (bf16[1184,256]{1,0:T(8,128)(2,1)S(1)}, bf16[1184,256]{1,0:T(8,128)(2,1)}, u32[]{:S(2)}, u32[]{:S(2)}) collective-permute-start(bf16[1184,256]{1,0:T(8,128)(2,1)S(1)} %collective-permute-done.39.refs_12_.refs_14_.refs_16_.refs_17_), channel_id=1, source_target_pairs={{0,12},{4,8},{8,4},{12,0},{1,13},{5,9},{9,5},{13,1},{2,14},{6,10},... | collective-permute-start | bytes 1818632 | tf_op jit(solution)/shard_map/ppermute | solution.py:883
  319.6 23.6 %collective-permute-start.44 = (bf16[512,1024]{1,0:T(8,128)(2,1)S(1)}, bf16[512,1024]{1,0:T(8,128)(2,1)}, u32[]{:S(2)}, u32[]{:S(2)}) collective-permute-start(bf16[512,1024]{1,0:T(8,128)(2,1)S(1)} %dynamic-slice_bitcast_fusion.1), channel_id=1, source_target_pairs={{0,2},{1,3},{18,16},{19,17},{4,6},{5,7},{22,20},{23,21},{8,10},{9,... | collective-permute-start | bytes 3145736 | tf_op jit(solution)/shard_map/ppermute | solution.py:899
  369.1 37.0 %collective-permute-start.46 = (bf16[1024,1024]{1,0:T(8,128)(2,1)}, bf16[1024,1024]{1,0:T(8,128)(2,1)S(1)}, u32[]{:S(2)}, u32[]{:S(2)}) collective-permute-start(bf16[1024,1024]{1,0:T(8,128)(2,1)} %get-tuple-element.109), channel_id=1, source_target_pairs={{0,16},{16,0},{1,17},{17,1},{2,18},{18,2},{3,19},{19,3},{4,20},{20... | collective-permute-start | bytes 6291464 | tf_op jit(solution)/shard_map/ppermute | solution.py:872
  401.7 28.9 %collective-permute-start.50 = (bf16[2,1056,256]{2,1,0:T(8,128)(2,1)}, bf16[2,1056,256]{2,1,0:T(8,128)(2,1)S(1)}, u32[]{:S(2)}, u32[]{:S(2)}) collective-permute-start(bf16[2,1056,256]{2,1,0:T(8,128)(2,1)} %get-tuple-element.216), channel_id=1, source_target_pairs={{0,4},{4,0},{8,12},{12,8},{1,5},{5,1},{9,13},{13,9},{2,6},{6,2},{1... | collective-permute-start | bytes 3244040 | tf_op jit(solution)/shard_map/ppermute | solution.py:883
  403.7 29.7 %collective-permute-start.51 = (bf16[2,1056,256]{2,1,0:T(8,128)(2,1)}, bf16[2,1056,256]{2,1,0:T(8,128)(2,1)}, u32[]{:S(2)}, u32[]{:S(2)}) collective-permute-start(bf16[2,1056,256]{2,1,0:T(8,128)(2,1)} %get-tuple-element.215), channel_id=1, source_target_pairs={{0,8},{4,12},{8,0},{12,4},{1,9},{5,13},{9,1},{13,5},{2,10},{6,14},... | collective-permute-start | bytes 3244040 | tf_op jit(solution)/shard_map/ppermute | solution.py:883
  405.9 77.9 %collective-permute-start.52 = (bf16[2,1056,256]{2,1,0:T(8,128)(2,1)}, bf16[2,1056,256]{2,1,0:T(8,128)(2,1)}, u32[]{:S(2)}, u32[]{:S(2)}) collective-permute-start(bf16[2,1056,256]{2,1,0:T(8,128)(2,1)} %get-tuple-element.214), channel_id=1, source_target_pairs={{0,4},{4,0},{8,12},{12,8},{1,5},{5,1},{9,13},{13,9},{2,6},{6,2},{1... | collective-permute-start | bytes 3244040 | tf_op jit(solution)/shard_map/ppermute | solution.py:883
  406.1 77.8 %collective-permute-start.53 = (bf16[2,1056,256]{2,1,0:T(8,128)(2,1)}, bf16[2,1056,256]{2,1,0:T(8,128)(2,1)}, u32[]{:S(2)}, u32[]{:S(2)}) collective-permute-start(bf16[2,1056,256]{2,1,0:T(8,128)(2,1)} %get-tuple-element.213), channel_id=1, source_target_pairs={{0,8},{4,12},{8,0},{12,4},{1,9},{5,13},{9,1},{13,5},{2,10},{6,14},... | collective-permute-start | bytes 3244040 | tf_op jit(solution)/shard_map/ppermute | solution.py:883
  412.7 41.3 %collective-permute-start.47 = (bf16[512,1024]{1,0:T(8,128)(2,1)}, bf16[512,1024]{1,0:T(8,128)(2,1)}, u32[]{:S(2)}, u32[]{:S(2)}) collective-permute-start(bf16[512,1024]{1,0:T(8,128)(2,1)} %dynamic-slice_bitcast_fusion), channel_id=1, source_target_pairs={{0,2},{1,3},{18,16},{19,17},{4,6},{5,7},{22,20},{23,21},{8,10},{9,... | collective-permute-start | bytes 3145736 | tf_op jit(solution)/shard_map/ppermute | solution.py:899
  436.0 47.8 %collective-permute-start.54 = (bf16[1056,256]{1,0:T(8,128)(2,1)}, bf16[1056,256]{1,0:T(8,128)(2,1)S(1)}, u32[]{:S(2)}, u32[]{:S(2)}) collective-permute-start(bf16[1056,256]{1,0:T(8,128)(2,1)} %get-tuple-element.212), channel_id=1, source_target_pairs={{0,4},{4,0},{8,12},{12,8},{1,5},{5,1},{9,13},{13,9},{2,6},{6,2},{1... | collective-permute-start | bytes 1622024 | tf_op jit(solution)/shard_map/ppermute | solution.py:883
  452.7 31.1 %collective-permute-start.55 = (bf16[1056,256]{1,0:T(8,128)(2,1)}, bf16[1056,256]{1,0:T(8,128)(2,1)}, u32[]{:S(2)}, u32[]{:S(2)}) collective-permute-start(bf16[1056,256]{1,0:T(8,128)(2,1)} %get-tuple-element.211), channel_id=1, source_target_pairs={{0,8},{4,12},{8,0},{12,4},{1,9},{5,13},{9,1},{13,5},{2,10},{6,14},... | collective-permute-start | bytes 1622024 | tf_op jit(solution)/shard_map/ppermute | solution.py:883
  503.8 25.3 %collective-permute-start.58 = (bf16[512,1024]{1,0:T(8,128)(2,1)S(1)}, bf16[512,1024]{1,0:T(8,128)(2,1)S(1)}, u32[]{:S(2)}, u32[]{:S(2)}) collective-permute-start(bf16[512,1024]{1,0:T(8,128)(2,1)S(1)} %fusion.34), channel_id=1, source_target_pairs={{0,1},{1,0},{2,3},{3,2},{4,5},{5,4},{6,7},{7,6},{8,9},{9,8},{10,11... | collective-permute-start | bytes 3145736 | tf_op jit(solution)/shard_map/ppermute | solution.py:890
  506.8 68.5 %collective-permute-start.65 = (bf16[2,128,768]{2,1,0:T(8,128)(2,1)}, bf16[2,128,768]{2,1,0:T(8,128)(2,1)S(1)}, u32[]{:S(2)}, u32[]{:S(2)}) collective-permute-start(bf16[2,128,768]{2,1,0:T(8,128)(2,1)} %get-tuple-element.230), channel_id=1, source_target_pairs={{0,4},{4,0},{8,12},{12,8},{1,5},{5,1},{9,13},{13,9},{2,6},{6,2},{1... | collective-permute-start | bytes 1179656 | tf_op jit(solution)/shard_map/ppermute | solution.py:883
  507.7 69.0 %collective-permute-start.66 = (bf16[2,128,768]{2,1,0:T(8,128)(2,1)}, bf16[2,128,768]{2,1,0:T(8,128)(2,1)}, u32[]{:S(2)}, u32[]{:S(2)}) collective-permute-start(bf16[2,128,768]{2,1,0:T(8,128)(2,1)} %get-tuple-element.229), channel_id=1, source_target_pairs={{0,8},{4,12},{8,0},{12,4},{1,9},{5,13},{9,1},{13,5},{2,10},{6,14},... | collective-permute-start | bytes 1179656 | tf_op jit(solution)/shard_map/ppermute | solution.py:883
  508.5 28.4 %collective-permute-start.63 = (bf16[2,256,256]{2,1,0:T(8,128)(2,1)S(1)}, bf16[2,256,256]{2,1,0:T(8,128)(2,1)S(1)}, u32[]{:S(2)}, u32[]{:S(2)}) collective-permute-start(bf16[2,256,256]{2,1,0:T(8,128)(2,1)S(1)} %get-tuple-element.258), channel_id=1, source_target_pairs={{0,4},{4,0},{8,12},{12,8},{1,5},{5,1},{9,13},{13,9},{2,6},{6,2},{1... | collective-permute-start | bytes 786440 | tf_op jit(solution)/shard_map/ppermute | solution.py:883
  509.7 29.4 %collective-permute-start.64 = (bf16[2,256,256]{2,1,0:T(8,128)(2,1)S(1)}, bf16[2,256,256]{2,1,0:T(8,128)(2,1)S(1)}, u32[]{:S(2)}, u32[]{:S(2)}) collective-permute-start(bf16[2,256,256]{2,1,0:T(8,128)(2,1)S(1)} %get-tuple-element.257), channel_id=1, source_target_pairs={{0,8},{4,12},{8,0},{12,4},{1,9},{5,13},{9,1},{13,5},{2,10},{6,14},... | collective-permute-start | bytes 786440 | tf_op jit(solution)/shard_map/ppermute | solution.py:883
  536.8 51.7 %collective-permute-start.67 = (bf16[1056,256]{1,0:T(8,128)(2,1)}, bf16[1056,256]{1,0:T(8,128)(2,1)}, u32[]{:S(2)}, u32[]{:S(2)}) collective-permute-start(bf16[1056,256]{1,0:T(8,128)(2,1)} %get-tuple-element.208), channel_id=1, source_target_pairs={{0,2},{1,0},{3,1},{2,3},{4,6},{5,4},{7,5},{6,7},{8,10},{9,8},{11,9... | collective-permute-start | bytes 1622024 | tf_op jit(solution)/shard_map/ppermute | solution.py:880
  539.1 58.9 %collective-permute-start.68 = (bf16[1056,256]{1,0:T(8,128)(2,1)S(1)}, bf16[1056,256]{1,0:T(8,128)(2,1)}, u32[]{:S(2)}, u32[]{:S(2)}) collective-permute-start(bf16[1056,256]{1,0:T(8,128)(2,1)S(1)} %get-tuple-element.207), channel_id=1, source_target_pairs={{0,3},{1,2},{3,0},{2,1},{4,7},{5,6},{7,4},{6,5},{8,11},{9,10},{11,... | collective-permute-start | bytes 1622024 | tf_op jit(solution)/shard_map/ppermute | solution.py:880
  541.1 36.6 %collective-permute-start.69 = (bf16[256,256]{1,0:T(8,128)(2,1)}, bf16[256,256]{1,0:T(8,128)(2,1)S(1)}, u32[]{:S(2)}, u32[]{:S(2)}) collective-permute-start(bf16[256,256]{1,0:T(8,128)(2,1)} %get-tuple-element.256), channel_id=1, source_target_pairs={{0,4},{4,0},{8,12},{12,8},{1,5},{5,1},{9,13},{13,9},{2,6},{6,2},{1... | collective-permute-start | bytes 393224 | tf_op jit(solution)/shard_map/ppermute | solution.py:883
  576.7 25.4 %collective-permute-start.60 = (bf16[1024,1024]{1,0:T(8,128)(2,1)}, bf16[1024,1024]{1,0:T(8,128)(2,1)S(1)}, u32[]{:S(2)}, u32[]{:S(2)}) collective-permute-start(bf16[1024,1024]{1,0:T(8,128)(2,1)} %get-tuple-element.134.refs_2_), channel_id=1, source_target_pairs={{0,16},{16,0},{1,17},{17,1},{2,18},{18,2},{3,19},{19,3},{4,20},{20... | collective-permute-start | bytes 6291464 | tf_op jit(solution)/shard_map/ppermute | solution.py:872
  598.0 34.2 %collective-permute-start.77 = (bf16[128,256]{1,0:T(8,128)(2,1)}, bf16[128,256]{1,0:T(8,128)(2,1)S(1)}, u32[]{:S(2)}, u32[]{:S(2)}) collective-permute-start(bf16[128,256]{1,0:T(8,128)(2,1)} %get-tuple-element.254), channel_id=1, source_target_pairs={{0,2},{1,0},{3,1},{2,3},{4,6},{5,4},{7,5},{6,7},{8,10},{9,8},{11,9... | collective-permute-start | bytes 196616 | tf_op jit(solution)/shard_map/ppermute | solution.py:880
  598.4 35.1 %collective-permute-start.78 = (bf16[128,256]{1,0:T(8,128)(2,1)}, bf16[128,256]{1,0:T(8,128)(2,1)S(1)}, u32[]{:S(2)}, u32[]{:S(2)}) collective-permute-start(bf16[128,256]{1,0:T(8,128)(2,1)} %get-tuple-element.236), channel_id=1, source_target_pairs={{0,3},{1,2},{3,0},{2,1},{4,7},{5,6},{7,4},{6,5},{8,11},{9,10},{11,... | collective-permute-start | bytes 196616 | tf_op jit(solution)/shard_map/ppermute | solution.py:880
  600.8 33.4 %collective-permute-start.79 = (bf16[128,256]{1,0:T(8,128)(2,1)}, bf16[128,256]{1,0:T(8,128)(2,1)}, u32[]{:S(2)}, u32[]{:S(2)}) collective-permute-start(bf16[128,256]{1,0:T(8,128)(2,1)} %get-tuple-element.235), channel_id=1, source_target_pairs={{0,1},{1,3},{3,2},{2,0},{4,5},{5,7},{7,6},{6,4},{8,9},{9,11},{11,1... | collective-permute-start | bytes 196616 | tf_op jit(solution)/shard_map/ppermute | solution.py:880
  602.1 24.3 %collective-permute-start.74 = (bf16[2,1056,256]{2,1,0:T(8,128)(2,1)}, bf16[2,1056,256]{2,1,0:T(8,128)(2,1)}, u32[]{:S(2)}, u32[]{:S(2)}) collective-permute-start(bf16[2,1056,256]{2,1,0:T(8,128)(2,1)} %get-tuple-element.205), channel_id=1, source_target_pairs={{0,8},{4,12},{8,0},{12,4},{1,9},{5,13},{9,1},{13,5},{2,10},{6,14},... | collective-permute-start | bytes 3244040 | tf_op jit(solution)/shard_map/ppermute | solution.py:883
  626.4 51.0 %collective-permute-start.80 = (bf16[2,1056,256]{2,1,0:T(8,128)(2,1)}, bf16[2,1056,256]{2,1,0:T(8,128)(2,1)}, u32[]{:S(2)}, u32[]{:S(2)}) collective-permute-start(bf16[2,1056,256]{2,1,0:T(8,128)(2,1)} %get-tuple-element.204), channel_id=1, source_target_pairs={{0,4},{4,0},{8,12},{12,8},{1,5},{5,1},{9,13},{13,9},{2,6},{6,2},{1... | collective-permute-start | bytes 3244040 | tf_op jit(solution)/shard_map/ppermute | solution.py:883
  632.2 45.2 %collective-permute-start.81 = (bf16[2,1056,256]{2,1,0:T(8,128)(2,1)}, bf16[2,1056,256]{2,1,0:T(8,128)(2,1)S(1)}, u32[]{:S(2)}, u32[]{:S(2)}) collective-permute-start(bf16[2,1056,256]{2,1,0:T(8,128)(2,1)} %get-tuple-element.203), channel_id=1, source_target_pairs={{0,8},{4,12},{8,0},{12,4},{1,9},{5,13},{9,1},{13,5},{2,10},{6,14},... | collective-permute-start | bytes 3244040 | tf_op jit(solution)/shard_map/ppermute | solution.py:883
  634.2 43.2 %collective-permute-start.82 = (bf16[1056,256]{1,0:T(8,128)(2,1)}, bf16[1056,256]{1,0:T(8,128)(2,1)S(1)}, u32[]{:S(2)}, u32[]{:S(2)}) collective-permute-start(bf16[1056,256]{1,0:T(8,128)(2,1)} %get-tuple-element.202), channel_id=1, source_target_pairs={{0,4},{4,0},{8,12},{12,8},{1,5},{5,1},{9,13},{13,9},{2,6},{6,2},{1... | collective-permute-start | bytes 1622024 | tf_op jit(solution)/shard_map/ppermute | solution.py:883
  634.2 43.2 %collective-permute-start.83 = (bf16[1056,256]{1,0:T(8,128)(2,1)}, bf16[1056,256]{1,0:T(8,128)(2,1)S(1)}, u32[]{:S(2)}, u32[]{:S(2)}) collective-permute-start(bf16[1056,256]{1,0:T(8,128)(2,1)} %get-tuple-element.201), channel_id=1, source_target_pairs={{0,8},{4,12},{8,0},{12,4},{1,9},{5,13},{9,1},{13,5},{2,10},{6,14},... | collective-permute-start | bytes 1622024 | tf_op jit(solution)/shard_map/ppermute | solution.py:883
  696.1 25.3 %collective-permute-start.85 = (bf16[512,1024]{1,0:T(8,128)(2,1)S(1)}, bf16[512,1024]{1,0:T(8,128)(2,1)S(1)}, u32[]{:S(2)}, u32[]{:S(2)}) collective-permute-start(bf16[512,1024]{1,0:T(8,128)(2,1)S(1)} %fusion.35), channel_id=1, source_target_pairs={{0,1},{1,0},{2,3},{3,2},{4,5},{5,4},{6,7},{7,6},{8,9},{9,8},{10,11... | collective-permute-start | bytes 3145736 | tf_op jit(solution)/shard_map/ppermute | solution.py:890
  699.7 24.3 %collective-permute-start.101 = (bf16[256,256]{1,0:T(8,128)(2,1)S(1)}, bf16[256,256]{1,0:T(8,128)(2,1)S(1)}, u32[]{:S(2)}, u32[]{:S(2)}) collective-permute-start(bf16[256,256]{1,0:T(8,128)(2,1)S(1)} %get-tuple-element.250), channel_id=1, source_target_pairs={{0,8},{4,12},{8,0},{12,4},{1,9},{5,13},{9,1},{13,5},{2,10},{6,14},... | collective-permute-start | bytes 393224 | tf_op jit(solution)/shard_map/ppermute | solution.py:883
  701.1 23.3 %collective-permute-start.104 = (bf16[256,256]{1,0:T(8,128)(2,1)S(1)}, bf16[256,256]{1,0:T(8,128)(2,1)S(1)}, u32[]{:S(2)}, u32[]{:S(2)}) collective-permute-start(bf16[256,256]{1,0:T(8,128)(2,1)S(1)} %get-tuple-element.251), channel_id=1, source_target_pairs={{0,4},{4,0},{8,12},{12,8},{1,5},{5,1},{9,13},{13,9},{2,6},{6,2},{1... | collective-permute-start | bytes 393224 | tf_op jit(solution)/shard_map/ppermute | solution.py:883
  703.4 23.2 %collective-permute-start.88 = (bf16[2,128,768]{2,1,0:T(8,128)(2,1)S(1)}, bf16[2,128,768]{2,1,0:T(8,128)(2,1)S(1)}, u32[]{:S(2)}, u32[]{:S(2)}) collective-permute-start(bf16[2,128,768]{2,1,0:T(8,128)(2,1)S(1)} %get-tuple-element.223), channel_id=1, source_target_pairs={{0,4},{4,0},{8,12},{12,8},{1,5},{5,1},{9,13},{13,9},{2,6},{6,2},{1... | collective-permute-start | bytes 1179656 | tf_op jit(solution)/shard_map/ppermute | solution.py:883
  704.9 23.2 %collective-permute-start.90 = (bf16[2,128,768]{2,1,0:T(8,128)(2,1)S(1)}, bf16[2,128,768]{2,1,0:T(8,128)(2,1)S(1)}, u32[]{:S(2)}, u32[]{:S(2)}) collective-permute-start(bf16[2,128,768]{2,1,0:T(8,128)(2,1)S(1)} %get-tuple-element.224), channel_id=1, source_target_pairs={{0,8},{4,12},{8,0},{12,4},{1,9},{5,13},{9,1},{13,5},{2,10},{6,14},... | collective-permute-start | bytes 1179656 | tf_op jit(solution)/shard_map/ppermute | solution.py:883
  724.5 93.4 %collective-permute-start.95 = (bf16[1056,256]{1,0:T(8,128)(2,1)S(1)}, bf16[1056,256]{1,0:T(8,128)(2,1)S(1)}, u32[]{:S(2)}, u32[]{:S(2)}) collective-permute-start(bf16[1056,256]{1,0:T(8,128)(2,1)S(1)} %get-tuple-element.197), channel_id=1, source_target_pairs={{0,4},{4,0},{8,12},{12,8},{1,5},{5,1},{9,13},{13,9},{2,6},{6,2},{1... | collective-permute-start | bytes 1622024 | tf_op jit(solution)/shard_map/ppermute | solution.py:883
  726.6 37.6 %collective-permute-start.102 = (bf16[128,256]{1,0:T(8,128)(2,1)S(1)}, bf16[128,256]{1,0:T(8,128)(2,1)S(1)}, u32[]{:S(2)}, u32[]{:S(2)}) collective-permute-start(bf16[128,256]{1,0:T(8,128)(2,1)S(1)} %get-tuple-element.249), channel_id=1, source_target_pairs={{0,2},{1,0},{3,1},{2,3},{4,6},{5,4},{7,5},{6,7},{8,10},{9,8},{11,9... | collective-permute-start | bytes 196616 | tf_op jit(solution)/shard_map/ppermute | solution.py:880
  728.3 38.1 %collective-permute-start.89 = (bf16[128,768]{1,0:T(8,128)(2,1)S(1)}, bf16[128,768]{1,0:T(8,128)(2,1)S(1)}, u32[]{:S(2)}, u32[]{:S(2)}) collective-permute-start(bf16[128,768]{1,0:T(8,128)(2,1)S(1)} %get-tuple-element.221), channel_id=1, source_target_pairs={{0,8},{4,12},{8,0},{12,4},{1,9},{5,13},{9,1},{13,5},{2,10},{6,14},... | collective-permute-start | bytes 589832 | tf_op jit(solution)/shard_map/ppermute | solution.py:883
  728.6 39.4 %collective-permute-start.91 = (bf16[128,768]{1,0:T(8,128)(2,1)S(1)}, bf16[128,768]{1,0:T(8,128)(2,1)S(1)}, u32[]{:S(2)}, u32[]{:S(2)}) collective-permute-start(bf16[128,768]{1,0:T(8,128)(2,1)S(1)} %get-tuple-element.222), channel_id=1, source_target_pairs={{0,4},{4,0},{8,12},{12,8},{1,5},{5,1},{9,13},{13,9},{2,6},{6,2},{1... | collective-permute-start | bytes 589832 | tf_op jit(solution)/shard_map/ppermute | solution.py:883
  739.2 25.0 %collective-permute-start.87 = (bf16[512,512]{1,0:T(8,128)(2,1)S(1)}, bf16[512,512]{1,0:T(8,128)(2,1)S(1)}, u32[]{:S(2)}, u32[]{:S(2)}) collective-permute-start(bf16[512,512]{1,0:T(8,128)(2,1)S(1)} %fusion.44), channel_id=1, source_target_pairs={{0,2},{1,3},{2,0},{3,1},{4,6},{5,7},{6,4},{7,5},{8,10},{9,11},{10,... | collective-permute-start | bytes 1572872 | tf_op jit(solution)/shard_map/ppermute | solution.py:886
  764.2 56.7 %collective-permute-start.96 = (bf16[1056,256]{1,0:T(8,128)(2,1)S(1)}, bf16[1056,256]{1,0:T(8,128)(2,1)S(1)}, u32[]{:S(2)}, u32[]{:S(2)}) collective-permute-start(bf16[1056,256]{1,0:T(8,128)(2,1)S(1)} %get-tuple-element.199), channel_id=1, source_target_pairs={{0,2},{1,0},{3,1},{2,3},{4,6},{5,4},{7,5},{6,7},{8,10},{9,8},{11,9... | collective-permute-start | bytes 1622024 | tf_op jit(solution)/shard_map/ppermute | solution.py:880
  764.2 56.7 %collective-permute-start.97 = (bf16[1056,256]{1,0:T(8,128)(2,1)S(1)}, bf16[1056,256]{1,0:T(8,128)(2,1)S(1)}, u32[]{:S(2)}, u32[]{:S(2)}) collective-permute-start(bf16[1056,256]{1,0:T(8,128)(2,1)S(1)} %get-tuple-element.200), channel_id=1, source_target_pairs={{0,3},{1,2},{3,0},{2,1},{4,7},{5,6},{7,4},{6,5},{8,11},{9,10},{11,... | collective-permute-start | bytes 1622024 | tf_op jit(solution)/shard_map/ppermute | solution.py:880
  766.4 26.1 %collective-permute-start.105 = (bf16[128,256]{1,0:T(8,128)(2,1)S(1)}, bf16[128,256]{1,0:T(8,128)(2,1)S(1)}, u32[]{:S(2)}, u32[]{:S(2)}) collective-permute-start(bf16[128,256]{1,0:T(8,128)(2,1)S(1)} %get-tuple-element.233), channel_id=1, source_target_pairs={{0,3},{1,2},{3,0},{2,1},{4,7},{5,6},{7,4},{6,5},{8,11},{9,10},{11,... | collective-permute-start | bytes 196616 | tf_op jit(solution)/shard_map/ppermute | solution.py:880
  768.0 52.8 %collective-permute-start.99 = (bf16[1056,256]{1,0:T(8,128)(2,1)S(1)}, bf16[1056,256]{1,0:T(8,128)(2,1)S(1)}, u32[]{:S(2)}, u32[]{:S(2)}) collective-permute-start(bf16[1056,256]{1,0:T(8,128)(2,1)S(1)} %fusion.20), channel_id=1, source_target_pairs={{0,1},{1,3},{3,2},{2,0},{4,5},{5,7},{7,6},{6,4},{8,9},{9,11},{11,1... | collective-permute-start | bytes 1622024 | tf_op jit(solution)/shard_map/ppermute | solution.py:880
  792.5 25.3 %collective-permute-start.106 = (bf16[128,256]{1,0:T(8,128)(2,1)S(1)}, bf16[128,256]{1,0:T(8,128)(2,1)S(1)}, u32[]{:S(2)}, u32[]{:S(2)}) collective-permute-start(bf16[128,256]{1,0:T(8,128)(2,1)S(1)} %get-tuple-element.234), channel_id=1, source_target_pairs={{0,1},{1,3},{3,2},{2,0},{4,5},{5,7},{7,6},{6,4},{8,9},{9,11},{11,1... | collective-permute-start | bytes 196616 | tf_op jit(solution)/shard_map/ppermute | solution.py:880
  (155 other events, 1807.0 us)

commit v5 on v4

--- a/solution.py
+++ b/solution.py
@@ -1185,7 +1185,8 @@
                 gather.step(layer)
             w_proj[1] = projection.layer(1)
         elif layer == 0:
-            deps[1] = rings[:2] + w_proj[1:]
+            deps[1] = rings[:2]
+            deps[3] = w_proj[1:]
             deps[2] = rings[2:] + first[1]
         else:
             deps[1] = gather.step(1, a_blocks.arrays[1])[0]

time: 872 us -> 892 us (1.023)
  waiting for transfers between devices: 317 us -> 335 us
    ppermute x57, waiting for transfers between devices: 74.8 us -> 101 us  [along(): return lax.ppermute(x, 'dp', [(i, i ^ bit) for i in range(self.DP)])]
  transfers between devices with their start and end apart: 114 -> 114, of which waited for: 39 -> 40; matrix products, arithmetic and copies ran while one was open for 12% -> 12% of each run, Pallas kernels for 25% -> 24%
where the time goes in v5:
time: 892 us; the launch traced here: 882 us
  waiting for transfers between devices  335 us (38%)
  Pallas kernels  260 us (29%)
  starting transfers between devices  149 us (17%)
  other arithmetic  85.4 us (10%)
  local copies, waits for them, and re-layouts  44.7 us (5%)
    pallas_call x16, Pallas kernels, call(): pl.pallas_call(body, in_specs=in_specs + [any_spec()] * extra, **rest)  260 us
    ppermute x8, waiting for transfers between devices, shift(): return lax.ppermute(x, 'tensor', pairs)  108 us
    ppermute x57, waiting for transfers between devices, along(): return lax.ppermute(x, 'dp', [(i, i ^ bit) for i in range(self.DP)])  101 us
    ppermute x57, starting transfers between devices, along(): return lax.ppermute(x, 'dp', [(i, i ^ bit) for i in range(self.DP)])  68.2 us
    ppermute x5, waiting for transfers between devices, across(): lax.ppermute(x, 'tensor', [(z, (z + self.G) % self.T) for z in range(self...  46.6 us
    ppermute x15, waiting for transfers between devices, back(): lax.ppermute(x, 'tensor', [(order[i], order[(i - k) % self.T]) for i in r...  39.7 us
    convert_element_type x24, other arithmetic, add_low(): return total.astype(BF)  35.3 us
    ppermute x15, starting transfers between devices, back(): lax.ppermute(x, 'tensor', [(order[i], order[(i - k) % self.T]) for i in r...  30.7 us
  transfers between devices with their start and end apart: 114, of which 40 were waited for; matrix products, arithmetic and copies ran while one was open for 12% of the time, Pallas kernels for 24%

profile of v5, /device:TPU:0, one launch (start us, length us, event | category | flops | bytes accessed | tf_op | source)
XLA Modules:
  0.0 881.9 jit_solution(15475911667829588039)
XLA Ops:
  3.1 7.0 collective-permute-start
  18.4 3.2 collective-permute-done
  21.7 10.0 %collective-permute-start.1 = (bf16[512,1024]{1,0:T(8,128)(2,1)}, bf16[512,1024]{1,0:T(8,128)(2,1)}, u32[]{:S(2)}, u32[]{:S(2)}) collective-permute-start(bf16[512,1024]{1,0:T(8,128)(2,1)} %collective-permute-done), channel_id=1, source_target_pairs={{0,16},{16,0},{1,17},{17,1},{2,18},{18,2},{3,19},{19,3},{4,20},{20... | collective-permute-start | bytes 3145736 | tf_op jit(solution)/shard_map/ppermute | solution.py:872
  42.6 5.8 collective-permute-start.3
  48.4 3.5 broadcast_select_fusion
  55.1 30.0 %collective-permute-done.3.refs_2_ = bf16[1,512,1024]{2,1,0:T(8,128)(2,1)} collective-permute-done((bf16[1,512,1024]{2,1,0:T(8,128)(2,1)}, bf16[1,512,1024]{2,1,0:T(8,128)(2,1)}, u32[]{:S(2)}, u32[]{:S(2)}) %collective-permute-start.3) | collective-permute-done | bytes 1048608 | tf_op jit(solution)/shard_map/ppermute | solution.py:890
  89.9 8.1 collective-permute-done.8
  106.3 10.2 %project.2 = (bf16[4,2048,128]{2,1,0:T(8,128)(2,1)}, bf16[4,2048,128]{2,1,0:T(8,128)(2,1)}, bf16[4,2048,128]{2,1,0:T(8,128)(2,1)}) custom-call(s32[64]{0:T(128)} %fusion.75.refs_0_, bf16[2,512,1024]{2,1,0:T(8,128)(2,1)} %copy-done.9, bf16[1,512,1024]{2,1,0:T(8,128)(2,1)} %collective-permute-done.3.refs_2_, ...), custom_call_target="tpu_custom_call" | custom-call | flops 11500000256 | tf_op jit(solution)/shard_map/project/pallas_call | solution.py:71
  117.7 11.6 %collective-permute-done.14.refs_6_.refs_18_.refs_8_.refs_10_.refs_11_ = bf16[1184,256]{1,0:T(8,128)(2,1)} collective-permute-done((bf16[1184,256]{1,0:T(8,128)(2,1)S(1)}, bf16[1184,256]{1,0:T(8,128)(2,1)}, u32[]{:S(2)}, u32[]{:S(2)}) %collective-permute-start.14) | collective-permute-done | bytes 606240 | tf_op jit(solution)/shard_map/ppermute | solution.py:883
  130.0 3.3 collective-permute-start.20
  133.4 9.0 %collective-permute-done.16.refs_9_.refs_11_.refs_13_.refs_14_ = bf16[1184,256]{1,0:T(8,128)(2,1)} collective-permute-done((bf16[1184,256]{1,0:T(8,128)(2,1)S(1)}, bf16[1184,256]{1,0:T(8,128)(2,1)}, u32[]{:S(2)}, u32[]{:S(2)}) %collective-permute-start.16) | collective-permute-done | bytes 606240 | tf_op jit(solution)/shard_map/ppermute | solution.py:883
  144.8 14.4 %attend.2 = (bf16[4,512,256]{2,1,0:T(8,128)(2,1)}, bf16[4,2048,128]{2,1,0:T(8,128)(2,1)}) custom-call(s32[64]{0:T(128)} %fusion.75.refs_0_, bf16[4,2048,128]{2,1,0:T(8,128)(2,1)} %get-tuple-element.93.refs_1_, bf16[4,2048,128]{2,1,0:T(8,128)(2,1)} %get-tuple-element.94.refs_2_, bf16[4,2048,128]{2,1,0:T(8,128)(2,1)} %get-tuple-element.95.refs_3_.refs_9_, ...), custom_call_target="tpu_custom_call" | custom-call | flops 16675000320 | tf_op jit(solution)/shard_map/attend/pallas_call | solution.py:71
  160.4 11.1 %collective-permute-done.12 = bf16[1024,256]{1,0:T(8,128)(2,1)S(1)} collective-permute-done((bf16[1024,256]{1,0:T(8,128)(2,1)S(1)}, bf16[1024,256]{1,0:T(8,128)(2,1)S(1)}, u32[]{:S(2)}, u32[]{:S(2)}) %collective-permute-start.12) | collective-permute-done | bytes 524320 | tf_op jit(solution)/shard_map/ppermute | solution.py:890
  171.5 9.6 %collective-permute-done.21.refs_14_.refs_16_.refs_18_.refs_19_ = bf16[1184,256]{1,0:T(8,128)(2,1)S(1)} collective-permute-done((bf16[1184,256]{1,0:T(8,128)(2,1)}, bf16[1184,256]{1,0:T(8,128)(2,1)S(1)}, u32[]{:S(2)}, u32[]{:S(2)}) %collective-permute-start.21) | collective-permute-done | bytes 606240 | tf_op jit(solution)/shard_map/ppermute | solution.py:883
  182.1 4.9 output.2.refs_2_
  187.2 11.6 %collective-permute-done.24 = bf16[256,384]{1,0:T(8,128)(2,1)S(1)} collective-permute-done((bf16[256,384]{1,0:T(8,128)(2,1)S(1)}, bf16[256,384]{1,0:T(8,128)(2,1)S(1)}, u32[]{:S(2)}, u32[]{:S(2)}) %collective-permute-start.24) | collective-permute-done | bytes 196640 | tf_op jit(solution)/shard_map/ppermute | solution.py:886
  200.0 5.8 collective-permute-done.25
  207.4 8.7 collective-permute-done.26
  220.3 18.7 %mlp.2 = (bf16[1024,1024]{1,0:T(8,128)(2,1)}, f32[1024,1024]{1,0:T(8,128)}, bf16[1024,1024]{1,0:T(8,128)(2,1)}, bf16[1024,704]{1,0:T(8,128)(2,1)}, bf16[1024,704...) custom-call(s32[64]{0:T(128)} %fusion.75.refs_0_, bf16[1024,1024]{1,0:T(8,128)(2,1)} %bitcast.267, ...), custom_call_target="tpu_custom_call" | custom-call | flops 21849999360 | tf_op jit(solution)/shard_map/mlp/pallas_call | solution.py:71
  239.8 3.7 collective-permute-done.28
  243.4 3.9 fusion.13
  256.1 13.1 %collective-permute-done.30.refs_5_.refs_7_.refs_9_.refs_10_ = bf16[1184,256]{1,0:T(8,128)(2,1)S(1)} collective-permute-done((bf16[1184,256]{1,0:T(8,128)(2,1)S(1)}, bf16[1184,256]{1,0:T(8,128)(2,1)S(1)}, u32[]{:S(2)}, u32[]{:S(2)}) %collective-permute-start.30) | collective-permute-done | bytes 606240 | tf_op jit(solution)/shard_map/ppermute | solution.py:883
  269.2 11.2 %collective-permute-done.31.refs_6_.refs_8_.refs_10_.refs_11_ = bf16[1184,256]{1,0:T(8,128)(2,1)S(1)} collective-permute-done((bf16[1184,256]{1,0:T(8,128)(2,1)S(1)}, bf16[1184,256]{1,0:T(8,128)(2,1)S(1)}, u32[]{:S(2)}, u32[]{:S(2)}) %collective-permute-start.31) | collective-permute-done | bytes 606240 | tf_op jit(solution)/shard_map/ppermute | solution.py:883
  282.5 16.7 %collective-permute-done.34.refs_4_.refs_8_.refs_10_.refs_12_.refs_13_ = bf16[1184,256]{1,0:T(8,128)(2,1)} collective-permute-done((bf16[1184,256]{1,0:T(8,128)(2,1)S(1)}, bf16[1184,256]{1,0:T(8,128)(2,1)}, u32[]{:S(2)}, u32[]{:S(2)}) %collective-permute-start.34) | collective-permute-done | bytes 606240 | tf_op jit(solution)/shard_map/ppermute | solution.py:876
  303.7 10.8 %project.3 = (bf16[4,2048,128]{2,1,0:T(8,128)(2,1)}, bf16[4,2048,128]{2,1,0:T(8,128)(2,1)}, bf16[4,2048,128]{2,1,0:T(8,128)(2,1)}) custom-call(s32[64]{0:T(128)} %fusion.75.refs_0_, bf16[2,512,1024]{2,1,0:T(8,128)(2,1)} %bitcast.273, bf16[1,512,1024]{2,1,0:T(8,128)(2,1)} %copy-done.84, bf16[1,512,1024]{2,1,0:T(8,128)(2,1)} %copy-done.85, ...), custom_call_target="tpu_custom_call" | custom-call | flops 11500000256 | tf_op jit(solution)/shard_map/project/pallas_call | solution.py:71
  319.0 14.5 %attend.3 = (bf16[4,512,256]{2,1,0:T(8,128)(2,1)}, bf16[4,2048,128]{2,1,0:T(8,128)(2,1)}) custom-call(s32[64]{0:T(128)} %fusion.75.refs_0_, bf16[4,2048,128]{2,1,0:T(8,128)(2,1)} %get-tuple-element.103.refs_1_, bf16[4,2048,128]{2,1,0:T(8,128)(2,1)} %get-tuple-element.104.refs_2_, bf16[4,2048,128]{2,1,0:T(8,128)(2,1)} %get-tuple-element.105.refs_3_, ...), custom_call_target="tpu_custom_call" | custom-call | flops 16675000320 | tf_op jit(solution)/shard_map/attend/pallas_call | solution.py:71
  336.8 3.5 collective-permute-start.44
  340.3 14.8 %collective-permute-done.35 = bf16[1024,256]{1,0:T(8,128)(2,1)S(1)} collective-permute-done((bf16[1024,256]{1,0:T(8,128)(2,1)S(1)}, bf16[1024,256]{1,0:T(8,128)(2,1)S(1)}, u32[]{:S(2)}, u32[]{:S(2)}) %collective-permute-start.35) | collective-permute-done | bytes 524320 | tf_op jit(solution)/shard_map/ppermute | solution.py:890
  356.0 4.9 output.3.refs_2_
  361.6 5.1 collective-permute-done.45
  368.4 18.4 %mlp.3 = (bf16[1024,1024]{1,0:T(8,128)(2,1)}, f32[1024,1024]{1,0:T(8,128)}, bf16[1024,1024]{1,0:T(8,128)(2,1)}, bf16[1024,704]{1,0:T(8,128)(2,1)}, bf16[1024,704...) custom-call(s32[64]{0:T(128)} %fusion.75.refs_0_, bf16[1024,1024]{1,0:T(8,128)(2,1)} %copy-done.4, ...), custom_call_target="tpu_custom_call" | custom-call | flops 21849999360 | tf_op jit(solution)/shard_map/mlp/pallas_call | solution.py:71
  388.3 27.9 %mlp_back.2 = (bf16[4,2112,256]{2,1,0:T(8,128)(2,1)}, bf16[4,2112,256]{2,1,0:T(8,128)(2,1)}, bf16[1024,1024]{1,0:T(8,128)(2,1)}) custom-call(s32[64]{0:T(128)} %fusion.75.refs_0_, bf16[1024,1024]{1,0:T(8,128)(2,1)} %bitcast.276, bf16[1024,1024]{1,0:T(8,128)(2,1)} %get-tuple-element.110.refs_2_, bf16[1024,704]{1,0:T(8,128)(2,1)} %get-tuple-element.111.refs_3_, ...), custom_call_target="tpu_custom_call" | custom-call | flops 32199999488 | tf_op jit(solution)/shard_map/mlp_back/pallas_call | solution.py:71
  416.2 3.2 fusion.82
  426.0 3.5 add_convert_fusion
  430.6 4.6 collective-permute-start.47
  435.2 12.4 %middle.2 = (f32[1024,1024]{1,0:T(8,128)}, f32[1,1024]{1,0:T(1,128)}, bf16[2,1024,256]{2,1,0:T(8,128)(2,1)}, bf16[4,512,256]{2,1,0:T(8,128)(2,1)}) custom-call(s32[64]{0:T(128)} %fusion.75.refs_0_, bf16[1024,1024]{1,0:T(8,128)(2,1)} %bitcast.277, bf16[1024,1024]{1,0:T(8,128)(2,1)} %get-tuple-element.118.refs_2_, ...), custom_call_target="tpu_custom_call" | custom-call | flops 14949999616 | tf_op jit(solution)/shard_map/middle/pallas_call | solution.py:71
  448.7 2.7 collective-permute-start.49
  455.4 14.3 %collective-permute-done.49 = bf16[1024,256]{1,0:T(8,128)(2,1)S(1)} collective-permute-done((bf16[1024,256]{1,0:T(8,128)(2,1)S(1)}, bf16[1024,256]{1,0:T(8,128)(2,1)S(1)}, u32[]{:S(2)}, u32[]{:S(2)}) %collective-permute-start.49) | collective-permute-done | bytes 524320 | tf_op jit(solution)/shard_map/ppermute | solution.py:890
  471.4 29.8 %attend_back.2 = (bf16[2048,256]{1,0:T(8,128)(2,1)}, bf16[2048,256]{1,0:T(8,128)(2,1)}, bf16[2048,256]{1,0:T(8,128)(2,1)}, f32[2048,256]{1,0:T(8,128)}) custom-call(s32[64]{0:T(128)} %fusion.75.refs_0_, bf16[4,2048,128]{2,1,0:T(8,128)(2,1)} %get-tuple-element.117.refs_1_, bf16[4,2048,128]{2,1,0:T(8,128)(2,1)} %get-tuple-element.104.refs_2_, ...), custom_call_target="tpu_custom_call" | custom-call | flops 33924999168 | tf_op jit(solution)/shard_map/attend_back/pallas_call | solution.py:71
  502.0 11.2 %project_back.2 = (bf16[2,512,1024]{2,1,0:T(8,128)(2,1)}, bf16[2,512,1024]{2,1,0:T(8,128)(2,1)}, bf16[4,256,768]{2,1,0:T(8,128)(2,1)}) custom-call(s32[64]{0:T(128)} %fusion.75.refs_0_, bf16[2,512,1024]{2,1,0:T(8,128)(2,1)} %bitcast.274, bf16[1,512,1024]{2,1,0:T(8,128)(2,1)} %copy-done.84, bf16[1,512,1024]{2,1,0:T(8,128)(2,1)} %copy-done.85, ...), custom_call_target="tpu_custom_call" | custom-call | flops 13799999488 | tf_op jit(solution)/shard_map/project_back/pallas_call | solution.py:71
  514.4 4.8 collective-permute-done.57
  528.3 18.1 %collective-permute-done.58 = bf16[512,1024]{1,0:T(8,128)(2,1)S(1)} collective-permute-done((bf16[512,1024]{1,0:T(8,128)(2,1)S(1)}, bf16[512,1024]{1,0:T(8,128)(2,1)S(1)}, u32[]{:S(2)}, u32[]{:S(2)}) %collective-permute-start.58) | collective-permute-done | bytes 1048608 | tf_op jit(solution)/shard_map/ppermute | solution.py:890
  548.4 2.8 fusion.32
  551.3 2.9 fusion.39
  561.8 3.7 fusion.77
  565.5 27.9 %mlp_back.3 = (bf16[4,2112,256]{2,1,0:T(8,128)(2,1)}, bf16[4,2112,256]{2,1,0:T(8,128)(2,1)}, bf16[1024,1024]{1,0:T(8,128)(2,1)}) custom-call(s32[64]{0:T(128)} %fusion.75.refs_0_, bf16[1024,1024]{1,0:T(8,128)(2,1)} %get-tuple-element.189.refs_1_, bf16[1024,1024]{1,0:T(8,128)(2,1)} %get-tuple-element.129.refs_2_, ...), custom_call_target="tpu_custom_call" | custom-call | flops 32199999488 | tf_op jit(solution)/shard_map/mlp_back/pallas_call | solution.py:71
  601.4 3.2 fusion.80
  607.6 4.8 collective-permute-done.62.refs_22_
  621.6 12.9 %middle.3 = (f32[1024,1024]{1,0:T(8,128)}, f32[1,1024]{1,0:T(1,128)}, bf16[2,1024,256]{2,1,0:T(8,128)(2,1)}, bf16[4,512,256]{2,1,0:T(8,128)(2,1)}) custom-call(s32[64]{0:T(128)} %fusion.75.refs_0_, f32[1024,1024]{1,0:T(8,128)} %get-tuple-element.190.refs_1_, bf16[1024,1024]{1,0:T(8,128)(2,1)} %get-tuple-element.134.refs_2_, bf16[1024,1024]{1,0:T(8,128)(2,1)} %copy-done.82, ...), custom_call_target="tpu_custom_call" | custom-call | flops 14949999616 | tf_op jit(solution)/shard_map/middle/pallas_call | solution.py:71
  634.5 6.9 collective-permute-done.73.refs_17_
  646.8 2.7 fusion.41
  656.1 2.8 fusion.30.refs_12_
  658.9 5.1 collective-permute-done.75
  664.8 29.7 %attend_back.3 = (bf16[2048,256]{1,0:T(8,128)(2,1)}, bf16[2048,256]{1,0:T(8,128)(2,1)}, bf16[2048,256]{1,0:T(8,128)(2,1)}) custom-call(s32[64]{0:T(128)} %fusion.75.refs_0_, bf16[4,2048,128]{2,1,0:T(8,128)(2,1)} %get-tuple-element.144.refs_1_, bf16[4,2048,128]{2,1,0:T(8,128)(2,1)} %get-tuple-element.94.refs_2_, ...), custom_call_target="tpu_custom_call" | custom-call | flops 33924999168 | tf_op jit(solution)/shard_map/attend_back/pallas_call | solution.py:71
  695.9 11.3 %project_back.3 = (bf16[2,512,1024]{2,1,0:T(8,128)(2,1)}, bf16[2,512,1024]{2,1,0:T(8,128)(2,1)}, bf16[4,256,768]{2,1,0:T(8,128)(2,1)}) custom-call(s32[64]{0:T(128)} %fusion.75.refs_0_, bf16[2,512,1024]{2,1,0:T(8,128)(2,1)} %copy-done.9, bf16[1,512,1024]{2,1,0:T(8,128)(2,1)} %collective-permute-done.3.refs_2_, ...), custom_call_target="tpu_custom_call" | custom-call | flops 13799999488 | tf_op jit(solution)/shard_map/project_back/pallas_call | solution.py:71
  723.8 14.7 %collective-permute-done.85 = bf16[512,1024]{1,0:T(8,128)(2,1)S(1)} collective-permute-done((bf16[512,1024]{1,0:T(8,128)(2,1)S(1)}, bf16[512,1024]{1,0:T(8,128)(2,1)S(1)}, u32[]{:S(2)}, u32[]{:S(2)}) %collective-permute-start.85) | collective-permute-done | bytes 1048608 | tf_op jit(solution)/shard_map/ppermute | solution.py:890
  751.6 4.8 collective-permute-done.98
  759.7 21.7 %collective-permute-done.87 = bf16[512,512]{1,0:T(8,128)(2,1)S(1)} collective-permute-done((bf16[512,512]{1,0:T(8,128)(2,1)S(1)}, bf16[512,512]{1,0:T(8,128)(2,1)S(1)}, u32[]{:S(2)}, u32[]{:S(2)}) %collective-permute-start.87) | collective-permute-done | bytes 524320 | tf_op jit(solution)/shard_map/ppermute | solution.py:886
  785.6 24.5 %collective-permute-done.105 = bf16[128,256]{1,0:T(8,128)(2,1)S(1)} collective-permute-done((bf16[128,256]{1,0:T(8,128)(2,1)S(1)}, bf16[128,256]{1,0:T(8,128)(2,1)S(1)}, u32[]{:S(2)}, u32[]{:S(2)}) %collective-permute-start.105) | collective-permute-done | bytes 65568 | tf_op jit(solution)/shard_map/ppermute | solution.py:880
  810.1 12.9 %collective-permute-start.106 = (bf16[128,256]{1,0:T(8,128)(2,1)S(1)}, bf16[128,256]{1,0:T(8,128)(2,1)S(1)}, u32[]{:S(2)}, u32[]{:S(2)}) collective-permute-start(bf16[128,256]{1,0:T(8,128)(2,1)S(1)} %get-tuple-element.234), channel_id=1, source_target_pairs={{0,1},{1,3},{3,2},{2,0},{4,5},{5,7},{7,6},{6,4},{8,9},{9,11},{11,1... | collective-permute-start | bytes 196616 | tf_op jit(solution)/shard_map/ppermute | solution.py:880
  823.0 12.3 %collective-permute-done.106 = bf16[128,256]{1,0:T(8,128)(2,1)S(1)} collective-permute-done((bf16[128,256]{1,0:T(8,128)(2,1)S(1)}, bf16[128,256]{1,0:T(8,128)(2,1)S(1)}, u32[]{:S(2)}, u32[]{:S(2)}) %collective-permute-start.106) | collective-permute-done | bytes 65568 | tf_op jit(solution)/shard_map/ppermute | solution.py:880
  835.3 3.0 collective-permute-start.92
  840.2 9.2 %collective-permute-done.93 = bf16[256,384]{1,0:T(8,128)(2,1)S(1)} collective-permute-done((bf16[256,384]{1,0:T(8,128)(2,1)S(1)}, bf16[256,384]{1,0:T(8,128)(2,1)S(1)}, u32[]{:S(2)}, u32[]{:S(2)}) %collective-permute-start.93) | collective-permute-done | bytes 196640 | tf_op jit(solution)/shard_map/ppermute | solution.py:886
  849.4 4.1 collective-permute-done.92
  (507 shorter events, 210.8 us)
Async XLA Ops:
  12.1 23.0 %collective-permute-start.5 = (bf16[1024,384]{1,0:T(8,128)(2,1)}, bf16[1024,384]{1,0:T(8,128)(2,1)}, u32[]{:S(2)}, u32[]{:S(2)}) collective-permute-start(bf16[1024,384]{1,0:T(8,128)(2,1)} %pad_maximum_fusion.5), channel_id=1, source_target_pairs={{0,16},{16,0},{1,17},{17,1},{2,18},{18,2},{3,19},{19,3},{4,20},{20... | collective-permute-start | bytes 2359304 | tf_op jit(solution)/shard_map/ppermute | solution.py:872
  17.9 30.5 %collective-permute-start.9 = (bf16[1184,1024]{1,0:T(8,128)(2,1)}, bf16[1184,1024]{1,0:T(8,128)(2,1)}, u32[]{:S(2)}, u32[]{:S(2)}) collective-permute-start(bf16[1184,1024]{1,0:T(8,128)(2,1)} %pad_maximum_fusion.1), channel_id=1, source_target_pairs={{0,16},{16,0},{1,17},{17,1},{2,18},{18,2},{3,19},{19,3},{4,20},{20... | collective-permute-start | bytes 7274504 | tf_op jit(solution)/shard_map/ppermute | solution.py:872
  42.6 42.5 %collective-permute-start.3 = (bf16[1,512,1024]{2,1,0:T(8,128)(2,1)}, bf16[1,512,1024]{2,1,0:T(8,128)(2,1)}, u32[]{:S(2)}, u32[]{:S(2)}) collective-permute-start(bf16[1,512,1024]{2,1,0:T(8,128)(2,1)} %constant_dynamic-slice_fusion.7), channel_id=1, source_target_pairs={{0,1},{1,0},{2,3},{3,2},{4,5},{5,4},{6,7},{7,6},{8,9},{9,8},{10,11... | collective-permute-start | bytes 3145736 | tf_op jit(solution)/shard_map/ppermute | solution.py:890
  53.4 34.6 %collective-permute-start.10 = (bf16[1184,256]{1,0:T(8,128)(2,1)S(1)}, bf16[1184,256]{1,0:T(8,128)(2,1)S(1)}, u32[]{:S(2)}, u32[]{:S(2)}) collective-permute-start(bf16[1184,256]{1,0:T(8,128)(2,1)S(1)} %constant_dynamic-slice_fusion.4), channel_id=1, source_target_pairs={{0,1},{1,3},{3,2},{2,0},{4,5},{5,7},{7,6},{6,4},{8,9},{9,11},{11,1... | collective-permute-start | bytes 1818632 | tf_op jit(solution)/shard_map/ppermute | solution.py:876
  53.5 32.8 %collective-permute-start.7 = (bf16[256,384]{1,0:T(8,128)(2,1)S(1)}, bf16[256,384]{1,0:T(8,128)(2,1)S(1)}, u32[]{:S(2)}, u32[]{:S(2)}) collective-permute-start(bf16[256,384]{1,0:T(8,128)(2,1)S(1)} %collective-permute-done.6), channel_id=1, source_target_pairs={{0,4},{4,0},{8,12},{12,8},{1,5},{5,1},{9,13},{13,9},{2,6},{6,2},{1... | collective-permute-start | bytes 589832 | tf_op jit(solution)/shard_map/ppermute | solution.py:883
  101.1 28.2 %collective-permute-start.14 = (bf16[1184,256]{1,0:T(8,128)(2,1)S(1)}, bf16[1184,256]{1,0:T(8,128)(2,1)}, u32[]{:S(2)}, u32[]{:S(2)}) collective-permute-start(bf16[1184,256]{1,0:T(8,128)(2,1)S(1)} %collective-permute-done.10.refs_4_.refs_6_.refs_8_.refs_9_), channel_id=1, source_target_pairs={{0,8},{4,12},{8,0},{12,4},{1,9},{5,13},{9,1},{13,5},{2,10},{6,14},... | collective-permute-start | bytes 1818632 | tf_op jit(solution)/shard_map/ppermute | solution.py:883
  102.6 30.7 %collective-permute-start.15 = (bf16[1184,256]{1,0:T(8,128)(2,1)S(1)}, bf16[1184,256]{1,0:T(8,128)(2,1)}, u32[]{:S(2)}, u32[]{:S(2)}) collective-permute-start(bf16[1184,256]{1,0:T(8,128)(2,1)S(1)} %collective-permute-done.10.refs_4_.refs_6_.refs_8_.refs_9_), channel_id=1, source_target_pairs={{0,12},{4,8},{8,4},{12,0},{1,13},{5,9},{9,5},{13,1},{2,14},{6,10},... | collective-permute-start | bytes 1818632 | tf_op jit(solution)/shard_map/ppermute | solution.py:883
  104.8 25.3 %collective-permute-start.19 = (bf16[1184,256]{1,0:T(8,128)(2,1)S(1)}, bf16[1184,256]{1,0:T(8,128)(2,1)}, u32[]{:S(2)}, u32[]{:S(2)}) collective-permute-start(bf16[1184,256]{1,0:T(8,128)(2,1)S(1)} %collective-permute-done.11.refs_5_.refs_8_.refs_10_.refs_12_.refs_13_), channel_id=1, source_target_pairs={{0,1},{1,3},{3,2},{2,0},{4,5},{5,7},{7,6},{6,4},{8,9},{9,11},{11,1... | collective-permute-start | bytes 1818632 | tf_op jit(solution)/shard_map/ppermute | solution.py:876
  104.8 37.6 %collective-permute-start.16 = (bf16[1184,256]{1,0:T(8,128)(2,1)S(1)}, bf16[1184,256]{1,0:T(8,128)(2,1)}, u32[]{:S(2)}, u32[]{:S(2)}) collective-permute-start(bf16[1184,256]{1,0:T(8,128)(2,1)S(1)} %collective-permute-done.11.refs_5_.refs_8_.refs_10_.refs_12_.refs_13_), channel_id=1, source_target_pairs={{0,4},{4,0},{8,12},{12,8},{1,5},{5,1},{9,13},{13,9},{2,6},{6,2},{1... | collective-permute-start | bytes 1818632 | tf_op jit(solution)/shard_map/ppermute | solution.py:883
  116.6 43.8 %collective-permute-start.17 = (bf16[1184,256]{1,0:T(8,128)(2,1)S(1)}, bf16[1184,256]{1,0:T(8,128)(2,1)}, u32[]{:S(2)}, u32[]{:S(2)}) collective-permute-start(bf16[1184,256]{1,0:T(8,128)(2,1)S(1)} %collective-permute-done.11.refs_5_.refs_8_.refs_10_.refs_12_.refs_13_), channel_id=1, source_target_pairs={{0,8},{4,12},{8,0},{12,4},{1,9},{5,13},{9,1},{13,5},{2,10},{6,14},... | collective-permute-start | bytes 1818632 | tf_op jit(solution)/shard_map/ppermute | solution.py:883
  129.3 31.1 %collective-permute-start.18 = (bf16[1184,256]{1,0:T(8,128)(2,1)S(1)}, bf16[1184,256]{1,0:T(8,128)(2,1)}, u32[]{:S(2)}, u32[]{:S(2)}) collective-permute-start(bf16[1184,256]{1,0:T(8,128)(2,1)S(1)} %collective-permute-done.11.refs_5_.refs_8_.refs_10_.refs_12_.refs_13_), channel_id=1, source_target_pairs={{0,12},{4,8},{8,4},{12,0},{1,13},{5,9},{9,5},{13,1},{2,14},{6,10},... | collective-permute-start | bytes 1818632 | tf_op jit(solution)/shard_map/ppermute | solution.py:883
  130.0 41.5 %collective-permute-start.20 = (bf16[1184,256]{1,0:T(8,128)(2,1)}, bf16[1184,256]{1,0:T(8,128)(2,1)}, u32[]{:S(2)}, u32[]{:S(2)}) collective-permute-start(bf16[1184,256]{1,0:T(8,128)(2,1)} %collective-permute-done.19.refs_12_.refs_16_.refs_14_.refs_17_), channel_id=1, source_target_pairs={{0,4},{4,0},{8,12},{12,8},{1,5},{5,1},{9,13},{13,9},{2,6},{6,2},{1... | collective-permute-start | bytes 1818632 | tf_op jit(solution)/shard_map/ppermute | solution.py:883
  133.4 47.8 %collective-permute-start.21 = (bf16[1184,256]{1,0:T(8,128)(2,1)}, bf16[1184,256]{1,0:T(8,128)(2,1)S(1)}, u32[]{:S(2)}, u32[]{:S(2)}) collective-permute-start(bf16[1184,256]{1,0:T(8,128)(2,1)} %collective-permute-done.19.refs_12_.refs_16_.refs_14_.refs_17_), channel_id=1, source_target_pairs={{0,8},{4,12},{8,0},{12,4},{1,9},{5,13},{9,1},{13,5},{2,10},{6,14},... | collective-permute-start | bytes 1818632 | tf_op jit(solution)/shard_map/ppermute | solution.py:883
  142.3 38.8 %collective-permute-start.22 = (bf16[1184,256]{1,0:T(8,128)(2,1)}, bf16[1184,256]{1,0:T(8,128)(2,1)S(1)}, u32[]{:S(2)}, u32[]{:S(2)}) collective-permute-start(bf16[1184,256]{1,0:T(8,128)(2,1)} %collective-permute-done.19.refs_12_.refs_16_.refs_14_.refs_17_), channel_id=1, source_target_pairs={{0,12},{4,8},{8,4},{12,0},{1,13},{5,9},{9,5},{13,1},{2,14},{6,10},... | collective-permute-start | bytes 1818632 | tf_op jit(solution)/shard_map/ppermute | solution.py:883
  187.0 31.9 %collective-permute-start.23 = (bf16[1024,1024]{1,0:T(8,128)(2,1)}, bf16[1024,1024]{1,0:T(8,128)(2,1)S(1)}, u32[]{:S(2)}, u32[]{:S(2)}) collective-permute-start(bf16[1024,1024]{1,0:T(8,128)(2,1)} %output.2.refs_2_), channel_id=1, source_target_pairs={{0,16},{16,0},{1,17},{17,1},{2,18},{18,2},{3,19},{19,3},{4,20},{20... | collective-permute-start | bytes 6291464 | tf_op jit(solution)/shard_map/ppermute | solution.py:872
  250.1 32.0 %collective-permute-start.29 = (bf16[1,512,1024]{2,1,0:T(8,128)(2,1)S(1)}, bf16[1,512,1024]{2,1,0:T(8,128)(2,1)S(1)}, u32[]{:S(2)}, u32[]{:S(2)}) collective-permute-start(bf16[1,512,1024]{2,1,0:T(8,128)(2,1)S(1)} %constant_dynamic-slice_fusion.1), channel_id=1, source_target_pairs={{0,1},{1,0},{2,3},{3,2},{4,5},{5,4},{6,7},{7,6},{8,9},{9,8},{10,11... | collective-permute-start | bytes 3145736 | tf_op jit(solution)/shard_map/ppermute | solution.py:890
  253.7 26.6 %collective-permute-start.31 = (bf16[1184,256]{1,0:T(8,128)(2,1)S(1)}, bf16[1184,256]{1,0:T(8,128)(2,1)S(1)}, u32[]{:S(2)}, u32[]{:S(2)}) collective-permute-start(bf16[1184,256]{1,0:T(8,128)(2,1)S(1)} %copy-done.92), channel_id=1, source_target_pairs={{0,8},{4,12},{8,0},{12,4},{1,9},{5,13},{9,1},{13,5},{2,10},{6,14},... | collective-permute-start | bytes 1818632 | tf_op jit(solution)/shard_map/ppermute | solution.py:883
  254.7 27.3 %collective-permute-start.32 = (bf16[1184,256]{1,0:T(8,128)(2,1)S(1)}, bf16[1184,256]{1,0:T(8,128)(2,1)S(1)}, u32[]{:S(2)}, u32[]{:S(2)}) collective-permute-start(bf16[1184,256]{1,0:T(8,128)(2,1)S(1)} %copy-done.92), channel_id=1, source_target_pairs={{0,12},{4,8},{8,4},{12,0},{1,13},{5,9},{9,5},{13,1},{2,14},{6,10},... | collective-permute-start | bytes 1818632 | tf_op jit(solution)/shard_map/ppermute | solution.py:883
  300.7 33.9 %collective-permute-start.37 = (bf16[1184,256]{1,0:T(8,128)(2,1)}, bf16[1184,256]{1,0:T(8,128)(2,1)}, u32[]{:S(2)}, u32[]{:S(2)}) collective-permute-start(bf16[1184,256]{1,0:T(8,128)(2,1)} %collective-permute-done.34.refs_4_.refs_8_.refs_10_.refs_12_.refs_13_), channel_id=1, source_target_pairs={{0,8},{4,12},{8,0},{12,4},{1,9},{5,13},{9,1},{13,5},{2,10},{6,14},... | collective-permute-start | bytes 1818632 | tf_op jit(solution)/shard_map/ppermute | solution.py:883
  302.2 34.6 %collective-permute-start.38 = (bf16[1184,256]{1,0:T(8,128)(2,1)}, bf16[1184,256]{1,0:T(8,128)(2,1)}, u32[]{:S(2)}, u32[]{:S(2)}) collective-permute-start(bf16[1184,256]{1,0:T(8,128)(2,1)} %collective-permute-done.34.refs_4_.refs_8_.refs_10_.refs_12_.refs_13_), channel_id=1, source_target_pairs={{0,12},{4,8},{8,4},{12,0},{1,13},{5,9},{9,5},{13,1},{2,14},{6,10},... | collective-permute-start | bytes 1818632 | tf_op jit(solution)/shard_map/ppermute | solution.py:883
  315.6 39.6 %collective-permute-start.40 = (bf16[1184,256]{1,0:T(8,128)(2,1)S(1)}, bf16[1184,256]{1,0:T(8,128)(2,1)}, u32[]{:S(2)}, u32[]{:S(2)}) collective-permute-start(bf16[1184,256]{1,0:T(8,128)(2,1)S(1)} %collective-permute-done.39.refs_12_.refs_14_.refs_16_.refs_17_), channel_id=1, source_target_pairs={{0,4},{4,0},{8,12},{12,8},{1,5},{5,1},{9,13},{13,9},{2,6},{6,2},{1... | collective-permute-start | bytes 1818632 | tf_op jit(solution)/shard_map/ppermute | solution.py:883
  317.1 38.0 %collective-permute-start.41 = (bf16[1184,256]{1,0:T(8,128)(2,1)S(1)}, bf16[1184,256]{1,0:T(8,128)(2,1)}, u32[]{:S(2)}, u32[]{:S(2)}) collective-permute-start(bf16[1184,256]{1,0:T(8,128)(2,1)S(1)} %collective-permute-done.39.refs_12_.refs_14_.refs_16_.refs_17_), channel_id=1, source_target_pairs={{0,8},{4,12},{8,0},{12,4},{1,9},{5,13},{9,1},{13,5},{2,10},{6,14},... | collective-permute-start | bytes 1818632 | tf_op jit(solution)/shard_map/ppermute | solution.py:883
  318.6 36.5 %collective-permute-start.42 = (bf16[1184,256]{1,0:T(8,128)(2,1)S(1)}, bf16[1184,256]{1,0:T(8,128)(2,1)}, u32[]{:S(2)}, u32[]{:S(2)}) collective-permute-start(bf16[1184,256]{1,0:T(8,128)(2,1)S(1)} %collective-permute-done.39.refs_12_.refs_14_.refs_16_.refs_17_), channel_id=1, source_target_pairs={{0,12},{4,8},{8,4},{12,0},{1,13},{5,9},{9,5},{13,1},{2,14},{6,10},... | collective-permute-start | bytes 1818632 | tf_op jit(solution)/shard_map/ppermute | solution.py:883
  336.8 24.1 %collective-permute-start.44 = (bf16[512,1024]{1,0:T(8,128)(2,1)S(1)}, bf16[512,1024]{1,0:T(8,128)(2,1)}, u32[]{:S(2)}, u32[]{:S(2)}) collective-permute-start(bf16[512,1024]{1,0:T(8,128)(2,1)S(1)} %dynamic-slice_bitcast_fusion.1), channel_id=1, source_target_pairs={{0,2},{1,3},{18,16},{19,17},{4,6},{5,7},{22,20},{23,21},{8,10},{9,... | collective-permute-start | bytes 3145736 | tf_op jit(solution)/shard_map/ppermute | solution.py:899
  386.8 37.9 %collective-permute-start.46 = (bf16[1024,1024]{1,0:T(8,128)(2,1)}, bf16[1024,1024]{1,0:T(8,128)(2,1)S(1)}, u32[]{:S(2)}, u32[]{:S(2)}) collective-permute-start(bf16[1024,1024]{1,0:T(8,128)(2,1)} %get-tuple-element.109), channel_id=1, source_target_pairs={{0,16},{16,0},{1,17},{17,1},{2,18},{18,2},{3,19},{19,3},{4,20},{20... | collective-permute-start | bytes 6291464 | tf_op jit(solution)/shard_map/ppermute | solution.py:872
  419.5 29.2 %collective-permute-start.50 = (bf16[2,1056,256]{2,1,0:T(8,128)(2,1)}, bf16[2,1056,256]{2,1,0:T(8,128)(2,1)S(1)}, u32[]{:S(2)}, u32[]{:S(2)}) collective-permute-start(bf16[2,1056,256]{2,1,0:T(8,128)(2,1)} %get-tuple-element.216), channel_id=1, source_target_pairs={{0,4},{4,0},{8,12},{12,8},{1,5},{5,1},{9,13},{13,9},{2,6},{6,2},{1... | collective-permute-start | bytes 3244040 | tf_op jit(solution)/shard_map/ppermute | solution.py:883
  421.0 30.3 %collective-permute-start.51 = (bf16[2,1056,256]{2,1,0:T(8,128)(2,1)}, bf16[2,1056,256]{2,1,0:T(8,128)(2,1)}, u32[]{:S(2)}, u32[]{:S(2)}) collective-permute-start(bf16[2,1056,256]{2,1,0:T(8,128)(2,1)} %get-tuple-element.215), channel_id=1, source_target_pairs={{0,8},{4,12},{8,0},{12,4},{1,9},{5,13},{9,1},{13,5},{2,10},{6,14},... | collective-permute-start | bytes 3244040 | tf_op jit(solution)/shard_map/ppermute | solution.py:883
  424.1 77.1 %collective-permute-start.52 = (bf16[2,1056,256]{2,1,0:T(8,128)(2,1)}, bf16[2,1056,256]{2,1,0:T(8,128)(2,1)}, u32[]{:S(2)}, u32[]{:S(2)}) collective-permute-start(bf16[2,1056,256]{2,1,0:T(8,128)(2,1)} %get-tuple-element.214), channel_id=1, source_target_pairs={{0,4},{4,0},{8,12},{12,8},{1,5},{5,1},{9,13},{13,9},{2,6},{6,2},{1... | collective-permute-start | bytes 3244040 | tf_op jit(solution)/shard_map/ppermute | solution.py:883
  424.7 76.5 %collective-permute-start.53 = (bf16[2,1056,256]{2,1,0:T(8,128)(2,1)}, bf16[2,1056,256]{2,1,0:T(8,128)(2,1)}, u32[]{:S(2)}, u32[]{:S(2)}) collective-permute-start(bf16[2,1056,256]{2,1,0:T(8,128)(2,1)} %get-tuple-element.213), channel_id=1, source_target_pairs={{0,8},{4,12},{8,0},{12,4},{1,9},{5,13},{9,1},{13,5},{2,10},{6,14},... | collective-permute-start | bytes 3244040 | tf_op jit(solution)/shard_map/ppermute | solution.py:883
  430.6 40.8 %collective-permute-start.47 = (bf16[512,1024]{1,0:T(8,128)(2,1)}, bf16[512,1024]{1,0:T(8,128)(2,1)}, u32[]{:S(2)}, u32[]{:S(2)}) collective-permute-start(bf16[512,1024]{1,0:T(8,128)(2,1)} %dynamic-slice_bitcast_fusion), channel_id=1, source_target_pairs={{0,2},{1,3},{18,16},{19,17},{4,6},{5,7},{22,20},{23,21},{8,10},{9,... | collective-permute-start | bytes 3145736 | tf_op jit(solution)/shard_map/ppermute | solution.py:899
  453.9 47.2 %collective-permute-start.54 = (bf16[1056,256]{1,0:T(8,128)(2,1)}, bf16[1056,256]{1,0:T(8,128)(2,1)S(1)}, u32[]{:S(2)}, u32[]{:S(2)}) collective-permute-start(bf16[1056,256]{1,0:T(8,128)(2,1)} %get-tuple-element.212), channel_id=1, source_target_pairs={{0,4},{4,0},{8,12},{12,8},{1,5},{5,1},{9,13},{13,9},{2,6},{6,2},{1... | collective-permute-start | bytes 1622024 | tf_op jit(solution)/shard_map/ppermute | solution.py:883
  470.6 30.6 %collective-permute-start.55 = (bf16[1056,256]{1,0:T(8,128)(2,1)}, bf16[1056,256]{1,0:T(8,128)(2,1)}, u32[]{:S(2)}, u32[]{:S(2)}) collective-permute-start(bf16[1056,256]{1,0:T(8,128)(2,1)} %get-tuple-element.211), channel_id=1, source_target_pairs={{0,8},{4,12},{8,0},{12,4},{1,9},{5,13},{9,1},{13,5},{2,10},{6,14},... | collective-permute-start | bytes 1622024 | tf_op jit(solution)/shard_map/ppermute | solution.py:883
  521.2 25.3 %collective-permute-start.58 = (bf16[512,1024]{1,0:T(8,128)(2,1)S(1)}, bf16[512,1024]{1,0:T(8,128)(2,1)S(1)}, u32[]{:S(2)}, u32[]{:S(2)}) collective-permute-start(bf16[512,1024]{1,0:T(8,128)(2,1)S(1)} %fusion.34), channel_id=1, source_target_pairs={{0,1},{1,0},{2,3},{3,2},{4,5},{5,4},{6,7},{7,6},{8,9},{9,8},{10,11... | collective-permute-start | bytes 3145736 | tf_op jit(solution)/shard_map/ppermute | solution.py:890
  524.1 69.2 %collective-permute-start.65 = (bf16[2,128,768]{2,1,0:T(8,128)(2,1)}, bf16[2,128,768]{2,1,0:T(8,128)(2,1)S(1)}, u32[]{:S(2)}, u32[]{:S(2)}) collective-permute-start(bf16[2,128,768]{2,1,0:T(8,128)(2,1)} %get-tuple-element.230), channel_id=1, source_target_pairs={{0,4},{4,0},{8,12},{12,8},{1,5},{5,1},{9,13},{13,9},{2,6},{6,2},{1... | collective-permute-start | bytes 1179656 | tf_op jit(solution)/shard_map/ppermute | solution.py:883
  525.0 69.2 %collective-permute-start.66 = (bf16[2,128,768]{2,1,0:T(8,128)(2,1)}, bf16[2,128,768]{2,1,0:T(8,128)(2,1)}, u32[]{:S(2)}, u32[]{:S(2)}) collective-permute-start(bf16[2,128,768]{2,1,0:T(8,128)(2,1)} %get-tuple-element.229), channel_id=1, source_target_pairs={{0,8},{4,12},{8,0},{12,4},{1,9},{5,13},{9,1},{13,5},{2,10},{6,14},... | collective-permute-start | bytes 1179656 | tf_op jit(solution)/shard_map/ppermute | solution.py:883
  526.6 27.6 %collective-permute-start.63 = (bf16[2,256,256]{2,1,0:T(8,128)(2,1)S(1)}, bf16[2,256,256]{2,1,0:T(8,128)(2,1)S(1)}, u32[]{:S(2)}, u32[]{:S(2)}) collective-permute-start(bf16[2,256,256]{2,1,0:T(8,128)(2,1)S(1)} %get-tuple-element.258), channel_id=1, source_target_pairs={{0,4},{4,0},{8,12},{12,8},{1,5},{5,1},{9,13},{13,9},{2,6},{6,2},{1... | collective-permute-start | bytes 786440 | tf_op jit(solution)/shard_map/ppermute | solution.py:883
  527.5 29.0 %collective-permute-start.64 = (bf16[2,256,256]{2,1,0:T(8,128)(2,1)S(1)}, bf16[2,256,256]{2,1,0:T(8,128)(2,1)S(1)}, u32[]{:S(2)}, u32[]{:S(2)}) collective-permute-start(bf16[2,256,256]{2,1,0:T(8,128)(2,1)S(1)} %get-tuple-element.257), channel_id=1, source_target_pairs={{0,8},{4,12},{8,0},{12,4},{1,9},{5,13},{9,1},{13,5},{2,10},{6,14},... | collective-permute-start | bytes 786440 | tf_op jit(solution)/shard_map/ppermute | solution.py:883
  554.2 51.9 %collective-permute-start.67 = (bf16[1056,256]{1,0:T(8,128)(2,1)}, bf16[1056,256]{1,0:T(8,128)(2,1)}, u32[]{:S(2)}, u32[]{:S(2)}) collective-permute-start(bf16[1056,256]{1,0:T(8,128)(2,1)} %get-tuple-element.208), channel_id=1, source_target_pairs={{0,2},{1,0},{3,1},{2,3},{4,6},{5,4},{7,5},{6,7},{8,10},{9,8},{11,9... | collective-permute-start | bytes 1622024 | tf_op jit(solution)/shard_map/ppermute | solution.py:880
  556.6 58.9 %collective-permute-start.68 = (bf16[1056,256]{1,0:T(8,128)(2,1)S(1)}, bf16[1056,256]{1,0:T(8,128)(2,1)}, u32[]{:S(2)}, u32[]{:S(2)}) collective-permute-start(bf16[1056,256]{1,0:T(8,128)(2,1)S(1)} %get-tuple-element.207), channel_id=1, source_target_pairs={{0,3},{1,2},{3,0},{2,1},{4,7},{5,6},{7,4},{6,5},{8,11},{9,10},{11,... | collective-permute-start | bytes 1622024 | tf_op jit(solution)/shard_map/ppermute | solution.py:880
  558.6 36.7 %collective-permute-start.69 = (bf16[256,256]{1,0:T(8,128)(2,1)}, bf16[256,256]{1,0:T(8,128)(2,1)S(1)}, u32[]{:S(2)}, u32[]{:S(2)}) collective-permute-start(bf16[256,256]{1,0:T(8,128)(2,1)} %get-tuple-element.256), channel_id=1, source_target_pairs={{0,4},{4,0},{8,12},{12,8},{1,5},{5,1},{9,13},{13,9},{2,6},{6,2},{1... | collective-permute-start | bytes 393224 | tf_op jit(solution)/shard_map/ppermute | solution.py:883
  594.3 25.9 %collective-permute-start.60 = (bf16[1024,1024]{1,0:T(8,128)(2,1)}, bf16[1024,1024]{1,0:T(8,128)(2,1)S(1)}, u32[]{:S(2)}, u32[]{:S(2)}) collective-permute-start(bf16[1024,1024]{1,0:T(8,128)(2,1)} %get-tuple-element.134.refs_2_), channel_id=1, source_target_pairs={{0,16},{16,0},{1,17},{17,1},{2,18},{18,2},{3,19},{19,3},{4,20},{20... | collective-permute-start | bytes 6291464 | tf_op jit(solution)/shard_map/ppermute | solution.py:872
  615.5 34.8 %collective-permute-start.77 = (bf16[128,256]{1,0:T(8,128)(2,1)}, bf16[128,256]{1,0:T(8,128)(2,1)S(1)}, u32[]{:S(2)}, u32[]{:S(2)}) collective-permute-start(bf16[128,256]{1,0:T(8,128)(2,1)} %get-tuple-element.254), channel_id=1, source_target_pairs={{0,2},{1,0},{3,1},{2,3},{4,6},{5,4},{7,5},{6,7},{8,10},{9,8},{11,9... | collective-permute-start | bytes 196616 | tf_op jit(solution)/shard_map/ppermute | solution.py:880
  616.0 34.9 %collective-permute-start.78 = (bf16[128,256]{1,0:T(8,128)(2,1)}, bf16[128,256]{1,0:T(8,128)(2,1)S(1)}, u32[]{:S(2)}, u32[]{:S(2)}) collective-permute-start(bf16[128,256]{1,0:T(8,128)(2,1)} %get-tuple-element.236), channel_id=1, source_target_pairs={{0,3},{1,2},{3,0},{2,1},{4,7},{5,6},{7,4},{6,5},{8,11},{9,10},{11,... | collective-permute-start | bytes 196616 | tf_op jit(solution)/shard_map/ppermute | solution.py:880
  618.3 34.4 %collective-permute-start.79 = (bf16[128,256]{1,0:T(8,128)(2,1)}, bf16[128,256]{1,0:T(8,128)(2,1)}, u32[]{:S(2)}, u32[]{:S(2)}) collective-permute-start(bf16[128,256]{1,0:T(8,128)(2,1)} %get-tuple-element.235), channel_id=1, source_target_pairs={{0,1},{1,3},{3,2},{2,0},{4,5},{5,7},{7,6},{6,4},{8,9},{9,11},{11,1... | collective-permute-start | bytes 196616 | tf_op jit(solution)/shard_map/ppermute | solution.py:880
  618.6 22.8 %collective-permute-start.73 = (bf16[2,1056,256]{2,1,0:T(8,128)(2,1)}, bf16[2,1056,256]{2,1,0:T(8,128)(2,1)S(1)}, u32[]{:S(2)}, u32[]{:S(2)}) collective-permute-start(bf16[2,1056,256]{2,1,0:T(8,128)(2,1)} %get-tuple-element.206), channel_id=1, source_target_pairs={{0,4},{4,0},{8,12},{12,8},{1,5},{5,1},{9,13},{13,9},{2,6},{6,2},{1... | collective-permute-start | bytes 3244040 | tf_op jit(solution)/shard_map/ppermute | solution.py:883
  620.2 23.3 %collective-permute-start.74 = (bf16[2,1056,256]{2,1,0:T(8,128)(2,1)}, bf16[2,1056,256]{2,1,0:T(8,128)(2,1)}, u32[]{:S(2)}, u32[]{:S(2)}) collective-permute-start(bf16[2,1056,256]{2,1,0:T(8,128)(2,1)} %get-tuple-element.205), channel_id=1, source_target_pairs={{0,8},{4,12},{8,0},{12,4},{1,9},{5,13},{9,1},{13,5},{2,10},{6,14},... | collective-permute-start | bytes 3244040 | tf_op jit(solution)/shard_map/ppermute | solution.py:883
  643.5 51.0 %collective-permute-start.80 = (bf16[2,1056,256]{2,1,0:T(8,128)(2,1)}, bf16[2,1056,256]{2,1,0:T(8,128)(2,1)}, u32[]{:S(2)}, u32[]{:S(2)}) collective-permute-start(bf16[2,1056,256]{2,1,0:T(8,128)(2,1)} %get-tuple-element.204), channel_id=1, source_target_pairs={{0,4},{4,0},{8,12},{12,8},{1,5},{5,1},{9,13},{13,9},{2,6},{6,2},{1... | collective-permute-start | bytes 3244040 | tf_op jit(solution)/shard_map/ppermute | solution.py:883
  650.3 44.2 %collective-permute-start.81 = (bf16[2,1056,256]{2,1,0:T(8,128)(2,1)}, bf16[2,1056,256]{2,1,0:T(8,128)(2,1)S(1)}, u32[]{:S(2)}, u32[]{:S(2)}) collective-permute-start(bf16[2,1056,256]{2,1,0:T(8,128)(2,1)} %get-tuple-element.203), channel_id=1, source_target_pairs={{0,8},{4,12},{8,0},{12,4},{1,9},{5,13},{9,1},{13,5},{2,10},{6,14},... | collective-permute-start | bytes 3244040 | tf_op jit(solution)/shard_map/ppermute | solution.py:883
  651.6 43.0 %collective-permute-start.82 = (bf16[1056,256]{1,0:T(8,128)(2,1)}, bf16[1056,256]{1,0:T(8,128)(2,1)S(1)}, u32[]{:S(2)}, u32[]{:S(2)}) collective-permute-start(bf16[1056,256]{1,0:T(8,128)(2,1)} %get-tuple-element.202), channel_id=1, source_target_pairs={{0,4},{4,0},{8,12},{12,8},{1,5},{5,1},{9,13},{13,9},{2,6},{6,2},{1... | collective-permute-start | bytes 1622024 | tf_op jit(solution)/shard_map/ppermute | solution.py:883
  652.7 41.9 %collective-permute-start.83 = (bf16[1056,256]{1,0:T(8,128)(2,1)}, bf16[1056,256]{1,0:T(8,128)(2,1)S(1)}, u32[]{:S(2)}, u32[]{:S(2)}) collective-permute-start(bf16[1056,256]{1,0:T(8,128)(2,1)} %get-tuple-element.201), channel_id=1, source_target_pairs={{0,8},{4,12},{8,0},{12,4},{1,9},{5,13},{9,1},{13,5},{2,10},{6,14},... | collective-permute-start | bytes 1622024 | tf_op jit(solution)/shard_map/ppermute | solution.py:883
  713.3 25.3 %collective-permute-start.85 = (bf16[512,1024]{1,0:T(8,128)(2,1)S(1)}, bf16[512,1024]{1,0:T(8,128)(2,1)S(1)}, u32[]{:S(2)}, u32[]{:S(2)}) collective-permute-start(bf16[512,1024]{1,0:T(8,128)(2,1)S(1)} %fusion.35), channel_id=1, source_target_pairs={{0,1},{1,0},{2,3},{3,2},{4,5},{5,4},{6,7},{7,6},{8,9},{9,8},{10,11... | collective-permute-start | bytes 3145736 | tf_op jit(solution)/shard_map/ppermute | solution.py:890
  717.9 23.3 %collective-permute-start.101 = (bf16[256,256]{1,0:T(8,128)(2,1)S(1)}, bf16[256,256]{1,0:T(8,128)(2,1)S(1)}, u32[]{:S(2)}, u32[]{:S(2)}) collective-permute-start(bf16[256,256]{1,0:T(8,128)(2,1)S(1)} %get-tuple-element.250), channel_id=1, source_target_pairs={{0,8},{4,12},{8,0},{12,4},{1,9},{5,13},{9,1},{13,5},{2,10},{6,14},... | collective-permute-start | bytes 393224 | tf_op jit(solution)/shard_map/ppermute | solution.py:883
  718.5 24.5 %collective-permute-start.104 = (bf16[256,256]{1,0:T(8,128)(2,1)S(1)}, bf16[256,256]{1,0:T(8,128)(2,1)S(1)}, u32[]{:S(2)}, u32[]{:S(2)}) collective-permute-start(bf16[256,256]{1,0:T(8,128)(2,1)S(1)} %get-tuple-element.251), channel_id=1, source_target_pairs={{0,4},{4,0},{8,12},{12,8},{1,5},{5,1},{9,13},{13,9},{2,6},{6,2},{1... | collective-permute-start | bytes 393224 | tf_op jit(solution)/shard_map/ppermute | solution.py:883
  722.3 22.9 %collective-permute-start.90 = (bf16[2,128,768]{2,1,0:T(8,128)(2,1)S(1)}, bf16[2,128,768]{2,1,0:T(8,128)(2,1)S(1)}, u32[]{:S(2)}, u32[]{:S(2)}) collective-permute-start(bf16[2,128,768]{2,1,0:T(8,128)(2,1)S(1)} %get-tuple-element.224), channel_id=1, source_target_pairs={{0,8},{4,12},{8,0},{12,4},{1,9},{5,13},{9,1},{13,5},{2,10},{6,14},... | collective-permute-start | bytes 1179656 | tf_op jit(solution)/shard_map/ppermute | solution.py:883
  743.0 92.3 %collective-permute-start.95 = (bf16[1056,256]{1,0:T(8,128)(2,1)S(1)}, bf16[1056,256]{1,0:T(8,128)(2,1)S(1)}, u32[]{:S(2)}, u32[]{:S(2)}) collective-permute-start(bf16[1056,256]{1,0:T(8,128)(2,1)S(1)} %get-tuple-element.197), channel_id=1, source_target_pairs={{0,4},{4,0},{8,12},{12,8},{1,5},{5,1},{9,13},{13,9},{2,6},{6,2},{1... | collective-permute-start | bytes 1622024 | tf_op jit(solution)/shard_map/ppermute | solution.py:883
  744.0 37.4 %collective-permute-start.102 = (bf16[128,256]{1,0:T(8,128)(2,1)S(1)}, bf16[128,256]{1,0:T(8,128)(2,1)S(1)}, u32[]{:S(2)}, u32[]{:S(2)}) collective-permute-start(bf16[128,256]{1,0:T(8,128)(2,1)S(1)} %get-tuple-element.249), channel_id=1, source_target_pairs={{0,2},{1,0},{3,1},{2,3},{4,6},{5,4},{7,5},{6,7},{8,10},{9,8},{11,9... | collective-permute-start | bytes 196616 | tf_op jit(solution)/shard_map/ppermute | solution.py:880
  745.3 38.6 %collective-permute-start.89 = (bf16[128,768]{1,0:T(8,128)(2,1)S(1)}, bf16[128,768]{1,0:T(8,128)(2,1)S(1)}, u32[]{:S(2)}, u32[]{:S(2)}) collective-permute-start(bf16[128,768]{1,0:T(8,128)(2,1)S(1)} %get-tuple-element.221), channel_id=1, source_target_pairs={{0,8},{4,12},{8,0},{12,4},{1,9},{5,13},{9,1},{13,5},{2,10},{6,14},... | collective-permute-start | bytes 589832 | tf_op jit(solution)/shard_map/ppermute | solution.py:883
  747.1 38.1 %collective-permute-start.91 = (bf16[128,768]{1,0:T(8,128)(2,1)S(1)}, bf16[128,768]{1,0:T(8,128)(2,1)S(1)}, u32[]{:S(2)}, u32[]{:S(2)}) collective-permute-start(bf16[128,768]{1,0:T(8,128)(2,1)S(1)} %get-tuple-element.222), channel_id=1, source_target_pairs={{0,4},{4,0},{8,12},{12,8},{1,5},{5,1},{9,13},{13,9},{2,6},{6,2},{1... | collective-permute-start | bytes 589832 | tf_op jit(solution)/shard_map/ppermute | solution.py:883
  756.4 25.0 %collective-permute-start.87 = (bf16[512,512]{1,0:T(8,128)(2,1)S(1)}, bf16[512,512]{1,0:T(8,128)(2,1)S(1)}, u32[]{:S(2)}, u32[]{:S(2)}) collective-permute-start(bf16[512,512]{1,0:T(8,128)(2,1)S(1)} %fusion.44), channel_id=1, source_target_pairs={{0,2},{1,3},{2,0},{3,1},{4,6},{5,7},{6,4},{7,5},{8,10},{9,11},{10,... | collective-permute-start | bytes 1572872 | tf_op jit(solution)/shard_map/ppermute | solution.py:886
  781.4 57.0 %collective-permute-start.96 = (bf16[1056,256]{1,0:T(8,128)(2,1)S(1)}, bf16[1056,256]{1,0:T(8,128)(2,1)S(1)}, u32[]{:S(2)}, u32[]{:S(2)}) collective-permute-start(bf16[1056,256]{1,0:T(8,128)(2,1)S(1)} %get-tuple-element.199), channel_id=1, source_target_pairs={{0,2},{1,0},{3,1},{2,3},{4,6},{5,4},{7,5},{6,7},{8,10},{9,8},{11,9... | collective-permute-start | bytes 1622024 | tf_op jit(solution)/shard_map/ppermute | solution.py:880
  781.4 57.0 %collective-permute-start.97 = (bf16[1056,256]{1,0:T(8,128)(2,1)S(1)}, bf16[1056,256]{1,0:T(8,128)(2,1)S(1)}, u32[]{:S(2)}, u32[]{:S(2)}) collective-permute-start(bf16[1056,256]{1,0:T(8,128)(2,1)S(1)} %get-tuple-element.200), channel_id=1, source_target_pairs={{0,3},{1,2},{3,0},{2,1},{4,7},{5,6},{7,4},{6,5},{8,11},{9,10},{11,... | collective-permute-start | bytes 1622024 | tf_op jit(solution)/shard_map/ppermute | solution.py:880
  783.9 26.1 %collective-permute-start.105 = (bf16[128,256]{1,0:T(8,128)(2,1)S(1)}, bf16[128,256]{1,0:T(8,128)(2,1)S(1)}, u32[]{:S(2)}, u32[]{:S(2)}) collective-permute-start(bf16[128,256]{1,0:T(8,128)(2,1)S(1)} %get-tuple-element.233), channel_id=1, source_target_pairs={{0,3},{1,2},{3,0},{2,1},{4,7},{5,6},{7,4},{6,5},{8,11},{9,10},{11,... | collective-permute-start | bytes 196616 | tf_op jit(solution)/shard_map/ppermute | solution.py:880
  785.2 53.1 %collective-permute-start.99 = (bf16[1056,256]{1,0:T(8,128)(2,1)S(1)}, bf16[1056,256]{1,0:T(8,128)(2,1)S(1)}, u32[]{:S(2)}, u32[]{:S(2)}) collective-permute-start(bf16[1056,256]{1,0:T(8,128)(2,1)S(1)} %fusion.20), channel_id=1, source_target_pairs={{0,1},{1,3},{3,2},{2,0},{4,5},{5,7},{7,6},{6,4},{8,9},{9,11},{11,1... | collective-permute-start | bytes 1622024 | tf_op jit(solution)/shard_map/ppermute | solution.py:880
  810.1 25.2 %collective-permute-start.106 = (bf16[128,256]{1,0:T(8,128)(2,1)S(1)}, bf16[128,256]{1,0:T(8,128)(2,1)S(1)}, u32[]{:S(2)}, u32[]{:S(2)}) collective-permute-start(bf16[128,256]{1,0:T(8,128)(2,1)S(1)} %get-tuple-element.234), channel_id=1, source_target_pairs={{0,1},{1,3},{3,2},{2,0},{4,5},{5,7},{7,6},{6,4},{8,9},{9,11},{11,1... | collective-permute-start | bytes 196616 | tf_op jit(solution)/shard_map/ppermute | solution.py:880
  (151 other events, 1656.6 us)
